TPU v7x, 32 devices: a whole 2x2x4 slice. The times are simulated.
32 devices in a mesh: dp: 8 (over y, x, core), seq: 4 (over z).
Axes of the slice: x: 2, y: 2, z: 4, core: 2. Of those that a mesh axis runs over, the one named last changes fastest.
Arguments:
- block_input: float32 [12288, 768], P(('dp', 'seq')), may hold values from -6 to 6
- embedding: float32 [12288, 768], P(('dp', 'seq')), may hold values from -6 to 6
- earlier_outs: float32 [3, 12288, 768], P(None, ('dp', 'seq')), may hold values from -6 to 6
- dwa_weights: float32 [5], replicated, may hold values from 0.3 to 1.2
- ln1_gain: float32 [768], replicated, may hold values from 0.5 to 1.5
- ln1_bias: float32 [768], replicated, may hold values from -2 to 2
- w_qkv: float32 [768, 2304], P('dp'), may hold values from -0.21875 to 0.21875
- w_out: float32 [768, 768], P('dp'), may hold values from -1.75 to 1.75
- ln2_gain: float32 [768], replicated, may hold values from 0.5 to 1.5
- ln2_bias: float32 [768], replicated, may hold values from -2 to 2
- w_up: float32 [768, 3072], P('dp'), may hold values from -0.21875 to 0.21875
- w_down: float32 [3072, 768], P('dp'), may hold values from -0.109375 to 0.109375
- segments: int32 [8, 1536], P('dp', 'seq'), may hold values from 0 to 11, never falling along the last dimension, each value on 1 to 768 neighbouring positions
- cotangent: float32 [12288, 768], P(('dp', 'seq')), may hold values from -6 to 6
Outputs:
- output: float32 [12288, 768], P(('dp', 'seq'))
- grad_input: float32 [12288, 768], P(('dp', 'seq'))
- grad_dwa: float32 [5], replicated
- grad_ln1_gain: float32 [768], replicated
- grad_ln1_bias: float32 [768], replicated
- grad_qkv: float32 [768, 2304], P('dp')
- grad_wout: float32 [768, 768], P('dp')
- grad_ln2_gain: float32 [768], replicated
- grad_ln2_bias: float32 [768], replicated
- grad_up: float32 [768, 3072], P('dp')
- grad_down: float32 [3072, 768], P('dp')
Inputs may be any that keep to these rules, and one draw needn't show every extreme that they name: `segments`: within a sequence the numbers never fall; equal numbers mark one document, of at most 768 tokens.
All inputs are finite; a program needn't handle non-finite values.
Results may differ from a plain program's by a relative error of at most 0.0003.
Values sent between devices are 32-bit elements; how exact they have to be, the bound alone decides.
No kernel may reach another device: no remote copies, remote signals or barrier semaphores. Data moves between devices by JAX's collectives and lax.ppermute only.
A program may use at most 192 MiB of HBM per device.

v0:
```python
import functools
import math

import jax
import jax.numpy as jnp
import numpy as np
from jax import lax
from jax.experimental import pallas as pl
from jax.experimental.pallas import tpu as pltpu
from jax.sharding import PartitionSpec as P

HD = 64
DOC_MOST = 768
LOG2E = math.log2(math.e)
SCALE = 1.0 / math.sqrt(HD)
NEG = -1e30
F32 = jnp.float32
BF16 = jnp.bfloat16
HIGH = lax.Precision.HIGH
VMEM_LIMIT = 56 * 1024 * 1024
BLK = 128


def cost(micros):
    return pl.CostEstimate(
        flops=int(micros * 1.1e9), bytes_accessed=1 << 20, transcendentals=0
    )


def params():
    return pltpu.CompilerParams(
        dimension_semantics=("arbitrary",), vmem_limit_bytes=VMEM_LIMIT
    )


def split(values):
    high = values.astype(BF16)
    return high, (values - high.astype(F32)).astype(BF16)


def dot_nn(left, right):
    return lax.dot_general(left, right, (((1,), (0,)), ((), ())), preferred_element_type=F32)


def dot_nt(left, right):
    return lax.dot_general(left, right, (((1,), (1,)), ((), ())), preferred_element_type=F32)


def dot_tn(left, right):
    return lax.dot_general(left, right, (((0,), (0,)), ((), ())), preferred_element_type=F32)


def three(dot, left, right):
    return (
        dot(left[0], right[0]) + dot(left[0], right[1]) + dot(left[1], right[0])
    )


def norm_stats(values):
    row_mean = jnp.mean(values, axis=-1, keepdims=True)
    centred = values - row_mean
    row_var = jnp.mean(centred * centred, axis=-1, keepdims=True)
    rate = lax.rsqrt(row_var + 1e-05)
    return centred * rate, rate


def turned(values):
    lane = lax.broadcasted_iota(jnp.int32, values.shape, 1)
    return jnp.where(
        (lane & 63) < 32, pltpu.roll(values, 96, 1), pltpu.roll(values, 32, 1)
    )


def rotate(values, cosine, sine):
    return values * cosine + turned(values) * sine


def unrotate(values, cosine, sine):
    return values * cosine - turned(values) * sine


def rotary_tables(length, halo):
    half = HD // 2
    inv_freq = (10000.0 ** (-(np.arange(half, dtype=np.float32) * 2.0 / HD))).astype(np.float32)
    place = np.arange(-halo, length, dtype=np.float32)
    angles = place[:, None] * inv_freq[None, :]
    cosine = np.cos(angles.astype(np.float64)).astype(np.float32)
    sine = np.sin(angles.astype(np.float64)).astype(np.float32)
    return (
        np.concatenate([cosine] * 4, axis=1),
        np.concatenate([-sine, sine, -sine, sine], axis=1),
    )


def qkv_kernel(far_ref, near_ref, own_ref, gain_ref, bias_ref, w_ref, cos_ref, sin_ref,
               q_ref, kv_ref, hi_ref, lo_ref):
    step = pl.program_id(0)
    rows = own_ref.shape[0]
    third = pl.num_programs(0) // 3
    halo = hi_ref.shape[0] - rows

    @pl.when(step == 0)
    def _():
        for at, ref in enumerate((far_ref, near_ref, own_ref)):
            xhat, _ = norm_stats(ref[...])
            high, low = split(xhat * gain_ref[...] + bias_ref[...])
            hi_ref[at * rows:(at + 1) * rows] = high
            lo_ref[at * rows:(at + 1) * rows] = low

    weights = split(w_ref[...])

    @pl.when(step < third)
    def _():
        got = three(dot_nn, (hi_ref[halo:], lo_ref[halo:]), weights)
        for at in range(0, got.shape[1], 128):
            q_ref[:, at:at + 128] = rotate(got[:, at:at + 128], cos_ref[halo:], sin_ref[halo:])

    @pl.when((step >= third) & (step < 2 * third))
    def _():
        got = three(dot_nn, (hi_ref[...], lo_ref[...]), weights)
        for at in range(0, got.shape[1], 128):
            kv_ref[:, at:at + 128] = rotate(got[:, at:at + 128], cos_ref[...], sin_ref[...])

    @pl.when(step >= 2 * third)
    def _():
        kv_ref[...] = three(dot_nn, (hi_ref[...], lo_ref[...]), weights)


def project(far, near, own, gain, bias, w_full, cosine, sine):
    rows, model = own.shape
    total = 3 * rows
    wide = 256
    third = model // wide
    whole = lambda shape: pl.BlockSpec(shape, lambda j: (0, 0))
    return pl.pallas_call(
        qkv_kernel,
        grid=(3 * third,),
        in_specs=[
            whole((rows, model)), whole((rows, model)), whole((rows, model)),
            whole((1, model)), whole((1, model)),
            pl.BlockSpec((model, wide), lambda j: (0, j)),
            whole((total, 128)), whole((total, 128)),
        ],
        out_specs=[
            pl.BlockSpec((rows, wide), lambda j: (0, jnp.minimum(j, third - 1))),
            pl.BlockSpec((total, wide), lambda j: (0, jnp.maximum(j - third, 0))),
            whole((total, model)), whole((total, model)),
        ],
        out_shape=[
            jax.ShapeDtypeStruct((rows, model), F32),
            jax.ShapeDtypeStruct((total, 2 * model), F32),
            jax.ShapeDtypeStruct((total, model), BF16),
            jax.ShapeDtypeStruct((total, model), BF16),
        ],
        cost_estimate=cost(20),
        compiler_params=params(),
    )(far, near, own, gain, bias, w_full, cosine, sine)


def own_pair(values, head):
    lane = lax.broadcasted_iota(jnp.int32, values.shape, 1)
    other = pltpu.roll(values, 64, 1)
    return jnp.where((lane < 64) == (head == 0), values, other)


def outer_form(values, head):
    high, low = split(own_pair(values, head))
    return jnp.concatenate([high, low], axis=1)


def mixed(values, head):
    pair = own_pair(values, head)
    lane = lax.broadcasted_iota(jnp.int32, pair.shape, 1)
    high = pair.astype(BF16).astype(F32)
    return jnp.where(lane < 64, high, pair - high).astype(BF16)


def inner_form(values, head):
    half = mixed(values, head)
    return jnp.concatenate([half, half], axis=1)


def fold(values):
    return values + pltpu.roll(values, 64, 1)


def attend_kernel(q_ref, k_ref, v_ref, segq_ref, segk_ref, out_ref, bias_ref):
    rows = q_ref.shape[0]
    halo = k_ref.shape[0] - rows
    span = halo + BLK

    @pl.when(pl.program_id(0) == 0)
    def _():
        for at in range(0, rows, BLK):
            row = lax.broadcasted_iota(jnp.int32, (BLK, span), 0)
            col = lax.broadcasted_iota(jnp.int32, (BLK, span), 1)
            same = segq_ref[at:at + BLK, :1] == segk_ref[:1, at:at + span]
            bias_ref[at:at + BLK] = jnp.where(same & (col - halo <= row), 0.0, NEG)

    lane = lax.broadcasted_iota(jnp.int32, (BLK, 128), 1)
    scaled = q_ref[...] * (SCALE * LOG2E)
    results = []
    for head in range(2):
        left = inner_form(scaled, head)
        right = outer_form(k_ref[...], head)
        vals = mixed(v_ref[...], head)
        outs = []
        for at in range(0, rows, BLK):
            scores = dot_nt(left[at:at + BLK], right[at:at + span]) + bias_ref[at:at + BLK]
            top = jnp.max(scores, axis=1, keepdims=True)
            expo = jnp.exp2(scores - top)
            total = jnp.sum(expo, axis=1, keepdims=True)
            high, low = split(expo)
            got = dot_nn(high, vals[at:at + span]) + dot_nn(low, vals[at:at + span])
            outs.append(fold(got) / total)
        results.append(outs)
    for at in range(0, rows, BLK):
        out_ref[at:at + BLK] = jnp.where(
            lane < 64, results[0][at // BLK], results[1][at // BLK]
        )


def attend(q_rot, kv, seg_q, seg_k):
    rows, model = q_rot.shape
    total = kv.shape[0]
    pairs = model // 128
    return pl.pallas_call(
        attend_kernel,
        grid=(pairs,),
        in_specs=[
            pl.BlockSpec((rows, 128), lambda p: (0, p)),
            pl.BlockSpec((total, 128), lambda p: (0, p)),
            pl.BlockSpec((total, 128), lambda p: (0, pairs + p)),
            pl.BlockSpec((rows, 128), lambda p: (0, 0)),
            pl.BlockSpec((8, total), lambda p: (0, 0)),
        ],
        out_specs=pl.BlockSpec((rows, 128), lambda p: (0, p)),
        out_shape=jax.ShapeDtypeStruct((rows, model), F32),
        scratch_shapes=[pltpu.VMEM((rows, total - rows + BLK), F32)],
        cost_estimate=cost(24),
        compiler_params=params(),
    )(q_rot, kv, kv, seg_q, seg_k)


def attend_back_kernel(q_ref, k_ref, v_ref, g_ref, segq_ref, segk_ref, cos_ref, sin_ref,
                       dq_ref, dk_ref, dv_ref, bias_ref):
    rows = q_ref.shape[0]
    halo = k_ref.shape[0] - rows
    span = halo + BLK

    @pl.when(pl.program_id(0) == 0)
    def _():
        for at in range(0, rows, BLK):
            key = lax.broadcasted_iota(jnp.int32, (span, BLK), 0)
            query = lax.broadcasted_iota(jnp.int32, (span, BLK), 1)
            same = segk_ref[at:at + span, :1] == segq_ref[:1, at:at + BLK]
            bias_ref[:, at:at + BLK] = jnp.where(same & (key - halo <= query), 0.0, NEG)

    scaled = q_ref[...] * (SCALE * LOG2E)
    dq, dk, dv = [], [], []
    for head in range(2):
        q_in = inner_form(scaled, head)
        g_in = inner_form(g_ref[...], head)
        k_out = outer_form(k_ref[...], head)
        v_out = outer_form(v_ref[...], head)
        q_mix = mixed(q_ref[...], head)
        g_mix = mixed(g_ref[...], head)
        k_mix = mixed(k_ref[...], head)
        dq_head = []
        dk_head = jnp.zeros((halo + rows, 128), F32)
        dv_head = jnp.zeros((halo + rows, 128), F32)
        dk_parts, dv_parts = [], []
        for at in range(0, rows, BLK):
            scores = dot_nt(k_out[at:at + span], q_in[at:at + BLK]) + bias_ref[:, at:at + BLK]
            top = jnp.max(scores, axis=0, keepdims=True)
            expo = jnp.exp2(scores - top)
            inverse = 1.0 / jnp.sum(expo, axis=0, keepdims=True)
            grad_probs = dot_nt(v_out[at:at + span], g_in[at:at + BLK])
            probs = expo * inverse
            delta = jnp.sum(probs * grad_probs, axis=0, keepdims=True)
            grad_scores = probs * (grad_probs - delta)
            probs_cat = jnp.concatenate(split(probs), axis=1)
            scores_cat = jnp.concatenate(split(grad_scores), axis=1)
            g_two = jnp.concatenate([g_mix[at:at + BLK]] * 2, axis=0)
            q_two = jnp.concatenate([q_mix[at:at + BLK]] * 2, axis=0)
            dv_parts.append(dot_nn(probs_cat, g_two))
            dk_parts.append(dot_nn(scores_cat, q_two))
            got = dot_tn(scores_cat, k_mix[at:at + span])
            dq_head.append(fold(got[:BLK] + got[BLK:]))
        for parts, full in ((dk_parts, dk), (dv_parts, dv)):
            pieces = []
            for kb in range((halo + rows) // BLK):
                terms = [
                    parts[qb][(kb - qb) * BLK:(kb - qb + 1) * BLK]
                    for qb in range(rows // BLK)
                    if 0 <= kb - qb < span // BLK
                ]
                pieces.append(fold(functools.reduce(lambda a, b: a + b, terms)))
            full.append(pieces)
        dq.append(dq_head)
    lane = lax.broadcasted_iota(jnp.int32, (BLK, 128), 1)
    for qb in range(rows // BLK):
        rng = slice(qb * BLK, (qb + 1) * BLK)
        far = slice(halo + qb * BLK, halo + (qb + 1) * BLK)
        both = jnp.where(lane < 64, dq[0][qb], dq[1][qb]) * SCALE
        dq_ref[rng] = unrotate(both, cos_ref[far], sin_ref[far])
    for kb in range((halo + rows) // BLK):
        rng = slice(kb * BLK, (kb + 1) * BLK)
        both = jnp.where(lane < 64, dk[0][kb], dk[1][kb]) * SCALE
        dk_ref[rng] = unrotate(both, cos_ref[rng], sin_ref[rng])
        dv_ref[rng] = jnp.where(lane < 64, dv[0][kb], dv[1][kb])


def attend_back(q_rot, kv, grad, seg_q, seg_k, cosine, sine):
    rows, model = q_rot.shape
    total = kv.shape[0]
    pairs = model // 128
    fixed = lambda shape: pl.BlockSpec(shape, lambda p: (0, 0))
    dq, dk, dv = pl.pallas_call(
        attend_back_kernel,
        grid=(pairs,),
        in_specs=[
            pl.BlockSpec((rows, 128), lambda p: (0, p)),
            pl.BlockSpec((total, 128), lambda p: (0, p)),
            pl.BlockSpec((total, 128), lambda p: (0, pairs + p)),
            pl.BlockSpec((rows, 128), lambda p: (0, p)),
            fixed((8, rows)), fixed((total, 128)),
            fixed((total, 128)), fixed((total, 128)),
        ],
        out_specs=[
            pl.BlockSpec((rows, 128), lambda p: (0, p)),
            pl.BlockSpec((total, 128), lambda p: (0, p)),
            pl.BlockSpec((total, 128), lambda p: (0, p)),
        ],
        out_shape=[
            jax.ShapeDtypeStruct((rows, model), F32),
            jax.ShapeDtypeStruct((total, model), F32),
            jax.ShapeDtypeStruct((total, model), F32),
        ],
        scratch_shapes=[pltpu.VMEM((total - rows + BLK, rows), F32)],
        cost_estimate=cost(42),
        compiler_params=params(),
    )(q_rot, kv, kv, grad, seg_q, seg_k, cosine, sine)
    return dq, dk, dv


def mlp_kernel(count, chip_ref, resid_ref, other_ref, cot_ref, cot_other_ref, gain_ref, bias_ref,
               scale_ref, *refs):
    up_refs, down_refs = refs[:count], refs[count:2 * count]
    out_ref, gnorm_ref, grad_ref = refs[2 * count:2 * count + 3]
    (x_hi, x_lo, xt_hi, xt_lo, g_hi, g_lo, up_hi, up_lo, down_hi, down_lo) = refs[2 * count + 3:]
    step = pl.program_id(0)
    rows = resid_ref.shape[0]

    @pl.when(step == 0)
    def _():
        for at, source, cot in ((0, resid_ref, cot_ref), (rows, other_ref, cot_other_ref)):
            xhat, _ = norm_stats(source[...])
            normed = xhat * gain_ref[...] + bias_ref[...]
            x_hi[at:at + rows], x_lo[at:at + rows] = split(normed)
            xt_hi[:, at:at + rows], xt_lo[:, at:at + rows] = split(normed.T)
            g_hi[at:at + rows], g_lo[at:at + rows] = split(cot[...] * scale_ref[0, 0])
        out_ref[...] = jnp.zeros_like(out_ref)
        gnorm_ref[...] = jnp.zeros_like(gnorm_ref)

    for at in range(count):
        spot = (chip_ref[0] ^ at) if count > 1 else 0
        up_rows = up_refs[at].shape[0]
        high, low = split(up_refs[at][...])
        here = pl.ds(pl.multiple_of(spot * up_rows, up_rows), up_rows)
        up_hi[here], up_lo[here] = high, low
        block = down_refs[at][...]
        block = block.reshape(-1, block.shape[-1])
        high, low = split(block)
        here = pl.ds(pl.multiple_of(spot * block.shape[0], block.shape[0]), block.shape[0])
        down_hi[here], down_lo[here] = high, low

    chips, _, tall, width = grad_ref.shape
    up_tall = up_hi.shape[0] // chips
    deep = down_hi.shape[0] // chips
    up = (up_hi[...], up_lo[...])
    down = (down_hi[...], down_lo[...])
    normed = (x_hi[...], x_lo[...])
    normed_t = (xt_hi[...], xt_lo[...])
    grad_block = (g_hi[...], g_lo[...])
    pre = three(dot_nn, normed, up)
    grad_act = three(dot_nt, grad_block, down)
    inner = 0.7978845608028654 * (pre + 0.044715 * pre * pre * pre)
    bent = jnp.tanh(inner)
    act = 0.5 * pre * (1.0 + bent)
    slope = 0.5 * (1.0 + bent) + 0.5 * pre * (1.0 - bent * bent) * (
        0.7978845608028654 * (1.0 + 3.0 * 0.044715 * pre * pre)
    )
    act2 = split(act)
    grad_pre = split(grad_act * slope)
    out_ref[...] += three(dot_nn, act2, down)
    gnorm_ref[...] += three(dot_nt, grad_pre, up)
    gup = three(dot_nn, normed_t, grad_pre)
    gdown = three(dot_tn, act2, grad_block)
    half = deep // 2
    for chip in range(chips):
        grad_ref[chip, 0, :up_tall] = gup[chip * up_tall:(chip + 1) * up_tall]
        part = gdown[chip * deep:(chip + 1) * deep]
        grad_ref[chip, 0, up_tall:up_tall + deep] = part[:, :width]
        grad_ref[chip, 0, up_tall + deep:] = jnp.concatenate(
            [part[:half, width:], part[half:, width:]], axis=1
        )


def mlp(first, steps, chip, chips, resid, other, cot, cot_other, gain, bias, scale, ups, downs):
    rows, model = resid.shape
    width = 512
    up_tall = model // chips
    deep = width // chips
    fixed = lambda shape: pl.BlockSpec(shape, lambda j, c: (0, 0))
    if len(ups) > 1:
        down_spec = pl.BlockSpec((deep, model), lambda j, c: (first + j, 0))
    else:
        downs = [downs[0].reshape(chips, -1, model)]
        down_spec = pl.BlockSpec((chips, deep, model), lambda j, c: (0, first + j, 0))
    tall = up_tall + deep + deep // 2
    grid_spec = pltpu.PrefetchScalarGridSpec(
        num_scalar_prefetch=1,
        grid=(steps,),
        in_specs=[fixed((rows, model))] * 4 + [fixed((1, model))] * 2
        + [pl.BlockSpec(memory_space=pltpu.SMEM)]
        + [pl.BlockSpec((up.shape[0], width), lambda j, c: (0, first + j)) for up in ups]
        + [down_spec] * len(downs),
        out_specs=[
            fixed((2 * rows, model)), fixed((2 * rows, model)),
            pl.BlockSpec((chips, 1, tall, width), lambda j, c: (0, j, 0, 0)),
        ],
        scratch_shapes=[
            pltpu.VMEM((2 * rows, model), BF16), pltpu.VMEM((2 * rows, model), BF16),
            pltpu.VMEM((model, 2 * rows), BF16), pltpu.VMEM((model, 2 * rows), BF16),
            pltpu.VMEM((2 * rows, model), BF16), pltpu.VMEM((2 * rows, model), BF16),
            pltpu.VMEM((model, width), BF16), pltpu.VMEM((model, width), BF16),
            pltpu.VMEM((width, model), BF16), pltpu.VMEM((width, model), BF16),
        ],
    )
    return pl.pallas_call(
        functools.partial(mlp_kernel, len(ups)),
        grid_spec=grid_spec,
        out_shape=[
            jax.ShapeDtypeStruct((2 * rows, model), F32),
            jax.ShapeDtypeStruct((2 * rows, model), F32),
            jax.ShapeDtypeStruct((chips, steps, tall, width), F32),
        ],
        cost_estimate=cost(18 * steps),
        compiler_params=params(),
    )(chip, resid, other, cot, cot_other, gain, bias, scale, *ups, *downs)


def unpack_grads(up, down, sibling_swap, core, chips):
    steps, up_tall, width = up.shape
    deep = up_tall * 2 // 3
    half = up_tall // 2
    mine = jnp.where(core == 0, up[:, :half], up[:, half:])
    other = sibling_swap(jnp.where(core == 0, up[:, half:], up[:, :half]))
    by_core = jnp.stack(
        [jnp.where(core == 0, mine, other), jnp.where(core == 0, other, mine)], axis=0
    )
    by_core = by_core.reshape(2, steps, half, chips, width // chips)
    grad_up = jnp.transpose(by_core, (2, 3, 0, 1, 4)).reshape(half, -1)
    quarter = width // 2
    tail = down[:, deep:]
    right = jnp.concatenate([tail[:, :, :quarter], tail[:, :, quarter:]], axis=1)
    grad_down = jnp.concatenate([down[:, :deep], right], axis=2).reshape(steps * deep, -1)
    return grad_up, grad_down


def weights_kernel(hi_ref, lo_ref, dq_ref, dk_ref, dv_ref, att_ref, res_ref, out_ref,
                   nt_hi, nt_lo, at_hi, at_lo):
    step = pl.program_id(0)
    part = pl.num_programs(0) // 4
    halo = hi_ref.shape[0] - dq_ref.shape[0]

    @pl.when(step == 0)
    def _():
        nt_hi[...] = hi_ref[...].T
        nt_lo[...] = lo_ref[...].T
        at_hi[...], at_lo[...] = split(att_ref[...].T)

    @pl.when(step < part)
    def _():
        out_ref[...] = three(dot_nn, (nt_hi[:, halo:], nt_lo[:, halo:]), split(dq_ref[...]))

    @pl.when((step >= part) & (step < 2 * part))
    def _():
        out_ref[...] = three(dot_nn, (nt_hi[...], nt_lo[...]), split(dk_ref[...]))

    @pl.when((step >= 2 * part) & (step < 3 * part))
    def _():
        out_ref[...] = three(dot_nn, (nt_hi[...], nt_lo[...]), split(dv_ref[...]))

    @pl.when(step >= 3 * part)
    def _():
        out_ref[...] = three(dot_nn, (at_hi[...], at_lo[...]), split(res_ref[...]))


def weight_grads(normed_hi, normed_lo, dq, dk, dv, attended, grad_resid):
    rows, model = dq.shape
    total = dk.shape[0]
    wide = 256
    part = model // wide
    fixed = lambda shape: pl.BlockSpec(shape, lambda j: (0, 0))
    piece = lambda tall, at: pl.BlockSpec(
        (tall, wide), lambda j: (0, jnp.clip(j - at * part, 0, part - 1))
    )
    return pl.pallas_call(
        weights_kernel,
        grid=(4 * part,),
        in_specs=[
            fixed((total, model)), fixed((total, model)),
            piece(rows, 0), piece(total, 1), piece(total, 2),
            fixed((rows, model)), piece(rows, 3),
        ],
        out_specs=pl.BlockSpec((model, wide), lambda j: (0, j)),
        out_shape=jax.ShapeDtypeStruct((model, 4 * model), F32),
        scratch_shapes=[
            pltpu.VMEM((model, total), BF16), pltpu.VMEM((model, total), BF16),
            pltpu.VMEM((model, rows), BF16), pltpu.VMEM((model, rows), BF16),
        ],
        cost_estimate=cost(15),
        compiler_params=params(),
    )(normed_hi, normed_lo, dq, dk, dv, attended, grad_resid)


def norm_back(grad, gain, xhat, rate):
    scaled = grad * gain
    return rate * (
        scaled
        - jnp.mean(scaled, axis=-1, keepdims=True)
        - xhat * jnp.mean(scaled * xhat, axis=-1, keepdims=True)
    )


def matmul(left, right):
    return jnp.dot(left, right, precision=HIGH)


def inner_rows(left, right):
    return lax.dot_general(left, right, (((0,), (0,)), ((), ())), precision=HIGH)


def outer_cols(left, right):
    return lax.dot_general(left, right, (((1,), (1,)), ((), ())), precision=HIGH)


def body(
    block_input,
    embedding,
    earlier_outs,
    dwa_weights,
    ln1_gain,
    ln1_bias,
    w_qkv,
    w_out,
    ln2_gain,
    ln2_bias,
    w_up,
    w_down,
    segments,
    cotangent,
):
    groups = lax.axis_size("seq")
    rows, model = block_input.shape
    length = rows * groups
    halo = 2 * rows
    place = lax.axis_index("seq")
    ahead = [(i, i + 1) for i in range(groups - 1)]
    behind = [(i + 1, i) for i in range(groups - 1)]
    gain1, bias1 = ln1_gain[None], ln1_bias[None]
    gain2, bias2 = ln2_gain[None], ln2_bias[None]

    devices = lax.axis_size("dp")
    chips = devices // 2
    spot = lax.axis_index("dp")
    core = spot % 2
    chip = (spot // 2).reshape(1).astype(jnp.int32)
    same_core = [[2 * i + c for i in range(chips)] for c in range(2)]
    exchange = lambda v, bit: lax.ppermute(v, "dp", [(i, i ^ bit) for i in range(devices)])
    swap = lambda v: exchange(v, 1)

    gather = lambda v: lax.all_gather(v, "dp", axis=0, tiled=True)
    qkv_full = gather(w_qkv)

    shard = w_down.shape[0]
    third = shard // 3
    by_core = w_up.reshape(w_up.shape[0], chips, 2, 3, third)
    by_core = jnp.transpose(by_core, (2, 0, 3, 1, 4)).reshape(2, w_up.shape[0], -1)
    mine = jnp.where(core == 0, by_core[0], by_core[1])
    given = swap(jnp.where(core == 0, by_core[1], by_core[0]))
    up_chip = jnp.concatenate(
        [jnp.where(core == 0, mine, given), jnp.where(core == 0, given, mine)], axis=0
    )
    if chips == 4:
        up_x, down_x = exchange(up_chip, 2), exchange(w_down, 2)
        up_y, down_y = exchange(up_chip, 4), exchange(w_down, 4)
        ups = [up_chip, up_x, up_y, exchange(up_y, 2)]
        downs = [w_down, down_x, down_y, exchange(down_x, 4)]
    else:
        ups, downs = (
            [lax.all_gather(v, "dp", axis=0, tiled=True, axis_index_groups=same_core)]
            for v in (up_chip, w_down)
        )

    seg_own = segments + 1
    near = lax.ppermute(block_input, "seq", ahead)
    seg_near = lax.ppermute(seg_own, "seq", ahead)
    far = lax.ppermute(near, "seq", ahead)
    seg_far = lax.ppermute(seg_near, "seq", ahead)
    seg_all = jnp.concatenate([seg_far, seg_near, seg_own], axis=1)
    seg_k_row = jnp.broadcast_to(seg_all, (8, halo + rows))
    seg_k_col = jnp.broadcast_to(seg_all.reshape(-1, 1), (halo + rows, 128))
    seg_q_row = seg_k_row[:, halo:]
    seg_q_col = seg_k_col[halo:]

    cos_all, sin_all = rotary_tables(length, halo)
    cosine = lax.dynamic_slice_in_dim(jnp.asarray(cos_all), place * rows, halo + rows, 0)
    sine = lax.dynamic_slice_in_dim(jnp.asarray(sin_all), place * rows, halo + rows, 0)

    q_rot, kv, normed_hi, normed_lo = project(
        far, near, block_input, gain1, bias1, qkv_full, cosine, sine
    )
    attended = attend(q_rot, kv, seg_q_col, seg_k_row)

    out_full = gather(w_out)
    resid = block_input + matmul(attended, out_full)
    resid_other = swap(resid)
    cot_other = swap(cotangent)
    scale = dwa_weights[4].reshape(1, 1)
    call = functools.partial(
        mlp, chip=chip, chips=chips, resid=resid, other=resid_other, cot=cotangent,
        cot_other=cot_other, gain=gain2, bias=bias2, scale=scale, ups=ups, downs=downs,
    )
    scatter = lambda v: lax.psum_scatter(v, "dp", scatter_dimension=0, tiled=True)
    scatter_chips = lambda v: lax.psum_scatter(
        v, "dp", scatter_dimension=0, tiled=True, axis_index_groups=same_core
    )
    out_a, gnorm_a, grads_a = call(0, 1)
    shard_a = scatter_chips(grads_a)[0]
    out_b, gnorm_b, grads_b = call(1, 2)
    shard_b = scatter_chips(grads_b)[0]
    grad_normed_two = gnorm_a[:rows] + gnorm_b[:rows] + swap(gnorm_a[rows:] + gnorm_b[rows:])
    mlp_out = out_a[:rows] + out_b[:rows] + swap(out_a[rows:] + out_b[rows:])

    block_out = resid + mlp_out
    output = (
        dwa_weights[0] * embedding
        + dwa_weights[1] * earlier_outs[0]
        + dwa_weights[2] * earlier_outs[1]
        + dwa_weights[3] * earlier_outs[2]
        + dwa_weights[4] * block_out
    )
    dwa_local = jnp.stack(
        [
            jnp.sum(cotangent * embedding),
            jnp.sum(cotangent * earlier_outs[0]),
            jnp.sum(cotangent * earlier_outs[1]),
            jnp.sum(cotangent * earlier_outs[2]),
            jnp.sum(cotangent * block_out),
        ]
    )
    xhat2, rate2 = norm_stats(resid)
    grad_resid = dwa_weights[4] * cotangent + norm_back(grad_normed_two, gain2, xhat2, rate2)
    grad_gain_two = jnp.sum(grad_normed_two * xhat2, axis=0)
    grad_bias_two = jnp.sum(grad_normed_two, axis=0)
    grad_attended = outer_cols(grad_resid, out_full)

    dq, dk, dv = attend_back(
        q_rot, kv, grad_attended, seg_q_row, seg_k_col, cosine, sine
    )
    shard_c = scatter(
        weight_grads(normed_hi, normed_lo, dq, dk, dv, attended, grad_resid)
    )
    dkv = jnp.concatenate([dk, dv], axis=1)

    wq, wkv = qkv_full[:, :model], qkv_full[:, model:]
    partial = outer_cols(dkv, wkv)
    own_part = partial[halo:] + outer_cols(dq, wq)
    back_near = partial[rows:halo] + lax.ppermute(partial[:rows], "seq", behind)
    grad_normed_one = own_part + lax.ppermute(back_near, "seq", behind)
    xhat1, rate1 = norm_stats(block_input)
    grad_input = grad_resid + norm_back(grad_normed_one, gain1, xhat1, rate1)
    grad_gain_one = jnp.sum(grad_normed_one * xhat1, axis=0)
    grad_bias_one = jnp.sum(grad_normed_one, axis=0)

    shard = jnp.concatenate([shard_a, shard_b], axis=0)
    tall = shard.shape[1] // 2
    halves = (shard[:, :tall], shard[:, tall:])
    even = place % 2 == 0
    shift = lambda v, bit: lax.ppermute(v, "seq", [(i, i ^ bit) for i in range(groups)])
    kept = jnp.where(even, halves[0], halves[1])
    kept = kept + shift(jnp.where(even, halves[1], halves[0]), 1)
    bit = 2
    while bit < groups:
        kept = kept + shift(kept, bit)
        bit *= 2
    other = shift(kept, 1)
    grad_up, grad_down = unpack_grads(
        jnp.where(even, kept, other), jnp.where(even, other, kept), swap, core, chips
    )
    sum_c = lax.psum(shard_c, "seq")
    grad_qkv, grad_wout = sum_c[:, :3 * model], sum_c[:, 3 * model:]

    small = jnp.concatenate(
        [
            grad_gain_one[None], grad_bias_one[None], grad_gain_two[None], grad_bias_two[None],
            jnp.pad(dwa_local, (0, model - 5))[None], jnp.zeros((3, model), F32),
        ],
        axis=0,
    )
    bit = 1
    while bit < devices:
        small = small + exchange(small, bit)
        bit *= 2
    bit = 1
    while bit < groups:
        small = small + shift(small, bit)
        bit *= 2
    gain_one, bias_one, gain_two, bias_two = small[0], small[1], small[2], small[3]
    grad_dwa = small[4, :5]
    return (
        output,
        grad_input,
        grad_dwa,
        gain_one,
        bias_one,
        grad_qkv,
        grad_wout,
        gain_two,
        bias_two,
        grad_up,
        grad_down,
    )


def solution(mesh):
    in_specs = (
        P(("dp", "seq"), None),
        P(("dp", "seq"), None),
        P(None, ("dp", "seq"), None),
        P(),
        P(),
        P(),
        P("dp", None),
        P("dp", None),
        P(),
        P(),
        P("dp", None),
        P("dp", None),
        P("dp", "seq"),
        P(("dp", "seq"), None),
    )
    out_specs = (
        P(("dp", "seq"), None),
        P(("dp", "seq"), None),
        P(),
        P(),
        P(),
        P("dp", None),
        P("dp", None),
        P(),
        P(),
        P("dp", None),
        P("dp", None),
    )
    return jax.shard_map(body, mesh=mesh, in_specs=in_specs, out_specs=out_specs, check_vma=False)
```

profile of v0, /device:TPU:0, one launch (start us, length us, event | category | flops | bytes accessed | tf_op | source)
XLA Modules:
  0.0 514.5 jit_solution(3178349233633098348)
XLA Ops:
  8.0 1.9 reshape.95
  11.9 5.5 %collective-permute-start = (f32[384,768]{1,0:T(8,128)S(1)}, f32[384,768]{1,0:T(8,128)}, u32[]{:S(2)}, u32[]{:S(2)}) collective-permute-start(f32[384,768]{1,0:T(8,128)S(1)} %copy-done), channel_id=1, source_target_pairs={{0,1},{1,2},{2,3},{4,5},{5,6},{6,7},{8,9},{9,10},{10,11},{12,13},{... | collective-permute-start | bytes 3538952 | tf_op jit(solution)/shard_map/ppermute | solution.py:609
  19.6 1.6 collective-permute-start.8
  21.1 21.1 %collective-permute-done.near_ref = f32[384,768]{1,0:T(8,128)} collective-permute-done((f32[384,768]{1,0:T(8,128)S(1)}, f32[384,768]{1,0:T(8,128)}, u32[]{:S(2)}, u32[]{:S(2)}) %collective-permute-start) | collective-permute-done | bytes 1179680 | tf_op jit(solution)/shard_map/ppermute | solution.py:609
  42.2 5.5 %collective-permute-start.1 = (f32[384,768]{1,0:T(8,128)}, f32[384,768]{1,0:T(8,128)}, u32[]{:S(2)}, u32[]{:S(2)}) collective-permute-start(f32[384,768]{1,0:T(8,128)} %collective-permute-done.near_ref), channel_id=1, source_target_pairs={{0,1},{1,2},{2,3},{4,5},{5,6},{6,7},{8,9},{9,10},{10,11},{12,13},{... | collective-permute-start | bytes 3538952 | tf_op jit(solution)/shard_map/ppermute | solution.py:611
  47.8 2.4 collective-permute-start.2
  50.3 1.6 collective-permute-start.11
  51.9 20.2 %collective-permute-done.2 = s32[1,384]{1,0:T(1,128)S(1)} collective-permute-done((s32[1,384]{1,0:T(1,128)S(1)}, s32[1,384]{1,0:T(1,128)S(1)}, u32[]{:S(2)}, u32[]{:S(2)}) %collective-permute-start.2) | collective-permute-done | bytes 1568 | tf_op jit(solution)/shard_map/ppermute | solution.py:610
  72.1 4.4 collective-permute-start.3
  76.5 2.2 constant_dynamic-slice_fusion
  79.9 1.6 collective-permute-start.7
  81.5 1.5 collective-permute-start.12
  83.5 6.6 %all-gather.3.cloned.1.call-done.w_ref = f32[768,2304]{1,0:T(8,128)} async-done(((f32[96,2304]{1,0:T(8,128)}), f32[768,2304]{1,0:T(8,128)}) %all-gather.3.cloned.1.call-update) | async-done | bytes 7077904 | tf_op jit(solution)/shard_map/all_gather | solution.py:585
  90.2 21.5 %shard_map.239 = (f32[384,768]{1,0:T(8,128)}, f32[1152,1536]{1,0:T(8,128)}, bf16[1152,768]{1,0:T(8,128)(2,1)}, bf16[1152,768]{1,0:T(8,128)(2,1)}) custom-call(f32[384,768]{1,0:T(8,128)} %collective-permute-done.1.far_ref, f32[384,768]{1,0:T(8,128)} %collective-permute-done.near_ref, f32[384,768]{1,0:T(8,128)} %own_ref.1, ...), custom_call_target="tpu_custom_call" | custom-call | flops 22000001024 | bytes 1048576 | tf_op jit(solution)/shard_map/pallas_call | solution.py:135
  113.1 23.6 %shard_map.240.att_ref = f32[384,768]{1,0:T(8,128)} custom-call(f32[384,768]{1,0:T(8,128)} %get-tuple-element.24.q_ref, f32[1152,1536]{1,0:T(8,128)} %get-tuple-element.25.k_ref.v_ref, f32[1152,1536]{1,0:T(8,128)} %get-tuple-element.25.k_ref.v_ref, s32[384,128]{1,0:T(8,128)} %broadcast_in_dim.56.segq_ref, s32[8,1152]{1,0:T(8,128)} %broadcast_in_dim.58.segk_ref), custom_call_target="tpu_custom_call" | custom-call | flops 26400000000 | bytes 1048576 | tf_op jit(solution)/shard_map/pallas_call | solution.py:227
  136.8 4.4 fusion.25
  146.0 19.3 %shard_map.241 = (f32[768,768]{1,0:T(8,128)}, f32[768,768]{1,0:T(8,128)}, f32[4,1,384,512]{3,2,1,0:T(8,128)}) custom-call(s32[1]{0:T(128)} %bitcast.8.chip_ref, f32[384,768]{1,0:T(8,128)} %copy-done.3, f32[384,768]{1,0:T(8,128)} %copy-done.35, f32[384,768]{1,0:T(8,128)} %cot_ref.3, f32[384,768]{1,0:T(8,128)} %collective-permute-done.5.cot_other_ref, ...), custom_call_target="tpu_custom_call" | custom-call | flops 19800000512 | bytes 1048576 | tf_op jit(solution)/shard_map/pallas_call | solution.py:441
  165.4 35.4 %shard_map.242 = (f32[768,768]{1,0:T(8,128)}, f32[768,768]{1,0:T(8,128)}, f32[4,2,384,512]{3,2,1,0:T(8,128)}) custom-call(s32[1]{0:T(128)} %bitcast.8.chip_ref, f32[384,768]{1,0:T(8,128)} %copy-done.3, f32[384,768]{1,0:T(8,128)} %copy-done.35, f32[384,768]{1,0:T(8,128)} %cot_ref.3, f32[384,768]{1,0:T(8,128)} %collective-permute-done.5.cot_other_ref, ...), custom_call_target="tpu_custom_call" | custom-call | flops 39600001024 | bytes 1048576 | tf_op jit(solution)/shard_map/pallas_call | solution.py:441
  200.9 1.6 copy-done.15
  202.4 1.6 slice_add_fusion.1
  204.5 1.6 slice_add_fusion.2
  209.6 4.8 multiply_reduce_fusion
  214.4 2.8 fusion.26.g_ref
  218.7 43.1 %shard_map.243 = (f32[384,768]{1,0:T(8,128)}, f32[1152,768]{1,0:T(8,128)}, f32[1152,768]{1,0:T(8,128)}) custom-call(f32[384,768]{1,0:T(8,128)} %get-tuple-element.24.q_ref, f32[1152,1536]{1,0:T(8,128)} %get-tuple-element.25.k_ref.v_ref, f32[1152,1536]{1,0:T(8,128)} %get-tuple-element.25.k_ref.v_ref, f32[384,768]{1,0:T(8,128)} %fusion.26.g_ref, ...), custom_call_target="tpu_custom_call" | custom-call | flops 46200000512 | bytes 1048576 | tf_op jit(solution)/shard_map/pallas_call | solution.py:319
  261.8 22.6 %shard_map.244 = f32[768,3072]{1,0:T(8,128)} custom-call(bf16[1152,768]{1,0:T(8,128)(2,1)} %get-tuple-element.33.hi_ref, bf16[1152,768]{1,0:T(8,128)(2,1)} %get-tuple-element.34.lo_ref, f32[384,768]{1,0:T(8,128)} %get-tuple-element.32.dq_ref, f32[1152,768]{1,0:T(8,128)} %get-tuple-element.30.dk_ref, f32[1152,768]{1,0:T(8,128)} %get-tuple-element.31.dv_ref, ...), custom_call_target="tpu_custom_call" | custom-call | flops 16499999744 | bytes 1048576 | tf_op jit(solution)/shard_map/pallas_call | solution.py:510
  284.5 12.4 %fusion = f32[1152,768]{1,0:T(8,128)S(1)} fusion(f32[1152,768]{1,0:T(8,128)} %get-tuple-element.31.dv_ref, f32[1152,768]{1,0:T(8,128)} %get-tuple-element.30.dk_ref, f32[768,2304]{1,0:T(8,128)} %all-gather.3.cloned.1.call-done.w_ref), kind=kOutput, calls=%fused_computation | convolution fusion | flops 8155496448 | bytes 15335424 | tf_op jit(solution)/shard_map/dot_general | solution.py:547
  299.4 2.4 broadcast_select_fusion.2
  301.8 2.5 collective-permute-start.22
  304.3 24.7 %collective-permute-done.15 = f32[384,768]{1,0:T(8,128)} collective-permute-done((f32[384,768]{1,0:T(8,128)}, f32[384,768]{1,0:T(8,128)}, u32[]{:S(2)}, u32[]{:S(2)}) %collective-permute-start.15) | collective-permute-done | bytes 1179680 | tf_op jit(solution)/shard_map/ppermute | solution.py:682
  329.1 2.4 slice_add_fusion
  331.5 1.6 collective-permute-start.16
  333.1 21.2 %collective-permute-done.22 = f32[3,192,512]{2,1,0:T(8,128)S(1)} collective-permute-done((f32[3,192,512]{2,1,0:T(8,128)S(1)}, f32[3,192,512]{2,1,0:T(8,128)S(1)}, u32[]{:S(2)}, u32[]{:S(2)}) %collective-permute-start.22) | collective-permute-done | bytes 1179680 | tf_op jit(solution)/shard_map/ppermute | solution.py:693
  354.7 2.7 collective-permute-start.23
  357.9 3.3 stack.32
  362.9 35.6 %collective-permute-done.16 = f32[384,768]{1,0:T(8,128)} collective-permute-done((f32[384,768]{1,0:T(8,128)}, f32[384,768]{1,0:T(8,128)}, u32[]{:S(2)}, u32[]{:S(2)}) %collective-permute-start.16) | collective-permute-done | bytes 1179680 | tf_op jit(solution)/shard_map/ppermute | solution.py:683
  398.5 5.3 %multiply_reduce_fusion.3 = (f32[768]{0:T(1024)S(1)}, f32[384]{0:T(512)}, f32[384]{0:T(512)}, f32[768]{0:T(1024)S(1)}, f32[384,768]{1,0:T(8,128)S(1)}) fusion(f32[384,768]{1,0:T(8,128)S(1)} %copy-done.2, f32[384]{0:T(512)S(1)} %add_rsqrt_fusion, f32[384]{0:T(512)S(1)} %broadcast_multiply_fusion.2, f32[768]{0:T(1024)S(1)} %copy-done.22, ...), kind=kOutput, calls=%fused_computation.35 | convolution fusion | flops 1362196224 | bytes 8272896 | tf_op jit(solution)/shard_map/dot_general | solution.py:547
  408.5 1.6 collective-permute-start.18
  410.1 2.0 collective-permute-done.23
  412.1 1.9 add.146
  414.1 6.2 %fusion.15 = f32[384,768]{1,0:T(8,128)} fusion(f32[384,768]{1,0:T(8,128)} %get-tuple-element.57, f32[384,768]{1,0:T(8,128)} %param.17, f32[3,384,768]{2,1,0:T(8,128)S(1)} %copy-done.6, f32[]{:T(128)} %bitcast.7, f32[]{:T(128)} %bitcast.5, f32[]{:T(128)} %bitcast.3, f32[]{:T(128)} %bitcast.1, f32[]{:T(128)} %bitcast), kind=kLoop, calls=%fused_computation.21 | loop fusion | flops 2654208 | bytes 7077908 | tf_op jit(solution)/shard_map/add | solution.py:650
  421.5 2.8 collective-permute-done.19
  424.3 2.0 collective-permute-start.20
  426.3 14.5 %collective-permute-done.20 = f32[8,768]{1,0:T(8,128)S(1)} collective-permute-done((f32[8,768]{1,0:T(8,128)S(1)}, f32[8,768]{1,0:T(8,128)S(1)}, u32[]{:S(2)}, u32[]{:S(2)}) %collective-permute-start.20) | collective-permute-done | bytes 24608 | tf_op jit(solution)/shard_map/ppermute | solution.py:693
  442.2 3.3 collective-permute-done.21
  446.1 1.5 broadcast_select_fusion
  449.6 50.6 %all-reduce.5.cloned.1.call-done = f32[96,3072]{1,0:T(8,128)} async-done(((f32[96,3072]{1,0:T(8,128)}), f32[96,3072]{1,0:T(8,128)}) %all-reduce.5.cloned.1.call-update) | async-done | bytes 1179664 | tf_op jit(solution)/shard_map/psum | solution.py:704
  500.2 2.1 slice.181
  502.3 1.7 slice.182
  (176 shorter events, 36.9 us)
Async XLA Ops:
  7.2 83.0 %all-gather.3.cloned.1.call-start = ((), (), s32[]{:S(2)}) async-start(), calls=%async_computation.3 | async-start | bytes 7962624 | tf_op jit(solution)/shard_map/all_gather | solution.py:585
  7.9 128.9 %all-gather.5.cloned.1.call-start = ((), (), s32[]{:S(2)}) async-start(), calls=%async_computation.4 | async-start | bytes 2654208 | tf_op jit(solution)/shard_map/all_gather | solution.py:585
  11.4 7.9 %collective-permute-start.6 = (f32[96,1536]{1,0:T(8,128)}, f32[96,1536]{1,0:T(8,128)S(1)}, u32[]{:S(2)}, u32[]{:S(2)}) collective-permute-start(f32[96,1536]{1,0:T(8,128)} %select_n.95), channel_id=1, source_target_pairs={{0,4},{4,0},{8,12},{12,8},{16,20},{20,16},{24,28},{28,24},{1,5},{5... | collective-permute-start | bytes 1769480 | tf_op jit(solution)/shard_map/ppermute | solution.py:582
  11.9 30.4 %collective-permute-start = (f32[384,768]{1,0:T(8,128)S(1)}, f32[384,768]{1,0:T(8,128)}, u32[]{:S(2)}, u32[]{:S(2)}) collective-permute-start(f32[384,768]{1,0:T(8,128)S(1)} %copy-done), channel_id=1, source_target_pairs={{0,1},{1,2},{2,3},{4,5},{5,6},{6,7},{8,9},{9,10},{10,11},{12,13},{... | collective-permute-start | bytes 3538952 | tf_op jit(solution)/shard_map/ppermute | solution.py:609
  17.4 62.5 %collective-permute-start.10 = (f32[384,768]{1,0:T(8,128)}, f32[384,768]{1,0:T(8,128)}, u32[]{:S(2)}, u32[]{:S(2)}) collective-permute-start(f32[384,768]{1,0:T(8,128)} %refs_4_.3), channel_id=1, source_target_pairs={{0,8},{4,12},{8,0},{12,4},{16,24},{20,28},{24,16},{28,20},{1,9},{5... | collective-permute-start | bytes 3538952 | tf_op jit(solution)/shard_map/ppermute | solution.py:582
  19.4 28.3 %copy-start.34 = (s32[1,384]{1,0:T(1,128)S(1)}, s32[1,384]{1,0:T(1,128)}, u32[]{:S(2)}) copy-start(s32[1,384]{1,0:T(1,128)} %param.28) | copy-start | bytes 4612
  19.5 57.1 %copy-start.20 = (f32[2304,128]{1,0:T(8,128)S(1)}, f32[2304,128]{1,0:T(8,128)}, u32[]{:S(2)}) copy-start(f32[2304,128]{1,0:T(8,128)} %constant.63.clone) | copy-start | bytes 3538948
  19.6 60.4 %copy-start.19 = (f32[192,1536]{1,0:T(8,128)}, f32[192,1536]{1,0:T(8,128)S(1)}, u32[]{:S(2)}) copy-start(f32[192,1536]{1,0:T(8,128)S(1)} %pad_maximum_fusion.1.refs_0_) | copy-start | bytes 3538948
  19.6 61.9 %collective-permute-start.8 = (f32[192,1536]{1,0:T(8,128)S(1)}, f32[192,1536]{1,0:T(8,128)}, u32[]{:S(2)}, u32[]{:S(2)}) collective-permute-start(f32[192,1536]{1,0:T(8,128)S(1)} %pad_maximum_fusion.1.refs_0_), channel_id=1, source_target_pairs={{0,16},{4,20},{8,24},{12,28},{16,0},{20,4},{24,8},{28,12},{1,17},{... | collective-permute-start | bytes 3538952 | tf_op jit(solution)/shard_map/ppermute | solution.py:582
  42.2 40.8 %collective-permute-start.1 = (f32[384,768]{1,0:T(8,128)}, f32[384,768]{1,0:T(8,128)}, u32[]{:S(2)}, u32[]{:S(2)}) collective-permute-start(f32[384,768]{1,0:T(8,128)} %collective-permute-done.near_ref), channel_id=1, source_target_pairs={{0,1},{1,2},{2,3},{4,5},{5,6},{6,7},{8,9},{9,10},{10,11},{12,13},{... | collective-permute-start | bytes 3538952 | tf_op jit(solution)/shard_map/ppermute | solution.py:611
  47.8 24.3 %collective-permute-start.2 = (s32[1,384]{1,0:T(1,128)S(1)}, s32[1,384]{1,0:T(1,128)S(1)}, u32[]{:S(2)}, u32[]{:S(2)}) collective-permute-start(s32[1,384]{1,0:T(1,128)S(1)} %get-tuple-element.70), channel_id=1, source_target_pairs={{0,1},{1,2},{2,3},{4,5},{5,6},{6,7},{8,9},{9,10},{10,11},{12,13},{... | collective-permute-start | bytes 4616 | tf_op jit(solution)/shard_map/ppermute | solution.py:610
  50.3 90.9 %collective-permute-start.11 = (f32[384,768]{1,0:T(8,128)}, f32[384,768]{1,0:T(8,128)}, u32[]{:S(2)}, u32[]{:S(2)}) collective-permute-start(f32[384,768]{1,0:T(8,128)} %refs_4_.3), channel_id=1, source_target_pairs={{0,16},{4,20},{8,24},{12,28},{16,0},{20,4},{24,8},{28,12},{1,17},{... | collective-permute-start | bytes 3538952 | tf_op jit(solution)/shard_map/ppermute | solution.py:582
  51.9 247.5 %reduce-scatter.10.cloned.1.call-start = ((), (), s32[]{:S(2)}) async-start(), calls=%async_computation.7 | async-start | bytes 3932160
  51.9 26.8 %copy-start.21 = (f32[768]{0:T(1024)S(1)}, f32[768]{0:T(1024)}, u32[]{:S(2)}) copy-start(f32[768]{0:T(1024)} %param.20) | copy-start | bytes 9220
  51.9 27.4 %copy-start.33 = (f32[768]{0:T(1024)S(1)}, f32[768]{0:T(1024)}, u32[]{:S(2)}) copy-start(f32[768]{0:T(1024)} %param.21) | copy-start | bytes 9220
  72.1 7.8 %collective-permute-start.3 = (s32[1,384]{1,0:T(1,128)S(1)}, s32[1,384]{1,0:T(1,128)S(1)}, u32[]{:S(2)}, u32[]{:S(2)}) collective-permute-start(s32[1,384]{1,0:T(1,128)S(1)} %collective-permute-done.2), channel_id=1, source_target_pairs={{0,1},{1,2},{2,3},{4,5},{5,6},{6,7},{8,9},{9,10},{10,11},{12,13},{... | collective-permute-start | bytes 4616 | tf_op jit(solution)/shard_map/ppermute | solution.py:612
  79.9 65.0 %collective-permute-start.5 = (f32[384,768]{1,0:T(8,128)}, f32[384,768]{1,0:T(8,128)}, u32[]{:S(2)}, u32[]{:S(2)}) collective-permute-start(f32[384,768]{1,0:T(8,128)} %cot_ref.3), channel_id=1, source_target_pairs={{0,4},{4,0},{8,12},{12,8},{16,20},{20,16},{24,28},{28,24},{1,5},{5... | collective-permute-start | bytes 3538952 | tf_op jit(solution)/shard_map/ppermute | solution.py:582
  79.9 65.0 %collective-permute-start.7 = (f32[192,1536]{1,0:T(8,128)S(1)}, f32[192,1536]{1,0:T(8,128)}, u32[]{:S(2)}, u32[]{:S(2)}) collective-permute-start(f32[192,1536]{1,0:T(8,128)S(1)} %pad_maximum_fusion.1.refs_0_), channel_id=1, source_target_pairs={{0,8},{4,12},{8,0},{12,4},{16,24},{20,28},{24,16},{28,20},{1,9},{5... | collective-permute-start | bytes 3538952 | tf_op jit(solution)/shard_map/ppermute | solution.py:582
  81.5 63.5 %collective-permute-start.12 = (f32[384,768]{1,0:T(8,128)}, f32[384,768]{1,0:T(8,128)}, u32[]{:S(2)}, u32[]{:S(2)}) collective-permute-start(f32[384,768]{1,0:T(8,128)} %collective-permute-done.10.refs_5_), channel_id=1, source_target_pairs={{0,16},{4,20},{8,24},{12,28},{16,0},{20,4},{24,8},{28,12},{1,17},{... | collective-permute-start | bytes 3538952 | tf_op jit(solution)/shard_map/ppermute | solution.py:582
  83.0 61.9 %collective-permute-start.9 = (f32[192,1536]{1,0:T(8,128)}, f32[192,1536]{1,0:T(8,128)}, u32[]{:S(2)}, u32[]{:S(2)}) collective-permute-start(f32[192,1536]{1,0:T(8,128)} %collective-permute-done.8.refs_2_), channel_id=1, source_target_pairs={{0,8},{4,12},{8,0},{12,4},{16,24},{20,28},{24,16},{28,20},{1,9},{5... | collective-permute-start | bytes 3538952 | tf_op jit(solution)/shard_map/ppermute | solution.py:582
  113.1 23.7 %copy-start.1 = (f32[384,768]{1,0:T(8,128)S(1)}, f32[384,768]{1,0:T(8,128)}, u32[]{:S(2)}) copy-start(f32[384,768]{1,0:T(8,128)} %own_ref.1) | copy-start | bytes 3538948
  141.2 3.8 collective-permute-start.4
  165.4 134.1 %reduce-scatter.12.cloned.1.call-start = ((), (), s32[]{:S(2)}) async-start(), calls=%async_computation.8 | async-start | bytes 7864320
  200.8 245.3 %reduce-scatter.8.cloned.1.call-start = ((), (), s32[]{:S(2)}) async-start(), calls=%async_computation.5 | async-start | bytes 10616832 | tf_op jit(solution)/shard_map/reduce_scatter | solution.py:637
  204.0 2.9 collective-permute-start.14
  206.1 2.9 collective-permute-start.13
  284.5 215.7 %all-reduce.5.cloned.1.call-start = ((), (), s32[]{:S(2)}) async-start(), calls=%async_computation.6 | async-start | bytes 2359296 | tf_op jit(solution)/shard_map/psum | solution.py:704
  296.9 32.2 %copy-start.13 = (f32[1152,768]{1,0:T(8,128)}, f32[1152,768]{1,0:T(8,128)S(1)}, u32[]{:S(2)}) copy-start(f32[1152,768]{1,0:T(8,128)S(1)} %fusion) | copy-start | bytes 10616836
  298.1 31.0 %collective-permute-start.15 = (f32[384,768]{1,0:T(8,128)}, f32[384,768]{1,0:T(8,128)}, u32[]{:S(2)}, u32[]{:S(2)}) collective-permute-start(f32[384,768]{1,0:T(8,128)} %slice.177), channel_id=1, source_target_pairs={{1,0},{2,1},{3,2},{5,4},{6,5},{7,6},{9,8},{10,9},{11,10},{13,12},{... | collective-permute-start | bytes 3538952 | tf_op jit(solution)/shard_map/ppermute | solution.py:682
  301.8 52.5 %copy-start.10 = (f32[1,2,384,512]{3,2,1,0:T(8,128)S(1)}, f32[1,2,384,512]{3,2,1,0:T(8,128)}, u32[]{:S(2)}) copy-start(f32[1,2,384,512]{3,2,1,0:T(8,128)} %reduce-scatter.12.cloned.1.call-done) | copy-start | bytes 4718596
  301.8 52.4 %copy-start.14 = (f32[1,1,384,512]{3,2,1,0:T(8,128)S(1)}, f32[1,1,384,512]{3,2,1,0:T(8,128)}, u32[]{:S(2)}) copy-start(f32[1,1,384,512]{3,2,1,0:T(8,128)} %reduce-scatter.10.cloned.1.call-done) | copy-start | bytes 2359300
  301.8 52.4 %collective-permute-start.22 = (f32[3,192,512]{2,1,0:T(8,128)S(1)}, f32[3,192,512]{2,1,0:T(8,128)S(1)}, u32[]{:S(2)}, u32[]{:S(2)}) collective-permute-start(f32[3,192,512]{2,1,0:T(8,128)S(1)} %broadcast_select_fusion.2), channel_id=1, source_target_pairs={{0,1},{1,0},{2,3},{3,2},{4,5},{5,4},{6,7},{7,6},{8,9},{9,8},{10,11... | collective-permute-start | bytes 3538952 | tf_op jit(solution)/shard_map/ppermute | solution.py:693
  331.5 25.9 %copy-start.2 = (f32[384,768]{1,0:T(8,128)S(1)}, f32[384,768]{1,0:T(8,128)}, u32[]{:S(2)}) copy-start(f32[384,768]{1,0:T(8,128)} %own_ref.1) | copy-start | bytes 3538948
  331.5 67.0 %collective-permute-start.16 = (f32[384,768]{1,0:T(8,128)}, f32[384,768]{1,0:T(8,128)}, u32[]{:S(2)}, u32[]{:S(2)}) collective-permute-start(f32[384,768]{1,0:T(8,128)} %slice_add_fusion), channel_id=1, source_target_pairs={{1,0},{2,1},{3,2},{5,4},{6,5},{7,6},{9,8},{10,9},{11,10},{13,12},{... | collective-permute-start | bytes 3538952 | tf_op jit(solution)/shard_map/ppermute | solution.py:683
  354.7 43.9 %copy-start.22 = (f32[768]{0:T(1024)S(1)}, f32[768]{0:T(1024)}, u32[]{:S(2)}) copy-start(f32[768]{0:T(1024)} %param.20) | copy-start | bytes 9220
  354.7 57.4 %collective-permute-start.23 = (f32[3,192,512]{2,1,0:T(8,128)S(1)}, f32[3,192,512]{2,1,0:T(8,128)}, u32[]{:S(2)}, u32[]{:S(2)}) collective-permute-start(f32[3,192,512]{2,1,0:T(8,128)S(1)} %select_add_fusion), channel_id=1, source_target_pairs={{0,2},{1,3},{2,0},{3,1},{4,6},{5,7},{6,4},{7,5},{8,10},{9,11},{10,... | collective-permute-start | bytes 3538952 | tf_op jit(solution)/shard_map/ppermute | solution.py:693
  357.6 46.3 %copy-start.24 = (f32[384]{0:T(512)}, f32[384]{0:T(512)S(1)}, u32[]{:S(2)}) copy-start(f32[384]{0:T(512)S(1)} %broadcast_multiply_fusion.2) | copy-start | bytes 4612
  357.8 46.0 %copy-start.26 = (f32[384]{0:T(512)}, f32[384]{0:T(512)S(1)}, u32[]{:S(2)}) copy-start(f32[384]{0:T(512)S(1)} %add_rsqrt_fusion) | copy-start | bytes 4612
  406.4 1.4 collective-permute-start.17
  408.5 11.8 %collective-permute-start.18 = (f32[8,768]{1,0:T(8,128)S(1)}, f32[8,768]{1,0:T(8,128)S(1)}, u32[]{:S(2)}, u32[]{:S(2)}) collective-permute-start(f32[8,768]{1,0:T(8,128)S(1)} %add.139), channel_id=1, source_target_pairs={{0,8},{4,12},{8,0},{12,4},{16,24},{20,28},{24,16},{28,20},{1,9},{5... | collective-permute-start | bytes 73736 | tf_op jit(solution)/shard_map/ppermute | solution.py:582
  414.0 32.1 %collective-permute-start.24 = (f32[3,192,512]{2,1,0:T(8,128)S(1)}, f32[3,192,512]{2,1,0:T(8,128)}, u32[]{:S(2)}, u32[]{:S(2)}) collective-permute-start(f32[3,192,512]{2,1,0:T(8,128)S(1)} %add.146), channel_id=1, source_target_pairs={{0,1},{1,0},{2,3},{3,2},{4,5},{5,4},{6,7},{7,6},{8,9},{9,8},{10,11... | collective-permute-start | bytes 3538952 | tf_op jit(solution)/shard_map/ppermute | solution.py:693
  414.1 26.6 %copy-start.8 = (f32[384,768]{1,0:T(8,128)S(1)}, f32[384,768]{1,0:T(8,128)}, u32[]{:S(2)}) copy-start(f32[384,768]{1,0:T(8,128)} %copy-done.7) | copy-start | bytes 3538948
  414.1 26.6 %copy-start.25 = (f32[384]{0:T(512)S(1)}, f32[384]{0:T(512)}, u32[]{:S(2)}) copy-start(f32[384]{0:T(512)} %copy-done.24) | copy-start | bytes 4612
  414.1 26.6 %copy-start.27 = (f32[384]{0:T(512)S(1)}, f32[384]{0:T(512)}, u32[]{:S(2)}) copy-start(f32[384]{0:T(512)} %copy-done.26) | copy-start | bytes 4612
  420.4 3.9 collective-permute-start.19
  424.3 16.5 %collective-permute-start.20 = (f32[8,768]{1,0:T(8,128)S(1)}, f32[8,768]{1,0:T(8,128)S(1)}, u32[]{:S(2)}, u32[]{:S(2)}) collective-permute-start(f32[8,768]{1,0:T(8,128)S(1)} %add.141), channel_id=1, source_target_pairs={{0,1},{1,0},{2,3},{3,2},{4,5},{5,4},{6,7},{7,6},{8,9},{9,8},{10,11... | collective-permute-start | bytes 73736 | tf_op jit(solution)/shard_map/ppermute | solution.py:693
  440.8 4.7 collective-permute-start.21
  447.8 56.2 %collective-permute-start.25 = (f32[3,96,512]{2,1,0:T(8,128)S(1)}, f32[3,96,512]{2,1,0:T(8,128)S(1)}, u32[]{:S(2)}, u32[]{:S(2)}) collective-permute-start(f32[3,96,512]{2,1,0:T(8,128)S(1)} %slice_select_fusion.2), channel_id=1, source_target_pairs={{0,4},{4,0},{8,12},{12,8},{16,20},{20,16},{24,28},{28,24},{1,5},{5... | collective-permute-start | bytes 1769480 | tf_op jit(solution)/shard_map/ppermute | solution.py:582
  (20 other events, 79.3 us)
Sparse Core Ops, SparseCore 0:
  9.9 80.2 all-gather.2
  92.1 38.7 all-gather.4
  165.5 43.6 reduce-scatter.9
  212.0 70.1 reduce-scatter.11
  285.6 76.4 reduce-scatter.7
  446.3 53.8 all-reduce.4
where the time goes:
time: 523 us; the launch traced here: 514 us
  waiting for transfers between devices  206 us (39%)
  Pallas kernels  166 us (32%)
  starting transfers between devices  40.4 us (8%)
  local copies, waits for them, and re-layouts  33.6 us (6%)
  other arithmetic  29.3 us (6%)
  matrix products  24.8 us (5%)
  between operations  15 us (3%)
    pallas_call x2, Pallas kernels, mlp(): pl.pallas_call(functools.partial(mlp_kernel, len(ups)), grid_spec=grid_sp...  54.7 us
    psum x1, waiting for transfers between devices, body(): sum_c = lax.psum(shard_c, 'seq')  50.6 us
    pallas_call x1, Pallas kernels, attend_back(): pl.pallas_call(attend_back_kernel, grid=(pairs,), in_specs=[pl.BlockSpec(...  43.1 us
    ppermute x5, waiting for transfers between devices, body(): lax.ppermute(v, 'seq', [(i, i ^ bit) for i in range(groups)])  40.9 us
    ppermute x1, waiting for transfers between devices, body(): grad_normed_one = own_part + lax.ppermute(back_near, 'seq', behind)  35.6 us
    ppermute x1, waiting for transfers between devices, body(): back_near = partial[rows:halo] + lax.ppermute(partial[:rows], 'seq', behind)  24.7 us
    pallas_call x1, Pallas kernels, attend(): pl.pallas_call(attend_kernel, grid=(pairs,), in_specs=[pl.BlockSpec((rows...  23.6 us
    pallas_call x1, Pallas kernels, weight_grads(): pl.pallas_call(weights_kernel, grid=(4 * part,), in_specs=[fixed((total,...  22.6 us
  transfers between devices with their start and end apart: 32, of which 14 were waited for; matrix products, arithmetic and copies ran while one was open for 16% of the time, Pallas kernels for 28%

commit v1 on v0

--- a/solution.py
+++ b/solution.py
@@ -242,8 +242,8 @@
     )(q_rot, kv, kv, seg_q, seg_k)
 
 
-def attend_back_kernel(q_ref, k_ref, v_ref, g_ref, segq_ref, segk_ref, cos_ref, sin_ref,
-                       dq_ref, dk_ref, dv_ref, bias_ref):
+def attend_back_kernel(q_ref, k_ref, v_ref, g_ref, segq_ref, segk_ref, cos_ref, sin_ref, *refs):
+    dq_ref, dk_ref, dv_ref, bias_ref = refs[-4:]
     rows = q_ref.shape[0]
     halo = k_ref.shape[0] - rows
     span = halo + BLK
@@ -311,26 +311,26 @@
         dv_ref[rng] = jnp.where(lane < 64, dv[0][kb], dv[1][kb])
 
 
-def attend_back(q_rot, kv, grad, seg_q, seg_k, cosine, sine):
+def attend_back(first, count, q_rot, kv, grad, seg_q, seg_k, cosine, sine, before=()):
     rows, model = q_rot.shape
     total = kv.shape[0]
     pairs = model // 128
     fixed = lambda shape: pl.BlockSpec(shape, lambda p: (0, 0))
-    dq, dk, dv = pl.pallas_call(
+    return pl.pallas_call(
         attend_back_kernel,
-        grid=(pairs,),
+        grid=(count,),
         in_specs=[
-            pl.BlockSpec((rows, 128), lambda p: (0, p)),
-            pl.BlockSpec((total, 128), lambda p: (0, p)),
-            pl.BlockSpec((total, 128), lambda p: (0, pairs + p)),
-            pl.BlockSpec((rows, 128), lambda p: (0, p)),
+            pl.BlockSpec((rows, 128), lambda p: (0, first + p)),
+            pl.BlockSpec((total, 128), lambda p: (0, first + p)),
+            pl.BlockSpec((total, 128), lambda p: (0, pairs + first + p)),
+            pl.BlockSpec((rows, 128), lambda p: (0, first + p)),
             fixed((8, rows)), fixed((total, 128)),
             fixed((total, 128)), fixed((total, 128)),
-        ],
+        ] + [pl.BlockSpec(memory_space=pl.ANY)] * len(before),
         out_specs=[
-            pl.BlockSpec((rows, 128), lambda p: (0, p)),
-            pl.BlockSpec((total, 128), lambda p: (0, p)),
-            pl.BlockSpec((total, 128), lambda p: (0, p)),
+            pl.BlockSpec((rows, 128), lambda p: (0, first + p)),
+            pl.BlockSpec((total, 128), lambda p: (0, first + p)),
+            pl.BlockSpec((total, 128), lambda p: (0, first + p)),
         ],
         out_shape=[
             jax.ShapeDtypeStruct((rows, model), F32),
@@ -338,17 +338,19 @@
             jax.ShapeDtypeStruct((total, model), F32),
         ],
         scratch_shapes=[pltpu.VMEM((total - rows + BLK, rows), F32)],
-        cost_estimate=cost(42),
+        input_output_aliases={8 + i: i for i in range(len(before))},
+        cost_estimate=cost(7 * count),
         compiler_params=params(),
-    )(q_rot, kv, kv, grad, seg_q, seg_k, cosine, sine)
-    return dq, dk, dv
-
-
-def mlp_kernel(count, chip_ref, resid_ref, other_ref, cot_ref, cot_other_ref, gain_ref, bias_ref,
+    )(q_rot, kv, kv, grad, seg_q, seg_k, cosine, sine, *before)
+
+
+def mlp_kernel(count, begun, chip_ref, resid_ref, other_ref, cot_ref, cot_other_ref, gain_ref, bias_ref,
                scale_ref, *refs):
     up_refs, down_refs = refs[:count], refs[count:2 * count]
-    out_ref, gnorm_ref, grad_ref = refs[2 * count:2 * count + 3]
-    (x_hi, x_lo, xt_hi, xt_lo, g_hi, g_lo, up_hi, up_lo, down_hi, down_lo) = refs[2 * count + 3:]
+    refs = refs[2 * count:]
+    so_far, refs = refs[:2 * begun], refs[2 * begun:]
+    out_ref, gnorm_ref, grad_ref = refs[:3]
+    (x_hi, x_lo, xt_hi, xt_lo, g_hi, g_lo, up_hi, up_lo, down_hi, down_lo) = refs[3:]
     step = pl.program_id(0)
     rows = resid_ref.shape[0]
 
@@ -360,8 +362,12 @@
             x_hi[at:at + rows], x_lo[at:at + rows] = split(normed)
             xt_hi[:, at:at + rows], xt_lo[:, at:at + rows] = split(normed.T)
             g_hi[at:at + rows], g_lo[at:at + rows] = split(cot[...] * scale_ref[0, 0])
-        out_ref[...] = jnp.zeros_like(out_ref)
-        gnorm_ref[...] = jnp.zeros_like(gnorm_ref)
+        if begun:
+            out_ref[...] = so_far[0][...]
+            gnorm_ref[...] = so_far[1][...]
+        else:
+            out_ref[...] = jnp.zeros_like(out_ref)
+            gnorm_ref[...] = jnp.zeros_like(gnorm_ref)
 
     for at in range(count):
         spot = (chip_ref[0] ^ at) if count > 1 else 0
@@ -407,7 +413,7 @@
         )
 
 
-def mlp(first, steps, chip, chips, resid, other, cot, cot_other, gain, bias, scale, ups, downs):
+def mlp(first, steps, so_far, chip, chips, resid, other, cot, cot_other, gain, bias, scale, ups, downs):
     rows, model = resid.shape
     width = 512
     up_tall = model // chips
@@ -425,7 +431,8 @@
         in_specs=[fixed((rows, model))] * 4 + [fixed((1, model))] * 2
         + [pl.BlockSpec(memory_space=pltpu.SMEM)]
         + [pl.BlockSpec((up.shape[0], width), lambda j, c: (0, first + j)) for up in ups]
-        + [down_spec] * len(downs),
+        + [down_spec] * len(downs)
+        + [fixed((2 * rows, model))] * len(so_far),
         out_specs=[
             fixed((2 * rows, model)), fixed((2 * rows, model)),
             pl.BlockSpec((chips, 1, tall, width), lambda j, c: (0, j, 0, 0)),
@@ -439,7 +446,7 @@
         ],
     )
     return pl.pallas_call(
-        functools.partial(mlp_kernel, len(ups)),
+        functools.partial(mlp_kernel, len(ups), len(so_far) // 2),
         grid_spec=grid_spec,
         out_shape=[
             jax.ShapeDtypeStruct((2 * rows, model), F32),
@@ -448,7 +455,7 @@
         ],
         cost_estimate=cost(18 * steps),
         compiler_params=params(),
-    )(chip, resid, other, cot, cot_other, gain, bias, scale, *ups, *downs)
+    )(chip, resid, other, cot, cot_other, gain, bias, scale, *ups, *downs, *so_far)
 
 
 def unpack_grads(up, down, sibling_swap, core, chips):
@@ -469,11 +476,38 @@
     return grad_up, grad_down
 
 
-def weights_kernel(hi_ref, lo_ref, dq_ref, dk_ref, dv_ref, att_ref, res_ref, out_ref,
-                   nt_hi, nt_lo, at_hi, at_lo):
+def place_rows(core_ref, out_ref, got):
+    chips = out_ref.shape[1]
+    tall = out_ref.shape[2]
+    for block in range(2 * chips):
+        out_ref[(block & 1) ^ core_ref[0], block // 2] = got[block * tall:(block + 1) * tall]
+
+
+def weights_qk_kernel(core_ref, hi_ref, lo_ref, dq_ref, dk_ref, out_ref, nt_hi, nt_lo):
     step = pl.program_id(0)
-    part = pl.num_programs(0) // 4
+    part = pl.num_programs(0) // 2
     halo = hi_ref.shape[0] - dq_ref.shape[0]
+
+    @pl.when(step == 0)
+    def _():
+        nt_hi[...] = hi_ref[...].T
+        nt_lo[...] = lo_ref[...].T
+
+    @pl.when(step < part)
+    def _():
+        left = (nt_hi[:, halo:], nt_lo[:, halo:])
+        place_rows(core_ref, out_ref, three(dot_nn, left, split(dq_ref[...])))
+
+    @pl.when(step >= part)
+    def _():
+        left = (nt_hi[...], nt_lo[...])
+        place_rows(core_ref, out_ref, three(dot_nn, left, split(dk_ref[...])))
+
+
+def weights_vo_kernel(core_ref, hi_ref, lo_ref, dv_ref, att_ref, res_ref, out_ref,
+                      nt_hi, nt_lo, at_hi, at_lo):
+    step = pl.program_id(0)
+    part = pl.num_programs(0) // 2
 
     @pl.when(step == 0)
     def _():
@@ -483,47 +517,41 @@
 
     @pl.when(step < part)
     def _():
-        out_ref[...] = three(dot_nn, (nt_hi[:, halo:], nt_lo[:, halo:]), split(dq_ref[...]))
-
-    @pl.when((step >= part) & (step < 2 * part))
-    def _():
-        out_ref[...] = three(dot_nn, (nt_hi[...], nt_lo[...]), split(dk_ref[...]))
-
-    @pl.when((step >= 2 * part) & (step < 3 * part))
-    def _():
-        out_ref[...] = three(dot_nn, (nt_hi[...], nt_lo[...]), split(dv_ref[...]))
-
-    @pl.when(step >= 3 * part)
-    def _():
-        out_ref[...] = three(dot_nn, (at_hi[...], at_lo[...]), split(res_ref[...]))
-
-
-def weight_grads(normed_hi, normed_lo, dq, dk, dv, attended, grad_resid):
-    rows, model = dq.shape
-    total = dk.shape[0]
+        left = (nt_hi[...], nt_lo[...])
+        place_rows(core_ref, out_ref, three(dot_nn, left, split(dv_ref[...])))
+
+    @pl.when(step >= part)
+    def _():
+        left = (at_hi[...], at_lo[...])
+        place_rows(core_ref, out_ref, three(dot_nn, left, split(res_ref[...])))
+
+
+def weight_call(kernel, micros, core, chips, fixed_args, pieces, scratch):
+    model = fixed_args[0].shape[1]
     wide = 256
     part = model // wide
-    fixed = lambda shape: pl.BlockSpec(shape, lambda j: (0, 0))
-    piece = lambda tall, at: pl.BlockSpec(
-        (tall, wide), lambda j: (0, jnp.clip(j - at * part, 0, part - 1))
-    )
+    tall = model // chips // 2
+    fixed = lambda v: pl.BlockSpec(v.shape, lambda j, c: (0, 0))
+    piece = lambda v, at: pl.BlockSpec(
+        (v.shape[0], wide), lambda j, c: (0, jnp.clip(j - at * part, 0, part - 1))
+    )
+    specs, args = [], []
+    for value, at in pieces:
+        args.append(value)
+        specs.append(fixed(value) if at is None else piece(value, at))
     return pl.pallas_call(
-        weights_kernel,
-        grid=(4 * part,),
-        in_specs=[
-            fixed((total, model)), fixed((total, model)),
-            piece(rows, 0), piece(total, 1), piece(total, 2),
-            fixed((rows, model)), piece(rows, 3),
-        ],
-        out_specs=pl.BlockSpec((model, wide), lambda j: (0, j)),
-        out_shape=jax.ShapeDtypeStruct((model, 4 * model), F32),
-        scratch_shapes=[
-            pltpu.VMEM((model, total), BF16), pltpu.VMEM((model, total), BF16),
-            pltpu.VMEM((model, rows), BF16), pltpu.VMEM((model, rows), BF16),
-        ],
-        cost_estimate=cost(15),
+        kernel,
+        grid_spec=pltpu.PrefetchScalarGridSpec(
+            num_scalar_prefetch=1,
+            grid=(2 * part,),
+            in_specs=[fixed(v) for v in fixed_args] + specs,
+            out_specs=pl.BlockSpec((2, chips, tall, wide), lambda j, c: (0, 0, 0, j)),
+            scratch_shapes=[pltpu.VMEM((model, n), BF16) for n in scratch],
+        ),
+        out_shape=jax.ShapeDtypeStruct((2, chips, tall, 2 * model), F32),
+        cost_estimate=cost(micros),
         compiler_params=params(),
-    )(normed_hi, normed_lo, dq, dk, dv, attended, grad_resid)
+    )(core, *fixed_args, *args)
 
 
 def norm_back(grad, gain, xhat, rate):
@@ -638,12 +666,12 @@
     scatter_chips = lambda v: lax.psum_scatter(
         v, "dp", scatter_dimension=0, tiled=True, axis_index_groups=same_core
     )
-    out_a, gnorm_a, grads_a = call(0, 1)
+    out_part, gnorm_part, grads_a = call(0, 1, ())
     shard_a = scatter_chips(grads_a)[0]
-    out_b, gnorm_b, grads_b = call(1, 2)
+    out_part, gnorm_part, grads_b = call(1, 2, (out_part, gnorm_part))
     shard_b = scatter_chips(grads_b)[0]
-    grad_normed_two = gnorm_a[:rows] + gnorm_b[:rows] + swap(gnorm_a[rows:] + gnorm_b[rows:])
-    mlp_out = out_a[:rows] + out_b[:rows] + swap(out_a[rows:] + out_b[rows:])
+    grad_normed_two = gnorm_part[:rows] + swap(gnorm_part[rows:])
+    mlp_out = out_part[:rows] + swap(out_part[rows:])
 
     block_out = resid + mlp_out
     output = (
@@ -668,12 +696,50 @@
     grad_bias_two = jnp.sum(grad_normed_two, axis=0)
     grad_attended = outer_cols(grad_resid, out_full)
 
-    dq, dk, dv = attend_back(
-        q_rot, kv, grad_attended, seg_q_row, seg_k_col, cosine, sine
-    )
-    shard_c = scatter(
-        weight_grads(normed_hi, normed_lo, dq, dk, dv, attended, grad_resid)
-    )
+    back_args = (q_rot, kv, grad_attended, seg_q_row, seg_k_col, cosine, sine)
+    pairs = model // 128
+    first_half = attend_back(0, pairs // 2, *back_args)
+    shift = lambda v, bit: lax.ppermute(v, "seq", [(i, i ^ bit) for i in range(groups)])
+    even = place % 2 == 0
+
+    def line_start(shard):
+        tall = shard.shape[1] // 2
+        halves = (shard[:, :tall], shard[:, tall:])
+        kept = jnp.where(even, halves[0], halves[1])
+        return kept + shift(jnp.where(even, halves[1], halves[0]), 1)
+
+    def line_middle(kept):
+        bit = 2
+        while bit < groups:
+            kept = kept + shift(kept, bit)
+            bit *= 2
+        return kept
+
+    def line_end(kept):
+        other = shift(kept, 1)
+        return jnp.where(even, kept, other), jnp.where(even, other, kept)
+
+    line_sum = lambda shard: line_end(line_middle(line_start(shard)))
+
+    kept_a = line_start(shard_a)
+    kept_a, back_args, first_half = lax.optimization_barrier((kept_a, back_args, first_half))
+    kept_a = line_middle(kept_a)
+    dq, dk, dv = attend_back(pairs // 2, pairs - pairs // 2, *back_args, before=first_half)
+    kept_a, dq, dk, dv = lax.optimization_barrier((kept_a, dq, dk, dv))
+    core_at = core.reshape(1).astype(jnp.int32)
+    normed_parts = (normed_hi, normed_lo)
+    grads_qk = weight_call(
+        weights_qk_kernel, 9, core_at, chips, normed_parts, [(dq, 0), (dk, 1)], [halo + rows] * 2
+    )
+    grads_vo = weight_call(
+        weights_vo_kernel, 9, core_at, chips, normed_parts,
+        [(dv, 0), (attended, None), (grad_resid, 1)], [halo + rows] * 2 + [rows] * 2,
+    )
+    shard_c = scatter_chips(
+        jnp.concatenate(
+            [grads_qk[0] + swap(grads_qk[1]), grads_vo[0] + swap(grads_vo[1])], axis=2
+        )
+    )[0]
     dkv = jnp.concatenate([dk, dv], axis=1)
 
     wq, wkv = qkv_full[:, :model], qkv_full[:, model:]
@@ -686,20 +752,12 @@
     grad_gain_one = jnp.sum(grad_normed_one * xhat1, axis=0)
     grad_bias_one = jnp.sum(grad_normed_one, axis=0)
 
-    shard = jnp.concatenate([shard_a, shard_b], axis=0)
-    tall = shard.shape[1] // 2
-    halves = (shard[:, :tall], shard[:, tall:])
-    even = place % 2 == 0
-    shift = lambda v, bit: lax.ppermute(v, "seq", [(i, i ^ bit) for i in range(groups)])
-    kept = jnp.where(even, halves[0], halves[1])
-    kept = kept + shift(jnp.where(even, halves[1], halves[0]), 1)
-    bit = 2
-    while bit < groups:
-        kept = kept + shift(kept, bit)
-        bit *= 2
-    other = shift(kept, 1)
     grad_up, grad_down = unpack_grads(
-        jnp.where(even, kept, other), jnp.where(even, other, kept), swap, core, chips
+        *(
+            jnp.concatenate(parts, axis=0)
+            for parts in zip(line_end(kept_a), line_sum(shard_b))
+        ),
+        swap, core, chips,
     )
     sum_c = lax.psum(shard_c, "seq")
     grad_qkv, grad_wout = sum_c[:, :3 * model], sum_c[:, 3 * model:]

time: 523 us -> 533 us (1.019)
  waiting for transfers between devices: 206 us -> 195 us
  Pallas kernels: 166 us -> 175 us
  other arithmetic: 29.3 us -> 36.1 us
    pallas_call x4 -> x6, Pallas kernels: 120 us -> 130 us  [the longest x2 56.3 us: mlp(): pl.pallas_call(functools.partial(mlp_kernel, len(ups), len(so_far) // 2),...]
    ppermute x1, waiting for transfers between devices: 35.6 us -> 29.1 us  [body(): grad_normed_one = own_part + lax.ppermute(back_near, 'seq', behind)]
    add x5 -> x7, other arithmetic: 11.7 us -> 6.8 us  [the longest x2 2.45 us: line_middle(): kept = kept + shift(kept, bit)]
    ppermute x5 -> x8, waiting for transfers between devices: 40.9 us -> 39.2 us  [body(): lax.ppermute(v, 'seq', [(i, i ^ bit) for i in range(groups)])]
    ppermute x15 -> x17, starting transfers between devices: 12.1 us -> 12.5 us  [body(): lax.ppermute(v, 'dp', [(i, i ^ bit) for i in range(devices)])]
  transfers between devices with their start and end apart: 32 -> 37, of which waited for: 14 -> 15; matrix products, arithmetic and copies ran while one was open for 16% -> 17% of each run, Pallas kernels for 28% -> 30%
where the time goes in v1:
time: 533 us; the launch traced here: 524 us
  waiting for transfers between devices  195 us (37%)
  Pallas kernels  175 us (33%)
  starting transfers between devices  42.7 us (8%)
  local copies, waits for them, and re-layouts  36.2 us (7%)
  other arithmetic  36.1 us (7%)
  matrix products  24.8 us (5%)
  between operations  15 us (3%)
    pallas_call x2, Pallas kernels, mlp(): pl.pallas_call(functools.partial(mlp_kernel, len(ups), len(so_far) // 2),...  56.3 us
    pallas_call x2, Pallas kernels, attend_back(): pl.pallas_call(attend_back_kernel, grid=(count,), in_specs=[pl.BlockSpec(...  47.2 us
    psum x1, waiting for transfers between devices, body(): sum_c = lax.psum(shard_c, 'seq')  46.8 us
    ppermute x8, waiting for transfers between devices, body(): lax.ppermute(v, 'seq', [(i, i ^ bit) for i in range(groups)])  39.2 us
    ppermute x1, waiting for transfers between devices, body(): grad_normed_one = own_part + lax.ppermute(back_near, 'seq', behind)  29.1 us
    pallas_call x2, Pallas kernels, weight_call(): pl.pallas_call(kernel, grid_spec=pltpu.PrefetchScalarGridSpec(num_scalar_...  26.1 us
    ppermute x1, waiting for transfers between devices, body(): back_near = partial[rows:halo] + lax.ppermute(partial[:rows], 'seq', behind)  24.5 us
    pallas_call x1, Pallas kernels, attend(): pl.pallas_call(attend_kernel, grid=(pairs,), in_specs=[pl.BlockSpec((rows...  23.6 us
  transfers between devices with their start and end apart: 37, of which 15 were waited for; matrix products, arithmetic and copies ran while one was open for 17% of the time, Pallas kernels for 30%

profile of v1, /device:TPU:0, one launch (start us, length us, event | category | flops | bytes accessed | tf_op | source)
XLA Modules:
  0.0 524.2 jit_solution(17800177429369893571)
XLA Ops:
  8.0 1.9 reshape.98
  11.9 5.5 %collective-permute-start = (f32[384,768]{1,0:T(8,128)S(1)}, f32[384,768]{1,0:T(8,128)}, u32[]{:S(2)}, u32[]{:S(2)}) collective-permute-start(f32[384,768]{1,0:T(8,128)S(1)} %copy-done), channel_id=1, source_target_pairs={{0,1},{1,2},{2,3},{4,5},{5,6},{6,7},{8,9},{9,10},{10,11},{12,13},{... | collective-permute-start | bytes 3538952 | tf_op jit(solution)/shard_map/ppermute | solution.py:637
  22.1 20.2 %collective-permute-done.near_ref = f32[384,768]{1,0:T(8,128)} collective-permute-done((f32[384,768]{1,0:T(8,128)S(1)}, f32[384,768]{1,0:T(8,128)}, u32[]{:S(2)}, u32[]{:S(2)}) %collective-permute-start) | collective-permute-done | bytes 1179680 | tf_op jit(solution)/shard_map/ppermute | solution.py:637
  42.2 5.5 %collective-permute-start.1 = (f32[384,768]{1,0:T(8,128)}, f32[384,768]{1,0:T(8,128)}, u32[]{:S(2)}, u32[]{:S(2)}) collective-permute-start(f32[384,768]{1,0:T(8,128)} %collective-permute-done.near_ref), channel_id=1, source_target_pairs={{0,1},{1,2},{2,3},{4,5},{5,6},{6,7},{8,9},{9,10},{10,11},{12,13},{... | collective-permute-start | bytes 3538952 | tf_op jit(solution)/shard_map/ppermute | solution.py:639
  47.8 2.5 collective-permute-start.2
  50.3 1.6 collective-permute-start.11
  52.0 20.1 %collective-permute-done.2 = s32[1,384]{1,0:T(1,128)S(1)} collective-permute-done((s32[1,384]{1,0:T(1,128)S(1)}, s32[1,384]{1,0:T(1,128)S(1)}, u32[]{:S(2)}, u32[]{:S(2)}) %collective-permute-start.2) | collective-permute-done | bytes 1568 | tf_op jit(solution)/shard_map/ppermute | solution.py:638
  72.1 4.4 collective-permute-start.3
  79.6 1.6 collective-permute-start.7
  83.2 7.0 %all-gather.3.cloned.1.call-done.w_ref = f32[768,2304]{1,0:T(8,128)} async-done(((f32[96,2304]{1,0:T(8,128)}), f32[768,2304]{1,0:T(8,128)}) %all-gather.3.cloned.1.call-update) | async-done | bytes 7077904 | tf_op jit(solution)/shard_map/all_gather | solution.py:613
  90.2 21.5 %shard_map.239 = (f32[384,768]{1,0:T(8,128)}, f32[1152,1536]{1,0:T(8,128)}, bf16[1152,768]{1,0:T(8,128)(2,1)}, bf16[1152,768]{1,0:T(8,128)(2,1)}) custom-call(f32[384,768]{1,0:T(8,128)} %collective-permute-done.1.far_ref, f32[384,768]{1,0:T(8,128)} %collective-permute-done.near_ref, f32[384,768]{1,0:T(8,128)} %own_ref.1, ...), custom_call_target="tpu_custom_call" | custom-call | flops 22000001024 | bytes 1048576 | tf_op jit(solution)/shard_map/pallas_call | solution.py:135
  113.1 23.6 %shard_map.240.att_ref = f32[384,768]{1,0:T(8,128)} custom-call(f32[384,768]{1,0:T(8,128)} %get-tuple-element.53.q_ref, f32[1152,1536]{1,0:T(8,128)} %get-tuple-element.54.k_ref.v_ref, f32[1152,1536]{1,0:T(8,128)} %get-tuple-element.54.k_ref.v_ref, s32[384,128]{1,0:T(8,128)} %broadcast_in_dim.56.segq_ref, s32[8,1152]{1,0:T(8,128)} %broadcast_in_dim.58.segk_ref), custom_call_target="tpu_custom_call" | custom-call | flops 26400000000 | bytes 1048576 | tf_op jit(solution)/shard_map/pallas_call | solution.py:227
  136.8 4.4 fusion.30
  145.1 19.5 %shard_map.241 = (f32[768,768]{1,0:T(8,128)}, f32[768,768]{1,0:T(8,128)}, f32[4,1,384,512]{3,2,1,0:T(8,128)}) custom-call(s32[1]{0:T(128)} %bitcast.8.chip_ref, f32[384,768]{1,0:T(8,128)} %copy-done.3, f32[384,768]{1,0:T(8,128)} %copy-done.32, f32[384,768]{1,0:T(8,128)} %cot_ref.3, f32[384,768]{1,0:T(8,128)} %collective-permute-done.5.cot_other_ref, ...), custom_call_target="tpu_custom_call" | custom-call | flops 19800000512 | bytes 1048576 | tf_op jit(solution)/shard_map/pallas_call | solution.py:448
  164.7 36.8 %shard_map.242 = (f32[768,768]{1,0:T(8,128)}, f32[768,768]{1,0:T(8,128)}, f32[4,2,384,512]{3,2,1,0:T(8,128)}) custom-call(s32[1]{0:T(128)} %bitcast.8.chip_ref, f32[384,768]{1,0:T(8,128)} %copy-done.3, f32[384,768]{1,0:T(8,128)} %copy-done.32, f32[384,768]{1,0:T(8,128)} %cot_ref.3, f32[384,768]{1,0:T(8,128)} %collective-permute-done.5.cot_other_ref, ...), custom_call_target="tpu_custom_call" | custom-call | flops 39600001024 | bytes 1048576 | tf_op jit(solution)/shard_map/pallas_call | solution.py:448
  201.6 2.5 slice.151
  207.4 9.3 %fusion.19 = (f32[]{:T(128)}, f32[]{:T(128)}, f32[]{:T(128)}, f32[]{:T(128)}, f32[384,768]{1,0:T(8,128)}, /*index=5*/f32[384]{0:T(512)S(1)}) fusion(f32[384,768]{1,0:T(8,128)S(1)} %copy-done.6, f32[3,384,768]{2,1,0:T(8,128)} %param.18, f32[384,768]{1,0:T(8,128)} %param.17, f32[384,768]{1,0:T(8,128)S(1)} %copy-done.4, ...), kind=kLoop, calls=%fused_computation.35 | loop fusion | flops 6487676 | bytes 10619940 | tf_op jit(solution)/shard_map/reduce_sum | solution.py:689
  216.7 2.9 multiply_reduce_fusion.2
  221.3 2.8 fusion.31.g_ref
  228.0 23.4 %shard_map.243 = (f32[384,768]{1,0:T(8,128)}, f32[1152,768]{1,0:T(8,128)}, f32[1152,768]{1,0:T(8,128)}) custom-call(f32[384,768]{1,0:T(8,128)} %get-tuple-element.53.q_ref, f32[1152,1536]{1,0:T(8,128)} %get-tuple-element.54.k_ref.v_ref, f32[1152,1536]{1,0:T(8,128)} %get-tuple-element.54.k_ref.v_ref, f32[384,768]{1,0:T(8,128)} %fusion.31.g_ref, ...), custom_call_target="tpu_custom_call" | custom-call | flops 23100000256 | bytes 1048576 | tf_op jit(solution)/shard_map/pallas_call | solution.py:319
  251.5 2.5 collective-permute-start.16
  254.0 23.8 %shard_map.244 = (f32[384,768]{1,0:T(8,128)}, f32[1152,768]{1,0:T(8,128)}, f32[1152,768]{1,0:T(8,128)}) custom-call(f32[384,768]{1,0:T(8,128)} %get-tuple-element.53.q_ref, f32[1152,1536]{1,0:T(8,128)} %get-tuple-element.54.k_ref.v_ref, f32[1152,1536]{1,0:T(8,128)} %get-tuple-element.54.k_ref.v_ref, ...), custom_call_target="tpu_custom_call", output_to_operand_aliasing={{0}: (8, {}), {1}: (9, {}), {2}: (10, {})} | custom-call | flops 23100000256 | bytes 1048576 | tf_op jit(solution)/shard_map/pallas_call | solution.py:319
  277.9 12.6 %shard_map.245 = f32[2,4,96,1536]{3,2,1,0:T(8,128)} custom-call(s32[1]{0:T(128)} %bitcast.18.core_ref, bf16[1152,768]{1,0:T(8,128)(2,1)} %get-tuple-element.69.hi_ref, bf16[1152,768]{1,0:T(8,128)(2,1)} %get-tuple-element.70.lo_ref, f32[384,768]{1,0:T(8,128)} %get-tuple-element.68.dq_ref, f32[1152,768]{1,0:T(8,128)} %get-tuple-element.66.dk_ref), custom_call_target="tpu_custom_call" | custom-call | flops 9900000256 | bytes 1048576 | tf_op jit(solution)/shard_map/pallas_call | solution.py:542
  290.5 3.4 slice_bitcast_fusion.2
  293.9 13.5 %shard_map.246 = f32[2,4,96,1536]{3,2,1,0:T(8,128)} custom-call(s32[1]{0:T(128)} %bitcast.18.core_ref, bf16[1152,768]{1,0:T(8,128)(2,1)} %get-tuple-element.69.hi_ref, bf16[1152,768]{1,0:T(8,128)(2,1)} %get-tuple-element.70.lo_ref, f32[1152,768]{1,0:T(8,128)} %get-tuple-element.67.dv_ref, f32[384,768]{1,0:T(8,128)} %shard_map.240.att_ref, f32[384,768]{1,0:T(8,128)} %copy-done.7), custom_call_target="tpu_custom_call" | custom-call | flops 9900000256 | bytes 1048576 | tf_op jit(solution)/shard_map/pallas_call | solution.py:542
  307.4 1.8 slice_bitcast_fusion
  310.2 3.7 collective-permute-done.25
  314.3 2.5 pad_maximum_fusion
  316.9 12.4 %fusion = f32[1152,768]{1,0:T(8,128)S(1)} fusion(f32[1152,768]{1,0:T(8,128)} %get-tuple-element.67.dv_ref, f32[1152,768]{1,0:T(8,128)} %get-tuple-element.66.dk_ref, f32[768,2304]{1,0:T(8,128)} %all-gather.3.cloned.1.call-done.w_ref), kind=kOutput, calls=%fused_computation | convolution fusion | flops 8155496448 | bytes 15335424 | tf_op jit(solution)/shard_map/dot_general | solution.py:575
  329.3 1.8 copy-done.13
  333.5 2.4 slice_select_fusion
  336.0 2.7 collective-permute-start.27
  338.6 24.5 %collective-permute-done.17 = f32[384,768]{1,0:T(8,128)S(1)} collective-permute-done((f32[384,768]{1,0:T(8,128)}, f32[384,768]{1,0:T(8,128)S(1)}, u32[]{:S(2)}, u32[]{:S(2)}) %collective-permute-start.17) | collective-permute-done | bytes 1179680 | tf_op jit(solution)/shard_map/ppermute | solution.py:748
  363.1 2.4 slice_add_fusion
  365.5 1.6 collective-permute-start.18
  367.6 12.4 %collective-permute-done.27 = f32[2,192,512]{2,1,0:T(8,128)} collective-permute-done((f32[2,192,512]{2,1,0:T(8,128)}, f32[2,192,512]{2,1,0:T(8,128)}, u32[]{:S(2)}, u32[]{:S(2)}) %collective-permute-start.27) | collective-permute-done | bytes 786464 | tf_op jit(solution)/shard_map/ppermute | solution.py:702
  380.0 2.3 select_add_fusion
  382.8 3.3 stack.32
  386.2 29.1 %collective-permute-done.18 = f32[384,768]{1,0:T(8,128)} collective-permute-done((f32[384,768]{1,0:T(8,128)}, f32[384,768]{1,0:T(8,128)}, u32[]{:S(2)}, u32[]{:S(2)}) %collective-permute-start.18) | collective-permute-done | bytes 1179680 | tf_op jit(solution)/shard_map/ppermute | solution.py:749
  415.3 5.3 %multiply_reduce_fusion.3 = (f32[768]{0:T(1024)S(1)}, f32[384]{0:T(512)}, f32[384]{0:T(512)S(1)}, f32[768]{0:T(1024)S(1)}, f32[384,768]{1,0:T(8,128)S(1)}) fusion(f32[384,768]{1,0:T(8,128)S(1)} %copy-done.2, f32[384]{0:T(512)S(1)} %add_rsqrt_fusion, f32[384]{0:T(512)S(1)} %broadcast_multiply_fusion.2, f32[768]{0:T(1024)S(1)} %copy-done.20, ...), kind=kOutput, calls=%fused_computation.47 | convolution fusion | flops 1362196224 | bytes 8272896 | tf_op jit(solution)/shard_map/dot_general | solution.py:575
  423.3 6.7 %collective-permute-done.26 = f32[1,192,512]{2,1,0:T(8,128)} collective-permute-done((f32[1,192,512]{2,1,0:T(8,128)S(1)}, f32[1,192,512]{2,1,0:T(8,128)}, u32[]{:S(2)}, u32[]{:S(2)}) %collective-permute-start.26) | collective-permute-done | bytes 393248 | tf_op jit(solution)/shard_map/ppermute | solution.py:702
  432.2 2.4 add.146
  435.1 1.6 collective-permute-start.22
  436.7 17.3 %collective-permute-done.22 = f32[8,768]{1,0:T(8,128)S(1)} collective-permute-done((f32[8,768]{1,0:T(8,128)S(1)}, f32[8,768]{1,0:T(8,128)S(1)}, u32[]{:S(2)}, u32[]{:S(2)}) %collective-permute-start.22) | collective-permute-done | bytes 24608 | tf_op jit(solution)/shard_map/ppermute | solution.py:702
  456.0 2.7 collective-permute-done.23
  466.5 46.8 %all-reduce.6.cloned.1.call-done = f32[96,3072]{1,0:T(8,128)} async-done(((f32[96,3072]{1,0:T(8,128)}), f32[96,3072]{1,0:T(8,128)}) %all-reduce.6.cloned.1.call-update) | async-done | bytes 1179664 | tf_op jit(solution)/shard_map/psum | solution.py:762
  513.3 2.1 slice.195
  515.4 1.7 slice.196
  (195 shorter events, 46.9 us)
Async XLA Ops:
  7.2 83.0 %all-gather.3.cloned.1.call-start = ((), (), s32[]{:S(2)}) async-start(), calls=%async_computation.3 | async-start | bytes 7962624 | tf_op jit(solution)/shard_map/all_gather | solution.py:613
  7.9 128.9 %all-gather.5.cloned.1.call-start = ((), (), s32[]{:S(2)}) async-start(), calls=%async_computation.4 | async-start | bytes 2654208 | tf_op jit(solution)/shard_map/all_gather | solution.py:613
  11.4 7.9 %collective-permute-start.6 = (f32[96,1536]{1,0:T(8,128)}, f32[96,1536]{1,0:T(8,128)S(1)}, u32[]{:S(2)}, u32[]{:S(2)}) collective-permute-start(f32[96,1536]{1,0:T(8,128)} %select_n.115), channel_id=1, source_target_pairs={{0,4},{4,0},{8,12},{12,8},{16,20},{20,16},{24,28},{28,24},{1,5},{5... | collective-permute-start | bytes 1769480 | tf_op jit(solution)/shard_map/ppermute | solution.py:610
  11.9 30.4 %collective-permute-start = (f32[384,768]{1,0:T(8,128)S(1)}, f32[384,768]{1,0:T(8,128)}, u32[]{:S(2)}, u32[]{:S(2)}) collective-permute-start(f32[384,768]{1,0:T(8,128)S(1)} %copy-done), channel_id=1, source_target_pairs={{0,1},{1,2},{2,3},{4,5},{5,6},{6,7},{8,9},{9,10},{10,11},{12,13},{... | collective-permute-start | bytes 3538952 | tf_op jit(solution)/shard_map/ppermute | solution.py:637
  17.4 62.1 %collective-permute-start.10 = (f32[384,768]{1,0:T(8,128)}, f32[384,768]{1,0:T(8,128)}, u32[]{:S(2)}, u32[]{:S(2)}) collective-permute-start(f32[384,768]{1,0:T(8,128)} %refs_4_.3), channel_id=1, source_target_pairs={{0,8},{4,12},{8,0},{12,4},{16,24},{20,28},{24,16},{28,20},{1,9},{5... | collective-permute-start | bytes 3538952 | tf_op jit(solution)/shard_map/ppermute | solution.py:610
  19.3 28.4 %copy-start.31 = (s32[1,384]{1,0:T(1,128)S(1)}, s32[1,384]{1,0:T(1,128)}, u32[]{:S(2)}) copy-start(s32[1,384]{1,0:T(1,128)} %param.28) | copy-start | bytes 4612
  19.4 57.1 %copy-start.17 = (f32[2304,128]{1,0:T(8,128)S(1)}, f32[2304,128]{1,0:T(8,128)}, u32[]{:S(2)}) copy-start(f32[2304,128]{1,0:T(8,128)} %constant.63.clone) | copy-start | bytes 3538948
  19.5 57.1 %copy-start.18 = (f32[2304,128]{1,0:T(8,128)S(1)}, f32[2304,128]{1,0:T(8,128)}, u32[]{:S(2)}) copy-start(f32[2304,128]{1,0:T(8,128)} %constant.64.clone) | copy-start | bytes 3538948
  20.6 60.6 %collective-permute-start.8 = (f32[192,1536]{1,0:T(8,128)}, f32[192,1536]{1,0:T(8,128)}, u32[]{:S(2)}, u32[]{:S(2)}) collective-permute-start(f32[192,1536]{1,0:T(8,128)} %pad_maximum_fusion.1.refs_0_), channel_id=1, source_target_pairs={{0,16},{4,20},{8,24},{12,28},{16,0},{20,4},{24,8},{28,12},{1,17},{... | collective-permute-start | bytes 3538952 | tf_op jit(solution)/shard_map/ppermute | solution.py:610
  42.2 40.4 %collective-permute-start.1 = (f32[384,768]{1,0:T(8,128)}, f32[384,768]{1,0:T(8,128)}, u32[]{:S(2)}, u32[]{:S(2)}) collective-permute-start(f32[384,768]{1,0:T(8,128)} %collective-permute-done.near_ref), channel_id=1, source_target_pairs={{0,1},{1,2},{2,3},{4,5},{5,6},{6,7},{8,9},{9,10},{10,11},{12,13},{... | collective-permute-start | bytes 3538952 | tf_op jit(solution)/shard_map/ppermute | solution.py:639
  47.8 64.5 %copy-start.22 = (s32[384]{0:T(512)}, s32[384]{0:T(512)S(1)}, u32[]{:S(2)}) copy-start(s32[384]{0:T(512)S(1)} %get-tuple-element.104) | copy-start | bytes 4612
  47.8 24.3 %collective-permute-start.2 = (s32[1,384]{1,0:T(1,128)S(1)}, s32[1,384]{1,0:T(1,128)S(1)}, u32[]{:S(2)}, u32[]{:S(2)}) collective-permute-start(s32[1,384]{1,0:T(1,128)S(1)} %get-tuple-element.103), channel_id=1, source_target_pairs={{0,1},{1,2},{2,3},{4,5},{5,6},{6,7},{8,9},{9,10},{10,11},{12,13},{... | collective-permute-start | bytes 4616 | tf_op jit(solution)/shard_map/ppermute | solution.py:638
  50.3 90.9 %collective-permute-start.11 = (f32[384,768]{1,0:T(8,128)}, f32[384,768]{1,0:T(8,128)}, u32[]{:S(2)}, u32[]{:S(2)}) collective-permute-start(f32[384,768]{1,0:T(8,128)} %refs_4_.3), channel_id=1, source_target_pairs={{0,16},{4,20},{8,24},{12,28},{16,0},{20,4},{24,8},{28,12},{1,17},{... | collective-permute-start | bytes 3538952 | tf_op jit(solution)/shard_map/ppermute | solution.py:610
  51.9 172.2 %reduce-scatter.10.cloned.1.call-start = ((), (), s32[]{:S(2)}) async-start(), calls=%async_computation.6 | async-start | bytes 3932160
  51.9 25.8 %copy-start.19 = (f32[768]{0:T(1024)S(1)}, f32[768]{0:T(1024)}, u32[]{:S(2)}) copy-start(f32[768]{0:T(1024)} %param.20) | copy-start | bytes 9220
  51.9 26.3 %copy-start.29 = (f32[768]{0:T(1024)S(1)}, f32[768]{0:T(1024)}, u32[]{:S(2)}) copy-start(f32[768]{0:T(1024)} %param.21) | copy-start | bytes 9220
  52.0 26.9 %copy-start.5 = (f32[384,768]{1,0:T(8,128)S(1)}, f32[384,768]{1,0:T(8,128)}, u32[]{:S(2)}) copy-start(f32[384,768]{1,0:T(8,128)} %cot_ref.3) | copy-start | bytes 3538948
  72.1 6.7 %collective-permute-start.3 = (s32[1,384]{1,0:T(1,128)S(1)}, s32[1,384]{1,0:T(1,128)S(1)}, u32[]{:S(2)}, u32[]{:S(2)}) collective-permute-start(s32[1,384]{1,0:T(1,128)S(1)} %collective-permute-done.2), channel_id=1, source_target_pairs={{0,1},{1,2},{2,3},{4,5},{5,6},{6,7},{8,9},{9,10},{10,11},{12,13},{... | collective-permute-start | bytes 4616 | tf_op jit(solution)/shard_map/ppermute | solution.py:640
  78.9 65.2 %collective-permute-start.5 = (f32[384,768]{1,0:T(8,128)S(1)}, f32[384,768]{1,0:T(8,128)}, u32[]{:S(2)}, u32[]{:S(2)}) collective-permute-start(f32[384,768]{1,0:T(8,128)S(1)} %copy-done.5), channel_id=1, source_target_pairs={{0,4},{4,0},{8,12},{12,8},{16,20},{20,16},{24,28},{28,24},{1,5},{5... | collective-permute-start | bytes 3538952 | tf_op jit(solution)/shard_map/ppermute | solution.py:610
  79.6 64.5 %collective-permute-start.7 = (f32[192,1536]{1,0:T(8,128)}, f32[192,1536]{1,0:T(8,128)}, u32[]{:S(2)}, u32[]{:S(2)}) collective-permute-start(f32[192,1536]{1,0:T(8,128)} %pad_maximum_fusion.1.refs_0_), channel_id=1, source_target_pairs={{0,8},{4,12},{8,0},{12,4},{16,24},{20,28},{24,16},{28,20},{1,9},{5... | collective-permute-start | bytes 3538952 | tf_op jit(solution)/shard_map/ppermute | solution.py:610
  81.1 62.9 %collective-permute-start.12 = (f32[384,768]{1,0:T(8,128)}, f32[384,768]{1,0:T(8,128)}, u32[]{:S(2)}, u32[]{:S(2)}) collective-permute-start(f32[384,768]{1,0:T(8,128)} %collective-permute-done.10.refs_5_), channel_id=1, source_target_pairs={{0,16},{4,20},{8,24},{12,28},{16,0},{20,4},{24,8},{28,12},{1,17},{... | collective-permute-start | bytes 3538952 | tf_op jit(solution)/shard_map/ppermute | solution.py:610
  82.7 61.4 %collective-permute-start.9 = (f32[192,1536]{1,0:T(8,128)}, f32[192,1536]{1,0:T(8,128)}, u32[]{:S(2)}, u32[]{:S(2)}) collective-permute-start(f32[192,1536]{1,0:T(8,128)} %collective-permute-done.8.refs_2_), channel_id=1, source_target_pairs={{0,8},{4,12},{8,0},{12,4},{16,24},{20,28},{24,16},{28,20},{1,9},{5... | collective-permute-start | bytes 3538952 | tf_op jit(solution)/shard_map/ppermute | solution.py:610
  113.1 23.7 %copy-start.1 = (f32[384,768]{1,0:T(8,128)S(1)}, f32[384,768]{1,0:T(8,128)}, u32[]{:S(2)}) copy-start(f32[384,768]{1,0:T(8,128)} %own_ref.1) | copy-start | bytes 3538948
  141.2 2.9 collective-permute-start.4
  164.7 168.8 %reduce-scatter.14.cloned.1.call-start = ((), (), s32[]{:S(2)}) async-start(), calls=%async_computation.8 | async-start | bytes 7864320
  204.1 3.1 collective-permute-start.13
  205.4 11.3 %collective-permute-start.14 = (f32[384,768]{1,0:T(8,128)}, f32[384,768]{1,0:T(8,128)}, u32[]{:S(2)}, u32[]{:S(2)}) collective-permute-start(f32[384,768]{1,0:T(8,128)} %slice.153), channel_id=1, source_target_pairs={{0,4},{4,0},{8,12},{12,8},{16,20},{20,16},{24,28},{28,24},{1,5},{5... | collective-permute-start | bytes 3538952 | tf_op jit(solution)/shard_map/ppermute | solution.py:610
  205.7 253.7 %reduce-scatter.12.cloned.1.call-start = ((), (), s32[]{:S(2)}) async-start(), calls=%async_computation.7 | async-start | bytes 5898240
  225.2 26.2 %collective-permute-start.15 = (f32[1,192,512]{2,1,0:T(8,128)S(1)}, f32[1,192,512]{2,1,0:T(8,128)S(1)}, u32[]{:S(2)}, u32[]{:S(2)}) collective-permute-start(f32[1,192,512]{2,1,0:T(8,128)S(1)} %slice_select_fusion.3), channel_id=1, source_target_pairs={{0,1},{1,0},{2,3},{3,2},{4,5},{5,4},{6,7},{7,6},{8,9},{9,8},{10,11... | collective-permute-start | bytes 1179656 | tf_op jit(solution)/shard_map/ppermute | solution.py:702
  251.5 26.3 %collective-permute-start.16 = (f32[1,192,512]{2,1,0:T(8,128)S(1)}, f32[1,192,512]{2,1,0:T(8,128)S(1)}, u32[]{:S(2)}, u32[]{:S(2)}) collective-permute-start(f32[1,192,512]{2,1,0:T(8,128)S(1)} %select_add_fusion.1), channel_id=1, source_target_pairs={{0,2},{1,3},{2,0},{3,1},{4,6},{5,7},{6,4},{7,5},{8,10},{9,11},{10,... | collective-permute-start | bytes 1179656 | tf_op jit(solution)/shard_map/ppermute | solution.py:702
  293.9 15.8 %collective-permute-start.24 = (f32[4,96,1536]{2,1,0:T(8,128)}, f32[4,96,1536]{2,1,0:T(8,128)S(1)}, u32[]{:S(2)}, u32[]{:S(2)}) collective-permute-start(f32[4,96,1536]{2,1,0:T(8,128)} %slice_bitcast_fusion.2), channel_id=1, source_target_pairs={{0,4},{4,0},{8,12},{12,8},{16,20},{20,16},{24,28},{28,24},{1,5},{5... | collective-permute-start | bytes 7077896 | tf_op jit(solution)/shard_map/ppermute | solution.py:610
  309.2 4.7 collective-permute-start.25
  316.8 196.4 %all-reduce.6.cloned.1.call-start = ((), (), s32[]{:S(2)}) async-start(), calls=%async_computation.5 | async-start | bytes 2359296 | tf_op jit(solution)/shard_map/psum | solution.py:762
  332.2 30.9 %collective-permute-start.17 = (f32[384,768]{1,0:T(8,128)}, f32[384,768]{1,0:T(8,128)S(1)}, u32[]{:S(2)}, u32[]{:S(2)}) collective-permute-start(f32[384,768]{1,0:T(8,128)} %slice.187), channel_id=1, source_target_pairs={{1,0},{2,1},{3,2},{5,4},{6,5},{7,6},{9,8},{10,9},{11,10},{13,12},{... | collective-permute-start | bytes 3538952 | tf_op jit(solution)/shard_map/ppermute | solution.py:748
  335.9 31.2 %copy-start.2 = (f32[384,768]{1,0:T(8,128)S(1)}, f32[384,768]{1,0:T(8,128)}, u32[]{:S(2)}) copy-start(f32[384,768]{1,0:T(8,128)} %own_ref.1) | copy-start | bytes 3538948
  336.0 44.1 %collective-permute-start.27 = (f32[2,192,512]{2,1,0:T(8,128)}, f32[2,192,512]{2,1,0:T(8,128)}, u32[]{:S(2)}, u32[]{:S(2)}) collective-permute-start(f32[2,192,512]{2,1,0:T(8,128)} %slice_select_fusion), channel_id=1, source_target_pairs={{0,1},{1,0},{2,3},{3,2},{4,5},{5,4},{6,7},{7,6},{8,9},{9,8},{10,11... | collective-permute-start | bytes 2359304 | tf_op jit(solution)/shard_map/ppermute | solution.py:702
  365.5 49.8 %collective-permute-start.18 = (f32[384,768]{1,0:T(8,128)}, f32[384,768]{1,0:T(8,128)}, u32[]{:S(2)}, u32[]{:S(2)}) collective-permute-start(f32[384,768]{1,0:T(8,128)} %slice_add_fusion), channel_id=1, source_target_pairs={{1,0},{2,1},{3,2},{5,4},{6,5},{7,6},{9,8},{10,9},{11,10},{13,12},{... | collective-permute-start | bytes 3538952 | tf_op jit(solution)/shard_map/ppermute | solution.py:749
  367.6 47.7 %copy-start.20 = (f32[768]{0:T(1024)S(1)}, f32[768]{0:T(1024)}, u32[]{:S(2)}) copy-start(f32[768]{0:T(1024)} %param.20) | copy-start | bytes 9220
  382.3 49.9 %collective-permute-start.28 = (f32[2,192,512]{2,1,0:T(8,128)}, f32[2,192,512]{2,1,0:T(8,128)}, u32[]{:S(2)}, u32[]{:S(2)}) collective-permute-start(f32[2,192,512]{2,1,0:T(8,128)} %select_add_fusion), channel_id=1, source_target_pairs={{0,2},{1,3},{2,0},{3,1},{4,6},{5,7},{6,4},{7,5},{8,10},{9,11},{10,... | collective-permute-start | bytes 2359304 | tf_op jit(solution)/shard_map/ppermute | solution.py:702
  386.1 43.9 %collective-permute-start.26 = (f32[1,192,512]{2,1,0:T(8,128)S(1)}, f32[1,192,512]{2,1,0:T(8,128)}, u32[]{:S(2)}, u32[]{:S(2)}) collective-permute-start(f32[1,192,512]{2,1,0:T(8,128)S(1)} %add.133), channel_id=1, source_target_pairs={{0,1},{1,0},{2,3},{3,2},{4,5},{5,4},{6,7},{7,6},{8,9},{9,8},{10,11... | collective-permute-start | bytes 1179656 | tf_op jit(solution)/shard_map/ppermute | solution.py:702
  420.6 1.3 collective-permute-start.19
  421.9 9.3 %collective-permute-start.20 = (f32[8,768]{1,0:T(8,128)S(1)}, f32[8,768]{1,0:T(8,128)S(1)}, u32[]{:S(2)}, u32[]{:S(2)}) collective-permute-start(f32[8,768]{1,0:T(8,128)S(1)} %add.138), channel_id=1, source_target_pairs={{0,8},{4,12},{8,0},{12,4},{16,24},{20,28},{24,16},{28,20},{1,9},{5... | collective-permute-start | bytes 73736 | tf_op jit(solution)/shard_map/ppermute | solution.py:610
  431.2 23.5 %copy-start.8 = (f32[384,768]{1,0:T(8,128)S(1)}, f32[384,768]{1,0:T(8,128)}, u32[]{:S(2)}) copy-start(f32[384,768]{1,0:T(8,128)} %copy-done.7) | copy-start | bytes 3538948
  431.2 3.9 collective-permute-start.21
  434.6 24.9 %collective-permute-start.29 = (f32[2,192,512]{2,1,0:T(8,128)}, f32[2,192,512]{2,1,0:T(8,128)}, u32[]{:S(2)}, u32[]{:S(2)}) collective-permute-start(f32[2,192,512]{2,1,0:T(8,128)} %add.146), channel_id=1, source_target_pairs={{0,1},{1,0},{2,3},{3,2},{4,5},{5,4},{6,7},{7,6},{8,9},{9,8},{10,11... | collective-permute-start | bytes 2359304 | tf_op jit(solution)/shard_map/ppermute | solution.py:702
  435.1 19.0 %collective-permute-start.22 = (f32[8,768]{1,0:T(8,128)S(1)}, f32[8,768]{1,0:T(8,128)S(1)}, u32[]{:S(2)}, u32[]{:S(2)}) collective-permute-start(f32[8,768]{1,0:T(8,128)S(1)} %add.140), channel_id=1, source_target_pairs={{0,1},{1,0},{2,3},{3,2},{4,5},{5,4},{6,7},{7,6},{8,9},{9,8},{10,11... | collective-permute-start | bytes 73736 | tf_op jit(solution)/shard_map/ppermute | solution.py:702
  454.0 4.7 collective-permute-start.23
  461.1 2.1 collective-permute-start.30
  (24 other events, 175.7 us)
Sparse Core Ops, SparseCore 0:
  9.9 80.2 all-gather.2
  92.0 38.7 all-gather.4
  164.8 43.8 reduce-scatter.9
  211.5 70.2 reduce-scatter.13
  317.0 55.0 reduce-scatter.11
  459.6 53.6 all-reduce.5

commit v2 on v1

--- a/solution.py
+++ b/solution.py
@@ -719,8 +719,6 @@
         other = shift(kept, 1)
         return jnp.where(even, kept, other), jnp.where(even, other, kept)
 
-    line_sum = lambda shard: line_end(line_middle(line_start(shard)))
-
     kept_a = line_start(shard_a)
     kept_a, back_args, first_half = lax.optimization_barrier((kept_a, back_args, first_half))
     kept_a = line_middle(kept_a)
@@ -731,36 +729,33 @@
     grads_qk = weight_call(
         weights_qk_kernel, 9, core_at, chips, normed_parts, [(dq, 0), (dk, 1)], [halo + rows] * 2
     )
+    given_qk = swap(grads_qk[1])
+    shard_b, dv = lax.optimization_barrier((shard_b, dv))
+    kept_b = line_start(shard_b)
     grads_vo = weight_call(
         weights_vo_kernel, 9, core_at, chips, normed_parts,
         [(dv, 0), (attended, None), (grad_resid, 1)], [halo + rows] * 2 + [rows] * 2,
     )
     shard_c = scatter_chips(
-        jnp.concatenate(
-            [grads_qk[0] + swap(grads_qk[1]), grads_vo[0] + swap(grads_vo[1])], axis=2
-        )
+        jnp.concatenate([grads_qk[0] + given_qk, grads_vo[0] + swap(grads_vo[1])], axis=2)
     )[0]
+    kept_b, dk = lax.optimization_barrier((kept_b, dk))
+    kept_b = line_middle(kept_b)
     dkv = jnp.concatenate([dk, dv], axis=1)
 
     wq, wkv = qkv_full[:, :model], qkv_full[:, model:]
     partial = outer_cols(dkv, wkv)
     own_part = partial[halo:] + outer_cols(dq, wq)
     back_near = partial[rows:halo] + lax.ppermute(partial[:rows], "seq", behind)
-    grad_normed_one = own_part + lax.ppermute(back_near, "seq", behind)
+
     xhat1, rate1 = norm_stats(block_input)
-    grad_input = grad_resid + norm_back(grad_normed_one, gain1, xhat1, rate1)
-    grad_gain_one = jnp.sum(grad_normed_one * xhat1, axis=0)
-    grad_bias_one = jnp.sum(grad_normed_one, axis=0)
-
-    grad_up, grad_down = unpack_grads(
-        *(
-            jnp.concatenate(parts, axis=0)
-            for parts in zip(line_end(kept_a), line_sum(shard_b))
-        ),
-        swap, core, chips,
-    )
-    sum_c = lax.psum(shard_c, "seq")
-    grad_qkv, grad_wout = sum_c[:, :3 * model], sum_c[:, 3 * model:]
+    terms = (
+        (norm_stats(far)[0], partial[:rows]),
+        (norm_stats(near)[0], partial[rows:halo]),
+        (xhat1, own_part),
+    )
+    grad_gain_one = sum(jnp.sum(xhat * part, axis=0) for xhat, part in terms)
+    grad_bias_one = sum(jnp.sum(part, axis=0) for _, part in terms)
 
     small = jnp.concatenate(
         [
@@ -777,8 +772,23 @@
     while bit < groups:
         small = small + shift(small, bit)
         bit *= 2
+    ends_a = line_end(kept_a)
+    shard_c, back_near, ends_a, kept_b, small = lax.optimization_barrier(
+        (shard_c, back_near, ends_a, kept_b, small)
+    )
     gain_one, bias_one, gain_two, bias_two = small[0], small[1], small[2], small[3]
     grad_dwa = small[4, :5]
+    sum_c = lax.psum(shard_c, "seq")
+    grad_qkv, grad_wout = sum_c[:, :3 * model], sum_c[:, 3 * model:]
+    grad_normed_one = own_part + lax.ppermute(back_near, "seq", behind)
+    grad_input = grad_resid + norm_back(grad_normed_one, gain1, xhat1, rate1)
+    grad_up, grad_down = unpack_grads(
+        *(
+            jnp.concatenate(parts, axis=0)
+            for parts in zip(ends_a, line_end(kept_b))
+        ),
+        swap, core, chips,
+    )
     return (
         output,
         grad_input,

time: 533 us -> 522 us (0.979)
  waiting for transfers between devices: 195 us -> 163 us
  other arithmetic: 36.1 us -> 49.7 us
  local copies, waits for them, and re-layouts: 36.2 us -> 45.2 us
    psum x1, waiting for transfers between devices: 46.8 us -> 0.62 us  [body(): sum_c = lax.psum(shard_c, 'seq')]
    ppermute x8, waiting for transfers between devices: 39.2 us -> 72 us  [body(): lax.ppermute(v, 'seq', [(i, i ^ bit) for i in range(groups)])]
    ppermute x1, waiting for transfers between devices: 24.5 us -> 0.01 us  [body(): back_near = partial[rows:halo] + lax.ppermute(partial[:rows], 'seq', behind)]
    ppermute x1, waiting for transfers between devices: 29.1 us -> 35.5 us  [body(): grad_normed_one = own_part + lax.ppermute(back_near, 'seq', behind)]
  transfers between devices with their start and end apart: 37 -> 37, of which waited for: 15 -> 14; matrix products, arithmetic and copies ran while one was open for 17% -> 21% of each run, Pallas kernels for 30% -> 30%
where the time goes in v2:
time: 522 us; the launch traced here: 512 us
  Pallas kernels  175 us (34%)
  waiting for transfers between devices  163 us (31%)
  other arithmetic  49.7 us (10%)
  local copies, waits for them, and re-layouts  45.2 us (9%)
  starting transfers between devices  41.2 us (8%)
  matrix products  23.1 us (4%)
  between operations  15.1 us (3%)
    ppermute x8, waiting for transfers between devices, body(): lax.ppermute(v, 'seq', [(i, i ^ bit) for i in range(groups)])  72 us
    pallas_call x2, Pallas kernels, mlp(): pl.pallas_call(functools.partial(mlp_kernel, len(ups), len(so_far) // 2),...  56.3 us
    pallas_call x2, Pallas kernels, attend_back(): pl.pallas_call(attend_back_kernel, grid=(count,), in_specs=[pl.BlockSpec(...  47.4 us
    ppermute x1, waiting for transfers between devices, body(): grad_normed_one = own_part + lax.ppermute(back_near, 'seq', behind)  35.5 us
    pallas_call x2, Pallas kernels, weight_call(): pl.pallas_call(kernel, grid_spec=pltpu.PrefetchScalarGridSpec(num_scalar_...  26.2 us
    pallas_call x1, Pallas kernels, attend(): pl.pallas_call(attend_kernel, grid=(pairs,), in_specs=[pl.BlockSpec((rows...  23.8 us
    pallas_call x1, Pallas kernels, project(): pl.pallas_call(qkv_kernel, grid=(3 * third,), in_specs=[whole((rows, mode...  21.6 us
    ppermute x1, waiting for transfers between devices, body(): seg_near = lax.ppermute(seg_own, 'seq', ahead)  19.5 us
  transfers between devices with their start and end apart: 37, of which 14 were waited for; matrix products, arithmetic and copies ran while one was open for 21% of the time, Pallas kernels for 30%

profile of v2, /device:TPU:0, one launch (start us, length us, event | category | flops | bytes accessed | tf_op | source)
XLA Modules:
  0.0 512.4 jit_solution(8867188952458544887)
XLA Ops:
  8.0 1.9 reshape.162
  11.9 4.6 collective-permute-start
  16.5 1.6 collective-permute-start.10
  24.3 18.0 %collective-permute-done.near_ref = f32[384,768]{1,0:T(8,128)S(1)} collective-permute-done((f32[384,768]{1,0:T(8,128)S(1)}, f32[384,768]{1,0:T(8,128)S(1)}, u32[]{:S(2)}, u32[]{:S(2)}) %collective-permute-start) | collective-permute-done | bytes 1179680 | tf_op jit(solution)/shard_map/ppermute | solution.py:637
  42.2 4.4 collective-permute-start.1
  46.7 4.0 collective-permute-start.2
  52.4 19.5 %collective-permute-done.2 = s32[1,384]{1,0:T(1,128)} collective-permute-done((s32[1,384]{1,0:T(1,128)S(1)}, s32[1,384]{1,0:T(1,128)}, u32[]{:S(2)}, u32[]{:S(2)}) %collective-permute-start.2) | collective-permute-done | bytes 1568 | tf_op jit(solution)/shard_map/ppermute | solution.py:638
  71.8 4.5 collective-permute-start.3
  76.3 2.4 constant_dynamic-slice_fusion
  80.6 1.6 collective-permute-start.7
  84.2 5.8 %all-gather.3.cloned.1.call-done.w_ref = f32[768,2304]{1,0:T(8,128)} async-done(((f32[96,2304]{1,0:T(8,128)}), f32[768,2304]{1,0:T(8,128)}) %all-gather.3.cloned.1.call-update) | async-done | bytes 7077904 | tf_op jit(solution)/shard_map/all_gather | solution.py:613
  90.0 21.6 %shard_map.239 = (f32[384,768]{1,0:T(8,128)}, f32[1152,1536]{1,0:T(8,128)}, bf16[1152,768]{1,0:T(8,128)(2,1)}, bf16[1152,768]{1,0:T(8,128)(2,1)}) custom-call(f32[384,768]{1,0:T(8,128)} %copy-done.9, f32[384,768]{1,0:T(8,128)} %copy-done.7, f32[384,768]{1,0:T(8,128)} %own_ref.1, f32[1,768]{1,0:T(1,128)} %broadcast_in_dim.26.gain_ref, ...), custom_call_target="tpu_custom_call" | custom-call | flops 22000001024 | bytes 1048576 | tf_op jit(solution)/shard_map/pallas_call | solution.py:135
  113.0 23.8 %shard_map.240.att_ref = f32[384,768]{1,0:T(8,128)} custom-call(f32[384,768]{1,0:T(8,128)} %get-tuple-element.64.q_ref, f32[1152,1536]{1,0:T(8,128)} %get-tuple-element.65.k_ref.v_ref, f32[1152,1536]{1,0:T(8,128)} %get-tuple-element.65.k_ref.v_ref, s32[384,128]{1,0:T(8,128)} %broadcast_in_dim.56.segq_ref, s32[8,1152]{1,0:T(8,128)} %broadcast_in_dim.58.segk_ref), custom_call_target="tpu_custom_call" | custom-call | flops 26400000000 | bytes 1048576 | tf_op jit(solution)/shard_map/pallas_call | solution.py:227
  136.8 4.4 fusion.29
  146.0 19.5 %shard_map.241 = (f32[768,768]{1,0:T(8,128)}, f32[768,768]{1,0:T(8,128)}, f32[4,1,384,512]{3,2,1,0:T(8,128)}) custom-call(s32[1]{0:T(128)} %bitcast.8.chip_ref, f32[384,768]{1,0:T(8,128)} %copy-done.3, f32[384,768]{1,0:T(8,128)} %copy-done.37, f32[384,768]{1,0:T(8,128)} %cot_ref.3, f32[384,768]{1,0:T(8,128)} %collective-permute-done.5.cot_other_ref, ...), custom_call_target="tpu_custom_call" | custom-call | flops 19800000512 | bytes 1048576 | tf_op jit(solution)/shard_map/pallas_call | solution.py:448
  165.5 36.8 %shard_map.242 = (f32[768,768]{1,0:T(8,128)}, f32[768,768]{1,0:T(8,128)}, f32[4,2,384,512]{3,2,1,0:T(8,128)}) custom-call(s32[1]{0:T(128)} %bitcast.8.chip_ref, f32[384,768]{1,0:T(8,128)} %copy-done.3, f32[384,768]{1,0:T(8,128)} %copy-done.37, f32[384,768]{1,0:T(8,128)} %cot_ref.3, f32[384,768]{1,0:T(8,128)} %collective-permute-done.5.cot_other_ref, ...), custom_call_target="tpu_custom_call" | custom-call | flops 39600001024 | bytes 1048576 | tf_op jit(solution)/shard_map/pallas_call | solution.py:448
  202.4 1.6 copy-done.15
  208.3 9.3 %fusion.16 = (f32[]{:T(128)}, f32[]{:T(128)}, f32[]{:T(128)}, f32[]{:T(128)}, f32[384,768]{1,0:T(8,128)}, /*index=5*/f32[384]{0:T(512)S(1)}) fusion(f32[384,768]{1,0:T(8,128)S(1)} %copy-done.6, f32[3,384,768]{2,1,0:T(8,128)} %param.18, f32[384,768]{1,0:T(8,128)} %param.17, f32[384,768]{1,0:T(8,128)S(1)} %copy-done.4, ...), kind=kLoop, calls=%fused_computation.33 | loop fusion | flops 6487676 | bytes 10619940 | tf_op jit(solution)/shard_map/reduce_sum | solution.py:689
  217.6 3.1 multiply_reduce_fusion.3
  222.3 2.8 fusion.30.g_ref
  228.9 23.5 %shard_map.243 = (f32[384,768]{1,0:T(8,128)}, f32[1152,768]{1,0:T(8,128)}, f32[1152,768]{1,0:T(8,128)}) custom-call(f32[384,768]{1,0:T(8,128)} %get-tuple-element.64.q_ref, f32[1152,1536]{1,0:T(8,128)} %get-tuple-element.65.k_ref.v_ref, f32[1152,1536]{1,0:T(8,128)} %get-tuple-element.65.k_ref.v_ref, f32[384,768]{1,0:T(8,128)} %fusion.30.g_ref, ...), custom_call_target="tpu_custom_call" | custom-call | flops 23100000256 | bytes 1048576 | tf_op jit(solution)/shard_map/pallas_call | solution.py:319
  252.5 2.4 collective-permute-start.16
  255.0 24.0 %shard_map.244 = (f32[384,768]{1,0:T(8,128)}, f32[1152,768]{1,0:T(8,128)}, f32[1152,768]{1,0:T(8,128)}) custom-call(f32[384,768]{1,0:T(8,128)} %get-tuple-element.64.q_ref, f32[1152,1536]{1,0:T(8,128)} %get-tuple-element.65.k_ref.v_ref, f32[1152,1536]{1,0:T(8,128)} %get-tuple-element.65.k_ref.v_ref, ...), custom_call_target="tpu_custom_call", output_to_operand_aliasing={{0}: (8, {}), {1}: (9, {}), {2}: (10, {})} | custom-call | flops 23100000256 | bytes 1048576 | tf_op jit(solution)/shard_map/pallas_call | solution.py:319
  279.7 12.6 %shard_map.245 = f32[2,4,96,1536]{3,2,1,0:T(8,128)} custom-call(s32[1]{0:T(128)} %bitcast.13.core_ref, bf16[1152,768]{1,0:T(8,128)(2,1)} %get-tuple-element.83.hi_ref, bf16[1152,768]{1,0:T(8,128)(2,1)} %get-tuple-element.84.lo_ref, f32[384,768]{1,0:T(8,128)} %get-tuple-element.82.dq_ref, f32[1152,768]{1,0:T(8,128)} %get-tuple-element.80.dk_ref), custom_call_target="tpu_custom_call" | custom-call | flops 9900000256 | bytes 1048576 | tf_op jit(solution)/shard_map/pallas_call | solution.py:542
  292.4 3.3 slice_bitcast_fusion.2
  295.6 13.6 %shard_map.246 = f32[2,4,96,1536]{3,2,1,0:T(8,128)} custom-call(s32[1]{0:T(128)} %bitcast.13.core_ref, bf16[1152,768]{1,0:T(8,128)(2,1)} %get-tuple-element.83.hi_ref, bf16[1152,768]{1,0:T(8,128)(2,1)} %get-tuple-element.84.lo_ref, f32[1152,768]{1,0:T(8,128)} %get-tuple-element.81.dv_ref, f32[384,768]{1,0:T(8,128)} %shard_map.240.att_ref, f32[384,768]{1,0:T(8,128)} %copy-done.11), custom_call_target="tpu_custom_call" | custom-call | flops 9900000256 | bytes 1048576 | tf_op jit(solution)/shard_map/pallas_call | solution.py:542
  309.2 1.8 slice_bitcast_fusion
  312.0 3.7 collective-permute-done.19
  316.2 2.5 pad_maximum_fusion
  320.8 2.5 slice_select_fusion
  326.7 3.7 stack.32
  335.8 8.3 %collective-permute-done.17 = f32[2,192,512]{2,1,0:T(8,128)} collective-permute-done((f32[2,192,512]{2,1,0:T(8,128)}, f32[2,192,512]{2,1,0:T(8,128)}, u32[]{:S(2)}, u32[]{:S(2)}) %collective-permute-start.17) | collective-permute-done | bytes 786464 | tf_op jit(solution)/shard_map/ppermute | solution.py:702
  344.0 2.7 select_add_fusion
  347.4 12.5 %fusion = f32[1152,768]{1,0:T(8,128)S(1)} fusion(f32[1152,768]{1,0:T(8,128)} %get-tuple-element.81.dv_ref, f32[1152,768]{1,0:T(8,128)} %get-tuple-element.80.dk_ref, f32[768,2304]{1,0:T(8,128)} %all-gather.3.cloned.1.call-done.w_ref), kind=kOutput, calls=%fused_computation | convolution fusion | flops 8155496448 | bytes 15335424 | tf_op jit(solution)/shard_map/dot_general | solution.py:575
  361.4 1.6 collective-permute-start.20
  363.0 3.5 fusion.27
  369.4 2.8 collective-permute-done.24
  373.2 2.8 collective-permute-done.25
  376.1 2.2 collective-permute-start.26
  378.2 26.9 %collective-permute-done.26 = f32[8,768]{1,0:T(8,128)S(1)} collective-permute-done((f32[8,768]{1,0:T(8,128)S(1)}, f32[8,768]{1,0:T(8,128)S(1)}, u32[]{:S(2)}, u32[]{:S(2)}) %collective-permute-start.26) | collective-permute-done | bytes 24608 | tf_op jit(solution)/shard_map/ppermute | solution.py:702
  405.2 1.8 broadcast_select_fusion.8
  407.0 2.9 collective-permute-done.27
  412.0 3.1 slice_add_fusion.1
  419.1 34.0 %collective-permute-done.29 = f32[2,192,512]{2,1,0:T(8,128)} collective-permute-done((f32[2,192,512]{2,1,0:T(8,128)S(1)}, f32[2,192,512]{2,1,0:T(8,128)}, u32[]{:S(2)}, u32[]{:S(2)}) %collective-permute-start.29) | collective-permute-done | bytes 786464 | tf_op jit(solution)/shard_map/ppermute | solution.py:702
  456.8 35.5 %collective-permute-done.28 = f32[384,768]{1,0:T(8,128)} collective-permute-done((f32[384,768]{1,0:T(8,128)}, f32[384,768]{1,0:T(8,128)}, u32[]{:S(2)}, u32[]{:S(2)}) %collective-permute-start.28) | collective-permute-done | bytes 1179680 | tf_op jit(solution)/shard_map/ppermute | solution.py:783
  492.3 2.6 fusion.26
  495.6 2.2 slice.194
  497.8 1.7 slice.195
  (216 shorter events, 65.7 us)
Async XLA Ops:
  7.2 82.8 %all-gather.3.cloned.1.call-start = ((), (), s32[]{:S(2)}) async-start(), calls=%async_computation.3 | async-start | bytes 7962624 | tf_op jit(solution)/shard_map/all_gather | solution.py:613
  7.9 128.9 %all-gather.5.cloned.1.call-start = ((), (), s32[]{:S(2)}) async-start(), calls=%async_computation.4 | async-start | bytes 2654208 | tf_op jit(solution)/shard_map/all_gather | solution.py:613
  11.4 8.9 %collective-permute-start.6 = (f32[96,1536]{1,0:T(8,128)}, f32[96,1536]{1,0:T(8,128)}, u32[]{:S(2)}, u32[]{:S(2)}) collective-permute-start(f32[96,1536]{1,0:T(8,128)} %select_n.115), channel_id=1, source_target_pairs={{0,4},{4,0},{8,12},{12,8},{16,20},{20,16},{24,28},{28,24},{1,5},{5... | collective-permute-start | bytes 1769480 | tf_op jit(solution)/shard_map/ppermute | solution.py:610
  11.9 30.4 %collective-permute-start = (f32[384,768]{1,0:T(8,128)S(1)}, f32[384,768]{1,0:T(8,128)S(1)}, u32[]{:S(2)}, u32[]{:S(2)}) collective-permute-start(f32[384,768]{1,0:T(8,128)S(1)} %copy-done), channel_id=1, source_target_pairs={{0,1},{1,2},{2,3},{4,5},{5,6},{6,7},{8,9},{9,10},{10,11},{12,13},{... | collective-permute-start | bytes 3538952 | tf_op jit(solution)/shard_map/ppermute | solution.py:637
  16.5 64.1 %collective-permute-start.10 = (f32[384,768]{1,0:T(8,128)}, f32[384,768]{1,0:T(8,128)}, u32[]{:S(2)}, u32[]{:S(2)}) collective-permute-start(f32[384,768]{1,0:T(8,128)} %refs_4_.3), channel_id=1, source_target_pairs={{0,8},{4,12},{8,0},{12,4},{16,24},{20,28},{24,16},{28,20},{1,9},{5... | collective-permute-start | bytes 3538952 | tf_op jit(solution)/shard_map/ppermute | solution.py:610
  21.6 25.1 %copy-start.36 = (s32[1,384]{1,0:T(1,128)S(1)}, s32[1,384]{1,0:T(1,128)}, u32[]{:S(2)}) copy-start(s32[1,384]{1,0:T(1,128)} %param.28) | copy-start | bytes 4612
  22.7 59.4 %collective-permute-start.8 = (f32[192,1536]{1,0:T(8,128)}, f32[192,1536]{1,0:T(8,128)}, u32[]{:S(2)}, u32[]{:S(2)}) collective-permute-start(f32[192,1536]{1,0:T(8,128)} %pad_maximum_fusion.1.refs_0_), channel_id=1, source_target_pairs={{0,16},{4,20},{8,24},{12,28},{16,0},{20,4},{24,8},{28,12},{1,17},{... | collective-permute-start | bytes 3538952 | tf_op jit(solution)/shard_map/ppermute | solution.py:610
  42.2 36.4 %copy-start.7 = (f32[384,768]{1,0:T(8,128)}, f32[384,768]{1,0:T(8,128)S(1)}, u32[]{:S(2)}) copy-start(f32[384,768]{1,0:T(8,128)S(1)} %collective-permute-done.near_ref) | copy-start | bytes 3538948
  42.2 41.4 %collective-permute-start.1 = (f32[384,768]{1,0:T(8,128)S(1)}, f32[384,768]{1,0:T(8,128)S(1)}, u32[]{:S(2)}, u32[]{:S(2)}) collective-permute-start(f32[384,768]{1,0:T(8,128)S(1)} %collective-permute-done.near_ref), channel_id=1, source_target_pairs={{0,1},{1,2},{2,3},{4,5},{5,6},{6,7},{8,9},{9,10},{10,11},{12,13},{... | collective-permute-start | bytes 3538952 | tf_op jit(solution)/shard_map/ppermute | solution.py:639
  46.7 25.1 %collective-permute-start.2 = (s32[1,384]{1,0:T(1,128)S(1)}, s32[1,384]{1,0:T(1,128)}, u32[]{:S(2)}, u32[]{:S(2)}) collective-permute-start(s32[1,384]{1,0:T(1,128)S(1)} %get-tuple-element.129), channel_id=1, source_target_pairs={{0,1},{1,2},{2,3},{4,5},{5,6},{6,7},{8,9},{9,10},{10,11},{12,13},{... | collective-permute-start | bytes 4616 | tf_op jit(solution)/shard_map/ppermute | solution.py:638
  50.7 90.5 %collective-permute-start.11 = (f32[384,768]{1,0:T(8,128)}, f32[384,768]{1,0:T(8,128)}, u32[]{:S(2)}, u32[]{:S(2)}) collective-permute-start(f32[384,768]{1,0:T(8,128)} %refs_4_.3), channel_id=1, source_target_pairs={{0,16},{4,20},{8,24},{12,28},{16,0},{20,4},{24,8},{28,12},{1,17},{... | collective-permute-start | bytes 3538952 | tf_op jit(solution)/shard_map/ppermute | solution.py:610
  52.3 172.8 %reduce-scatter.12.cloned.1.call-start = ((), (), s32[]{:S(2)}) async-start(), calls=%async_computation.7 | async-start | bytes 3932160
  52.3 26.3 %copy-start.28 = (f32[768]{0:T(1024)S(1)}, f32[768]{0:T(1024)}, u32[]{:S(2)}) copy-start(f32[768]{0:T(1024)} %param.20) | copy-start | bytes 9220
  52.3 26.9 %copy-start.35 = (f32[768]{0:T(1024)S(1)}, f32[768]{0:T(1024)}, u32[]{:S(2)}) copy-start(f32[768]{0:T(1024)} %param.21) | copy-start | bytes 9220
  52.3 27.5 %copy-start.5 = (f32[384,768]{1,0:T(8,128)S(1)}, f32[384,768]{1,0:T(8,128)}, u32[]{:S(2)}) copy-start(f32[384,768]{1,0:T(8,128)} %cot_ref.3) | copy-start | bytes 3538948
  71.8 8.0 %collective-permute-start.3 = (s32[1,384]{1,0:T(1,128)}, s32[1,384]{1,0:T(1,128)S(1)}, u32[]{:S(2)}, u32[]{:S(2)}) collective-permute-start(s32[1,384]{1,0:T(1,128)} %collective-permute-done.2), channel_id=1, source_target_pairs={{0,1},{1,2},{2,3},{4,5},{5,6},{6,7},{8,9},{9,10},{10,11},{12,13},{... | collective-permute-start | bytes 4616 | tf_op jit(solution)/shard_map/ppermute | solution.py:640
  79.8 65.0 %collective-permute-start.5 = (f32[384,768]{1,0:T(8,128)S(1)}, f32[384,768]{1,0:T(8,128)}, u32[]{:S(2)}, u32[]{:S(2)}) collective-permute-start(f32[384,768]{1,0:T(8,128)S(1)} %copy-done.5), channel_id=1, source_target_pairs={{0,4},{4,0},{8,12},{12,8},{16,20},{20,16},{24,28},{28,24},{1,5},{5... | collective-permute-start | bytes 3538952 | tf_op jit(solution)/shard_map/ppermute | solution.py:610
  80.6 64.3 %collective-permute-start.7 = (f32[192,1536]{1,0:T(8,128)}, f32[192,1536]{1,0:T(8,128)}, u32[]{:S(2)}, u32[]{:S(2)}) collective-permute-start(f32[192,1536]{1,0:T(8,128)} %pad_maximum_fusion.1.refs_0_), channel_id=1, source_target_pairs={{0,8},{4,12},{8,0},{12,4},{16,24},{20,28},{24,16},{28,20},{1,9},{5... | collective-permute-start | bytes 3538952 | tf_op jit(solution)/shard_map/ppermute | solution.py:610
  82.1 62.8 %collective-permute-start.12 = (f32[384,768]{1,0:T(8,128)}, f32[384,768]{1,0:T(8,128)}, u32[]{:S(2)}, u32[]{:S(2)}) collective-permute-start(f32[384,768]{1,0:T(8,128)} %collective-permute-done.10.refs_5_), channel_id=1, source_target_pairs={{0,16},{4,20},{8,24},{12,28},{16,0},{20,4},{24,8},{28,12},{1,17},{... | collective-permute-start | bytes 3538952 | tf_op jit(solution)/shard_map/ppermute | solution.py:610
  83.6 61.3 %collective-permute-start.9 = (f32[192,1536]{1,0:T(8,128)}, f32[192,1536]{1,0:T(8,128)}, u32[]{:S(2)}, u32[]{:S(2)}) collective-permute-start(f32[192,1536]{1,0:T(8,128)} %collective-permute-done.8.refs_2_), channel_id=1, source_target_pairs={{0,8},{4,12},{8,0},{12,4},{16,24},{20,28},{24,16},{28,20},{1,9},{5... | collective-permute-start | bytes 3538952 | tf_op jit(solution)/shard_map/ppermute | solution.py:610
  113.0 23.8 %copy-start.1 = (f32[384,768]{1,0:T(8,128)S(1)}, f32[384,768]{1,0:T(8,128)}, u32[]{:S(2)}) copy-start(f32[384,768]{1,0:T(8,128)} %own_ref.1) | copy-start | bytes 3538948
  141.2 3.7 collective-permute-start.4
  165.5 130.2 %reduce-scatter.10.cloned.1.call-start = ((), (), s32[]{:S(2)}) async-start(), calls=%async_computation.6 | async-start | bytes 7864320
  202.4 212.7 %reduce-scatter.14.cloned.1.call-start = ((), (), s32[]{:S(2)}) async-start(), calls=%async_computation.8 | async-start | bytes 5898240
  205.1 3.1 collective-permute-start.13
  207.3 10.3 %collective-permute-start.14 = (f32[384,768]{1,0:T(8,128)}, f32[384,768]{1,0:T(8,128)}, u32[]{:S(2)}, u32[]{:S(2)}) collective-permute-start(f32[384,768]{1,0:T(8,128)} %slice.155), channel_id=1, source_target_pairs={{0,4},{4,0},{8,12},{12,8},{16,20},{20,16},{24,28},{28,24},{1,5},{5... | collective-permute-start | bytes 3538952 | tf_op jit(solution)/shard_map/ppermute | solution.py:610
  226.3 26.1 %collective-permute-start.15 = (f32[1,192,512]{2,1,0:T(8,128)S(1)}, f32[1,192,512]{2,1,0:T(8,128)S(1)}, u32[]{:S(2)}, u32[]{:S(2)}) collective-permute-start(f32[1,192,512]{2,1,0:T(8,128)S(1)} %slice_select_fusion.3), channel_id=1, source_target_pairs={{0,1},{1,0},{2,3},{3,2},{4,5},{5,4},{6,7},{7,6},{8,9},{9,8},{10,11... | collective-permute-start | bytes 1179656 | tf_op jit(solution)/shard_map/ppermute | solution.py:702
  228.9 23.5 %copy-start.21 = (f32[1,1,384,512]{3,2,1,0:T(8,128)S(1)}, f32[1,1,384,512]{3,2,1,0:T(8,128)}, u32[]{:S(2)}) copy-start(f32[1,1,384,512]{3,2,1,0:T(8,128)} %reduce-scatter.12.cloned.1.call-done) | copy-start | bytes 2359300
  252.5 26.4 %collective-permute-start.16 = (f32[1,192,512]{2,1,0:T(8,128)S(1)}, f32[1,192,512]{2,1,0:T(8,128)S(1)}, u32[]{:S(2)}, u32[]{:S(2)}) collective-permute-start(f32[1,192,512]{2,1,0:T(8,128)S(1)} %select_add_fusion.1), channel_id=1, source_target_pairs={{0,2},{1,3},{2,0},{3,1},{4,6},{5,7},{6,4},{7,5},{8,10},{9,11},{10,... | collective-permute-start | bytes 1179656 | tf_op jit(solution)/shard_map/ppermute | solution.py:702
  295.6 16.0 %collective-permute-start.18 = (f32[4,96,1536]{2,1,0:T(8,128)}, f32[4,96,1536]{2,1,0:T(8,128)S(1)}, u32[]{:S(2)}, u32[]{:S(2)}) collective-permute-start(f32[4,96,1536]{2,1,0:T(8,128)} %slice_bitcast_fusion.2), channel_id=1, source_target_pairs={{0,4},{4,0},{8,12},{12,8},{16,20},{20,16},{24,28},{28,24},{1,5},{5... | collective-permute-start | bytes 7077896 | tf_op jit(solution)/shard_map/ppermute | solution.py:610
  295.6 16.0 %slice-start.1 = ((s8[4718592]{0:T(1024)(128)(4,1)}), s8[524288]{0:T(1024)(128)(4,1)S(1)}, s32[]{:S(2)}) async-start(s8[4718592]{0:T(1024)(128)(4,1)} %bitcast.70), calls=%async_computation.10 | async-start | bytes 1048576
  311.1 4.7 collective-permute-start.19
  318.7 176.8 %all-reduce.6.cloned.1.call-start = ((), (), s32[]{:S(2)}) async-start(), calls=%async_computation.5 | async-start | bytes 2359296 | tf_op jit(solution)/shard_map/psum | solution.py:781
  323.3 20.7 %collective-permute-start.17 = (f32[2,192,512]{2,1,0:T(8,128)}, f32[2,192,512]{2,1,0:T(8,128)}, u32[]{:S(2)}, u32[]{:S(2)}) collective-permute-start(f32[2,192,512]{2,1,0:T(8,128)} %slice_select_fusion), channel_id=1, source_target_pairs={{0,1},{1,0},{2,3},{3,2},{4,5},{5,4},{6,7},{7,6},{8,9},{9,8},{10,11... | collective-permute-start | bytes 2359304 | tf_op jit(solution)/shard_map/ppermute | solution.py:702
  334.2 70.9 %collective-permute-start.21 = (f32[1,192,512]{2,1,0:T(8,128)}, f32[1,192,512]{2,1,0:T(8,128)}, u32[]{:S(2)}, u32[]{:S(2)}) collective-permute-start(f32[1,192,512]{2,1,0:T(8,128)} %add.197), channel_id=1, source_target_pairs={{0,1},{1,0},{2,3},{3,2},{4,5},{5,4},{6,7},{7,6},{8,9},{9,8},{10,11... | collective-permute-start | bytes 1179656 | tf_op jit(solution)/shard_map/ppermute | solution.py:702
  346.7 63.7 %collective-permute-start.22 = (f32[2,192,512]{2,1,0:T(8,128)}, f32[2,192,512]{2,1,0:T(8,128)}, u32[]{:S(2)}, u32[]{:S(2)}) collective-permute-start(f32[2,192,512]{2,1,0:T(8,128)} %select_add_fusion), channel_id=1, source_target_pairs={{0,2},{1,3},{2,0},{3,1},{4,6},{5,7},{6,4},{7,5},{8,10},{9,11},{10,... | collective-permute-start | bytes 2359304 | tf_op jit(solution)/shard_map/ppermute | solution.py:702
  361.4 43.8 %copy-start.25 = (f32[1,192,512]{2,1,0:T(8,128)S(1)}, f32[1,192,512]{2,1,0:T(8,128)}, u32[]{:S(2)}) copy-start(f32[1,192,512]{2,1,0:T(8,128)} %add.197) | copy-start | bytes 1179652
  361.4 50.6 %collective-permute-start.20 = (f32[384,768]{1,0:T(8,128)}, f32[384,768]{1,0:T(8,128)}, u32[]{:S(2)}, u32[]{:S(2)}) collective-permute-start(f32[384,768]{1,0:T(8,128)} %get-tuple-element.117), channel_id=1, source_target_pairs={{1,0},{2,1},{3,2},{5,4},{6,5},{7,6},{9,8},{10,9},{11,10},{13,12},{... | collective-permute-start | bytes 3538952 | tf_op jit(solution)/shard_map/ppermute | solution.py:749
  366.6 1.3 collective-permute-start.23
  367.9 4.3 collective-permute-start.24
  372.2 3.8 collective-permute-start.25
  376.1 29.1 %collective-permute-start.26 = (f32[8,768]{1,0:T(8,128)S(1)}, f32[8,768]{1,0:T(8,128)S(1)}, u32[]{:S(2)}, u32[]{:S(2)}) collective-permute-start(f32[8,768]{1,0:T(8,128)S(1)} %add.214), channel_id=1, source_target_pairs={{0,1},{1,0},{2,3},{3,2},{4,5},{5,4},{6,7},{7,6},{8,9},{9,8},{10,11... | collective-permute-start | bytes 73736 | tf_op jit(solution)/shard_map/ppermute | solution.py:702
  405.1 4.7 collective-permute-start.27
  415.1 38.0 %collective-permute-start.29 = (f32[2,192,512]{2,1,0:T(8,128)S(1)}, f32[2,192,512]{2,1,0:T(8,128)}, u32[]{:S(2)}, u32[]{:S(2)}) collective-permute-start(f32[2,192,512]{2,1,0:T(8,128)S(1)} %add.203), channel_id=1, source_target_pairs={{0,1},{1,0},{2,3},{3,2},{4,5},{5,4},{6,7},{7,6},{8,9},{9,8},{10,11... | collective-permute-start | bytes 2359304 | tf_op jit(solution)/shard_map/ppermute | solution.py:702
  415.1 77.2 %collective-permute-start.28 = (f32[384,768]{1,0:T(8,128)}, f32[384,768]{1,0:T(8,128)}, u32[]{:S(2)}, u32[]{:S(2)}) collective-permute-start(f32[384,768]{1,0:T(8,128)} %slice_add_fusion.1), channel_id=1, source_target_pairs={{1,0},{2,1},{3,2},{5,4},{6,5},{7,6},{9,8},{10,9},{11,10},{13,12},{... | collective-permute-start | bytes 3538952 | tf_op jit(solution)/shard_map/ppermute | solution.py:783
  419.1 35.5 %copy-start.19 = (f32[1,192,512]{2,1,0:T(8,128)S(1)}, f32[1,192,512]{2,1,0:T(8,128)}, u32[]{:S(2)}) copy-start(f32[1,192,512]{2,1,0:T(8,128)} %get-tuple-element.90) | copy-start | bytes 1179652
  455.6 45.3 %collective-permute-start.30 = (f32[3,96,512]{2,1,0:T(8,128)}, f32[3,96,512]{2,1,0:T(8,128)}, u32[]{:S(2)}, u32[]{:S(2)}) collective-permute-start(f32[3,96,512]{2,1,0:T(8,128)} %broadcast_select_fusion.4), channel_id=1, source_target_pairs={{0,4},{4,0},{8,12},{12,8},{16,20},{20,16},{24,28},{28,24},{1,5},{5... | collective-permute-start | bytes 1769480 | tf_op jit(solution)/shard_map/ppermute | solution.py:610
  455.7 36.6 %copy-start.29 = (f32[768]{0:T(1024)S(1)}, f32[768]{0:T(1024)}, u32[]{:S(2)}) copy-start(f32[768]{0:T(1024)} %param.20) | copy-start | bytes 9220
  (29 other events, 136.3 us)
Sparse Core Ops, SparseCore 0:
  9.9 80.0 all-gather.2
  91.9 38.7 all-gather.4
  165.6 43.6 reduce-scatter.11
  212.1 70.1 reduce-scatter.9
  318.8 55.5 reduce-scatter.13
  416.5 78.9 all-reduce.5

commit v3 on v2

--- a/solution.py
+++ b/solution.py
@@ -62,6 +62,15 @@
     row_var = jnp.mean(centred * centred, axis=-1, keepdims=True)
     rate = lax.rsqrt(row_var + 1e-05)
     return centred * rate, rate
+
+
+def norm_back(grad, gain, xhat, rate):
+    scaled = grad * gain
+    return rate * (
+        scaled
+        - jnp.mean(scaled, axis=-1, keepdims=True)
+        - xhat * jnp.mean(scaled * xhat, axis=-1, keepdims=True)
+    )
 
 
 def turned(values):
@@ -476,6 +485,39 @@
     return grad_up, grad_down
 
 
+def resid_back_kernel(part_ref, given_ref, resid_ref, cot_ref, gain_ref, scale_ref, w_ref,
+                      grad_ref, att_ref, sums_ref):
+    grad = part_ref[...] + given_ref[...]
+    xhat, rate = norm_stats(resid_ref[...])
+    grad_resid = cot_ref[...] * scale_ref[0, 0] + norm_back(grad, gain_ref[...], xhat, rate)
+    grad_ref[...] = grad_resid
+    att_ref[...] = three(dot_nt, split(grad_resid), split(w_ref[...]))
+    gain_sum = jnp.sum(grad * xhat, axis=0, keepdims=True)
+    bias_sum = jnp.sum(grad, axis=0, keepdims=True)
+    sums_ref[...] = jnp.concatenate(
+        [gain_sum, bias_sum, jnp.zeros((6, gain_sum.shape[1]), F32)], axis=0
+    )
+
+
+def resid_back(part, given, resid, cot, gain, scale, w_full):
+    rows, model = resid.shape
+    fixed = lambda shape: pl.BlockSpec(shape, lambda j: (0, 0))
+    return pl.pallas_call(
+        resid_back_kernel,
+        grid=(1,),
+        in_specs=[fixed((rows, model))] * 4 + [fixed((1, model))]
+        + [pl.BlockSpec(memory_space=pltpu.SMEM), fixed((model, model))],
+        out_specs=[fixed((rows, model)), fixed((rows, model)), fixed((8, model))],
+        out_shape=[
+            jax.ShapeDtypeStruct((rows, model), F32),
+            jax.ShapeDtypeStruct((rows, model), F32),
+            jax.ShapeDtypeStruct((8, model), F32),
+        ],
+        cost_estimate=cost(6),
+        compiler_params=params(),
+    )(part, given, resid, cot, gain, scale, w_full)
+
+
 def place_rows(core_ref, out_ref, got):
     chips = out_ref.shape[1]
     tall = out_ref.shape[2]
@@ -552,15 +594,6 @@
         cost_estimate=cost(micros),
         compiler_params=params(),
     )(core, *fixed_args, *args)
-
-
-def norm_back(grad, gain, xhat, rate):
-    scaled = grad * gain
-    return rate * (
-        scaled
-        - jnp.mean(scaled, axis=-1, keepdims=True)
-        - xhat * jnp.mean(scaled * xhat, axis=-1, keepdims=True)
-    )
 
 
 def matmul(left, right):
@@ -648,6 +681,11 @@
     cosine = lax.dynamic_slice_in_dim(jnp.asarray(cos_all), place * rows, halo + rows, 0)
     sine = lax.dynamic_slice_in_dim(jnp.asarray(sin_all), place * rows, halo + rows, 0)
 
+    earlier = (embedding, earlier_outs[0], earlier_outs[1], earlier_outs[2])
+    base = sum(dwa_weights[i] * value for i, value in enumerate(earlier))
+    dots = jnp.stack([jnp.sum(cotangent * value) for value in earlier])
+    far, base, dots = lax.optimization_barrier((far, base, dots))
+
     q_rot, kv, normed_hi, normed_lo = project(
         far, near, block_input, gain1, bias1, qkv_full, cosine, sine
     )
@@ -666,39 +704,13 @@
     scatter_chips = lambda v: lax.psum_scatter(
         v, "dp", scatter_dimension=0, tiled=True, axis_index_groups=same_core
     )
-    out_part, gnorm_part, grads_a = call(0, 1, ())
-    shard_a = scatter_chips(grads_a)[0]
-    out_part, gnorm_part, grads_b = call(1, 2, (out_part, gnorm_part))
-    shard_b = scatter_chips(grads_b)[0]
-    grad_normed_two = gnorm_part[:rows] + swap(gnorm_part[rows:])
-    mlp_out = out_part[:rows] + swap(out_part[rows:])
-
-    block_out = resid + mlp_out
-    output = (
-        dwa_weights[0] * embedding
-        + dwa_weights[1] * earlier_outs[0]
-        + dwa_weights[2] * earlier_outs[1]
-        + dwa_weights[3] * earlier_outs[2]
-        + dwa_weights[4] * block_out
-    )
-    dwa_local = jnp.stack(
-        [
-            jnp.sum(cotangent * embedding),
-            jnp.sum(cotangent * earlier_outs[0]),
-            jnp.sum(cotangent * earlier_outs[1]),
-            jnp.sum(cotangent * earlier_outs[2]),
-            jnp.sum(cotangent * block_out),
-        ]
-    )
-    xhat2, rate2 = norm_stats(resid)
-    grad_resid = dwa_weights[4] * cotangent + norm_back(grad_normed_two, gain2, xhat2, rate2)
-    grad_gain_two = jnp.sum(grad_normed_two * xhat2, axis=0)
-    grad_bias_two = jnp.sum(grad_normed_two, axis=0)
-    grad_attended = outer_cols(grad_resid, out_full)
-
-    back_args = (q_rot, kv, grad_attended, seg_q_row, seg_k_col, cosine, sine)
-    pairs = model // 128
-    first_half = attend_back(0, pairs // 2, *back_args)
+    so_far, shards = (), []
+    for third_at in range(3):
+        out_part, gnorm_part, grads = call(third_at, 1, so_far)
+        so_far = (out_part, gnorm_part)
+        shards.append(scatter_chips(grads)[0])
+    given = swap(gnorm_part[rows:])
+
     shift = lambda v, bit: lax.ppermute(v, "seq", [(i, i ^ bit) for i in range(groups)])
     even = place % 2 == 0
 
@@ -719,34 +731,56 @@
         other = shift(kept, 1)
         return jnp.where(even, kept, other), jnp.where(even, other, kept)
 
-    kept_a = line_start(shard_a)
-    kept_a, back_args, first_half = lax.optimization_barrier((kept_a, back_args, first_half))
-    kept_a = line_middle(kept_a)
+    together = lax.optimization_barrier
+    shards[0], given = together((shards[0], given))
+    line_a = line_start(shards[0])
+    grad_resid, grad_attended, sums_two = resid_back(
+        gnorm_part, given, resid, cotangent, gain2, scale, out_full
+    )
+
+    back_args = (q_rot, kv, grad_attended, seg_q_row, seg_k_col, cosine, sine)
+    pairs = model // 128
+    line_a, back_args = together((line_a, back_args))
+    line_a = line_middle(line_a)
+    first_half = attend_back(0, pairs // 2, *back_args)
+    line_a, shards[1], back_args, first_half = together(
+        (line_a, shards[1], back_args, first_half)
+    )
+    line_b = line_start(shards[1])
+    ends_a = line_end(line_a)
     dq, dk, dv = attend_back(pairs // 2, pairs - pairs // 2, *back_args, before=first_half)
-    kept_a, dq, dk, dv = lax.optimization_barrier((kept_a, dq, dk, dv))
+    line_b, ends_a, dq, dk, dv = together((line_b, ends_a, dq, dk, dv))
+    line_b = line_middle(line_b)
     core_at = core.reshape(1).astype(jnp.int32)
     normed_parts = (normed_hi, normed_lo)
     grads_qk = weight_call(
         weights_qk_kernel, 9, core_at, chips, normed_parts, [(dq, 0), (dk, 1)], [halo + rows] * 2
     )
     given_qk = swap(grads_qk[1])
-    shard_b, dv = lax.optimization_barrier((shard_b, dv))
-    kept_b = line_start(shard_b)
+    line_b, dv, grad_resid = together((line_b, dv, grad_resid))
+    ends_b = line_end(line_b)
     grads_vo = weight_call(
         weights_vo_kernel, 9, core_at, chips, normed_parts,
         [(dv, 0), (attended, None), (grad_resid, 1)], [halo + rows] * 2 + [rows] * 2,
     )
-    shard_c = scatter_chips(
-        jnp.concatenate([grads_qk[0] + given_qk, grads_vo[0] + swap(grads_vo[1])], axis=2)
-    )[0]
-    kept_b, dk = lax.optimization_barrier((kept_b, dk))
-    kept_b = line_middle(kept_b)
+    grads_c = jnp.concatenate([grads_qk[0] + given_qk, grads_vo[0] + swap(grads_vo[1])], axis=2)
+    grads_c, shards[2], out_part = together((grads_c, shards[2], out_part))
+    shard_c = scatter_chips(grads_c)[0]
+    line_c = line_start(shards[2])
+    out_sib = swap(out_part[rows:])
+    line_c, ends_b, dk, dv = together((line_c, ends_b, dk, dv))
+    line_c = line_middle(line_c)
     dkv = jnp.concatenate([dk, dv], axis=1)
+
+    block_out = resid + out_part[:rows] + out_sib
+    output = base + dwa_weights[4] * block_out
+    dwa_local = jnp.concatenate([dots, jnp.sum(cotangent * block_out)[None]])
 
     wq, wkv = qkv_full[:, :model], qkv_full[:, model:]
     partial = outer_cols(dkv, wkv)
     own_part = partial[halo:] + outer_cols(dq, wq)
-    back_near = partial[rows:halo] + lax.ppermute(partial[:rows], "seq", behind)
+    (sent,) = together((partial,))
+    back_near = sent[rows:halo] + lax.ppermute(sent[:rows], "seq", behind)
 
     xhat1, rate1 = norm_stats(block_input)
     terms = (
@@ -759,7 +793,7 @@
 
     small = jnp.concatenate(
         [
-            grad_gain_one[None], grad_bias_one[None], grad_gain_two[None], grad_bias_two[None],
+            grad_gain_one[None], grad_bias_one[None], sums_two[:2],
             jnp.pad(dwa_local, (0, model - 5))[None], jnp.zeros((3, model), F32),
         ],
         axis=0,
@@ -768,24 +802,21 @@
     while bit < devices:
         small = small + exchange(small, bit)
         bit *= 2
-    bit = 1
-    while bit < groups:
-        small = small + shift(small, bit)
-        bit *= 2
-    ends_a = line_end(kept_a)
-    shard_c, back_near, ends_a, kept_b, small = lax.optimization_barrier(
-        (shard_c, back_near, ends_a, kept_b, small)
-    )
+    tall = shard_c.shape[0]
+    payload = jnp.concatenate([shard_c, small.reshape(-1, shard_c.shape[1])], axis=0)
+    ends_c = line_end(line_c)
+    payload, back_near, ends_c = together((payload, back_near, ends_c))
+    summed = lax.psum(payload, "seq")
+    grad_qkv, grad_wout = summed[:tall, :3 * model], summed[:tall, 3 * model:]
+    small = summed[tall:].reshape(-1, model)
     gain_one, bias_one, gain_two, bias_two = small[0], small[1], small[2], small[3]
     grad_dwa = small[4, :5]
-    sum_c = lax.psum(shard_c, "seq")
-    grad_qkv, grad_wout = sum_c[:, :3 * model], sum_c[:, 3 * model:]
     grad_normed_one = own_part + lax.ppermute(back_near, "seq", behind)
     grad_input = grad_resid + norm_back(grad_normed_one, gain1, xhat1, rate1)
     grad_up, grad_down = unpack_grads(
         *(
             jnp.concatenate(parts, axis=0)
-            for parts in zip(ends_a, line_end(kept_b))
+            for parts in zip(ends_a, ends_b, ends_c)
         ),
         swap, core, chips,
     )

time: 522 us -> 516 us (0.989)
  Pallas kernels: 175 us -> 188 us
  waiting for transfers between devices: 163 us -> 155 us
    ppermute x8 -> x9, waiting for transfers between devices: 72 us -> 49.4 us  [body(): lax.ppermute(v, 'seq', [(i, i ^ bit) for i in range(groups)])]
    psum x1, waiting for transfers between devices: 0.62 us -> 18 us  [body(): summed = lax.psum(payload, 'seq')]
    pallas_call x0 -> x1, Pallas kernels: none -> 7.72 us  [resid_back(): pl.pallas_call(resid_back_kernel, grid=(1,), in_specs=[fixed((rows, model...]
    ppermute x1, waiting for transfers between devices: 19.5 us -> 11.9 us  [body(): seg_near = lax.ppermute(seg_own, 'seq', ahead)]
    all_gather x2, waiting for transfers between devices: 5.85 us -> 0.02 us  [body(): gather = lambda v: lax.all_gather(v, 'dp', axis=0, tiled=True)]
    pallas_call x2 -> x3, Pallas kernels: 56.3 us -> 61.9 us  [mlp(): pl.pallas_call(functools.partial(mlp_kernel, len(ups), len(so_far) // 2),...]
    ppermute x8 -> x9, starting transfers between devices: 8.24 us -> 13.2 us  [body(): lax.ppermute(v, 'seq', [(i, i ^ bit) for i in range(groups)])]
    dot_general x3 -> x2, matrix products: 18.7 us -> 16 us  [outer_cols(): lax.dot_general(left, right, (((1,), (1,)), ((), ())), precision=HIGH)]
  transfers between devices with their start and end apart: 37 -> 39, of which waited for: 14 -> 18; matrix products, arithmetic and copies ran while one was open for 21% -> 19% of each run, Pallas kernels for 30% -> 33%
where the time goes in v3:
time: 516 us; the launch traced here: 511 us
  Pallas kernels  188 us (36%)
  waiting for transfers between devices  155 us (30%)
  other arithmetic  46.4 us (9%)
  starting transfers between devices  45.3 us (9%)
  local copies, waits for them, and re-layouts  42 us (8%)
  matrix products  19.7 us (4%)
  between operations  15.2 us (3%)
    pallas_call x3, Pallas kernels, mlp(): pl.pallas_call(functools.partial(mlp_kernel, len(ups), len(so_far) // 2),...  61.9 us
    ppermute x9, waiting for transfers between devices, body(): lax.ppermute(v, 'seq', [(i, i ^ bit) for i in range(groups)])  49.4 us
    pallas_call x2, Pallas kernels, attend_back(): pl.pallas_call(attend_back_kernel, grid=(count,), in_specs=[pl.BlockSpec(...  47.2 us
    ppermute x1, waiting for transfers between devices, body(): grad_normed_one = own_part + lax.ppermute(back_near, 'seq', behind)  39.3 us
    pallas_call x2, Pallas kernels, weight_call(): pl.pallas_call(kernel, grid_spec=pltpu.PrefetchScalarGridSpec(num_scalar_...  26.2 us
    pallas_call x1, Pallas kernels, attend(): pl.pallas_call(attend_kernel, grid=(pairs,), in_specs=[pl.BlockSpec((rows...  23.1 us
    pallas_call x1, Pallas kernels, project(): pl.pallas_call(qkv_kernel, grid=(3 * third,), in_specs=[whole((rows, mode...  21.7 us
    ppermute x1, waiting for transfers between devices, body(): near = lax.ppermute(block_input, 'seq', ahead)  18 us
  transfers between devices with their start and end apart: 39, of which 18 were waited for; matrix products, arithmetic and copies ran while one was open for 19% of the time, Pallas kernels for 33%

profile of v3, /device:TPU:0, one launch (start us, length us, event | category | flops | bytes accessed | tf_op | source)
XLA Modules:
  0.0 511.4 jit_solution(6296537166675199650)
XLA Ops:
  8.0 1.9 reshape.148
  11.9 4.6 collective-permute-start
  24.2 18.0 %collective-permute-done.near_ref = f32[384,768]{1,0:T(8,128)S(1)} collective-permute-done((f32[384,768]{1,0:T(8,128)S(1)}, f32[384,768]{1,0:T(8,128)S(1)}, u32[]{:S(2)}, u32[]{:S(2)}) %collective-permute-start) | collective-permute-done | bytes 1179680 | tf_op jit(solution)/shard_map/ppermute | solution.py:670
  42.3 4.4 collective-permute-start.1
  46.7 4.0 collective-permute-start.2
  51.4 7.4 %fusion.17 = (f32[]{:T(128)}, f32[]{:T(128)}, f32[]{:T(128)}, f32[]{:T(128)}, f32[384,768]{1,0:T(8,128)}) fusion(f32[384,768]{1,0:T(8,128)S(1)} %copy-done.10, f32[3,384,768]{2,1,0:T(8,128)} %param.18, f32[384,768]{1,0:T(8,128)} %param.17, f32[]{:T(128)} %bitcast.5, f32[]{:T(128)} %bitcast.3, f32[]{:T(128)} %bitcast.1, f32[]{:T(128)} %bitcast), kind=kLoop, calls=%fused_computation.32 | loop fusion | flops 4423676 | bytes 7077920 | tf_op jit(solution)/shard_map/reduce_sum | solution.py:686
  59.9 11.9 %collective-permute-done.2 = s32[1,384]{1,0:T(1,128)} collective-permute-done((s32[1,384]{1,0:T(1,128)S(1)}, s32[1,384]{1,0:T(1,128)}, u32[]{:S(2)}, u32[]{:S(2)}) %collective-permute-start.2) | collective-permute-done | bytes 1568 | tf_op jit(solution)/shard_map/ppermute | solution.py:671
  71.8 4.9 collective-permute-start.3
  76.7 3.2 pad_maximum_fusion.3
  86.4 21.7 %shard_map.239 = (f32[384,768]{1,0:T(8,128)}, f32[1152,1536]{1,0:T(8,128)}, bf16[1152,768]{1,0:T(8,128)(2,1)}, bf16[1152,768]{1,0:T(8,128)(2,1)}) custom-call(f32[384,768]{1,0:T(8,128)} %copy-done.5, f32[384,768]{1,0:T(8,128)} %copy-done.3, f32[384,768]{1,0:T(8,128)} %own_ref.1, f32[1,768]{1,0:T(1,128)} %broadcast_in_dim.47.gain_ref, ...), custom_call_target="tpu_custom_call" | custom-call | flops 22000001024 | bytes 1048576 | tf_op jit(solution)/shard_map/pallas_call | solution.py:144
  109.5 23.1 %shard_map.240.att_ref = f32[384,768]{1,0:T(8,128)} custom-call(f32[384,768]{1,0:T(8,128)} %get-tuple-element.108.q_ref, f32[1152,1536]{1,0:T(8,128)} %get-tuple-element.109.k_ref.v_ref, f32[1152,1536]{1,0:T(8,128)} %get-tuple-element.109.k_ref.v_ref, s32[384,128]{1,0:T(8,128)} %broadcast_in_dim.49.segq_ref, s32[8,1152]{1,0:T(8,128)} %broadcast_in_dim.51.segk_ref), custom_call_target="tpu_custom_call" | custom-call | flops 26400000000 | bytes 1048576 | tf_op jit(solution)/shard_map/pallas_call | solution.py:236
  132.6 3.7 convolution_add_fusion.resid_ref
  138.4 4.3 collective-permute-done.12.refs_7_
  142.8 2.0 collective-permute-done.9.refs_3_
  145.8 19.9 %shard_map.241 = (f32[768,768]{1,0:T(8,128)}, f32[768,768]{1,0:T(8,128)}, f32[4,1,384,512]{3,2,1,0:T(8,128)}) custom-call(s32[1]{0:T(128)} %bitcast.13.chip_ref, f32[384,768]{1,0:T(8,128)} %copy-done.13, f32[384,768]{1,0:T(8,128)} %copy-done.37, f32[384,768]{1,0:T(8,128)} %cot_ref.7, f32[384,768]{1,0:T(8,128)} %collective-permute-done.5.cot_other_ref, ...), custom_call_target="tpu_custom_call" | custom-call | flops 19800000512 | bytes 1048576 | tf_op jit(solution)/shard_map/pallas_call | solution.py:457
  165.8 20.9 %shard_map.242 = (f32[768,768]{1,0:T(8,128)}, f32[768,768]{1,0:T(8,128)}, f32[4,1,384,512]{3,2,1,0:T(8,128)}) custom-call(s32[1]{0:T(128)} %bitcast.13.chip_ref, f32[384,768]{1,0:T(8,128)} %copy-done.13, f32[384,768]{1,0:T(8,128)} %copy-done.37, f32[384,768]{1,0:T(8,128)} %cot_ref.7, f32[384,768]{1,0:T(8,128)} %collective-permute-done.5.cot_other_ref, ...), custom_call_target="tpu_custom_call" | custom-call | flops 19800000512 | bytes 1048576 | tf_op jit(solution)/shard_map/pallas_call | solution.py:457
  186.9 21.1 %shard_map.243 = (f32[768,768]{1,0:T(8,128)}, f32[768,768]{1,0:T(8,128)}, f32[4,1,384,512]{3,2,1,0:T(8,128)}) custom-call(s32[1]{0:T(128)} %bitcast.13.chip_ref, f32[384,768]{1,0:T(8,128)} %copy-done.13, f32[384,768]{1,0:T(8,128)} %copy-done.37, f32[384,768]{1,0:T(8,128)} %cot_ref.7, f32[384,768]{1,0:T(8,128)} %collective-permute-done.5.cot_other_ref, ...), custom_call_target="tpu_custom_call" | custom-call | flops 19800000512 | bytes 1048576 | tf_op jit(solution)/shard_map/pallas_call | solution.py:457
  209.7 2.5 collective-permute-done.13.given_ref
  215.6 7.7 %shard_map.244 = (f32[384,768]{1,0:T(8,128)}, f32[384,768]{1,0:T(8,128)}, f32[8,768]{1,0:T(8,128)}) custom-call(f32[768,768]{1,0:T(8,128)} %get-tuple-element.90.part_ref, f32[384,768]{1,0:T(8,128)} %copy-done.38, f32[384,768]{1,0:T(8,128)} %copy-done.13, f32[384,768]{1,0:T(8,128)} %cot_ref.7, f32[1,768]{1,0:T(1,128)} %broadcast_in_dim.52.gain_ref, ...), custom_call_target="tpu_custom_call" | custom-call | flops 6600000000 | bytes 1048576 | tf_op jit(solution)/shard_map/pallas_call | solution.py:505
  223.3 1.8 collective-permute-done.14
  226.9 2.6 collective-permute-start.15
  229.5 23.5 %shard_map.245 = (f32[384,768]{1,0:T(8,128)}, f32[1152,768]{1,0:T(8,128)}, f32[1152,768]{1,0:T(8,128)}) custom-call(f32[384,768]{1,0:T(8,128)} %get-tuple-element.108.q_ref, f32[1152,1536]{1,0:T(8,128)} %get-tuple-element.109.k_ref.v_ref, f32[1152,1536]{1,0:T(8,128)} %get-tuple-element.109.k_ref.v_ref, f32[384,768]{1,0:T(8,128)} %get-tuple-element.110.g_ref, ...), custom_call_target="tpu_custom_call" | custom-call | flops 23100000256 | bytes 1048576 | tf_op jit(solution)/shard_map/pallas_call | solution.py:328
  253.0 2.9 reduce-scatter.15.cloned.1.call-done
  259.2 23.7 %shard_map.246 = (f32[384,768]{1,0:T(8,128)}, f32[1152,768]{1,0:T(8,128)}, f32[1152,768]{1,0:T(8,128)}) custom-call(f32[384,768]{1,0:T(8,128)} %get-tuple-element.108.q_ref, f32[1152,1536]{1,0:T(8,128)} %get-tuple-element.109.k_ref.v_ref, f32[1152,1536]{1,0:T(8,128)} %get-tuple-element.109.k_ref.v_ref, ...), custom_call_target="tpu_custom_call", output_to_operand_aliasing={{0}: (8, {}), {1}: (9, {}), {2}: (10, {})} | custom-call | flops 23100000256 | bytes 1048576 | tf_op jit(solution)/shard_map/pallas_call | solution.py:328
  284.0 2.4 collective-permute-start.19
  286.4 12.6 %shard_map.247 = f32[2,4,96,1536]{3,2,1,0:T(8,128)} custom-call(s32[1]{0:T(128)} %bitcast.12.core_ref, bf16[1152,768]{1,0:T(8,128)(2,1)} %get-tuple-element.83.hi_ref, bf16[1152,768]{1,0:T(8,128)(2,1)} %get-tuple-element.84.lo_ref, f32[384,768]{1,0:T(8,128)} %get-tuple-element.121.dq_ref, f32[1152,768]{1,0:T(8,128)} %get-tuple-element.133.dk_ref), custom_call_target="tpu_custom_call" | custom-call | flops 9900000256 | bytes 1048576 | tf_op jit(solution)/shard_map/pallas_call | solution.py:584
  299.1 3.3 slice_bitcast_fusion.2
  304.4 13.6 %shard_map.248 = f32[2,4,96,1536]{3,2,1,0:T(8,128)} custom-call(s32[1]{0:T(128)} %bitcast.12.core_ref, bf16[1152,768]{1,0:T(8,128)(2,1)} %get-tuple-element.83.hi_ref, bf16[1152,768]{1,0:T(8,128)(2,1)} %get-tuple-element.84.lo_ref, f32[1152,768]{1,0:T(8,128)} %get-tuple-element.134.dv_ref, f32[384,768]{1,0:T(8,128)} %shard_map.240.att_ref, ...), custom_call_target="tpu_custom_call" | custom-call | flops 9900000256 | bytes 1048576 | tf_op jit(solution)/shard_map/pallas_call | solution.py:584
  318.0 1.8 slice_bitcast_fusion
  320.3 4.1 collective-permute-done.20
  324.8 2.4 pad_maximum_fusion
  335.4 8.3 %collective-permute-done.23 = f32[1,192,512]{2,1,0:T(8,128)S(1)} collective-permute-done((f32[1,192,512]{2,1,0:T(8,128)S(1)}, f32[1,192,512]{2,1,0:T(8,128)S(1)}, u32[]{:S(2)}, u32[]{:S(2)}) %collective-permute-start.23) | collective-permute-done | bytes 393248 | tf_op jit(solution)/shard_map/ppermute | solution.py:714
  344.8 6.5 %collective-permute-done.22 = f32[1,192,512]{2,1,0:T(8,128)S(1)} collective-permute-done((f32[1,192,512]{2,1,0:T(8,128)S(1)}, f32[1,192,512]{2,1,0:T(8,128)S(1)}, u32[]{:S(2)}, u32[]{:S(2)}) %collective-permute-start.22) | collective-permute-done | bytes 393248 | tf_op jit(solution)/shard_map/ppermute | solution.py:714
  351.5 11.6 %fusion = f32[1152,768]{1,0:T(8,128)S(1)} fusion(f32[1152,768]{1,0:T(8,128)} %get-tuple-element.134.dv_ref, f32[1152,768]{1,0:T(8,128)S(1)} %copy-done.39, f32[768,2304]{1,0:T(8,128)} %all-gather.3.cloned.1.call-done.w_ref), kind=kOutput, calls=%fused_computation | convolution fusion | flops 8155496448 | bytes 15335424 | tf_op jit(solution)/shard_map/dot_general | solution.py:608
  363.0 2.3 collective-permute-start.28
  365.8 4.4 fusion.21
  372.8 10.9 %collective-permute-done.28 = f32[1,192,512]{2,1,0:T(8,128)S(1)} collective-permute-done((f32[1,192,512]{2,1,0:T(8,128)S(1)}, f32[1,192,512]{2,1,0:T(8,128)S(1)}, u32[]{:S(2)}, u32[]{:S(2)}) %collective-permute-start.28) | collective-permute-done | bytes 393248 | tf_op jit(solution)/shard_map/ppermute | solution.py:714
  384.7 2.7 multiply_reduce_fusion.1
  396.1 20.6 %collective-permute-done.29 = f32[1,192,512]{2,1,0:T(8,128)} collective-permute-done((f32[1,192,512]{2,1,0:T(8,128)}, f32[1,192,512]{2,1,0:T(8,128)}, u32[]{:S(2)}, u32[]{:S(2)}) %collective-permute-start.29) | collective-permute-done | bytes 393248 | tf_op jit(solution)/shard_map/ppermute | solution.py:714
  416.7 2.1 broadcast_select_fusion.4
  420.7 2.9 slice_add_fusion
  423.6 2.4 pad_maximum_fusion.1
  431.8 2.1 broadcast_select_fusion.1
  437.5 39.3 %collective-permute-done.30 = f32[384,768]{1,0:T(8,128)} collective-permute-done((f32[384,768]{1,0:T(8,128)}, f32[384,768]{1,0:T(8,128)}, u32[]{:S(2)}, u32[]{:S(2)}) %collective-permute-start.30) | collective-permute-done | bytes 1179680 | tf_op jit(solution)/shard_map/ppermute | solution.py:814
  476.8 2.2 fusion.20
  480.5 18.0 %all-reduce.7.cloned.1.call-done = f32[98,3072]{1,0:T(8,128)} async-done(((f32[98,3072]{1,0:T(8,128)}), f32[98,3072]{1,0:T(8,128)}) %all-reduce.7.cloned.1.call-update) | async-done | bytes 1204240 | tf_op jit(solution)/shard_map/psum | solution.py:809
  500.5 2.1 slice.212
  502.6 1.7 slice.213
  (233 shorter events, 74.2 us)
Async XLA Ops:
  7.2 78.7 %all-gather.3.cloned.1.call-start = ((), (), s32[]{:S(2)}) async-start(), calls=%async_computation.4 | async-start | bytes 7962624 | tf_op jit(solution)/shard_map/all_gather | solution.py:646
  7.9 124.7 %all-gather.5.cloned.1.call-start = ((), (), s32[]{:S(2)}) async-start(), calls=%async_computation.5 | async-start | bytes 2654208 | tf_op jit(solution)/shard_map/all_gather | solution.py:646
  11.4 8.9 %collective-permute-start.6 = (f32[96,1536]{1,0:T(8,128)}, f32[96,1536]{1,0:T(8,128)}, u32[]{:S(2)}, u32[]{:S(2)}) collective-permute-start(f32[96,1536]{1,0:T(8,128)} %select_n.129), channel_id=1, source_target_pairs={{0,4},{4,0},{8,12},{12,8},{16,20},{20,16},{24,28},{28,24},{1,5},{5... | collective-permute-start | bytes 1769480 | tf_op jit(solution)/shard_map/ppermute | solution.py:643
  11.9 30.4 %collective-permute-start = (f32[384,768]{1,0:T(8,128)S(1)}, f32[384,768]{1,0:T(8,128)S(1)}, u32[]{:S(2)}, u32[]{:S(2)}) collective-permute-start(f32[384,768]{1,0:T(8,128)S(1)} %copy-done), channel_id=1, source_target_pairs={{0,1},{1,2},{2,3},{4,5},{5,6},{6,7},{8,9},{9,10},{10,11},{12,13},{... | collective-permute-start | bytes 3538952 | tf_op jit(solution)/shard_map/ppermute | solution.py:670
  16.5 66.8 %collective-permute-start.10 = (f32[384,768]{1,0:T(8,128)}, f32[384,768]{1,0:T(8,128)}, u32[]{:S(2)}, u32[]{:S(2)}) collective-permute-start(f32[384,768]{1,0:T(8,128)} %refs_4_.5), channel_id=1, source_target_pairs={{0,8},{4,12},{8,0},{12,4},{16,24},{20,28},{24,16},{28,20},{1,9},{5... | collective-permute-start | bytes 3538952 | tf_op jit(solution)/shard_map/ppermute | solution.py:643
  21.6 25.1 %copy-start.36 = (s32[1,384]{1,0:T(1,128)S(1)}, s32[1,384]{1,0:T(1,128)}, u32[]{:S(2)}) copy-start(s32[1,384]{1,0:T(1,128)} %param.28) | copy-start | bytes 4612
  21.6 29.1 %copy-start.10 = (f32[384,768]{1,0:T(8,128)S(1)}, f32[384,768]{1,0:T(8,128)}, u32[]{:S(2)}) copy-start(f32[384,768]{1,0:T(8,128)} %cot_ref.7) | copy-start | bytes 3538948
  21.6 29.2 %copy-start.31 = (f32[5]{0:T(128)S(1)}, f32[5]{0:T(128)}, u32[]{:S(2)}) copy-start(f32[5]{0:T(128)} %param.19) | copy-start | bytes 64
  22.7 62.1 %collective-permute-start.8 = (f32[192,1536]{1,0:T(8,128)}, f32[192,1536]{1,0:T(8,128)}, u32[]{:S(2)}, u32[]{:S(2)}) collective-permute-start(f32[192,1536]{1,0:T(8,128)} %pad_maximum_fusion.2.refs_0_), channel_id=1, source_target_pairs={{0,16},{4,20},{8,24},{12,28},{16,0},{20,4},{24,8},{28,12},{1,17},{... | collective-permute-start | bytes 3538952 | tf_op jit(solution)/shard_map/ppermute | solution.py:643
  42.3 16.5 %copy-start.3 = (f32[384,768]{1,0:T(8,128)}, f32[384,768]{1,0:T(8,128)S(1)}, u32[]{:S(2)}) copy-start(f32[384,768]{1,0:T(8,128)S(1)} %collective-permute-done.near_ref) | copy-start | bytes 3538948
  42.3 43.1 %collective-permute-start.1 = (f32[384,768]{1,0:T(8,128)S(1)}, f32[384,768]{1,0:T(8,128)S(1)}, u32[]{:S(2)}, u32[]{:S(2)}) collective-permute-start(f32[384,768]{1,0:T(8,128)S(1)} %collective-permute-done.near_ref), channel_id=1, source_target_pairs={{0,1},{1,2},{2,3},{4,5},{5,6},{6,7},{8,9},{9,10},{10,11},{12,13},{... | collective-permute-start | bytes 3538952 | tf_op jit(solution)/shard_map/ppermute | solution.py:672
  46.7 25.1 %collective-permute-start.2 = (s32[1,384]{1,0:T(1,128)S(1)}, s32[1,384]{1,0:T(1,128)}, u32[]{:S(2)}, u32[]{:S(2)}) collective-permute-start(s32[1,384]{1,0:T(1,128)S(1)} %get-tuple-element.181), channel_id=1, source_target_pairs={{0,1},{1,2},{2,3},{4,5},{5,6},{6,7},{8,9},{9,10},{10,11},{12,13},{... | collective-permute-start | bytes 4616 | tf_op jit(solution)/shard_map/ppermute | solution.py:671
  50.7 85.6 %collective-permute-start.5 = (f32[384,768]{1,0:T(8,128)S(1)}, f32[384,768]{1,0:T(8,128)}, u32[]{:S(2)}, u32[]{:S(2)}) collective-permute-start(f32[384,768]{1,0:T(8,128)S(1)} %copy-done.10), channel_id=1, source_target_pairs={{0,4},{4,0},{8,12},{12,8},{16,20},{20,16},{24,28},{28,24},{1,5},{5... | collective-permute-start | bytes 3538952 | tf_op jit(solution)/shard_map/ppermute | solution.py:643
  50.8 161.5 %reduce-scatter.13.cloned.1.call-start = ((), (), s32[]{:S(2)}) async-start(), calls=%async_computation.7 | async-start | bytes 3932160
  58.8 21.1 %copy-start.29 = (f32[768]{0:T(1024)S(1)}, f32[768]{0:T(1024)}, u32[]{:S(2)}) copy-start(f32[768]{0:T(1024)} %param.20) | copy-start | bytes 9220
  58.8 21.7 %copy-start.33 = (f32[768]{0:T(1024)S(1)}, f32[768]{0:T(1024)}, u32[]{:S(2)}) copy-start(f32[768]{0:T(1024)} %param.21) | copy-start | bytes 9220
  71.8 9.2 %collective-permute-start.3 = (s32[1,384]{1,0:T(1,128)}, s32[1,384]{1,0:T(1,128)S(1)}, u32[]{:S(2)}, u32[]{:S(2)}) collective-permute-start(s32[1,384]{1,0:T(1,128)} %collective-permute-done.2), channel_id=1, source_target_pairs={{0,1},{1,2},{2,3},{4,5},{5,6},{6,7},{8,9},{9,10},{10,11},{12,13},{... | collective-permute-start | bytes 4616 | tf_op jit(solution)/shard_map/ppermute | solution.py:673
  81.1 57.4 %collective-permute-start.11 = (f32[384,768]{1,0:T(8,128)}, f32[384,768]{1,0:T(8,128)}, u32[]{:S(2)}, u32[]{:S(2)}) collective-permute-start(f32[384,768]{1,0:T(8,128)} %refs_4_.5), channel_id=1, source_target_pairs={{0,16},{4,20},{8,24},{12,28},{16,0},{20,4},{24,8},{28,12},{1,17},{... | collective-permute-start | bytes 3538952 | tf_op jit(solution)/shard_map/ppermute | solution.py:643
  83.3 55.2 %collective-permute-start.7 = (f32[192,1536]{1,0:T(8,128)}, f32[192,1536]{1,0:T(8,128)}, u32[]{:S(2)}, u32[]{:S(2)}) collective-permute-start(f32[192,1536]{1,0:T(8,128)} %pad_maximum_fusion.2.refs_0_), channel_id=1, source_target_pairs={{0,8},{4,12},{8,0},{12,4},{16,24},{20,28},{24,16},{28,20},{1,9},{5... | collective-permute-start | bytes 3538952 | tf_op jit(solution)/shard_map/ppermute | solution.py:643
  84.8 57.9 %collective-permute-start.12 = (f32[384,768]{1,0:T(8,128)}, f32[384,768]{1,0:T(8,128)}, u32[]{:S(2)}, u32[]{:S(2)}) collective-permute-start(f32[384,768]{1,0:T(8,128)} %collective-permute-done.10.refs_5_), channel_id=1, source_target_pairs={{0,16},{4,20},{8,24},{12,28},{16,0},{20,4},{24,8},{28,12},{1,17},{... | collective-permute-start | bytes 3538952 | tf_op jit(solution)/shard_map/ppermute | solution.py:643
  85.3 59.4 %collective-permute-start.9 = (f32[192,1536]{1,0:T(8,128)}, f32[192,1536]{1,0:T(8,128)}, u32[]{:S(2)}, u32[]{:S(2)}) collective-permute-start(f32[192,1536]{1,0:T(8,128)} %collective-permute-done.8.refs_2_), channel_id=1, source_target_pairs={{0,8},{4,12},{8,0},{12,4},{16,24},{20,28},{24,16},{28,20},{1,9},{5... | collective-permute-start | bytes 3538952 | tf_op jit(solution)/shard_map/ppermute | solution.py:643
  109.5 23.1 %copy-start.1 = (f32[384,768]{1,0:T(8,128)S(1)}, f32[384,768]{1,0:T(8,128)}, u32[]{:S(2)}) copy-start(f32[384,768]{1,0:T(8,128)} %own_ref.1) | copy-start | bytes 3538948
  136.3 8.4 %collective-permute-start.4 = (f32[384,768]{1,0:T(8,128)S(1)}, f32[384,768]{1,0:T(8,128)S(1)}, u32[]{:S(2)}, u32[]{:S(2)}) collective-permute-start(f32[384,768]{1,0:T(8,128)S(1)} %convolution_add_fusion.resid_ref), channel_id=1, source_target_pairs={{0,4},{4,0},{8,12},{12,8},{16,20},{20,16},{24,28},{28,24},{1,5},{5... | collective-permute-start | bytes 3538952 | tf_op jit(solution)/shard_map/ppermute | solution.py:643
  165.7 90.2 %reduce-scatter.15.cloned.1.call-start = ((), (), s32[]{:S(2)}) async-start(), calls=%async_computation.8 | async-start | bytes 3932160
  186.7 140.5 %reduce-scatter.17.cloned.1.call-start = ((), (), s32[]{:S(2)}) async-start(), calls=%async_computation.9 | async-start | bytes 3932160
  209.4 2.9 collective-permute-start.13
  209.5 214.1 %reduce-scatter.19.cloned.1.call-start = ((), (), s32[]{:S(2)}) async-start(), calls=%async_computation.10 | async-start | bytes 5898240
  213.9 11.2 %collective-permute-start.14 = (f32[1,192,512]{2,1,0:T(8,128)S(1)}, f32[1,192,512]{2,1,0:T(8,128)S(1)}, u32[]{:S(2)}, u32[]{:S(2)}) collective-permute-start(f32[1,192,512]{2,1,0:T(8,128)S(1)} %slice_select_fusion.6), channel_id=1, source_target_pairs={{0,1},{1,0},{2,3},{3,2},{4,5},{5,4},{6,7},{7,6},{8,9},{9,8},{10,11... | collective-permute-start | bytes 1179656 | tf_op jit(solution)/shard_map/ppermute | solution.py:714
  226.9 26.1 %collective-permute-start.15 = (f32[1,192,512]{2,1,0:T(8,128)S(1)}, f32[1,192,512]{2,1,0:T(8,128)S(1)}, u32[]{:S(2)}, u32[]{:S(2)}) collective-permute-start(f32[1,192,512]{2,1,0:T(8,128)S(1)} %select_add_fusion.2), channel_id=1, source_target_pairs={{0,2},{1,3},{2,0},{3,1},{4,6},{5,7},{6,4},{7,5},{8,10},{9,11},{10,... | collective-permute-start | bytes 1179656 | tf_op jit(solution)/shard_map/ppermute | solution.py:714
  257.1 25.8 %copy-start.16 = (f32[1,1,384,512]{3,2,1,0:T(8,128)S(1)}, f32[1,1,384,512]{3,2,1,0:T(8,128)}, u32[]{:S(2)}) copy-start(f32[1,1,384,512]{3,2,1,0:T(8,128)} %reduce-scatter.15.cloned.1.call-done) | copy-start | bytes 2359300
  257.1 25.8 %collective-permute-start.16 = (f32[1,192,512]{2,1,0:T(8,128)S(1)}, f32[1,192,512]{2,1,0:T(8,128)S(1)}, u32[]{:S(2)}, u32[]{:S(2)}) collective-permute-start(f32[1,192,512]{2,1,0:T(8,128)S(1)} %slice_select_fusion.5), channel_id=1, source_target_pairs={{0,1},{1,0},{2,3},{3,2},{4,5},{5,4},{6,7},{7,6},{8,9},{9,8},{10,11... | collective-permute-start | bytes 1179656 | tf_op jit(solution)/shard_map/ppermute | solution.py:714
  258.6 24.4 %collective-permute-start.17 = (f32[1,192,512]{2,1,0:T(8,128)S(1)}, f32[1,192,512]{2,1,0:T(8,128)S(1)}, u32[]{:S(2)}, u32[]{:S(2)}) collective-permute-start(f32[1,192,512]{2,1,0:T(8,128)S(1)} %add.178), channel_id=1, source_target_pairs={{0,1},{1,0},{2,3},{3,2},{4,5},{5,4},{6,7},{7,6},{8,9},{9,8},{10,11... | collective-permute-start | bytes 1179656 | tf_op jit(solution)/shard_map/ppermute | solution.py:714
  284.0 19.6 %collective-permute-start.19 = (f32[1,192,512]{2,1,0:T(8,128)S(1)}, f32[1,192,512]{2,1,0:T(8,128)S(1)}, u32[]{:S(2)}, u32[]{:S(2)}) collective-permute-start(f32[1,192,512]{2,1,0:T(8,128)S(1)} %select_add_fusion.1), channel_id=1, source_target_pairs={{0,2},{1,3},{2,0},{3,1},{4,6},{5,7},{6,4},{7,5},{8,10},{9,11},{10,... | collective-permute-start | bytes 1179656 | tf_op jit(solution)/shard_map/ppermute | solution.py:714
  302.3 17.6 %collective-permute-start.18 = (f32[4,96,1536]{2,1,0:T(8,128)}, f32[4,96,1536]{2,1,0:T(8,128)S(1)}, u32[]{:S(2)}, u32[]{:S(2)}) collective-permute-start(f32[4,96,1536]{2,1,0:T(8,128)} %slice_bitcast_fusion.2), channel_id=1, source_target_pairs={{0,4},{4,0},{8,12},{12,8},{16,20},{20,16},{24,28},{28,24},{1,5},{5... | collective-permute-start | bytes 7077896 | tf_op jit(solution)/shard_map/ppermute | solution.py:643
  319.8 4.6 collective-permute-start.20
  327.3 171.1 %all-reduce.7.cloned.1.call-start = ((), (), s32[]{:S(2)}) async-start(), calls=%async_computation.6 | async-start | bytes 2555904 | tf_op jit(solution)/shard_map/psum | solution.py:809
  331.7 12.0 %collective-permute-start.23 = (f32[1,192,512]{2,1,0:T(8,128)S(1)}, f32[1,192,512]{2,1,0:T(8,128)S(1)}, u32[]{:S(2)}, u32[]{:S(2)}) collective-permute-start(f32[1,192,512]{2,1,0:T(8,128)S(1)} %copy-done.22), channel_id=1, source_target_pairs={{0,1},{1,0},{2,3},{3,2},{4,5},{5,4},{6,7},{7,6},{8,9},{9,8},{10,11... | collective-permute-start | bytes 1179656 | tf_op jit(solution)/shard_map/ppermute | solution.py:714
  332.3 19.0 %collective-permute-start.22 = (f32[1,192,512]{2,1,0:T(8,128)S(1)}, f32[1,192,512]{2,1,0:T(8,128)S(1)}, u32[]{:S(2)}, u32[]{:S(2)}) collective-permute-start(f32[1,192,512]{2,1,0:T(8,128)S(1)} %slice_select_fusion.4), channel_id=1, source_target_pairs={{0,1},{1,0},{2,3},{3,2},{4,5},{5,4},{6,7},{7,6},{8,9},{9,8},{10,11... | collective-permute-start | bytes 1179656 | tf_op jit(solution)/shard_map/ppermute | solution.py:714
  344.7 39.9 %collective-permute-start.21 = (f32[384,768]{1,0:T(8,128)S(1)}, f32[384,768]{1,0:T(8,128)S(1)}, u32[]{:S(2)}, u32[]{:S(2)}) collective-permute-start(f32[384,768]{1,0:T(8,128)S(1)} %slice.171), channel_id=1, source_target_pairs={{0,4},{4,0},{8,12},{12,8},{16,20},{20,16},{24,28},{28,24},{1,5},{5... | collective-permute-start | bytes 3538952 | tf_op jit(solution)/shard_map/ppermute | solution.py:643
  363.0 20.7 %collective-permute-start.28 = (f32[1,192,512]{2,1,0:T(8,128)S(1)}, f32[1,192,512]{2,1,0:T(8,128)S(1)}, u32[]{:S(2)}, u32[]{:S(2)}) collective-permute-start(f32[1,192,512]{2,1,0:T(8,128)S(1)} %select_add_fusion), channel_id=1, source_target_pairs={{0,2},{1,3},{2,0},{3,1},{4,6},{5,7},{6,4},{7,5},{8,10},{9,11},{10,... | collective-permute-start | bytes 1179656 | tf_op jit(solution)/shard_map/ppermute | solution.py:714
  371.4 49.3 %collective-permute-start.27 = (f32[384,768]{1,0:T(8,128)}, f32[384,768]{1,0:T(8,128)}, u32[]{:S(2)}, u32[]{:S(2)}) collective-permute-start(f32[384,768]{1,0:T(8,128)} %slice.207), channel_id=1, source_target_pairs={{1,0},{2,1},{3,2},{5,4},{6,5},{7,6},{9,8},{10,9},{11,10},{13,12},{... | collective-permute-start | bytes 3538952 | tf_op jit(solution)/shard_map/ppermute | solution.py:783
  384.6 32.1 %collective-permute-start.29 = (f32[1,192,512]{2,1,0:T(8,128)}, f32[1,192,512]{2,1,0:T(8,128)}, u32[]{:S(2)}, u32[]{:S(2)}) collective-permute-start(f32[1,192,512]{2,1,0:T(8,128)} %add.201), channel_id=1, source_target_pairs={{0,1},{1,0},{2,3},{3,2},{4,5},{5,4},{6,7},{7,6},{8,9},{9,8},{10,11... | collective-permute-start | bytes 1179656 | tf_op jit(solution)/shard_map/ppermute | solution.py:714
  388.7 1.4 collective-permute-start.24
  390.9 3.8 collective-permute-start.25
  394.7 24.1 %collective-permute-start.26 = (f32[8,768]{1,0:T(8,128)S(1)}, f32[8,768]{1,0:T(8,128)S(1)}, u32[]{:S(2)}, u32[]{:S(2)}) collective-permute-start(f32[8,768]{1,0:T(8,128)S(1)} %add.198), channel_id=1, source_target_pairs={{0,16},{4,20},{8,24},{12,28},{16,0},{20,4},{24,8},{28,12},{1,17},{... | collective-permute-start | bytes 73736 | tf_op jit(solution)/shard_map/ppermute | solution.py:643
  426.1 50.8 %collective-permute-start.30 = (f32[384,768]{1,0:T(8,128)}, f32[384,768]{1,0:T(8,128)}, u32[]{:S(2)}, u32[]{:S(2)}) collective-permute-start(f32[384,768]{1,0:T(8,128)} %slice_add_fusion), channel_id=1, source_target_pairs={{1,0},{2,1},{3,2},{5,4},{6,5},{7,6},{9,8},{10,9},{11,10},{13,12},{... | collective-permute-start | bytes 3538952 | tf_op jit(solution)/shard_map/ppermute | solution.py:814
  429.4 2.3 collective-permute-start.31
  436.0 40.8 %copy-start.30 = (f32[768]{0:T(1024)S(1)}, f32[768]{0:T(1024)}, u32[]{:S(2)}) copy-start(f32[768]{0:T(1024)} %param.20) | copy-start | bytes 9220
  (33 other events, 205.9 us)
Sparse Core Ops, SparseCore 0:
  9.9 69.2 all-gather.2
  81.0 38.6 all-gather.4
  165.8 43.2 reduce-scatter.12
  212.0 43.8 reduce-scatter.14
  258.7 43.9 reduce-scatter.16
  327.4 57.0 reduce-scatter.18
  429.6 68.7 all-reduce.6

commit v4 on v3

--- a/solution.py
+++ b/solution.py
@@ -768,8 +768,7 @@
     shard_c = scatter_chips(grads_c)[0]
     line_c = line_start(shards[2])
     out_sib = swap(out_part[rows:])
-    line_c, ends_b, dk, dv = together((line_c, ends_b, dk, dv))
-    line_c = line_middle(line_c)
+    ends_b, dk, dv = together((ends_b, dk, dv))
     dkv = jnp.concatenate([dk, dv], axis=1)
 
     block_out = resid + out_part[:rows] + out_sib
@@ -778,6 +777,8 @@
 
     wq, wkv = qkv_full[:, :model], qkv_full[:, model:]
     partial = outer_cols(dkv, wkv)
+    line_c, partial = together((line_c, partial))
+    line_c = line_middle(line_c)
     own_part = partial[halo:] + outer_cols(dq, wq)
     (sent,) = together((partial,))
     back_near = sent[rows:halo] + lax.ppermute(sent[:rows], "seq", behind)
@@ -802,15 +803,18 @@
     while bit < devices:
         small = small + exchange(small, bit)
         bit *= 2
-    tall = shard_c.shape[0]
-    payload = jnp.concatenate([shard_c, small.reshape(-1, shard_c.shape[1])], axis=0)
+    shard_c, line_c, back_near, small = together((shard_c, line_c, back_near, small))
+    last = line_middle(line_start(shard_c[None]))
     ends_c = line_end(line_c)
-    payload, back_near, ends_c = together((payload, back_near, ends_c))
-    summed = lax.psum(payload, "seq")
-    grad_qkv, grad_wout = summed[:tall, :3 * model], summed[:tall, 3 * model:]
-    small = summed[tall:].reshape(-1, model)
+    last, ends_c, small, own_part = together((last, ends_c, small, own_part))
+    bit = 1
+    while bit < groups:
+        small = small + shift(small, bit)
+        bit *= 2
     gain_one, bias_one, gain_two, bias_two = small[0], small[1], small[2], small[3]
     grad_dwa = small[4, :5]
+    last = jnp.concatenate(line_end(last), axis=1)[0]
+    grad_qkv, grad_wout = last[:, :3 * model], last[:, 3 * model:]
     grad_normed_one = own_part + lax.ppermute(back_near, "seq", behind)
     grad_input = grad_resid + norm_back(grad_normed_one, gain1, xhat1, rate1)
     grad_up, grad_down = unpack_grads(

time: 516 us -> 503 us (0.975)
  local copies, waits for them, and re-layouts: 42 us -> 33 us
  starting transfers between devices: 45.3 us -> 54 us
  other arithmetic: 46.4 us -> 38.7 us
  waiting for transfers between devices: 155 us -> 148 us
    ppermute x1, waiting for transfers between devices: 39.3 us -> 16.2 us  [body(): grad_normed_one = own_part + lax.ppermute(back_near, 'seq', behind)]
    ppermute x1, waiting for transfers between devices: 0.01 us -> 18.4 us  [body(): back_near = sent[rows:halo] + lax.ppermute(sent[:rows], 'seq', behind)]
    psum x1 -> x0, waiting for transfers between devices: 18 us -> none  [body(): summed = lax.psum(payload, 'seq')]
    ppermute x9 -> x14, waiting for transfers between devices: 49.4 us -> 62.2 us  [body(): lax.ppermute(v, 'seq', [(i, i ^ bit) for i in range(groups)])]
    ppermute x9 -> x14, starting transfers between devices: 13.2 us -> 21.2 us  [body(): lax.ppermute(v, 'seq', [(i, i ^ bit) for i in range(groups)])]
  transfers between devices with their start and end apart: 39 -> 43, of which waited for: 18 -> 20; matrix products, arithmetic and copies ran while one was open for 19% -> 17% of each run, Pallas kernels for 33% -> 34%
where the time goes in v4:
time: 503 us; the launch traced here: 498 us
  Pallas kernels  188 us (37%)
  waiting for transfers between devices  148 us (29%)
  starting transfers between devices  54 us (11%)
  other arithmetic  38.7 us (8%)
  local copies, waits for them, and re-layouts  33 us (7%)
  matrix products  21.3 us (4%)
  between operations  15.3 us (3%)
    ppermute x14, waiting for transfers between devices, body(): lax.ppermute(v, 'seq', [(i, i ^ bit) for i in range(groups)])  62.2 us
    pallas_call x3, Pallas kernels, mlp(): pl.pallas_call(functools.partial(mlp_kernel, len(ups), len(so_far) // 2),...  62.1 us
    pallas_call x2, Pallas kernels, attend_back(): pl.pallas_call(attend_back_kernel, grid=(count,), in_specs=[pl.BlockSpec(...  47.2 us
    pallas_call x2, Pallas kernels, weight_call(): pl.pallas_call(kernel, grid_spec=pltpu.PrefetchScalarGridSpec(num_scalar_...  26.2 us
    pallas_call x1, Pallas kernels, attend(): pl.pallas_call(attend_kernel, grid=(pairs,), in_specs=[pl.BlockSpec((rows...  23.1 us
    pallas_call x1, Pallas kernels, project(): pl.pallas_call(qkv_kernel, grid=(3 * third,), in_specs=[whole((rows, mode...  21.7 us
    ppermute x14, starting transfers between devices, body(): lax.ppermute(v, 'seq', [(i, i ^ bit) for i in range(groups)])  21.2 us
    ppermute x1, waiting for transfers between devices, body(): back_near = sent[rows:halo] + lax.ppermute(sent[:rows], 'seq', behind)  18.4 us
  transfers between devices with their start and end apart: 43, of which 20 were waited for; matrix products, arithmetic and copies ran while one was open for 17% of the time, Pallas kernels for 34%

profile of v4, /device:TPU:0, one launch (start us, length us, event | category | flops | bytes accessed | tf_op | source)
XLA Modules:
  0.0 498.5 jit_solution(13831450268284351819)
XLA Ops:
  8.0 1.9 reshape.142
  12.8 4.6 collective-permute-start
  25.2 17.9 %collective-permute-done.near_ref = f32[384,768]{1,0:T(8,128)S(1)} collective-permute-done((f32[384,768]{1,0:T(8,128)S(1)}, f32[384,768]{1,0:T(8,128)S(1)}, u32[]{:S(2)}, u32[]{:S(2)}) %collective-permute-start) | collective-permute-done | bytes 1179680 | tf_op jit(solution)/shard_map/ppermute | solution.py:670
  43.1 4.4 collective-permute-start.1
  47.6 4.0 collective-permute-start.2
  52.3 7.4 %fusion.14 = (f32[]{:T(128)}, f32[]{:T(128)}, f32[]{:T(128)}, f32[]{:T(128)}, f32[384,768]{1,0:T(8,128)}) fusion(f32[384,768]{1,0:T(8,128)S(1)} %copy-done.10, f32[3,384,768]{2,1,0:T(8,128)} %param.18, f32[384,768]{1,0:T(8,128)} %param.17, f32[]{:T(128)} %bitcast.5, f32[]{:T(128)} %bitcast.3, f32[]{:T(128)} %bitcast.1, f32[]{:T(128)} %bitcast), kind=kLoop, calls=%fused_computation.31 | loop fusion | flops 4423676 | bytes 7077920 | tf_op jit(solution)/shard_map/reduce_sum | solution.py:686
  60.8 11.9 %collective-permute-done.2 = s32[1,384]{1,0:T(1,128)} collective-permute-done((s32[1,384]{1,0:T(1,128)S(1)}, s32[1,384]{1,0:T(1,128)}, u32[]{:S(2)}, u32[]{:S(2)}) %collective-permute-start.2) | collective-permute-done | bytes 1568 | tf_op jit(solution)/shard_map/ppermute | solution.py:671
  72.7 5.0 %collective-permute-start.3 = (s32[1,384]{1,0:T(1,128)}, s32[1,384]{1,0:T(1,128)S(1)}, u32[]{:S(2)}, u32[]{:S(2)}) collective-permute-start(s32[1,384]{1,0:T(1,128)} %collective-permute-done.2), channel_id=1, source_target_pairs={{0,1},{1,2},{2,3},{4,5},{5,6},{6,7},{8,9},{9,10},{10,11},{12,13},{... | collective-permute-start | bytes 4616 | tf_op jit(solution)/shard_map/ppermute | solution.py:673
  77.7 3.2 pad_maximum_fusion.2
  87.3 21.7 %shard_map.239 = (f32[384,768]{1,0:T(8,128)}, f32[1152,1536]{1,0:T(8,128)}, bf16[1152,768]{1,0:T(8,128)(2,1)}, bf16[1152,768]{1,0:T(8,128)(2,1)}) custom-call(f32[384,768]{1,0:T(8,128)} %copy-done.5, f32[384,768]{1,0:T(8,128)} %copy-done.3, f32[384,768]{1,0:T(8,128)} %own_ref.1, f32[1,768]{1,0:T(1,128)} %broadcast_in_dim.50.gain_ref, ...), custom_call_target="tpu_custom_call" | custom-call | flops 22000001024 | bytes 1048576 | tf_op jit(solution)/shard_map/pallas_call | solution.py:144
  110.5 23.1 %shard_map.240.att_ref = f32[384,768]{1,0:T(8,128)} custom-call(f32[384,768]{1,0:T(8,128)} %get-tuple-element.114.q_ref, f32[1152,1536]{1,0:T(8,128)} %get-tuple-element.115.k_ref.v_ref, f32[1152,1536]{1,0:T(8,128)} %get-tuple-element.115.k_ref.v_ref, s32[384,128]{1,0:T(8,128)} %broadcast_in_dim.52.segq_ref, s32[8,1152]{1,0:T(8,128)} %broadcast_in_dim.54.segk_ref), custom_call_target="tpu_custom_call" | custom-call | flops 26400000000 | bytes 1048576 | tf_op jit(solution)/shard_map/pallas_call | solution.py:236
  133.6 3.7 convolution_add_fusion.resid_ref
  139.4 4.2 collective-permute-done.12.refs_7_
  143.6 2.0 collective-permute-done.9.refs_3_
  146.6 19.9 %shard_map.241 = (f32[768,768]{1,0:T(8,128)}, f32[768,768]{1,0:T(8,128)}, f32[4,1,384,512]{3,2,1,0:T(8,128)}) custom-call(s32[1]{0:T(128)} %bitcast.13.chip_ref, f32[384,768]{1,0:T(8,128)} %copy-done.13, f32[384,768]{1,0:T(8,128)} %copy-done.40, f32[384,768]{1,0:T(8,128)} %cot_ref.7, f32[384,768]{1,0:T(8,128)} %collective-permute-done.5.cot_other_ref, ...), custom_call_target="tpu_custom_call" | custom-call | flops 19800000512 | bytes 1048576 | tf_op jit(solution)/shard_map/pallas_call | solution.py:457
  166.6 21.0 %shard_map.242 = (f32[768,768]{1,0:T(8,128)}, f32[768,768]{1,0:T(8,128)}, f32[4,1,384,512]{3,2,1,0:T(8,128)}) custom-call(s32[1]{0:T(128)} %bitcast.13.chip_ref, f32[384,768]{1,0:T(8,128)} %copy-done.13, f32[384,768]{1,0:T(8,128)} %copy-done.40, f32[384,768]{1,0:T(8,128)} %cot_ref.7, f32[384,768]{1,0:T(8,128)} %collective-permute-done.5.cot_other_ref, ...), custom_call_target="tpu_custom_call" | custom-call | flops 19800000512 | bytes 1048576 | tf_op jit(solution)/shard_map/pallas_call | solution.py:457
  187.9 21.1 %shard_map.243 = (f32[768,768]{1,0:T(8,128)}, f32[768,768]{1,0:T(8,128)}, f32[4,1,384,512]{3,2,1,0:T(8,128)}) custom-call(s32[1]{0:T(128)} %bitcast.13.chip_ref, f32[384,768]{1,0:T(8,128)} %copy-done.13, f32[384,768]{1,0:T(8,128)} %copy-done.40, f32[384,768]{1,0:T(8,128)} %cot_ref.7, f32[384,768]{1,0:T(8,128)} %collective-permute-done.5.cot_other_ref, ...), custom_call_target="tpu_custom_call" | custom-call | flops 19800000512 | bytes 1048576 | tf_op jit(solution)/shard_map/pallas_call | solution.py:457
  210.7 2.5 collective-permute-done.13.given_ref
  213.3 1.6 slice_select_fusion.7
  214.9 1.6 collective-permute-start.14
  216.5 7.7 %shard_map.244 = (f32[384,768]{1,0:T(8,128)}, f32[384,768]{1,0:T(8,128)}, f32[8,768]{1,0:T(8,128)}) custom-call(f32[768,768]{1,0:T(8,128)} %get-tuple-element.96.part_ref, f32[384,768]{1,0:T(8,128)} %copy-done.41, f32[384,768]{1,0:T(8,128)} %copy-done.13, f32[384,768]{1,0:T(8,128)} %cot_ref.7, f32[1,768]{1,0:T(1,128)} %broadcast_in_dim.55.gain_ref, ...), custom_call_target="tpu_custom_call" | custom-call | flops 6600000000 | bytes 1048576 | tf_op jit(solution)/shard_map/pallas_call | solution.py:505
  224.3 1.8 collective-permute-done.14
  227.9 2.6 collective-permute-start.15
  230.5 23.5 %shard_map.245 = (f32[384,768]{1,0:T(8,128)}, f32[1152,768]{1,0:T(8,128)}, f32[1152,768]{1,0:T(8,128)}) custom-call(f32[384,768]{1,0:T(8,128)} %get-tuple-element.114.q_ref, f32[1152,1536]{1,0:T(8,128)} %get-tuple-element.115.k_ref.v_ref, f32[1152,1536]{1,0:T(8,128)} %get-tuple-element.115.k_ref.v_ref, f32[384,768]{1,0:T(8,128)} %get-tuple-element.116.g_ref, ...), custom_call_target="tpu_custom_call" | custom-call | flops 23100000256 | bytes 1048576 | tf_op jit(solution)/shard_map/pallas_call | solution.py:328
  254.1 2.7 reduce-scatter.15.cloned.1.call-done
  260.0 23.7 %shard_map.246 = (f32[384,768]{1,0:T(8,128)}, f32[1152,768]{1,0:T(8,128)}, f32[1152,768]{1,0:T(8,128)}) custom-call(f32[384,768]{1,0:T(8,128)} %get-tuple-element.114.q_ref, f32[1152,1536]{1,0:T(8,128)} %get-tuple-element.115.k_ref.v_ref, f32[1152,1536]{1,0:T(8,128)} %get-tuple-element.115.k_ref.v_ref, ...), custom_call_target="tpu_custom_call", output_to_operand_aliasing={{0}: (8, {}), {1}: (9, {}), {2}: (10, {})} | custom-call | flops 23100000256 | bytes 1048576 | tf_op jit(solution)/shard_map/pallas_call | solution.py:328
  284.8 2.4 collective-permute-start.19
  287.2 12.6 %shard_map.247 = f32[2,4,96,1536]{3,2,1,0:T(8,128)} custom-call(s32[1]{0:T(128)} %bitcast.12.core_ref, bf16[1152,768]{1,0:T(8,128)(2,1)} %get-tuple-element.89.hi_ref, bf16[1152,768]{1,0:T(8,128)(2,1)} %get-tuple-element.90.lo_ref, f32[384,768]{1,0:T(8,128)} %get-tuple-element.127.dq_ref, f32[1152,768]{1,0:T(8,128)} %get-tuple-element.140.dk_ref), custom_call_target="tpu_custom_call" | custom-call | flops 9900000256 | bytes 1048576 | tf_op jit(solution)/shard_map/pallas_call | solution.py:584
  299.8 3.2 slice_bitcast_fusion.2
  305.2 13.6 %shard_map.248 = f32[2,4,96,1536]{3,2,1,0:T(8,128)} custom-call(s32[1]{0:T(128)} %bitcast.12.core_ref, bf16[1152,768]{1,0:T(8,128)(2,1)} %get-tuple-element.89.hi_ref, bf16[1152,768]{1,0:T(8,128)(2,1)} %get-tuple-element.90.lo_ref, f32[1152,768]{1,0:T(8,128)} %get-tuple-element.141.dv_ref, f32[384,768]{1,0:T(8,128)} %shard_map.240.att_ref, ...), custom_call_target="tpu_custom_call" | custom-call | flops 9900000256 | bytes 1048576 | tf_op jit(solution)/shard_map/pallas_call | solution.py:584
  318.8 1.8 slice_bitcast_fusion
  321.2 4.1 collective-permute-done.20
  325.6 2.5 pad_maximum_fusion
  334.0 9.9 %collective-permute-done.23 = f32[1,192,512]{2,1,0:T(8,128)S(1)} collective-permute-done((f32[1,192,512]{2,1,0:T(8,128)}, f32[1,192,512]{2,1,0:T(8,128)S(1)}, u32[]{:S(2)}, u32[]{:S(2)}) %collective-permute-start.23) | collective-permute-done | bytes 393248 | tf_op jit(solution)/shard_map/ppermute | solution.py:714
  345.5 12.8 %fusion = f32[1152,768]{1,0:T(8,128)S(1)} fusion(f32[1152,768]{1,0:T(8,128)} %get-tuple-element.141.dv_ref, f32[1152,768]{1,0:T(8,128)} %get-tuple-element.140.dk_ref, f32[768,2304]{1,0:T(8,128)} %all-gather.3.cloned.1.call-done.w_ref), kind=kOutput, calls=%fused_computation | convolution fusion | flops 8155496448 | bytes 15335424 | tf_op jit(solution)/shard_map/dot_general | solution.py:608
  359.6 3.2 collective-permute-start.24
  363.9 1.8 collective-permute-start.25
  365.7 4.8 slice_reduce_fusion
  370.6 2.6 multiply_reduce_fusion.1
  376.7 2.9 collective-permute-done.27
  383.9 18.4 %collective-permute-done.25 = f32[384,768]{1,0:T(8,128)} collective-permute-done((f32[384,768]{1,0:T(8,128)}, f32[384,768]{1,0:T(8,128)}, u32[]{:S(2)}, u32[]{:S(2)}) %collective-permute-start.25) | collective-permute-done | bytes 1179680 | tf_op jit(solution)/shard_map/ppermute | solution.py:784
  402.3 1.8 slice_add_fusion
  405.5 4.7 collective-permute-start.29
  411.8 12.6 %collective-permute-done.29 = f32[1,48,3072]{2,1,0:T(8,128)S(1)} collective-permute-done((f32[1,48,3072]{2,1,0:T(8,128)S(1)}, f32[1,48,3072]{2,1,0:T(8,128)S(1)}, u32[]{:S(2)}, u32[]{:S(2)}) %collective-permute-start.29) | collective-permute-done | bytes 589856 | tf_op jit(solution)/shard_map/ppermute | solution.py:714
  425.8 7.1 %collective-permute-done.31 = f32[1,192,512]{2,1,0:T(8,128)S(1)} collective-permute-done((f32[1,192,512]{2,1,0:T(8,128)S(1)}, f32[1,192,512]{2,1,0:T(8,128)S(1)}, u32[]{:S(2)}, u32[]{:S(2)}) %collective-permute-start.31) | collective-permute-done | bytes 393248 | tf_op jit(solution)/shard_map/ppermute | solution.py:714
  433.0 20.6 %collective-permute-done.30 = f32[1,48,3072]{2,1,0:T(8,128)S(1)} collective-permute-done((f32[1,48,3072]{2,1,0:T(8,128)S(1)}, f32[1,48,3072]{2,1,0:T(8,128)S(1)}, u32[]{:S(2)}, u32[]{:S(2)}) %collective-permute-start.30) | collective-permute-done | bytes 589856 | tf_op jit(solution)/shard_map/ppermute | solution.py:714
  453.7 16.2 %collective-permute-done.32 = f32[384,768]{1,0:T(8,128)S(1)} collective-permute-done((f32[384,768]{1,0:T(8,128)S(1)}, f32[384,768]{1,0:T(8,128)S(1)}, u32[]{:S(2)}, u32[]{:S(2)}) %collective-permute-start.32) | collective-permute-done | bytes 1179680 | tf_op jit(solution)/shard_map/ppermute | solution.py:818
  476.6 8.4 %collective-permute-done.34 = f32[8,768]{1,0:T(8,128)S(1)} collective-permute-done((f32[8,768]{1,0:T(8,128)S(1)}, f32[8,768]{1,0:T(8,128)S(1)}, u32[]{:S(2)}, u32[]{:S(2)}) %collective-permute-start.34) | collective-permute-done | bytes 24608 | tf_op jit(solution)/shard_map/ppermute | solution.py:714
  (246 shorter events, 70.4 us)
Async XLA Ops:
  7.2 79.7 %all-gather.3.cloned.1.call-start = ((), (), s32[]{:S(2)}) async-start(), calls=%async_computation.4 | async-start | bytes 7962624 | tf_op jit(solution)/shard_map/all_gather | solution.py:646
  7.9 125.7 %all-gather.5.cloned.1.call-start = ((), (), s32[]{:S(2)}) async-start(), calls=%async_computation.5 | async-start | bytes 2654208 | tf_op jit(solution)/shard_map/all_gather | solution.py:646
  12.3 8.9 %collective-permute-start.6 = (f32[96,1536]{1,0:T(8,128)}, f32[96,1536]{1,0:T(8,128)}, u32[]{:S(2)}, u32[]{:S(2)}) collective-permute-start(f32[96,1536]{1,0:T(8,128)} %select_n.149), channel_id=1, source_target_pairs={{0,4},{4,0},{8,12},{12,8},{16,20},{20,16},{24,28},{28,24},{1,5},{5... | collective-permute-start | bytes 1769480 | tf_op jit(solution)/shard_map/ppermute | solution.py:643
  12.8 30.4 %collective-permute-start = (f32[384,768]{1,0:T(8,128)S(1)}, f32[384,768]{1,0:T(8,128)S(1)}, u32[]{:S(2)}, u32[]{:S(2)}) collective-permute-start(f32[384,768]{1,0:T(8,128)S(1)} %copy-done), channel_id=1, source_target_pairs={{0,1},{1,2},{2,3},{4,5},{5,6},{6,7},{8,9},{9,10},{10,11},{12,13},{... | collective-permute-start | bytes 3538952 | tf_op jit(solution)/shard_map/ppermute | solution.py:670
  17.4 66.9 %collective-permute-start.10 = (f32[384,768]{1,0:T(8,128)}, f32[384,768]{1,0:T(8,128)}, u32[]{:S(2)}, u32[]{:S(2)}) collective-permute-start(f32[384,768]{1,0:T(8,128)} %refs_4_.5), channel_id=1, source_target_pairs={{0,8},{4,12},{8,0},{12,4},{16,24},{20,28},{24,16},{28,20},{1,9},{5... | collective-permute-start | bytes 3538952 | tf_op jit(solution)/shard_map/ppermute | solution.py:643
  22.5 29.1 %copy-start.10 = (f32[384,768]{1,0:T(8,128)S(1)}, f32[384,768]{1,0:T(8,128)}, u32[]{:S(2)}) copy-start(f32[384,768]{1,0:T(8,128)} %cot_ref.7) | copy-start | bytes 3538948
  22.5 29.1 %copy-start.34 = (f32[5]{0:T(128)S(1)}, f32[5]{0:T(128)}, u32[]{:S(2)}) copy-start(f32[5]{0:T(128)} %param.19) | copy-start | bytes 64
  23.7 62.1 %collective-permute-start.8 = (f32[192,1536]{1,0:T(8,128)}, f32[192,1536]{1,0:T(8,128)}, u32[]{:S(2)}, u32[]{:S(2)}) collective-permute-start(f32[192,1536]{1,0:T(8,128)} %pad_maximum_fusion.1.refs_0_), channel_id=1, source_target_pairs={{0,16},{4,20},{8,24},{12,28},{16,0},{20,4},{24,8},{28,12},{1,17},{... | collective-permute-start | bytes 3538952 | tf_op jit(solution)/shard_map/ppermute | solution.py:643
  43.1 43.2 %collective-permute-start.1 = (f32[384,768]{1,0:T(8,128)S(1)}, f32[384,768]{1,0:T(8,128)S(1)}, u32[]{:S(2)}, u32[]{:S(2)}) collective-permute-start(f32[384,768]{1,0:T(8,128)S(1)} %collective-permute-done.near_ref), channel_id=1, source_target_pairs={{0,1},{1,2},{2,3},{4,5},{5,6},{6,7},{8,9},{9,10},{10,11},{12,13},{... | collective-permute-start | bytes 3538952 | tf_op jit(solution)/shard_map/ppermute | solution.py:672
  47.6 25.1 %collective-permute-start.2 = (s32[1,384]{1,0:T(1,128)S(1)}, s32[1,384]{1,0:T(1,128)}, u32[]{:S(2)}, u32[]{:S(2)}) collective-permute-start(s32[1,384]{1,0:T(1,128)S(1)} %get-tuple-element.199), channel_id=1, source_target_pairs={{0,1},{1,2},{2,3},{4,5},{5,6},{6,7},{8,9},{9,10},{10,11},{12,13},{... | collective-permute-start | bytes 4616 | tf_op jit(solution)/shard_map/ppermute | solution.py:671
  51.6 85.7 %collective-permute-start.5 = (f32[384,768]{1,0:T(8,128)S(1)}, f32[384,768]{1,0:T(8,128)}, u32[]{:S(2)}, u32[]{:S(2)}) collective-permute-start(f32[384,768]{1,0:T(8,128)S(1)} %copy-done.10), channel_id=1, source_target_pairs={{0,4},{4,0},{8,12},{12,8},{16,20},{20,16},{24,28},{28,24},{1,5},{5... | collective-permute-start | bytes 3538952 | tf_op jit(solution)/shard_map/ppermute | solution.py:643
  51.6 161.7 %reduce-scatter.13.cloned.1.call-start = ((), (), s32[]{:S(2)}) async-start(), calls=%async_computation.6 | async-start | bytes 3932160
  72.7 9.4 %collective-permute-start.3 = (s32[1,384]{1,0:T(1,128)}, s32[1,384]{1,0:T(1,128)S(1)}, u32[]{:S(2)}, u32[]{:S(2)}) collective-permute-start(s32[1,384]{1,0:T(1,128)} %collective-permute-done.2), channel_id=1, source_target_pairs={{0,1},{1,2},{2,3},{4,5},{5,6},{6,7},{8,9},{9,10},{10,11},{12,13},{... | collective-permute-start | bytes 4616 | tf_op jit(solution)/shard_map/ppermute | solution.py:673
  82.1 57.3 %collective-permute-start.11 = (f32[384,768]{1,0:T(8,128)}, f32[384,768]{1,0:T(8,128)}, u32[]{:S(2)}, u32[]{:S(2)}) collective-permute-start(f32[384,768]{1,0:T(8,128)} %refs_4_.5), channel_id=1, source_target_pairs={{0,16},{4,20},{8,24},{12,28},{16,0},{20,4},{24,8},{28,12},{1,17},{... | collective-permute-start | bytes 3538952 | tf_op jit(solution)/shard_map/ppermute | solution.py:643
  84.2 55.1 %collective-permute-start.7 = (f32[192,1536]{1,0:T(8,128)}, f32[192,1536]{1,0:T(8,128)}, u32[]{:S(2)}, u32[]{:S(2)}) collective-permute-start(f32[192,1536]{1,0:T(8,128)} %pad_maximum_fusion.1.refs_0_), channel_id=1, source_target_pairs={{0,8},{4,12},{8,0},{12,4},{16,24},{20,28},{24,16},{28,20},{1,9},{5... | collective-permute-start | bytes 3538952 | tf_op jit(solution)/shard_map/ppermute | solution.py:643
  85.8 57.8 %collective-permute-start.12 = (f32[384,768]{1,0:T(8,128)}, f32[384,768]{1,0:T(8,128)}, u32[]{:S(2)}, u32[]{:S(2)}) collective-permute-start(f32[384,768]{1,0:T(8,128)} %collective-permute-done.10.refs_5_), channel_id=1, source_target_pairs={{0,16},{4,20},{8,24},{12,28},{16,0},{20,4},{24,8},{28,12},{1,17},{... | collective-permute-start | bytes 3538952 | tf_op jit(solution)/shard_map/ppermute | solution.py:643
  86.3 59.3 %collective-permute-start.9 = (f32[192,1536]{1,0:T(8,128)}, f32[192,1536]{1,0:T(8,128)}, u32[]{:S(2)}, u32[]{:S(2)}) collective-permute-start(f32[192,1536]{1,0:T(8,128)} %collective-permute-done.8.refs_2_), channel_id=1, source_target_pairs={{0,8},{4,12},{8,0},{12,4},{16,24},{20,28},{24,16},{28,20},{1,9},{5... | collective-permute-start | bytes 3538952 | tf_op jit(solution)/shard_map/ppermute | solution.py:643
  137.3 8.3 %collective-permute-start.4 = (f32[384,768]{1,0:T(8,128)S(1)}, f32[384,768]{1,0:T(8,128)S(1)}, u32[]{:S(2)}, u32[]{:S(2)}) collective-permute-start(f32[384,768]{1,0:T(8,128)S(1)} %convolution_add_fusion.resid_ref), channel_id=1, source_target_pairs={{0,4},{4,0},{8,12},{12,8},{16,20},{20,16},{24,28},{28,24},{1,5},{5... | collective-permute-start | bytes 3538952 | tf_op jit(solution)/shard_map/ppermute | solution.py:643
  166.5 90.2 %reduce-scatter.15.cloned.1.call-start = ((), (), s32[]{:S(2)}) async-start(), calls=%async_computation.7 | async-start | bytes 3932160
  187.6 140.5 %reduce-scatter.17.cloned.1.call-start = ((), (), s32[]{:S(2)}) async-start(), calls=%async_computation.8 | async-start | bytes 3932160
  210.4 2.9 collective-permute-start.13
  210.5 193.6 %reduce-scatter.19.cloned.1.call-start = ((), (), s32[]{:S(2)}) async-start(), calls=%async_computation.9 | async-start | bytes 5898240
  214.9 11.2 %collective-permute-start.14 = (f32[1,192,512]{2,1,0:T(8,128)S(1)}, f32[1,192,512]{2,1,0:T(8,128)S(1)}, u32[]{:S(2)}, u32[]{:S(2)}) collective-permute-start(f32[1,192,512]{2,1,0:T(8,128)S(1)} %slice_select_fusion.7), channel_id=1, source_target_pairs={{0,1},{1,0},{2,3},{3,2},{4,5},{5,4},{6,7},{7,6},{8,9},{9,8},{10,11... | collective-permute-start | bytes 1179656 | tf_op jit(solution)/shard_map/ppermute | solution.py:714
  227.9 26.1 %collective-permute-start.15 = (f32[1,192,512]{2,1,0:T(8,128)S(1)}, f32[1,192,512]{2,1,0:T(8,128)S(1)}, u32[]{:S(2)}, u32[]{:S(2)}) collective-permute-start(f32[1,192,512]{2,1,0:T(8,128)S(1)} %select_add_fusion.3), channel_id=1, source_target_pairs={{0,2},{1,3},{2,0},{3,1},{4,6},{5,7},{6,4},{7,5},{8,10},{9,11},{10,... | collective-permute-start | bytes 1179656 | tf_op jit(solution)/shard_map/ppermute | solution.py:714
  257.9 25.8 %copy-start.17 = (f32[1,1,384,512]{3,2,1,0:T(8,128)S(1)}, f32[1,1,384,512]{3,2,1,0:T(8,128)}, u32[]{:S(2)}) copy-start(f32[1,1,384,512]{3,2,1,0:T(8,128)} %reduce-scatter.15.cloned.1.call-done) | copy-start | bytes 2359300
  257.9 25.8 %collective-permute-start.16 = (f32[1,192,512]{2,1,0:T(8,128)S(1)}, f32[1,192,512]{2,1,0:T(8,128)S(1)}, u32[]{:S(2)}, u32[]{:S(2)}) collective-permute-start(f32[1,192,512]{2,1,0:T(8,128)S(1)} %slice_select_fusion.6), channel_id=1, source_target_pairs={{0,1},{1,0},{2,3},{3,2},{4,5},{5,4},{6,7},{7,6},{8,9},{9,8},{10,11... | collective-permute-start | bytes 1179656 | tf_op jit(solution)/shard_map/ppermute | solution.py:714
  259.5 24.3 %collective-permute-start.17 = (f32[1,192,512]{2,1,0:T(8,128)S(1)}, f32[1,192,512]{2,1,0:T(8,128)S(1)}, u32[]{:S(2)}, u32[]{:S(2)}) collective-permute-start(f32[1,192,512]{2,1,0:T(8,128)S(1)} %add.188), channel_id=1, source_target_pairs={{0,1},{1,0},{2,3},{3,2},{4,5},{5,4},{6,7},{7,6},{8,9},{9,8},{10,11... | collective-permute-start | bytes 1179656 | tf_op jit(solution)/shard_map/ppermute | solution.py:714
  284.8 19.6 %collective-permute-start.19 = (f32[1,192,512]{2,1,0:T(8,128)S(1)}, f32[1,192,512]{2,1,0:T(8,128)S(1)}, u32[]{:S(2)}, u32[]{:S(2)}) collective-permute-start(f32[1,192,512]{2,1,0:T(8,128)S(1)} %select_add_fusion.2), channel_id=1, source_target_pairs={{0,2},{1,3},{2,0},{3,1},{4,6},{5,7},{6,4},{7,5},{8,10},{9,11},{10,... | collective-permute-start | bytes 1179656 | tf_op jit(solution)/shard_map/ppermute | solution.py:714
  303.0 17.7 %collective-permute-start.18 = (f32[4,96,1536]{2,1,0:T(8,128)}, f32[4,96,1536]{2,1,0:T(8,128)S(1)}, u32[]{:S(2)}, u32[]{:S(2)}) collective-permute-start(f32[4,96,1536]{2,1,0:T(8,128)} %slice_bitcast_fusion.2), channel_id=1, source_target_pairs={{0,4},{4,0},{8,12},{12,8},{16,20},{20,16},{24,28},{28,24},{1,5},{5... | collective-permute-start | bytes 7077896 | tf_op jit(solution)/shard_map/ppermute | solution.py:643
  320.6 4.6 collective-permute-start.20
  332.4 11.4 %collective-permute-start.23 = (f32[1,192,512]{2,1,0:T(8,128)}, f32[1,192,512]{2,1,0:T(8,128)S(1)}, u32[]{:S(2)}, u32[]{:S(2)}) collective-permute-start(f32[1,192,512]{2,1,0:T(8,128)} %add.191), channel_id=1, source_target_pairs={{0,1},{1,0},{2,3},{3,2},{4,5},{5,4},{6,7},{7,6},{8,9},{9,8},{10,11... | collective-permute-start | bytes 1179656 | tf_op jit(solution)/shard_map/ppermute | solution.py:714
  344.9 13.6 %collective-permute-start.22 = (f32[1,192,512]{2,1,0:T(8,128)S(1)}, f32[1,192,512]{2,1,0:T(8,128)S(1)}, u32[]{:S(2)}, u32[]{:S(2)}) collective-permute-start(f32[1,192,512]{2,1,0:T(8,128)S(1)} %slice_select_fusion.5), channel_id=1, source_target_pairs={{0,1},{1,0},{2,3},{3,2},{4,5},{5,4},{6,7},{7,6},{8,9},{9,8},{10,11... | collective-permute-start | bytes 1179656 | tf_op jit(solution)/shard_map/ppermute | solution.py:714
  358.4 12.2 %collective-permute-start.21 = (f32[384,768]{1,0:T(8,128)S(1)}, f32[384,768]{1,0:T(8,128)S(1)}, u32[]{:S(2)}, u32[]{:S(2)}) collective-permute-start(f32[384,768]{1,0:T(8,128)S(1)} %slice.174), channel_id=1, source_target_pairs={{0,4},{4,0},{8,12},{12,8},{16,20},{20,16},{24,28},{28,24},{1,5},{5... | collective-permute-start | bytes 3538952 | tf_op jit(solution)/shard_map/ppermute | solution.py:643
  359.6 21.9 %collective-permute-start.24 = (f32[1,192,512]{2,1,0:T(8,128)}, f32[1,192,512]{2,1,0:T(8,128)}, u32[]{:S(2)}, u32[]{:S(2)}) collective-permute-start(f32[1,192,512]{2,1,0:T(8,128)} %select_add_fusion.1), channel_id=1, source_target_pairs={{0,2},{1,3},{2,0},{3,1},{4,6},{5,7},{6,4},{7,5},{8,10},{9,11},{10,... | collective-permute-start | bytes 1179656 | tf_op jit(solution)/shard_map/ppermute | solution.py:714
  363.9 38.4 %collective-permute-start.25 = (f32[384,768]{1,0:T(8,128)}, f32[384,768]{1,0:T(8,128)}, u32[]{:S(2)}, u32[]{:S(2)}) collective-permute-start(f32[384,768]{1,0:T(8,128)} %slice.207), channel_id=1, source_target_pairs={{1,0},{2,1},{3,2},{5,4},{6,5},{7,6},{9,8},{10,9},{11,10},{13,12},{... | collective-permute-start | bytes 3538952 | tf_op jit(solution)/shard_map/ppermute | solution.py:784
  374.0 1.3 collective-permute-start.26
  375.3 4.3 collective-permute-start.27
  379.6 4.3 collective-permute-start.28
  405.5 18.9 %collective-permute-start.29 = (f32[1,48,3072]{2,1,0:T(8,128)S(1)}, f32[1,48,3072]{2,1,0:T(8,128)S(1)}, u32[]{:S(2)}, u32[]{:S(2)}) collective-permute-start(f32[1,48,3072]{2,1,0:T(8,128)S(1)} %slice_select_fusion.4), channel_id=1, source_target_pairs={{0,1},{1,0},{2,3},{3,2},{4,5},{5,4},{6,7},{7,6},{8,9},{9,8},{10,11... | collective-permute-start | bytes 1769480 | tf_op jit(solution)/shard_map/ppermute | solution.py:714
  410.3 22.5 %collective-permute-start.31 = (f32[1,192,512]{2,1,0:T(8,128)S(1)}, f32[1,192,512]{2,1,0:T(8,128)S(1)}, u32[]{:S(2)}, u32[]{:S(2)}) collective-permute-start(f32[1,192,512]{2,1,0:T(8,128)S(1)} %add.198), channel_id=1, source_target_pairs={{0,1},{1,0},{2,3},{3,2},{4,5},{5,4},{6,7},{7,6},{8,9},{9,8},{10,11... | collective-permute-start | bytes 1179656 | tf_op jit(solution)/shard_map/ppermute | solution.py:714
  410.4 59.5 %collective-permute-start.32 = (f32[384,768]{1,0:T(8,128)S(1)}, f32[384,768]{1,0:T(8,128)S(1)}, u32[]{:S(2)}, u32[]{:S(2)}) collective-permute-start(f32[384,768]{1,0:T(8,128)S(1)} %slice_add_fusion), channel_id=1, source_target_pairs={{1,0},{2,1},{3,2},{5,4},{6,5},{7,6},{9,8},{10,9},{11,10},{13,12},{... | collective-permute-start | bytes 3538952 | tf_op jit(solution)/shard_map/ppermute | solution.py:818
  424.6 29.0 %collective-permute-start.30 = (f32[1,48,3072]{2,1,0:T(8,128)S(1)}, f32[1,48,3072]{2,1,0:T(8,128)S(1)}, u32[]{:S(2)}, u32[]{:S(2)}) collective-permute-start(f32[1,48,3072]{2,1,0:T(8,128)S(1)} %select_add_fusion), channel_id=1, source_target_pairs={{0,2},{1,3},{2,0},{3,1},{4,6},{5,7},{6,4},{7,5},{8,10},{9,11},{10,... | collective-permute-start | bytes 1769480 | tf_op jit(solution)/shard_map/ppermute | solution.py:714
  432.9 37.0 %copy-start.9 = (f32[384,768]{1,0:T(8,128)S(1)}, f32[384,768]{1,0:T(8,128)}, u32[]{:S(2)}) copy-start(f32[384,768]{1,0:T(8,128)} %get-tuple-element.149) | copy-start | bytes 3538948
  433.0 37.0 %copy-start.33 = (f32[768]{0:T(1024)S(1)}, f32[768]{0:T(1024)}, u32[]{:S(2)}) copy-start(f32[768]{0:T(1024)} %param.20) | copy-start | bytes 9220
  470.4 5.0 collective-permute-start.33
  471.3 14.8 %collective-permute-start.35 = (f32[1,48,3072]{2,1,0:T(8,128)S(1)}, f32[1,48,3072]{2,1,0:T(8,128)S(1)}, u32[]{:S(2)}, u32[]{:S(2)}) collective-permute-start(f32[1,48,3072]{2,1,0:T(8,128)S(1)} %add.213), channel_id=1, source_target_pairs={{0,1},{1,0},{2,3},{3,2},{4,5},{5,4},{6,7},{7,6},{8,9},{9,8},{10,11... | collective-permute-start | bytes 1769480 | tf_op jit(solution)/shard_map/ppermute | solution.py:714
  475.3 12.7 %collective-permute-start.36 = (f32[3,96,512]{2,1,0:T(8,128)S(1)}, f32[3,96,512]{2,1,0:T(8,128)S(1)}, u32[]{:S(2)}, u32[]{:S(2)}) collective-permute-start(f32[3,96,512]{2,1,0:T(8,128)S(1)} %slice_select_fusion.2), channel_id=1, source_target_pairs={{0,4},{4,0},{8,12},{12,8},{16,20},{20,16},{24,28},{28,24},{1,5},{5... | collective-permute-start | bytes 1769480 | tf_op jit(solution)/shard_map/ppermute | solution.py:643
  475.4 9.6 %collective-permute-start.34 = (f32[8,768]{1,0:T(8,128)S(1)}, f32[8,768]{1,0:T(8,128)S(1)}, u32[]{:S(2)}, u32[]{:S(2)}) collective-permute-start(f32[8,768]{1,0:T(8,128)S(1)} %add.216), channel_id=1, source_target_pairs={{0,2},{1,3},{2,0},{3,1},{4,6},{5,7},{6,4},{7,5},{8,10},{9,11},{10,... | collective-permute-start | bytes 73736 | tf_op jit(solution)/shard_map/ppermute | solution.py:714
  (39 other events, 345.8 us)
Sparse Core Ops, SparseCore 0:
  9.9 69.1 all-gather.2
  81.0 38.7 all-gather.4
  166.6 43.2 reduce-scatter.12
  212.8 43.9 reduce-scatter.14
  259.6 43.9 reduce-scatter.16
  328.2 57.5 reduce-scatter.18

commit v5 on v4

--- a/solution.py
+++ b/solution.py
@@ -757,16 +757,18 @@
         weights_qk_kernel, 9, core_at, chips, normed_parts, [(dq, 0), (dk, 1)], [halo + rows] * 2
     )
     given_qk = swap(grads_qk[1])
-    line_b, dv, grad_resid = together((line_b, dv, grad_resid))
+    line_b, shards[2], dv, grad_resid = together((line_b, shards[2], dv, grad_resid))
     ends_b = line_end(line_b)
+    line_c = line_start(shards[2])
     grads_vo = weight_call(
         weights_vo_kernel, 9, core_at, chips, normed_parts,
         [(dv, 0), (attended, None), (grad_resid, 1)], [halo + rows] * 2 + [rows] * 2,
     )
+    line_c, grads_vo = together((line_c, grads_vo))
+    line_c = line_middle(line_c)
     grads_c = jnp.concatenate([grads_qk[0] + given_qk, grads_vo[0] + swap(grads_vo[1])], axis=2)
-    grads_c, shards[2], out_part = together((grads_c, shards[2], out_part))
+    grads_c, out_part = together((grads_c, out_part))
     shard_c = scatter_chips(grads_c)[0]
-    line_c = line_start(shards[2])
     out_sib = swap(out_part[rows:])
     ends_b, dk, dv = together((ends_b, dk, dv))
     dkv = jnp.concatenate([dk, dv], axis=1)
@@ -778,7 +780,7 @@
     wq, wkv = qkv_full[:, :model], qkv_full[:, model:]
     partial = outer_cols(dkv, wkv)
     line_c, partial = together((line_c, partial))
-    line_c = line_middle(line_c)
+    ends_c = line_end(line_c)
     own_part = partial[halo:] + outer_cols(dq, wq)
     (sent,) = together((partial,))
     back_near = sent[rows:halo] + lax.ppermute(sent[:rows], "seq", behind)
@@ -803,10 +805,19 @@
     while bit < devices:
         small = small + exchange(small, bit)
         bit *= 2
-    shard_c, line_c, back_near, small = together((shard_c, line_c, back_near, small))
+    shard_c, ends_c, back_near, small = together((shard_c, ends_c, back_near, small))
     last = line_middle(line_start(shard_c[None]))
-    ends_c = line_end(line_c)
-    last, ends_c, small, own_part = together((last, ends_c, small, own_part))
+    given_back = lax.ppermute(back_near, "seq", behind)
+    grad_up, grad_down = unpack_grads(
+        *(
+            jnp.concatenate(parts, axis=0)
+            for parts in zip(ends_a, ends_b, ends_c)
+        ),
+        swap, core, chips,
+    )
+    last, grad_up, grad_down, small, given_back = together(
+        (last, grad_up, grad_down, small, given_back)
+    )
     bit = 1
     while bit < groups:
         small = small + shift(small, bit)
@@ -815,15 +826,8 @@
     grad_dwa = small[4, :5]
     last = jnp.concatenate(line_end(last), axis=1)[0]
     grad_qkv, grad_wout = last[:, :3 * model], last[:, 3 * model:]
-    grad_normed_one = own_part + lax.ppermute(back_near, "seq", behind)
+    grad_normed_one = own_part + given_back
     grad_input = grad_resid + norm_back(grad_normed_one, gain1, xhat1, rate1)
-    grad_up, grad_down = unpack_grads(
-        *(
-            jnp.concatenate(parts, axis=0)
-            for parts in zip(ends_a, ends_b, ends_c)
-        ),
-        swap, core, chips,
-    )
     return (
         output,
         grad_input,

time: 503 us -> 501 us (level)
  other arithmetic: 38.7 us -> 47.5 us
  waiting for transfers between devices: 148 us -> 140 us
  starting transfers between devices: 54 us -> 48.6 us
    ppermute x1, waiting for transfers between devices: 16.2 us -> 0.01 us  [body(): given_back = lax.ppermute(back_near, 'seq', behind)]
    ppermute x14, waiting for transfers between devices: 62.2 us -> 74.3 us  [body(): lax.ppermute(v, 'seq', [(i, i ^ bit) for i in range(groups)])]
    ppermute x14, starting transfers between devices: 21.2 us -> 14.9 us  [body(): lax.ppermute(v, 'seq', [(i, i ^ bit) for i in range(groups)])]
  transfers between devices with their start and end apart: 43 -> 43, of which waited for: 20 -> 18; matrix products, arithmetic and copies ran while one was open for 17% -> 18% of each run, Pallas kernels for 34% -> 34%
where the time goes in v5:
time: 501 us; the launch traced here: 497 us
  Pallas kernels  188 us (38%)
  waiting for transfers between devices  140 us (28%)
  starting transfers between devices  48.6 us (10%)
  other arithmetic  47.5 us (9%)
  local copies, waits for them, and re-layouts  36 us (7%)
  matrix products  21.3 us (4%)
  between operations  15.3 us (3%)
    ppermute x14, waiting for transfers between devices, body(): lax.ppermute(v, 'seq', [(i, i ^ bit) for i in range(groups)])  74.3 us
    pallas_call x3, Pallas kernels, mlp(): pl.pallas_call(functools.partial(mlp_kernel, len(ups), len(so_far) // 2),...  62 us
    pallas_call x2, Pallas kernels, attend_back(): pl.pallas_call(attend_back_kernel, grid=(count,), in_specs=[pl.BlockSpec(...  47.2 us
    pallas_call x2, Pallas kernels, weight_call(): pl.pallas_call(kernel, grid_spec=pltpu.PrefetchScalarGridSpec(num_scalar_...  26 us
    pallas_call x1, Pallas kernels, attend(): pl.pallas_call(attend_kernel, grid=(pairs,), in_specs=[pl.BlockSpec((rows...  23 us
    pallas_call x1, Pallas kernels, project(): pl.pallas_call(qkv_kernel, grid=(3 * third,), in_specs=[whole((rows, mode...  21.7 us
    ppermute x1, waiting for transfers between devices, body(): back_near = sent[rows:halo] + lax.ppermute(sent[:rows], 'seq', behind)  18.1 us
    ppermute x1, waiting for transfers between devices, body(): near = lax.ppermute(block_input, 'seq', ahead)  18 us
  transfers between devices with their start and end apart: 43, of which 18 were waited for; matrix products, arithmetic and copies ran while one was open for 18% of the time, Pallas kernels for 34%

profile of v5, /device:TPU:0, one launch (start us, length us, event | category | flops | bytes accessed | tf_op | source)
XLA Modules:
  0.0 496.6 jit_solution(1675415588665257212)
XLA Ops:
  8.0 1.9 reshape.142
  11.9 4.6 collective-permute-start
  24.2 18.0 %collective-permute-done.near_ref = f32[384,768]{1,0:T(8,128)S(1)} collective-permute-done((f32[384,768]{1,0:T(8,128)S(1)}, f32[384,768]{1,0:T(8,128)S(1)}, u32[]{:S(2)}, u32[]{:S(2)}) %collective-permute-start) | collective-permute-done | bytes 1179680 | tf_op jit(solution)/shard_map/ppermute | solution.py:670
  42.3 4.4 collective-permute-start.1
  46.7 3.9 collective-permute-start.2
  51.4 7.4 %fusion.13 = (f32[]{:T(128)}, f32[]{:T(128)}, f32[]{:T(128)}, f32[]{:T(128)}, f32[384,768]{1,0:T(8,128)}) fusion(f32[384,768]{1,0:T(8,128)S(1)} %copy-done.12, f32[3,384,768]{2,1,0:T(8,128)} %param.18, f32[384,768]{1,0:T(8,128)} %param.17, f32[]{:T(128)} %bitcast.5, f32[]{:T(128)} %bitcast.3, f32[]{:T(128)} %bitcast.1, f32[]{:T(128)} %bitcast), kind=kLoop, calls=%fused_computation.30 | loop fusion | flops 4423676 | bytes 7077920 | tf_op jit(solution)/shard_map/reduce_sum | solution.py:686
  59.9 11.9 %collective-permute-done.2 = s32[1,384]{1,0:T(1,128)} collective-permute-done((s32[1,384]{1,0:T(1,128)S(1)}, s32[1,384]{1,0:T(1,128)}, u32[]{:S(2)}, u32[]{:S(2)}) %collective-permute-start.2) | collective-permute-done | bytes 1568 | tf_op jit(solution)/shard_map/ppermute | solution.py:671
  71.8 5.0 %collective-permute-start.3 = (s32[1,384]{1,0:T(1,128)}, s32[1,384]{1,0:T(1,128)S(1)}, u32[]{:S(2)}, u32[]{:S(2)}) collective-permute-start(s32[1,384]{1,0:T(1,128)} %collective-permute-done.2), channel_id=1, source_target_pairs={{0,1},{1,2},{2,3},{4,5},{5,6},{6,7},{8,9},{9,10},{10,11},{12,13},{... | collective-permute-start | bytes 4616 | tf_op jit(solution)/shard_map/ppermute | solution.py:673
  76.8 3.2 pad_maximum_fusion.2
  86.4 21.7 %shard_map.239 = (f32[384,768]{1,0:T(8,128)}, f32[1152,1536]{1,0:T(8,128)}, bf16[1152,768]{1,0:T(8,128)(2,1)}, bf16[1152,768]{1,0:T(8,128)(2,1)}) custom-call(f32[384,768]{1,0:T(8,128)} %copy-done.5, f32[384,768]{1,0:T(8,128)} %copy-done.3, f32[384,768]{1,0:T(8,128)} %own_ref.1, f32[1,768]{1,0:T(1,128)} %broadcast_in_dim.50.gain_ref, ...), custom_call_target="tpu_custom_call" | custom-call | flops 22000001024 | bytes 1048576 | tf_op jit(solution)/shard_map/pallas_call | solution.py:144
  109.6 23.0 %shard_map.240.att_ref = f32[384,768]{1,0:T(8,128)} custom-call(f32[384,768]{1,0:T(8,128)} %get-tuple-element.117.q_ref, f32[1152,1536]{1,0:T(8,128)} %get-tuple-element.118.k_ref.v_ref, f32[1152,1536]{1,0:T(8,128)} %get-tuple-element.118.k_ref.v_ref, s32[384,128]{1,0:T(8,128)} %broadcast_in_dim.52.segq_ref, s32[8,1152]{1,0:T(8,128)} %broadcast_in_dim.54.segk_ref), custom_call_target="tpu_custom_call" | custom-call | flops 26400000000 | bytes 1048576 | tf_op jit(solution)/shard_map/pallas_call | solution.py:236
  132.7 3.7 convolution_add_fusion.resid_ref
  138.5 4.3 collective-permute-done.12.refs_7_
  142.8 2.0 collective-permute-done.9.refs_3_
  145.8 19.9 %shard_map.241 = (f32[768,768]{1,0:T(8,128)}, f32[768,768]{1,0:T(8,128)}, f32[4,1,384,512]{3,2,1,0:T(8,128)}) custom-call(s32[1]{0:T(128)} %bitcast.13.chip_ref, f32[384,768]{1,0:T(8,128)} %copy-done.15, f32[384,768]{1,0:T(8,128)} %copy-done.46, f32[384,768]{1,0:T(8,128)} %cot_ref.7, f32[384,768]{1,0:T(8,128)} %collective-permute-done.5.cot_other_ref, ...), custom_call_target="tpu_custom_call" | custom-call | flops 19800000512 | bytes 1048576 | tf_op jit(solution)/shard_map/pallas_call | solution.py:457
  165.7 21.0 %shard_map.242 = (f32[768,768]{1,0:T(8,128)}, f32[768,768]{1,0:T(8,128)}, f32[4,1,384,512]{3,2,1,0:T(8,128)}) custom-call(s32[1]{0:T(128)} %bitcast.13.chip_ref, f32[384,768]{1,0:T(8,128)} %copy-done.15, f32[384,768]{1,0:T(8,128)} %copy-done.46, f32[384,768]{1,0:T(8,128)} %cot_ref.7, f32[384,768]{1,0:T(8,128)} %collective-permute-done.5.cot_other_ref, ...), custom_call_target="tpu_custom_call" | custom-call | flops 19800000512 | bytes 1048576 | tf_op jit(solution)/shard_map/pallas_call | solution.py:457
  186.9 21.2 %shard_map.243 = (f32[768,768]{1,0:T(8,128)}, f32[768,768]{1,0:T(8,128)}, f32[4,1,384,512]{3,2,1,0:T(8,128)}) custom-call(s32[1]{0:T(128)} %bitcast.13.chip_ref, f32[384,768]{1,0:T(8,128)} %copy-done.15, f32[384,768]{1,0:T(8,128)} %copy-done.46, f32[384,768]{1,0:T(8,128)} %cot_ref.7, f32[384,768]{1,0:T(8,128)} %collective-permute-done.5.cot_other_ref, ...), custom_call_target="tpu_custom_call" | custom-call | flops 19800000512 | bytes 1048576 | tf_op jit(solution)/shard_map/pallas_call | solution.py:457
  209.8 2.5 collective-permute-done.13.given_ref
  215.7 7.7 %shard_map.244 = (f32[384,768]{1,0:T(8,128)}, f32[384,768]{1,0:T(8,128)}, f32[8,768]{1,0:T(8,128)}) custom-call(f32[768,768]{1,0:T(8,128)} %get-tuple-element.99.part_ref, f32[384,768]{1,0:T(8,128)} %copy-done.47, f32[384,768]{1,0:T(8,128)} %copy-done.15, f32[384,768]{1,0:T(8,128)} %cot_ref.7, f32[1,768]{1,0:T(1,128)} %broadcast_in_dim.55.gain_ref, ...), custom_call_target="tpu_custom_call" | custom-call | flops 6600000000 | bytes 1048576 | tf_op jit(solution)/shard_map/pallas_call | solution.py:505
  223.4 1.8 collective-permute-done.14
  226.9 2.6 collective-permute-start.15
  229.6 23.5 %shard_map.245 = (f32[384,768]{1,0:T(8,128)}, f32[1152,768]{1,0:T(8,128)}, f32[1152,768]{1,0:T(8,128)}) custom-call(f32[384,768]{1,0:T(8,128)} %get-tuple-element.117.q_ref, f32[1152,1536]{1,0:T(8,128)} %get-tuple-element.118.k_ref.v_ref, f32[1152,1536]{1,0:T(8,128)} %get-tuple-element.118.k_ref.v_ref, f32[384,768]{1,0:T(8,128)} %get-tuple-element.119.g_ref, ...), custom_call_target="tpu_custom_call" | custom-call | flops 23100000256 | bytes 1048576 | tf_op jit(solution)/shard_map/pallas_call | solution.py:328
  253.1 2.8 reduce-scatter.15.cloned.1.call-done
  259.1 23.8 %shard_map.246 = (f32[384,768]{1,0:T(8,128)}, f32[1152,768]{1,0:T(8,128)}, f32[1152,768]{1,0:T(8,128)}) custom-call(f32[384,768]{1,0:T(8,128)} %get-tuple-element.117.q_ref, f32[1152,1536]{1,0:T(8,128)} %get-tuple-element.118.k_ref.v_ref, f32[1152,1536]{1,0:T(8,128)} %get-tuple-element.118.k_ref.v_ref, ...), custom_call_target="tpu_custom_call", output_to_operand_aliasing={{0}: (8, {}), {1}: (9, {}), {2}: (10, {})} | custom-call | flops 23100000256 | bytes 1048576 | tf_op jit(solution)/shard_map/pallas_call | solution.py:328
  284.0 2.4 collective-permute-start.19
  286.4 12.6 %shard_map.247 = f32[2,4,96,1536]{3,2,1,0:T(8,128)} custom-call(s32[1]{0:T(128)} %bitcast.12.core_ref, bf16[1152,768]{1,0:T(8,128)(2,1)} %get-tuple-element.92.hi_ref, bf16[1152,768]{1,0:T(8,128)(2,1)} %get-tuple-element.93.lo_ref, f32[384,768]{1,0:T(8,128)} %get-tuple-element.130.dq_ref, f32[1152,768]{1,0:T(8,128)} %get-tuple-element.144.dk_ref), custom_call_target="tpu_custom_call" | custom-call | flops 9900000256 | bytes 1048576 | tf_op jit(solution)/shard_map/pallas_call | solution.py:584
  299.0 3.2 slice_bitcast_fusion
  304.4 2.1 slice_select_fusion.5
  307.0 13.4 %shard_map.248 = f32[2,4,96,1536]{3,2,1,0:T(8,128)} custom-call(s32[1]{0:T(128)} %bitcast.12.core_ref, bf16[1152,768]{1,0:T(8,128)(2,1)} %get-tuple-element.92.hi_ref, bf16[1152,768]{1,0:T(8,128)(2,1)} %get-tuple-element.93.lo_ref, f32[1152,768]{1,0:T(8,128)} %get-tuple-element.145.dv_ref, f32[384,768]{1,0:T(8,128)} %shard_map.240.att_ref, ...), custom_call_target="tpu_custom_call" | custom-call | flops 9900000256 | bytes 1048576 | tf_op jit(solution)/shard_map/pallas_call | solution.py:584
  321.3 1.8 slice_bitcast_fusion.2
  323.6 4.1 collective-permute-done.21
  328.1 2.5 pad_maximum_fusion
  339.8 1.9 collective-permute-start.23
  341.7 12.2 %collective-permute-done.24 = f32[1,192,512]{2,1,0:T(8,128)S(1)} collective-permute-done((f32[1,192,512]{2,1,0:T(8,128)S(1)}, f32[1,192,512]{2,1,0:T(8,128)S(1)}, u32[]{:S(2)}, u32[]{:S(2)}) %collective-permute-start.24) | collective-permute-done | bytes 393248 | tf_op jit(solution)/shard_map/ppermute | solution.py:714
  355.0 12.5 %fusion = f32[1152,768]{1,0:T(8,128)S(1)} fusion(f32[1152,768]{1,0:T(8,128)} %get-tuple-element.145.dv_ref, f32[1152,768]{1,0:T(8,128)} %get-tuple-element.144.dk_ref, f32[768,2304]{1,0:T(8,128)} %all-gather.3.cloned.1.call-done.w_ref), kind=kOutput, calls=%fused_computation | convolution fusion | flops 8155496448 | bytes 15335424 | tf_op jit(solution)/shard_map/dot_general | solution.py:608
  369.6 1.8 collective-permute-start.26
  371.4 5.1 %fusion.16 = (f32[768]{0:T(1024)S(1)}, f32[768]{0:T(1024)S(1)}, f32[768]{0:T(1024)S(1)}, f32[768]{0:T(1024)S(1)}, f32[768]{0:T(1024)S(1)}, /*index=5*/f32[768]{0:T(1024)S(1)}, f32[384,768]{1,0:T(8,128)}) fusion(f32[1152,768]{1,0:T(8,128)S(1)} %fusion, f32[384]{0:T(512)S(1)} %add_rsqrt_fusion.2, f32[384,768]{1,0:T(8,128)S(1)} %copy-done.2, ...), kind=kOutput, calls=%fused_computation.102 | convolution fusion | flops 1363668480 | bytes 11824128 | tf_op jit(solution)/shard_map/dot_general | solution.py:608
  376.6 2.7 multiply_reduce_fusion.1
  381.4 1.7 collective-permute-start.28
  383.1 2.1 broadcast_select_fusion.6
  387.5 18.1 %collective-permute-done.26 = f32[384,768]{1,0:T(8,128)} collective-permute-done((f32[384,768]{1,0:T(8,128)}, f32[384,768]{1,0:T(8,128)}, u32[]{:S(2)}, u32[]{:S(2)}) %collective-permute-start.26) | collective-permute-done | bytes 1179680 | tf_op jit(solution)/shard_map/ppermute | solution.py:786
  405.5 2.8 slice_add_fusion
  412.2 14.4 %collective-permute-done.30 = f32[1,48,3072]{2,1,0:T(8,128)S(1)} collective-permute-done((f32[1,48,3072]{2,1,0:T(8,128)S(1)}, f32[1,48,3072]{2,1,0:T(8,128)S(1)}, u32[]{:S(2)}, u32[]{:S(2)}) %collective-permute-start.30) | collective-permute-done | bytes 589856 | tf_op jit(solution)/shard_map/ppermute | solution.py:714
  434.8 33.3 %collective-permute-done.31 = f32[1,48,3072]{2,1,0:T(8,128)} collective-permute-done((f32[1,48,3072]{2,1,0:T(8,128)}, f32[1,48,3072]{2,1,0:T(8,128)}, u32[]{:S(2)}, u32[]{:S(2)}) %collective-permute-start.31) | collective-permute-done | bytes 589856 | tf_op jit(solution)/shard_map/ppermute | solution.py:714
  469.4 2.3 fusion.17
  471.8 2.0 collective-permute-start.36
  473.8 2.1 collective-permute-done.34
  477.4 9.0 %collective-permute-done.35 = f32[8,768]{1,0:T(8,128)S(1)} collective-permute-done((f32[8,768]{1,0:T(8,128)S(1)}, f32[8,768]{1,0:T(8,128)S(1)}, u32[]{:S(2)}, u32[]{:S(2)}) %collective-permute-start.35) | collective-permute-done | bytes 24608 | tf_op jit(solution)/shard_map/ppermute | solution.py:714
  (258 shorter events, 73.3 us)
Async XLA Ops:
  7.2 78.8 %all-gather.3.cloned.1.call-start = ((), (), s32[]{:S(2)}) async-start(), calls=%async_computation.4 | async-start | bytes 7962624 | tf_op jit(solution)/shard_map/all_gather | solution.py:646
  7.9 124.8 %all-gather.5.cloned.1.call-start = ((), (), s32[]{:S(2)}) async-start(), calls=%async_computation.5 | async-start | bytes 2654208 | tf_op jit(solution)/shard_map/all_gather | solution.py:646
  11.4 8.9 %collective-permute-start.6 = (f32[96,1536]{1,0:T(8,128)}, f32[96,1536]{1,0:T(8,128)}, u32[]{:S(2)}, u32[]{:S(2)}) collective-permute-start(f32[96,1536]{1,0:T(8,128)} %select_n.149), channel_id=1, source_target_pairs={{0,4},{4,0},{8,12},{12,8},{16,20},{20,16},{24,28},{28,24},{1,5},{5... | collective-permute-start | bytes 1769480 | tf_op jit(solution)/shard_map/ppermute | solution.py:643
  11.9 30.4 %collective-permute-start = (f32[384,768]{1,0:T(8,128)S(1)}, f32[384,768]{1,0:T(8,128)S(1)}, u32[]{:S(2)}, u32[]{:S(2)}) collective-permute-start(f32[384,768]{1,0:T(8,128)S(1)} %copy-done), channel_id=1, source_target_pairs={{0,1},{1,2},{2,3},{4,5},{5,6},{6,7},{8,9},{9,10},{10,11},{12,13},{... | collective-permute-start | bytes 3538952 | tf_op jit(solution)/shard_map/ppermute | solution.py:670
  16.5 66.9 %collective-permute-start.10 = (f32[384,768]{1,0:T(8,128)}, f32[384,768]{1,0:T(8,128)}, u32[]{:S(2)}, u32[]{:S(2)}) collective-permute-start(f32[384,768]{1,0:T(8,128)} %refs_4_.5), channel_id=1, source_target_pairs={{0,8},{4,12},{8,0},{12,4},{16,24},{20,28},{24,16},{28,20},{1,9},{5... | collective-permute-start | bytes 3538952 | tf_op jit(solution)/shard_map/ppermute | solution.py:643
  21.6 29.1 %copy-start.12 = (f32[384,768]{1,0:T(8,128)S(1)}, f32[384,768]{1,0:T(8,128)}, u32[]{:S(2)}) copy-start(f32[384,768]{1,0:T(8,128)} %cot_ref.7) | copy-start | bytes 3538948
  21.6 29.2 %copy-start.40 = (f32[5]{0:T(128)S(1)}, f32[5]{0:T(128)}, u32[]{:S(2)}) copy-start(f32[5]{0:T(128)} %param.19) | copy-start | bytes 64
  22.7 62.2 %collective-permute-start.8 = (f32[192,1536]{1,0:T(8,128)}, f32[192,1536]{1,0:T(8,128)}, u32[]{:S(2)}, u32[]{:S(2)}) collective-permute-start(f32[192,1536]{1,0:T(8,128)} %pad_maximum_fusion.1.refs_0_), channel_id=1, source_target_pairs={{0,16},{4,20},{8,24},{12,28},{16,0},{20,4},{24,8},{28,12},{1,17},{... | collective-permute-start | bytes 3538952 | tf_op jit(solution)/shard_map/ppermute | solution.py:643
  42.3 43.2 %collective-permute-start.1 = (f32[384,768]{1,0:T(8,128)S(1)}, f32[384,768]{1,0:T(8,128)S(1)}, u32[]{:S(2)}, u32[]{:S(2)}) collective-permute-start(f32[384,768]{1,0:T(8,128)S(1)} %collective-permute-done.near_ref), channel_id=1, source_target_pairs={{0,1},{1,2},{2,3},{4,5},{5,6},{6,7},{8,9},{9,10},{10,11},{12,13},{... | collective-permute-start | bytes 3538952 | tf_op jit(solution)/shard_map/ppermute | solution.py:672
  46.7 25.1 %collective-permute-start.2 = (s32[1,384]{1,0:T(1,128)S(1)}, s32[1,384]{1,0:T(1,128)}, u32[]{:S(2)}, u32[]{:S(2)}) collective-permute-start(s32[1,384]{1,0:T(1,128)S(1)} %get-tuple-element.201), channel_id=1, source_target_pairs={{0,1},{1,2},{2,3},{4,5},{5,6},{6,7},{8,9},{9,10},{10,11},{12,13},{... | collective-permute-start | bytes 4616 | tf_op jit(solution)/shard_map/ppermute | solution.py:671
  50.7 85.7 %collective-permute-start.5 = (f32[384,768]{1,0:T(8,128)S(1)}, f32[384,768]{1,0:T(8,128)}, u32[]{:S(2)}, u32[]{:S(2)}) collective-permute-start(f32[384,768]{1,0:T(8,128)S(1)} %copy-done.12), channel_id=1, source_target_pairs={{0,4},{4,0},{8,12},{12,8},{16,20},{20,16},{24,28},{28,24},{1,5},{5... | collective-permute-start | bytes 3538952 | tf_op jit(solution)/shard_map/ppermute | solution.py:643
  50.7 161.7 %reduce-scatter.13.cloned.1.call-start = ((), (), s32[]{:S(2)}) async-start(), calls=%async_computation.6 | async-start | bytes 3932160
  71.8 9.4 %collective-permute-start.3 = (s32[1,384]{1,0:T(1,128)}, s32[1,384]{1,0:T(1,128)S(1)}, u32[]{:S(2)}, u32[]{:S(2)}) collective-permute-start(s32[1,384]{1,0:T(1,128)} %collective-permute-done.2), channel_id=1, source_target_pairs={{0,1},{1,2},{2,3},{4,5},{5,6},{6,7},{8,9},{9,10},{10,11},{12,13},{... | collective-permute-start | bytes 4616 | tf_op jit(solution)/shard_map/ppermute | solution.py:673
  81.2 57.3 %collective-permute-start.11 = (f32[384,768]{1,0:T(8,128)}, f32[384,768]{1,0:T(8,128)}, u32[]{:S(2)}, u32[]{:S(2)}) collective-permute-start(f32[384,768]{1,0:T(8,128)} %refs_4_.5), channel_id=1, source_target_pairs={{0,16},{4,20},{8,24},{12,28},{16,0},{20,4},{24,8},{28,12},{1,17},{... | collective-permute-start | bytes 3538952 | tf_op jit(solution)/shard_map/ppermute | solution.py:643
  83.4 55.1 %collective-permute-start.7 = (f32[192,1536]{1,0:T(8,128)}, f32[192,1536]{1,0:T(8,128)}, u32[]{:S(2)}, u32[]{:S(2)}) collective-permute-start(f32[192,1536]{1,0:T(8,128)} %pad_maximum_fusion.1.refs_0_), channel_id=1, source_target_pairs={{0,8},{4,12},{8,0},{12,4},{16,24},{20,28},{24,16},{28,20},{1,9},{5... | collective-permute-start | bytes 3538952 | tf_op jit(solution)/shard_map/ppermute | solution.py:643
  84.9 57.8 %collective-permute-start.12 = (f32[384,768]{1,0:T(8,128)}, f32[384,768]{1,0:T(8,128)}, u32[]{:S(2)}, u32[]{:S(2)}) collective-permute-start(f32[384,768]{1,0:T(8,128)} %collective-permute-done.10.refs_5_), channel_id=1, source_target_pairs={{0,16},{4,20},{8,24},{12,28},{16,0},{20,4},{24,8},{28,12},{1,17},{... | collective-permute-start | bytes 3538952 | tf_op jit(solution)/shard_map/ppermute | solution.py:643
  85.4 59.3 %collective-permute-start.9 = (f32[192,1536]{1,0:T(8,128)}, f32[192,1536]{1,0:T(8,128)}, u32[]{:S(2)}, u32[]{:S(2)}) collective-permute-start(f32[192,1536]{1,0:T(8,128)} %collective-permute-done.8.refs_2_), channel_id=1, source_target_pairs={{0,8},{4,12},{8,0},{12,4},{16,24},{20,28},{24,16},{28,20},{1,9},{5... | collective-permute-start | bytes 3538952 | tf_op jit(solution)/shard_map/ppermute | solution.py:643
  136.4 8.3 %collective-permute-start.4 = (f32[384,768]{1,0:T(8,128)S(1)}, f32[384,768]{1,0:T(8,128)S(1)}, u32[]{:S(2)}, u32[]{:S(2)}) collective-permute-start(f32[384,768]{1,0:T(8,128)S(1)} %convolution_add_fusion.resid_ref), channel_id=1, source_target_pairs={{0,4},{4,0},{8,12},{12,8},{16,20},{20,16},{24,28},{28,24},{1,5},{5... | collective-permute-start | bytes 3538952 | tf_op jit(solution)/shard_map/ppermute | solution.py:643
  165.7 90.2 %reduce-scatter.15.cloned.1.call-start = ((), (), s32[]{:S(2)}) async-start(), calls=%async_computation.7 | async-start | bytes 3932160
  186.7 117.8 %reduce-scatter.17.cloned.1.call-start = ((), (), s32[]{:S(2)}) async-start(), calls=%async_computation.8 | async-start | bytes 3932160
  209.5 2.9 collective-permute-start.13
  209.6 199.4 %reduce-scatter.19.cloned.1.call-start = ((), (), s32[]{:S(2)}) async-start(), calls=%async_computation.9 | async-start | bytes 5898240
  214.0 11.2 %collective-permute-start.14 = (f32[1,192,512]{2,1,0:T(8,128)S(1)}, f32[1,192,512]{2,1,0:T(8,128)S(1)}, u32[]{:S(2)}, u32[]{:S(2)}) collective-permute-start(f32[1,192,512]{2,1,0:T(8,128)S(1)} %slice_select_fusion.7), channel_id=1, source_target_pairs={{0,1},{1,0},{2,3},{3,2},{4,5},{5,4},{6,7},{7,6},{8,9},{9,8},{10,11... | collective-permute-start | bytes 1179656 | tf_op jit(solution)/shard_map/ppermute | solution.py:714
  226.9 26.1 %collective-permute-start.15 = (f32[1,192,512]{2,1,0:T(8,128)S(1)}, f32[1,192,512]{2,1,0:T(8,128)S(1)}, u32[]{:S(2)}, u32[]{:S(2)}) collective-permute-start(f32[1,192,512]{2,1,0:T(8,128)S(1)} %select_add_fusion.3), channel_id=1, source_target_pairs={{0,2},{1,3},{2,0},{3,1},{4,6},{5,7},{6,4},{7,5},{8,10},{9,11},{10,... | collective-permute-start | bytes 1179656 | tf_op jit(solution)/shard_map/ppermute | solution.py:714
  257.0 25.9 %copy-start.17 = (f32[1,1,384,512]{3,2,1,0:T(8,128)S(1)}, f32[1,1,384,512]{3,2,1,0:T(8,128)}, u32[]{:S(2)}) copy-start(f32[1,1,384,512]{3,2,1,0:T(8,128)} %reduce-scatter.15.cloned.1.call-done) | copy-start | bytes 2359300
  257.0 25.9 %collective-permute-start.16 = (f32[1,192,512]{2,1,0:T(8,128)S(1)}, f32[1,192,512]{2,1,0:T(8,128)S(1)}, u32[]{:S(2)}, u32[]{:S(2)}) collective-permute-start(f32[1,192,512]{2,1,0:T(8,128)S(1)} %slice_select_fusion.6), channel_id=1, source_target_pairs={{0,1},{1,0},{2,3},{3,2},{4,5},{5,4},{6,7},{7,6},{8,9},{9,8},{10,11... | collective-permute-start | bytes 1179656 | tf_op jit(solution)/shard_map/ppermute | solution.py:714
  258.6 24.4 %collective-permute-start.17 = (f32[1,192,512]{2,1,0:T(8,128)S(1)}, f32[1,192,512]{2,1,0:T(8,128)S(1)}, u32[]{:S(2)}, u32[]{:S(2)}) collective-permute-start(f32[1,192,512]{2,1,0:T(8,128)S(1)} %add.188), channel_id=1, source_target_pairs={{0,1},{1,0},{2,3},{3,2},{4,5},{5,4},{6,7},{7,6},{8,9},{9,8},{10,11... | collective-permute-start | bytes 1179656 | tf_op jit(solution)/shard_map/ppermute | solution.py:714
  284.0 19.6 %collective-permute-start.19 = (f32[1,192,512]{2,1,0:T(8,128)S(1)}, f32[1,192,512]{2,1,0:T(8,128)S(1)}, u32[]{:S(2)}, u32[]{:S(2)}) collective-permute-start(f32[1,192,512]{2,1,0:T(8,128)S(1)} %select_add_fusion.2), channel_id=1, source_target_pairs={{0,2},{1,3},{2,0},{3,1},{4,6},{5,7},{6,4},{7,5},{8,10},{9,11},{10,... | collective-permute-start | bytes 1179656 | tf_op jit(solution)/shard_map/ppermute | solution.py:714
  302.3 20.9 %collective-permute-start.18 = (f32[4,96,1536]{2,1,0:T(8,128)}, f32[4,96,1536]{2,1,0:T(8,128)S(1)}, u32[]{:S(2)}, u32[]{:S(2)}) collective-permute-start(f32[4,96,1536]{2,1,0:T(8,128)} %slice_bitcast_fusion), channel_id=1, source_target_pairs={{0,4},{4,0},{8,12},{12,8},{16,20},{20,16},{24,28},{28,24},{1,5},{5... | collective-permute-start | bytes 7077896 | tf_op jit(solution)/shard_map/ppermute | solution.py:643
  306.5 13.9 %collective-permute-start.20 = (f32[1,192,512]{2,1,0:T(8,128)}, f32[1,192,512]{2,1,0:T(8,128)S(1)}, u32[]{:S(2)}, u32[]{:S(2)}) collective-permute-start(f32[1,192,512]{2,1,0:T(8,128)} %slice_select_fusion.5), channel_id=1, source_target_pairs={{0,1},{1,0},{2,3},{3,2},{4,5},{5,4},{6,7},{7,6},{8,9},{9,8},{10,11... | collective-permute-start | bytes 1179656 | tf_op jit(solution)/shard_map/ppermute | solution.py:714
  323.1 4.6 collective-permute-start.21
  335.9 18.0 %collective-permute-start.24 = (f32[1,192,512]{2,1,0:T(8,128)S(1)}, f32[1,192,512]{2,1,0:T(8,128)S(1)}, u32[]{:S(2)}, u32[]{:S(2)}) collective-permute-start(f32[1,192,512]{2,1,0:T(8,128)S(1)} %copy-done.29), channel_id=1, source_target_pairs={{0,1},{1,0},{2,3},{3,2},{4,5},{5,4},{6,7},{7,6},{8,9},{9,8},{10,11... | collective-permute-start | bytes 1179656 | tf_op jit(solution)/shard_map/ppermute | solution.py:714
  339.8 27.7 %collective-permute-start.23 = (f32[1,192,512]{2,1,0:T(8,128)S(1)}, f32[1,192,512]{2,1,0:T(8,128)S(1)}, u32[]{:S(2)}, u32[]{:S(2)}) collective-permute-start(f32[1,192,512]{2,1,0:T(8,128)S(1)} %copy-done.30), channel_id=1, source_target_pairs={{0,2},{1,3},{2,0},{3,1},{4,6},{5,7},{6,4},{7,5},{8,10},{9,11},{10,... | collective-permute-start | bytes 1179656 | tf_op jit(solution)/shard_map/ppermute | solution.py:714
  354.9 21.6 %collective-permute-start.22 = (f32[384,768]{1,0:T(8,128)S(1)}, f32[384,768]{1,0:T(8,128)S(1)}, u32[]{:S(2)}, u32[]{:S(2)}) collective-permute-start(f32[384,768]{1,0:T(8,128)S(1)} %slice.176), channel_id=1, source_target_pairs={{0,4},{4,0},{8,12},{12,8},{16,20},{20,16},{24,28},{28,24},{1,5},{5... | collective-permute-start | bytes 3538952 | tf_op jit(solution)/shard_map/ppermute | solution.py:643
  368.5 14.7 %collective-permute-start.25 = (f32[1,192,512]{2,1,0:T(8,128)}, f32[1,192,512]{2,1,0:T(8,128)}, u32[]{:S(2)}, u32[]{:S(2)}) collective-permute-start(f32[1,192,512]{2,1,0:T(8,128)} %add.198), channel_id=1, source_target_pairs={{0,1},{1,0},{2,3},{3,2},{4,5},{5,4},{6,7},{7,6},{8,9},{9,8},{10,11... | collective-permute-start | bytes 1179656 | tf_op jit(solution)/shard_map/ppermute | solution.py:714
  369.6 36.0 %collective-permute-start.26 = (f32[384,768]{1,0:T(8,128)}, f32[384,768]{1,0:T(8,128)}, u32[]{:S(2)}, u32[]{:S(2)}) collective-permute-start(f32[384,768]{1,0:T(8,128)} %slice.206), channel_id=1, source_target_pairs={{1,0},{2,1},{3,2},{5,4},{6,5},{7,6},{9,8},{10,9},{11,10},{13,12},{... | collective-permute-start | bytes 3538952 | tf_op jit(solution)/shard_map/ppermute | solution.py:786
  380.1 1.3 collective-permute-start.27
  381.4 4.4 collective-permute-start.28
  385.8 22.6 %collective-permute-start.29 = (f32[8,768]{1,0:T(8,128)S(1)}, f32[8,768]{1,0:T(8,128)S(1)}, u32[]{:S(2)}, u32[]{:S(2)}) collective-permute-start(f32[8,768]{1,0:T(8,128)S(1)} %add.210), channel_id=1, source_target_pairs={{0,16},{4,20},{8,24},{12,28},{16,0},{20,4},{24,8},{28,12},{1,17},{... | collective-permute-start | bytes 73736 | tf_op jit(solution)/shard_map/ppermute | solution.py:643
  410.3 16.3 %collective-permute-start.30 = (f32[1,48,3072]{2,1,0:T(8,128)S(1)}, f32[1,48,3072]{2,1,0:T(8,128)S(1)}, u32[]{:S(2)}, u32[]{:S(2)}) collective-permute-start(f32[1,48,3072]{2,1,0:T(8,128)S(1)} %slice_select_fusion.4), channel_id=1, source_target_pairs={{0,1},{1,0},{2,3},{3,2},{4,5},{5,4},{6,7},{7,6},{8,9},{9,8},{10,11... | collective-permute-start | bytes 1769480 | tf_op jit(solution)/shard_map/ppermute | solution.py:714
  410.6 18.1 %collective-permute-start.32 = (f32[3,96,512]{2,1,0:T(8,128)S(1)}, f32[3,96,512]{2,1,0:T(8,128)S(1)}, u32[]{:S(2)}, u32[]{:S(2)}) collective-permute-start(f32[3,96,512]{2,1,0:T(8,128)S(1)} %slice_select_fusion.2), channel_id=1, source_target_pairs={{0,4},{4,0},{8,12},{12,8},{16,20},{20,16},{24,28},{28,24},{1,5},{5... | collective-permute-start | bytes 1769480 | tf_op jit(solution)/shard_map/ppermute | solution.py:643
  410.7 58.6 %collective-permute-start.33 = (f32[384,768]{1,0:T(8,128)}, f32[384,768]{1,0:T(8,128)}, u32[]{:S(2)}, u32[]{:S(2)}) collective-permute-start(f32[384,768]{1,0:T(8,128)} %slice_add_fusion), channel_id=1, source_target_pairs={{1,0},{2,1},{3,2},{5,4},{6,5},{7,6},{9,8},{10,9},{11,10},{13,12},{... | collective-permute-start | bytes 3538952 | tf_op jit(solution)/shard_map/ppermute | solution.py:810
  427.5 40.5 %collective-permute-start.31 = (f32[1,48,3072]{2,1,0:T(8,128)}, f32[1,48,3072]{2,1,0:T(8,128)}, u32[]{:S(2)}, u32[]{:S(2)}) collective-permute-start(f32[1,48,3072]{2,1,0:T(8,128)} %select_add_fusion), channel_id=1, source_target_pairs={{0,2},{1,3},{2,0},{3,1},{4,6},{5,7},{6,4},{7,5},{8,10},{9,11},{10,... | collective-permute-start | bytes 1769480 | tf_op jit(solution)/shard_map/ppermute | solution.py:714
  434.7 34.6 %copy-start.11 = (f32[384,768]{1,0:T(8,128)S(1)}, f32[384,768]{1,0:T(8,128)}, u32[]{:S(2)}) copy-start(f32[384,768]{1,0:T(8,128)} %get-tuple-element.208) | copy-start | bytes 3538948
  434.8 34.6 %copy-start.39 = (f32[768]{0:T(1024)S(1)}, f32[768]{0:T(1024)}, u32[]{:S(2)}) copy-start(f32[768]{0:T(1024)} %param.20) | copy-start | bytes 9220
  471.7 4.2 collective-permute-start.34
  471.8 15.8 %collective-permute-start.36 = (f32[1,48,3072]{2,1,0:T(8,128)S(1)}, f32[1,48,3072]{2,1,0:T(8,128)S(1)}, u32[]{:S(2)}, u32[]{:S(2)}) collective-permute-start(f32[1,48,3072]{2,1,0:T(8,128)S(1)} %add.213), channel_id=1, source_target_pairs={{0,1},{1,0},{2,3},{3,2},{4,5},{5,4},{6,7},{7,6},{8,9},{9,8},{10,11... | collective-permute-start | bytes 1769480 | tf_op jit(solution)/shard_map/ppermute | solution.py:714
  476.0 10.4 %collective-permute-start.35 = (f32[8,768]{1,0:T(8,128)S(1)}, f32[8,768]{1,0:T(8,128)S(1)}, u32[]{:S(2)}, u32[]{:S(2)}) collective-permute-start(f32[8,768]{1,0:T(8,128)S(1)} %add.216), channel_id=1, source_target_pairs={{0,2},{1,3},{2,0},{3,1},{4,6},{5,7},{6,4},{7,5},{8,10},{9,11},{10,... | collective-permute-start | bytes 73736 | tf_op jit(solution)/shard_map/ppermute | solution.py:714
  (45 other events, 324.2 us)
Sparse Core Ops, SparseCore 0:
  9.9 69.1 all-gather.2
  81.0 38.7 all-gather.4
  165.8 43.2 reduce-scatter.12
  211.9 43.9 reduce-scatter.14
  258.7 43.9 reduce-scatter.16
  330.8 57.5 reduce-scatter.18

commit v6 on v5

--- a/solution.py
+++ b/solution.py
@@ -161,7 +161,7 @@
             jax.ShapeDtypeStruct((total, model), BF16),
             jax.ShapeDtypeStruct((total, model), BF16),
         ],
-        cost_estimate=cost(20),
+        cost_estimate=cost(2),
         compiler_params=params(),
     )(far, near, own, gain, bias, w_full, cosine, sine)
 
@@ -246,7 +246,7 @@
         out_specs=pl.BlockSpec((rows, 128), lambda p: (0, p)),
         out_shape=jax.ShapeDtypeStruct((rows, model), F32),
         scratch_shapes=[pltpu.VMEM((rows, total - rows + BLK), F32)],
-        cost_estimate=cost(24),
+        cost_estimate=cost(2),
         compiler_params=params(),
     )(q_rot, kv, kv, seg_q, seg_k)
 
@@ -355,6 +355,7 @@
 
 def mlp_kernel(count, begun, chip_ref, resid_ref, other_ref, cot_ref, cot_other_ref, gain_ref, bias_ref,
                scale_ref, *refs):
+    packed_ref, refs = (refs[:1], refs[1:]) if count == 0 else ((), refs)
     up_refs, down_refs = refs[:count], refs[count:2 * count]
     refs = refs[2 * count:]
     so_far, refs = refs[:2 * begun], refs[2 * begun:]
@@ -393,6 +394,19 @@
     chips, _, tall, width = grad_ref.shape
     up_tall = up_hi.shape[0] // chips
     deep = down_hi.shape[0] // chips
+    half = deep // 2
+    for ref in packed_ref:
+        for at in range(chips):
+            high, low = split(ref[at])
+            here = slice(at * up_tall, (at + 1) * up_tall)
+            up_hi[here], up_lo[here] = high[:up_tall], low[:up_tall]
+            here = slice(at * deep, (at + 1) * deep)
+            for part, target in ((high, down_hi), (low, down_lo)):
+                target[here, :width] = part[up_tall:up_tall + deep]
+                right = part[up_tall + deep:]
+                target[here, width:] = jnp.concatenate(
+                    [right[:, :width // 2], right[:, width // 2:]], axis=0
+                )
     up = (up_hi[...], up_lo[...])
     down = (down_hi[...], down_lo[...])
     normed = (x_hi[...], x_lo[...])
@@ -412,7 +426,6 @@
     gnorm_ref[...] += three(dot_nt, grad_pre, up)
     gup = three(dot_nn, normed_t, grad_pre)
     gdown = three(dot_tn, act2, grad_block)
-    half = deep // 2
     for chip in range(chips):
         grad_ref[chip, 0, :up_tall] = gup[chip * up_tall:(chip + 1) * up_tall]
         part = gdown[chip * deep:(chip + 1) * deep]
@@ -428,7 +441,14 @@
     up_tall = model // chips
     deep = width // chips
     fixed = lambda shape: pl.BlockSpec(shape, lambda j, c: (0, 0))
-    if len(ups) > 1:
+    pieces = len(downs)
+    if pieces == 0:
+        up_specs = [pl.BlockSpec(ups[0].shape, lambda j, c: (0, 0, 0))]
+    else:
+        up_specs = [
+            pl.BlockSpec((up.shape[0], width), lambda j, c: (0, first + j)) for up in ups
+        ]
+    if pieces != 1:
         down_spec = pl.BlockSpec((deep, model), lambda j, c: (first + j, 0))
     else:
         downs = [downs[0].reshape(chips, -1, model)]
@@ -439,7 +459,7 @@
         grid=(steps,),
         in_specs=[fixed((rows, model))] * 4 + [fixed((1, model))] * 2
         + [pl.BlockSpec(memory_space=pltpu.SMEM)]
-        + [pl.BlockSpec((up.shape[0], width), lambda j, c: (0, first + j)) for up in ups]
+        + up_specs
         + [down_spec] * len(downs)
         + [fixed((2 * rows, model))] * len(so_far),
         out_specs=[
@@ -455,7 +475,7 @@
         ],
     )
     return pl.pallas_call(
-        functools.partial(mlp_kernel, len(ups), len(so_far) // 2),
+        functools.partial(mlp_kernel, pieces, len(so_far) // 2),
         grid_spec=grid_spec,
         out_shape=[
             jax.ShapeDtypeStruct((2 * rows, model), F32),
@@ -465,6 +485,18 @@
         cost_estimate=cost(18 * steps),
         compiler_params=params(),
     )(chip, resid, other, cot, cot_other, gain, bias, scale, *ups, *downs, *so_far)
+
+
+def fold_rows(values, width):
+    rows = values.shape[0]
+    right = values[:, width:]
+    return jnp.concatenate(
+        [
+            values[:, :width],
+            jnp.concatenate([right[:rows // 2], right[rows // 2:]], axis=1),
+        ],
+        axis=0,
+    )
 
 
 def unpack_grads(up, down, sibling_swap, core, chips):
@@ -652,19 +684,27 @@
     by_core = jnp.transpose(by_core, (2, 0, 3, 1, 4)).reshape(2, w_up.shape[0], -1)
     mine = jnp.where(core == 0, by_core[0], by_core[1])
     given = swap(jnp.where(core == 0, by_core[1], by_core[0]))
+    together = lax.optimization_barrier
     up_chip = jnp.concatenate(
         [jnp.where(core == 0, mine, given), jnp.where(core == 0, given, mine)], axis=0
     )
+    width = up_chip.shape[1] // 3
+
+    chip_gather = functools.partial(
+        lax.all_gather, axis_name="dp", axis=0, axis_index_groups=same_core
+    )
+
+    up_near, down_near = up_chip[:, :2 * width], w_down[:2 * third]
     if chips == 4:
-        up_x, down_x = exchange(up_chip, 2), exchange(w_down, 2)
-        up_y, down_y = exchange(up_chip, 4), exchange(w_down, 4)
-        ups = [up_chip, up_x, up_y, exchange(up_y, 2)]
-        downs = [w_down, down_x, down_y, exchange(down_x, 4)]
+        sides = [
+            exchange(up_near, 2), exchange(up_near, 4),
+            exchange(down_near, 2), exchange(down_near, 4),
+        ]
     else:
-        ups, downs = (
-            [lax.all_gather(v, "dp", axis=0, tiled=True, axis_index_groups=same_core)]
-            for v in (up_chip, w_down)
-        )
+        sides = []
+    packed = chip_gather(
+        jnp.concatenate([up_chip[:, 2 * width:], fold_rows(w_down[2 * third:], width)], axis=0)
+    )
 
     seg_own = segments + 1
     near = lax.ppermute(block_input, "seq", ahead)
@@ -684,11 +724,20 @@
     earlier = (embedding, earlier_outs[0], earlier_outs[1], earlier_outs[2])
     base = sum(dwa_weights[i] * value for i, value in enumerate(earlier))
     dots = jnp.stack([jnp.sum(cotangent * value) for value in earlier])
-    far, base, dots = lax.optimization_barrier((far, base, dots))
+    far, base, dots, sides = together((far, base, dots, sides))
 
     q_rot, kv, normed_hi, normed_lo = project(
         far, near, block_input, gain1, bias1, qkv_full, cosine, sine
     )
+    if chips == 4:
+        diagonal = [exchange(sides[1], 2), exchange(sides[2], 4)]
+        q_rot, diagonal = together((q_rot, diagonal))
+        near_weights = (
+            [up_near, sides[0], sides[1], diagonal[0]],
+            [down_near, sides[2], sides[3], diagonal[1]],
+        )
+    else:
+        near_weights = tuple([chip_gather(v, tiled=True)] for v in (up_near, down_near))
     attended = attend(q_rot, kv, seg_q_col, seg_k_row)
 
     out_full = gather(w_out)
@@ -698,7 +747,7 @@
     scale = dwa_weights[4].reshape(1, 1)
     call = functools.partial(
         mlp, chip=chip, chips=chips, resid=resid, other=resid_other, cot=cotangent,
-        cot_other=cot_other, gain=gain2, bias=bias2, scale=scale, ups=ups, downs=downs,
+        cot_other=cot_other, gain=gain2, bias=bias2, scale=scale,
     )
     scatter = lambda v: lax.psum_scatter(v, "dp", scatter_dimension=0, tiled=True)
     scatter_chips = lambda v: lax.psum_scatter(
@@ -706,7 +755,8 @@
     )
     so_far, shards = (), []
     for third_at in range(3):
-        out_part, gnorm_part, grads = call(third_at, 1, so_far)
+        ups, downs = near_weights if third_at < 2 else ([packed], [])
+        out_part, gnorm_part, grads = call(third_at, 1, so_far, ups=ups, downs=downs)
         so_far = (out_part, gnorm_part)
         shards.append(scatter_chips(grads)[0])
     given = swap(gnorm_part[rows:])
@@ -731,7 +781,6 @@
         other = shift(kept, 1)
         return jnp.where(even, kept, other), jnp.where(even, other, kept)
 
-    together = lax.optimization_barrier
     shards[0], given = together((shards[0], given))
     line_a = line_start(shards[0])
     grad_resid, grad_attended, sums_two = resid_back(
@@ -770,7 +819,6 @@
     grads_c, out_part = together((grads_c, out_part))
     shard_c = scatter_chips(grads_c)[0]
     out_sib = swap(out_part[rows:])
-    ends_b, dk, dv = together((ends_b, dk, dv))
     dkv = jnp.concatenate([dk, dv], axis=1)
 
     block_out = resid + out_part[:rows] + out_sib
@@ -779,7 +827,7 @@
 
     wq, wkv = qkv_full[:, :model], qkv_full[:, model:]
     partial = outer_cols(dkv, wkv)
-    line_c, partial = together((line_c, partial))
+    line_c, ends_b, partial = together((line_c, ends_b, partial))
     ends_c = line_end(line_c)
     own_part = partial[halo:] + outer_cols(dq, wq)
     (sent,) = together((partial,))
@@ -805,9 +853,11 @@
     while bit < devices:
         small = small + exchange(small, bit)
         bit *= 2
-    shard_c, ends_c, back_near, small = together((shard_c, ends_c, back_near, small))
+    given_back = lax.ppermute(back_near, "seq", behind)
+    shard_c, ends_c, given_back, small = together((shard_c, ends_c, given_back, small))
     last = line_middle(line_start(shard_c[None]))
-    given_back = lax.ppermute(back_near, "seq", behind)
+    grad_normed_one = own_part + given_back
+    grad_input = grad_resid + norm_back(grad_normed_one, gain1, xhat1, rate1)
     grad_up, grad_down = unpack_grads(
         *(
             jnp.concatenate(parts, axis=0)
@@ -815,8 +865,8 @@
         ),
         swap, core, chips,
     )
-    last, grad_up, grad_down, small, given_back = together(
-        (last, grad_up, grad_down, small, given_back)
+    last, grad_up, grad_down, small, grad_input = together(
+        (last, grad_up, grad_down, small, grad_input)
     )
     bit = 1
     while bit < groups:
@@ -826,8 +876,6 @@
     grad_dwa = small[4, :5]
     last = jnp.concatenate(line_end(last), axis=1)[0]
     grad_qkv, grad_wout = last[:, :3 * model], last[:, 3 * model:]
-    grad_normed_one = own_part + given_back
-    grad_input = grad_resid + norm_back(grad_normed_one, gain1, xhat1, rate1)
     return (
         output,
         grad_input,

time: 501 us -> 509 us (1.016)
  local copies, waits for them, and re-layouts: 36 us -> 48.2 us
  waiting for transfers between devices: 140 us -> 133 us
    ppermute x14, waiting for transfers between devices: 74.3 us -> 55.1 us  [body(): lax.ppermute(v, 'seq', [(i, i ^ bit) for i in range(groups)])]
    ppermute x17, waiting for transfers between devices: 14.2 us -> 33.2 us  [body(): lax.ppermute(v, 'dp', [(i, i ^ bit) for i in range(devices)])]
    ppermute x1, waiting for transfers between devices: 0.01 us -> 13.5 us  [body(): given_back = lax.ppermute(back_near, 'seq', behind)]
    ppermute x1, waiting for transfers between devices: 11.9 us -> 1.18 us  [body(): seg_near = lax.ppermute(seg_own, 'seq', ahead)]
    ppermute x1, waiting for transfers between devices: 18 us -> 7.66 us  [body(): near = lax.ppermute(block_input, 'seq', ahead)]
  transfers between devices with their start and end apart: 43 -> 44, of which waited for: 18 -> 20; matrix products, arithmetic and copies ran while one was open for 18% -> 21% of each run, Pallas kernels for 34% -> 37%
where the time goes in v6:
time: 509 us; the launch traced here: 503 us
  Pallas kernels  187 us (37%)
  waiting for transfers between devices  133 us (26%)
  starting transfers between devices  51.8 us (10%)
  local copies, waits for them, and re-layouts  48.2 us (9%)
  other arithmetic  46.8 us (9%)
  matrix products  21 us (4%)
  between operations  15.2 us (3%)
    pallas_call x3, Pallas kernels, mlp(): pl.pallas_call(functools.partial(mlp_kernel, pieces, len(so_far) // 2), g...  61.5 us
    ppermute x14, waiting for transfers between devices, body(): lax.ppermute(v, 'seq', [(i, i ^ bit) for i in range(groups)])  55.1 us
    pallas_call x2, Pallas kernels, attend_back(): pl.pallas_call(attend_back_kernel, grid=(count,), in_specs=[pl.BlockSpec(...  47.2 us
    ppermute x17, waiting for transfers between devices, body(): lax.ppermute(v, 'dp', [(i, i ^ bit) for i in range(devices)])  33.2 us
    pallas_call x2, Pallas kernels, weight_call(): pl.pallas_call(kernel, grid_spec=pltpu.PrefetchScalarGridSpec(num_scalar_...  26 us
    pallas_call x1, Pallas kernels, attend(): pl.pallas_call(attend_kernel, grid=(pairs,), in_specs=[pl.BlockSpec((rows...  23 us
    pallas_call x1, Pallas kernels, project(): pl.pallas_call(qkv_kernel, grid=(3 * third,), in_specs=[whole((rows, mode...  21.6 us
    ppermute x14, starting transfers between devices, body(): lax.ppermute(v, 'seq', [(i, i ^ bit) for i in range(groups)])  19.1 us
  transfers between devices with their start and end apart: 44, of which 20 were waited for; matrix products, arithmetic and copies ran while one was open for 21% of the time, Pallas kernels for 37%

profile of v6, /device:TPU:0, one launch (start us, length us, event | category | flops | bytes accessed | tf_op | source)
XLA Modules:
  0.0 503.4 jit_solution(18305086123927497870)
XLA Ops:
  8.7 5.0 collective-permute-start
  13.7 2.9 reshape.140
  19.3 2.2 select_n.145
  21.4 2.1 slice.187.refs_4_
  31.2 7.7 %collective-permute-done.near_ref = f32[384,768]{1,0:T(8,128)S(1)} collective-permute-done((f32[384,768]{1,0:T(8,128)S(1)}, f32[384,768]{1,0:T(8,128)S(1)}, u32[]{:S(2)}, u32[]{:S(2)}) %collective-permute-start) | collective-permute-done | bytes 1179680 | tf_op jit(solution)/shard_map/ppermute | solution.py:710
  38.9 4.4 collective-permute-start.1
  50.9 7.2 %fusion.13 = (f32[]{:T(128)}, f32[]{:T(128)}, f32[]{:T(128)}, f32[]{:T(128)}, f32[384,768]{1,0:T(8,128)}) fusion(f32[384,768]{1,0:T(8,128)S(1)} %copy-done.12, f32[3,384,768]{2,1,0:T(8,128)} %param.18, f32[384,768]{1,0:T(8,128)} %param.17, f32[]{:T(128)} %bitcast.5, f32[]{:T(128)} %bitcast.3, f32[]{:T(128)} %bitcast.1, f32[]{:T(128)} %bitcast), kind=kLoop, calls=%fused_computation.31 | loop fusion | flops 4423676 | bytes 7077920 | tf_op jit(solution)/shard_map/reduce_sum | solution.py:726
  58.1 3.2 pad_maximum_fusion.2
  61.4 22.6 %collective-permute-done.3.refs_1_ = f32[192,1024]{1,0:T(8,128)} collective-permute-done((f32[192,1024]{1,0:T(8,128)}, f32[192,1024]{1,0:T(8,128)}, u32[]{:S(2)}, u32[]{:S(2)}) %collective-permute-start.3) | collective-permute-done | bytes 786464 | tf_op jit(solution)/shard_map/ppermute | solution.py:675
  87.1 3.4 collective-permute-start.9
  91.8 4.7 collective-permute-start.10
  96.5 2.4 constant_dynamic-slice_fusion
  100.1 21.6 %shard_map.239 = (f32[384,768]{1,0:T(8,128)}, f32[1152,1536]{1,0:T(8,128)}, bf16[1152,768]{1,0:T(8,128)(2,1)}, bf16[1152,768]{1,0:T(8,128)(2,1)}) custom-call(f32[384,768]{1,0:T(8,128)} %copy-done.5, f32[384,768]{1,0:T(8,128)} %copy-done.3, f32[384,768]{1,0:T(8,128)} %own_ref.1, f32[1,768]{1,0:T(1,128)} %broadcast_in_dim.50.gain_ref, ...), custom_call_target="tpu_custom_call" | custom-call | flops 2200000000 | bytes 1048576 | tf_op jit(solution)/shard_map/pallas_call | solution.py:144
  123.3 23.0 %shard_map.240.att_ref = f32[384,768]{1,0:T(8,128)} custom-call(f32[384,768]{1,0:T(8,128)} %get-tuple-element.129.q_ref, f32[1152,1536]{1,0:T(8,128)} %get-tuple-element.130.k_ref.v_ref, f32[1152,1536]{1,0:T(8,128)} %get-tuple-element.130.k_ref.v_ref, s32[384,128]{1,0:T(8,128)} %broadcast_in_dim.52.segq_ref, s32[8,1152]{1,0:T(8,128)} %broadcast_in_dim.54.segk_ref), custom_call_target="tpu_custom_call" | custom-call | flops 2200000000 | bytes 1048576 | tf_op jit(solution)/shard_map/pallas_call | solution.py:236
  146.4 3.7 convolution_add_fusion.resid_ref
  154.1 19.9 %shard_map.241 = (f32[768,768]{1,0:T(8,128)}, f32[768,768]{1,0:T(8,128)}, f32[4,1,384,512]{3,2,1,0:T(8,128)}) custom-call(s32[1]{0:T(128)} %bitcast.14.chip_ref, f32[384,768]{1,0:T(8,128)} %copy-done.15, f32[384,768]{1,0:T(8,128)} %copy-done.43, f32[384,768]{1,0:T(8,128)} %cot_ref.7, f32[384,768]{1,0:T(8,128)} %collective-permute-done.12.cot_other_ref, ...), custom_call_target="tpu_custom_call" | custom-call | flops 19800000512 | bytes 1048576 | tf_op jit(solution)/shard_map/pallas_call | solution.py:477
  174.0 21.1 %shard_map.242 = (f32[768,768]{1,0:T(8,128)}, f32[768,768]{1,0:T(8,128)}, f32[4,1,384,512]{3,2,1,0:T(8,128)}) custom-call(s32[1]{0:T(128)} %bitcast.14.chip_ref, f32[384,768]{1,0:T(8,128)} %copy-done.15, f32[384,768]{1,0:T(8,128)} %copy-done.43, f32[384,768]{1,0:T(8,128)} %cot_ref.7, f32[384,768]{1,0:T(8,128)} %collective-permute-done.12.cot_other_ref, ...), custom_call_target="tpu_custom_call" | custom-call | flops 19800000512 | bytes 1048576 | tf_op jit(solution)/shard_map/pallas_call | solution.py:477
  195.4 20.6 %shard_map.243 = (f32[768,768]{1,0:T(8,128)}, f32[768,768]{1,0:T(8,128)}, f32[4,1,384,512]{3,2,1,0:T(8,128)}) custom-call(s32[1]{0:T(128)} %bitcast.14.chip_ref, f32[384,768]{1,0:T(8,128)} %copy-done.15, f32[384,768]{1,0:T(8,128)} %copy-done.43, f32[384,768]{1,0:T(8,128)} %cot_ref.7, f32[384,768]{1,0:T(8,128)} %collective-permute-done.12.cot_other_ref, ...), custom_call_target="tpu_custom_call" | custom-call | flops 19800000512 | bytes 1048576 | tf_op jit(solution)/shard_map/pallas_call | solution.py:477
  217.8 2.4 collective-permute-done.13.given_ref
  223.4 7.7 %shard_map.244 = (f32[384,768]{1,0:T(8,128)}, f32[384,768]{1,0:T(8,128)}, f32[8,768]{1,0:T(8,128)}) custom-call(f32[768,768]{1,0:T(8,128)} %get-tuple-element.111.part_ref, f32[384,768]{1,0:T(8,128)} %copy-done.44, f32[384,768]{1,0:T(8,128)} %copy-done.15, f32[384,768]{1,0:T(8,128)} %cot_ref.7, f32[1,768]{1,0:T(1,128)} %broadcast_in_dim.55.gain_ref, ...), custom_call_target="tpu_custom_call" | custom-call | flops 6600000000 | bytes 1048576 | tf_op jit(solution)/shard_map/pallas_call | solution.py:537
  231.1 1.9 collective-permute-done.14
  234.8 2.4 collective-permute-start.15
  237.2 23.5 %shard_map.245 = (f32[384,768]{1,0:T(8,128)}, f32[1152,768]{1,0:T(8,128)}, f32[1152,768]{1,0:T(8,128)}) custom-call(f32[384,768]{1,0:T(8,128)} %get-tuple-element.129.q_ref, f32[1152,1536]{1,0:T(8,128)} %get-tuple-element.130.k_ref.v_ref, f32[1152,1536]{1,0:T(8,128)} %get-tuple-element.130.k_ref.v_ref, f32[384,768]{1,0:T(8,128)} %get-tuple-element.131.g_ref, ...), custom_call_target="tpu_custom_call" | custom-call | flops 23100000256 | bytes 1048576 | tf_op jit(solution)/shard_map/pallas_call | solution.py:328
  260.8 3.2 reduce-scatter.15.cloned.1.call-done
  267.3 23.7 %shard_map.246 = (f32[384,768]{1,0:T(8,128)}, f32[1152,768]{1,0:T(8,128)}, f32[1152,768]{1,0:T(8,128)}) custom-call(f32[384,768]{1,0:T(8,128)} %get-tuple-element.129.q_ref, f32[1152,1536]{1,0:T(8,128)} %get-tuple-element.130.k_ref.v_ref, f32[1152,1536]{1,0:T(8,128)} %get-tuple-element.130.k_ref.v_ref, ...), custom_call_target="tpu_custom_call", output_to_operand_aliasing={{0}: (8, {}), {1}: (9, {}), {2}: (10, {})} | custom-call | flops 23100000256 | bytes 1048576 | tf_op jit(solution)/shard_map/pallas_call | solution.py:328
  292.1 2.4 collective-permute-start.19
  294.5 12.6 %shard_map.247 = f32[2,4,96,1536]{3,2,1,0:T(8,128)} custom-call(s32[1]{0:T(128)} %bitcast.13.core_ref, bf16[1152,768]{1,0:T(8,128)(2,1)} %get-tuple-element.100.hi_ref, bf16[1152,768]{1,0:T(8,128)(2,1)} %get-tuple-element.101.lo_ref, f32[384,768]{1,0:T(8,128)} %get-tuple-element.142.dq_ref, f32[1152,768]{1,0:T(8,128)} %get-tuple-element.143.dk_ref), custom_call_target="tpu_custom_call" | custom-call | flops 9900000256 | bytes 1048576 | tf_op jit(solution)/shard_map/pallas_call | solution.py:616
  307.1 3.2 slice_bitcast_fusion
  312.5 2.1 slice_select_fusion.5
  315.1 13.4 %shard_map.248 = f32[2,4,96,1536]{3,2,1,0:T(8,128)} custom-call(s32[1]{0:T(128)} %bitcast.13.core_ref, bf16[1152,768]{1,0:T(8,128)(2,1)} %get-tuple-element.100.hi_ref, bf16[1152,768]{1,0:T(8,128)(2,1)} %get-tuple-element.101.lo_ref, f32[1152,768]{1,0:T(8,128)} %get-tuple-element.149.dv_ref, f32[384,768]{1,0:T(8,128)} %shard_map.240.att_ref, ...), custom_call_target="tpu_custom_call" | custom-call | flops 9900000256 | bytes 1048576 | tf_op jit(solution)/shard_map/pallas_call | solution.py:616
  329.4 1.8 slice_bitcast_fusion.2
  331.7 4.1 collective-permute-done.21
  336.2 2.4 pad_maximum_fusion
  345.8 1.9 collective-permute-start.23
  347.7 12.4 %fusion = f32[1152,768]{1,0:T(8,128)S(1)} fusion(f32[1152,768]{1,0:T(8,128)} %get-tuple-element.149.dv_ref, f32[1152,768]{1,0:T(8,128)} %get-tuple-element.143.dk_ref, f32[768,2304]{1,0:T(8,128)} %all-gather.5.cloned.1.call-done.w_ref), kind=kOutput, calls=%fused_computation | convolution fusion | flops 8155496448 | bytes 15335424 | tf_op jit(solution)/shard_map/dot_general | solution.py:640
  360.1 3.7 collective-permute-done.24
  370.2 3.0 collective-permute-start.25
  373.5 4.9 fusion.19
  379.0 18.0 %collective-permute-done.26 = f32[384,768]{1,0:T(8,128)S(1)} collective-permute-done((f32[384,768]{1,0:T(8,128)S(1)}, f32[384,768]{1,0:T(8,128)S(1)}, u32[]{:S(2)}, u32[]{:S(2)}) %collective-permute-start.26) | collective-permute-done | bytes 1179680 | tf_op jit(solution)/shard_map/ppermute | solution.py:834
  400.1 2.7 multiply_reduce_fusion.1
  412.9 2.1 broadcast_select_fusion.6
  416.0 13.5 %collective-permute-done.27 = f32[384,768]{1,0:T(8,128)} collective-permute-done((f32[384,768]{1,0:T(8,128)}, f32[384,768]{1,0:T(8,128)}, u32[]{:S(2)}, u32[]{:S(2)}) %collective-permute-start.27) | collective-permute-done | bytes 1179680 | tf_op jit(solution)/shard_map/ppermute | solution.py:856
  432.1 2.3 fusion.20
  435.9 8.9 %collective-permute-done.31 = f32[1,48,3072]{2,1,0:T(8,128)S(1)} collective-permute-done((f32[1,48,3072]{2,1,0:T(8,128)S(1)}, f32[1,48,3072]{2,1,0:T(8,128)S(1)}, u32[]{:S(2)}, u32[]{:S(2)}) %collective-permute-start.31) | collective-permute-done | bytes 589856 | tf_op jit(solution)/shard_map/ppermute | solution.py:764
  450.9 20.7 %collective-permute-done.32 = f32[1,48,3072]{2,1,0:T(8,128)} collective-permute-done((f32[1,48,3072]{2,1,0:T(8,128)S(1)}, f32[1,48,3072]{2,1,0:T(8,128)}, u32[]{:S(2)}, u32[]{:S(2)}) %collective-permute-start.32) | collective-permute-done | bytes 589856 | tf_op jit(solution)/shard_map/ppermute | solution.py:764
  472.8 2.0 collective-permute-start.34
  474.8 13.7 %collective-permute-done.34 = f32[8,768]{1,0:T(8,128)S(1)} collective-permute-done((f32[8,768]{1,0:T(8,128)S(1)}, f32[8,768]{1,0:T(8,128)S(1)}, u32[]{:S(2)}, u32[]{:S(2)}) %collective-permute-start.34) | collective-permute-done | bytes 24608 | tf_op jit(solution)/shard_map/ppermute | solution.py:764
  488.6 4.7 collective-permute-done.35
  (261 shorter events, 88.9 us)
Async XLA Ops:
  7.2 92.9 %all-gather.5.cloned.1.call-start = ((), (), s32[]{:S(2)}) async-start(), calls=%async_computation.4 | async-start | bytes 7962624 | tf_op jit(solution)/shard_map/all_gather | solution.py:678
  7.9 138.5 %all-gather.7.cloned.1.call-start = ((), (), s32[]{:S(2)}) async-start(), calls=%async_computation.5 | async-start | bytes 2654208 | tf_op jit(solution)/shard_map/all_gather | solution.py:678
  8.7 186.7 %all-gather.9.cloned.1.call-start = ((), (), s32[]{:S(2)}) async-start(), calls=%async_computation.6 | async-start | bytes 3932160 | tf_op jit(solution)/shard_map/all_gather | solution.py:705
  8.7 30.1 %collective-permute-start = (f32[384,768]{1,0:T(8,128)S(1)}, f32[384,768]{1,0:T(8,128)S(1)}, u32[]{:S(2)}, u32[]{:S(2)}) collective-permute-start(f32[384,768]{1,0:T(8,128)S(1)} %copy-done), channel_id=1, source_target_pairs={{0,1},{1,2},{2,3},{4,5},{5,6},{6,7},{8,9},{9,10},{10,11},{12,13},{... | collective-permute-start | bytes 3538952 | tf_op jit(solution)/shard_map/ppermute | solution.py:710
  21.4 21.9 %collective-permute-start.2 = (f32[96,1536]{1,0:T(8,128)}, f32[96,1536]{1,0:T(8,128)}, u32[]{:S(2)}, u32[]{:S(2)}) collective-permute-start(f32[96,1536]{1,0:T(8,128)} %select_n.145), channel_id=1, source_target_pairs={{0,4},{4,0},{8,12},{12,8},{16,20},{20,16},{24,28},{28,24},{1,5},{5... | collective-permute-start | bytes 1769480 | tf_op jit(solution)/shard_map/ppermute | solution.py:675
  23.6 37.8 %collective-permute-start.5 = (f32[256,768]{1,0:T(8,128)}, f32[256,768]{1,0:T(8,128)}, u32[]{:S(2)}, u32[]{:S(2)}) collective-permute-start(f32[256,768]{1,0:T(8,128)} %slice.187.refs_4_), channel_id=1, source_target_pairs={{0,8},{4,12},{8,0},{12,4},{16,24},{20,28},{24,16},{28,20},{1,9},{5... | collective-permute-start | bytes 2359304 | tf_op jit(solution)/shard_map/ppermute | solution.py:675
  25.1 36.2 %collective-permute-start.6 = (f32[256,768]{1,0:T(8,128)}, f32[256,768]{1,0:T(8,128)}, u32[]{:S(2)}, u32[]{:S(2)}) collective-permute-start(f32[256,768]{1,0:T(8,128)} %slice.187.refs_4_), channel_id=1, source_target_pairs={{0,16},{4,20},{8,24},{12,28},{16,0},{20,4},{24,8},{28,12},{1,17},{... | collective-permute-start | bytes 2359304 | tf_op jit(solution)/shard_map/ppermute | solution.py:675
  38.9 46.2 %collective-permute-start.1 = (f32[384,768]{1,0:T(8,128)S(1)}, f32[384,768]{1,0:T(8,128)S(1)}, u32[]{:S(2)}, u32[]{:S(2)}) collective-permute-start(f32[384,768]{1,0:T(8,128)S(1)} %collective-permute-done.near_ref), channel_id=1, source_target_pairs={{0,1},{1,2},{2,3},{4,5},{5,6},{6,7},{8,9},{9,10},{10,11},{12,13},{... | collective-permute-start | bytes 3538952 | tf_op jit(solution)/shard_map/ppermute | solution.py:712
  45.5 38.5 %collective-permute-start.3 = (f32[192,1024]{1,0:T(8,128)}, f32[192,1024]{1,0:T(8,128)}, u32[]{:S(2)}, u32[]{:S(2)}) collective-permute-start(f32[192,1024]{1,0:T(8,128)} %fusion.14.refs_0_), channel_id=1, source_target_pairs={{0,8},{4,12},{8,0},{12,4},{16,24},{20,28},{24,16},{28,20},{1,9},{5... | collective-permute-start | bytes 2359304 | tf_op jit(solution)/shard_map/ppermute | solution.py:675
  47.0 38.1 %collective-permute-start.4 = (f32[192,1024]{1,0:T(8,128)}, f32[192,1024]{1,0:T(8,128)}, u32[]{:S(2)}, u32[]{:S(2)}) collective-permute-start(f32[192,1024]{1,0:T(8,128)} %fusion.14.refs_0_), channel_id=1, source_target_pairs={{0,16},{4,20},{8,24},{12,28},{16,0},{20,4},{24,8},{28,12},{1,17},{... | collective-permute-start | bytes 2359304 | tf_op jit(solution)/shard_map/ppermute | solution.py:675
  50.4 169.8 %reduce-scatter.13.cloned.1.call-start = ((), (), s32[]{:S(2)}) async-start(), calls=%async_computation.7 | async-start | bytes 3932160
  50.9 36.2 %copy-start.42 = (s32[1,384]{1,0:T(1,128)S(1)}, s32[1,384]{1,0:T(1,128)}, u32[]{:S(2)}) copy-start(s32[1,384]{1,0:T(1,128)} %param.28) | copy-start | bytes 4612
  85.1 36.6 %collective-permute-start.7 = (f32[192,1024]{1,0:T(8,128)}, f32[192,1024]{1,0:T(8,128)S(1)}, u32[]{:S(2)}, u32[]{:S(2)}) collective-permute-start(f32[192,1024]{1,0:T(8,128)} %collective-permute-done.4.refs_2_), channel_id=1, source_target_pairs={{0,8},{4,12},{8,0},{12,4},{16,24},{20,28},{24,16},{28,20},{1,9},{5... | collective-permute-start | bytes 2359304 | tf_op jit(solution)/shard_map/ppermute | solution.py:675
  86.5 35.2 %collective-permute-start.8 = (f32[256,768]{1,0:T(8,128)}, f32[256,768]{1,0:T(8,128)}, u32[]{:S(2)}, u32[]{:S(2)}) collective-permute-start(f32[256,768]{1,0:T(8,128)} %collective-permute-done.5.refs_5_), channel_id=1, source_target_pairs={{0,16},{4,20},{8,24},{12,28},{16,0},{20,4},{24,8},{28,12},{1,17},{... | collective-permute-start | bytes 2359304 | tf_op jit(solution)/shard_map/ppermute | solution.py:675
  87.1 4.7 collective-permute-start.9
  90.5 61.7 %collective-permute-start.12 = (f32[384,768]{1,0:T(8,128)S(1)}, f32[384,768]{1,0:T(8,128)}, u32[]{:S(2)}, u32[]{:S(2)}) collective-permute-start(f32[384,768]{1,0:T(8,128)S(1)} %copy-done.12), channel_id=1, source_target_pairs={{0,4},{4,0},{8,12},{12,8},{16,20},{20,16},{24,28},{28,24},{1,5},{5... | collective-permute-start | bytes 3538952 | tf_op jit(solution)/shard_map/ppermute | solution.py:675
  91.8 8.3 %collective-permute-start.10 = (s32[1,384]{1,0:T(1,128)S(1)}, s32[1,384]{1,0:T(1,128)S(1)}, u32[]{:S(2)}, u32[]{:S(2)}) collective-permute-start(s32[1,384]{1,0:T(1,128)S(1)} %collective-permute-done.9), channel_id=1, source_target_pairs={{0,1},{1,2},{2,3},{4,5},{5,6},{6,7},{8,9},{9,10},{10,11},{12,13},{... | collective-permute-start | bytes 4616 | tf_op jit(solution)/shard_map/ppermute | solution.py:713
  150.1 2.9 collective-permute-start.11
  174.0 90.0 %reduce-scatter.15.cloned.1.call-start = ((), (), s32[]{:S(2)}) async-start(), calls=%async_computation.8 | async-start | bytes 3932160
  195.1 117.4 %reduce-scatter.17.cloned.1.call-start = ((), (), s32[]{:S(2)}) async-start(), calls=%async_computation.9 | async-start | bytes 3932160
  217.3 2.9 collective-permute-start.13
  217.5 211.9 %reduce-scatter.19.cloned.1.call-start = ((), (), s32[]{:S(2)}) async-start(), calls=%async_computation.10 | async-start | bytes 5898240
  221.8 11.2 %collective-permute-start.14 = (f32[1,192,512]{2,1,0:T(8,128)S(1)}, f32[1,192,512]{2,1,0:T(8,128)S(1)}, u32[]{:S(2)}, u32[]{:S(2)}) collective-permute-start(f32[1,192,512]{2,1,0:T(8,128)S(1)} %slice_select_fusion.7), channel_id=1, source_target_pairs={{0,1},{1,0},{2,3},{3,2},{4,5},{5,4},{6,7},{7,6},{8,9},{9,8},{10,11... | collective-permute-start | bytes 1179656 | tf_op jit(solution)/shard_map/ppermute | solution.py:764
  234.8 25.9 %collective-permute-start.15 = (f32[1,192,512]{2,1,0:T(8,128)S(1)}, f32[1,192,512]{2,1,0:T(8,128)S(1)}, u32[]{:S(2)}, u32[]{:S(2)}) collective-permute-start(f32[1,192,512]{2,1,0:T(8,128)S(1)} %select_add_fusion.3), channel_id=1, source_target_pairs={{0,2},{1,3},{2,0},{3,1},{4,6},{5,7},{6,4},{7,5},{8,10},{9,11},{10,... | collective-permute-start | bytes 1179656 | tf_op jit(solution)/shard_map/ppermute | solution.py:764
  265.2 25.8 %copy-start.17 = (f32[1,1,384,512]{3,2,1,0:T(8,128)S(1)}, f32[1,1,384,512]{3,2,1,0:T(8,128)}, u32[]{:S(2)}) copy-start(f32[1,1,384,512]{3,2,1,0:T(8,128)} %reduce-scatter.15.cloned.1.call-done) | copy-start | bytes 2359300
  265.2 25.8 %collective-permute-start.16 = (f32[1,192,512]{2,1,0:T(8,128)S(1)}, f32[1,192,512]{2,1,0:T(8,128)S(1)}, u32[]{:S(2)}, u32[]{:S(2)}) collective-permute-start(f32[1,192,512]{2,1,0:T(8,128)S(1)} %slice_select_fusion.6), channel_id=1, source_target_pairs={{0,1},{1,0},{2,3},{3,2},{4,5},{5,4},{6,7},{7,6},{8,9},{9,8},{10,11... | collective-permute-start | bytes 1179656 | tf_op jit(solution)/shard_map/ppermute | solution.py:764
  266.7 24.4 %collective-permute-start.17 = (f32[1,192,512]{2,1,0:T(8,128)S(1)}, f32[1,192,512]{2,1,0:T(8,128)S(1)}, u32[]{:S(2)}, u32[]{:S(2)}) collective-permute-start(f32[1,192,512]{2,1,0:T(8,128)S(1)} %add.188), channel_id=1, source_target_pairs={{0,1},{1,0},{2,3},{3,2},{4,5},{5,4},{6,7},{7,6},{8,9},{9,8},{10,11... | collective-permute-start | bytes 1179656 | tf_op jit(solution)/shard_map/ppermute | solution.py:764
  292.1 19.6 %collective-permute-start.19 = (f32[1,192,512]{2,1,0:T(8,128)S(1)}, f32[1,192,512]{2,1,0:T(8,128)S(1)}, u32[]{:S(2)}, u32[]{:S(2)}) collective-permute-start(f32[1,192,512]{2,1,0:T(8,128)S(1)} %select_add_fusion.2), channel_id=1, source_target_pairs={{0,2},{1,3},{2,0},{3,1},{4,6},{5,7},{6,4},{7,5},{8,10},{9,11},{10,... | collective-permute-start | bytes 1179656 | tf_op jit(solution)/shard_map/ppermute | solution.py:764
  310.3 21.0 %collective-permute-start.18 = (f32[4,96,1536]{2,1,0:T(8,128)}, f32[4,96,1536]{2,1,0:T(8,128)S(1)}, u32[]{:S(2)}, u32[]{:S(2)}) collective-permute-start(f32[4,96,1536]{2,1,0:T(8,128)} %slice_bitcast_fusion), channel_id=1, source_target_pairs={{0,4},{4,0},{8,12},{12,8},{16,20},{20,16},{24,28},{28,24},{1,5},{5... | collective-permute-start | bytes 7077896 | tf_op jit(solution)/shard_map/ppermute | solution.py:675
  314.6 13.9 %collective-permute-start.20 = (f32[1,192,512]{2,1,0:T(8,128)}, f32[1,192,512]{2,1,0:T(8,128)S(1)}, u32[]{:S(2)}, u32[]{:S(2)}) collective-permute-start(f32[1,192,512]{2,1,0:T(8,128)} %slice_select_fusion.5), channel_id=1, source_target_pairs={{0,1},{1,0},{2,3},{3,2},{4,5},{5,4},{6,7},{7,6},{8,9},{9,8},{10,11... | collective-permute-start | bytes 1179656 | tf_op jit(solution)/shard_map/ppermute | solution.py:764
  331.2 4.6 collective-permute-start.21
  341.2 32.3 %copy-start.34 = (f32[384]{0:T(512)}, f32[384]{0:T(512)S(1)}, u32[]{:S(2)}) copy-start(f32[384]{0:T(512)S(1)} %add_rsqrt_fusion) | copy-start | bytes 4612
  344.2 19.6 %collective-permute-start.24 = (f32[1,192,512]{2,1,0:T(8,128)S(1)}, f32[1,192,512]{2,1,0:T(8,128)S(1)}, u32[]{:S(2)}, u32[]{:S(2)}) collective-permute-start(f32[1,192,512]{2,1,0:T(8,128)S(1)} %copy-done.28), channel_id=1, source_target_pairs={{0,1},{1,0},{2,3},{3,2},{4,5},{5,4},{6,7},{7,6},{8,9},{9,8},{10,11... | collective-permute-start | bytes 1179656 | tf_op jit(solution)/shard_map/ppermute | solution.py:764
  345.8 19.0 %collective-permute-start.23 = (f32[1,192,512]{2,1,0:T(8,128)S(1)}, f32[1,192,512]{2,1,0:T(8,128)S(1)}, u32[]{:S(2)}, u32[]{:S(2)}) collective-permute-start(f32[1,192,512]{2,1,0:T(8,128)S(1)} %copy-done.29), channel_id=1, source_target_pairs={{0,2},{1,3},{2,0},{3,1},{4,6},{5,7},{6,4},{7,5},{8,10},{9,11},{10,... | collective-permute-start | bytes 1179656 | tf_op jit(solution)/shard_map/ppermute | solution.py:764
  360.1 36.9 %copy-start.8 = (f32[1152,768]{1,0:T(8,128)}, f32[1152,768]{1,0:T(8,128)S(1)}, u32[]{:S(2)}) copy-start(f32[1152,768]{1,0:T(8,128)S(1)} %fusion) | copy-start | bytes 10616836
  365.7 31.3 %collective-permute-start.26 = (f32[384,768]{1,0:T(8,128)S(1)}, f32[384,768]{1,0:T(8,128)S(1)}, u32[]{:S(2)}, u32[]{:S(2)}) collective-permute-start(f32[384,768]{1,0:T(8,128)S(1)} %slice.237), channel_id=1, source_target_pairs={{1,0},{2,1},{3,2},{5,4},{6,5},{7,6},{9,8},{10,9},{11,10},{13,12},{... | collective-permute-start | bytes 3538952 | tf_op jit(solution)/shard_map/ppermute | solution.py:834
  370.2 42.7 %collective-permute-start.25 = (f32[1,192,512]{2,1,0:T(8,128)}, f32[1,192,512]{2,1,0:T(8,128)}, u32[]{:S(2)}, u32[]{:S(2)}) collective-permute-start(f32[1,192,512]{2,1,0:T(8,128)} %add.197), channel_id=1, source_target_pairs={{0,1},{1,0},{2,3},{3,2},{4,5},{5,4},{6,7},{7,6},{8,9},{9,8},{10,11... | collective-permute-start | bytes 1179656 | tf_op jit(solution)/shard_map/ppermute | solution.py:764
  373.4 26.7 %collective-permute-start.22 = (f32[384,768]{1,0:T(8,128)S(1)}, f32[384,768]{1,0:T(8,128)S(1)}, u32[]{:S(2)}, u32[]{:S(2)}) collective-permute-start(f32[384,768]{1,0:T(8,128)S(1)} %slice.206), channel_id=1, source_target_pairs={{0,4},{4,0},{8,12},{12,8},{16,20},{20,16},{24,28},{28,24},{1,5},{5... | collective-permute-start | bytes 3538952 | tf_op jit(solution)/shard_map/ppermute | solution.py:675
  398.2 31.2 %collective-permute-start.27 = (f32[384,768]{1,0:T(8,128)}, f32[384,768]{1,0:T(8,128)}, u32[]{:S(2)}, u32[]{:S(2)}) collective-permute-start(f32[384,768]{1,0:T(8,128)} %slice_add_fusion), channel_id=1, source_target_pairs={{1,0},{2,1},{3,2},{5,4},{6,5},{7,6},{9,8},{10,9},{11,10},{13,12},{... | collective-permute-start | bytes 3538952 | tf_op jit(solution)/shard_map/ppermute | solution.py:856
  405.5 1.4 collective-permute-start.28
  407.7 3.8 collective-permute-start.29
  411.5 3.8 collective-permute-start.30
  430.8 14.0 %collective-permute-start.31 = (f32[1,48,3072]{2,1,0:T(8,128)S(1)}, f32[1,48,3072]{2,1,0:T(8,128)S(1)}, u32[]{:S(2)}, u32[]{:S(2)}) collective-permute-start(f32[1,48,3072]{2,1,0:T(8,128)S(1)} %slice_select_fusion.4), channel_id=1, source_target_pairs={{0,1},{1,0},{2,3},{3,2},{4,5},{5,4},{6,7},{7,6},{8,9},{9,8},{10,11... | collective-permute-start | bytes 1769480 | tf_op jit(solution)/shard_map/ppermute | solution.py:764
  431.0 16.5 %collective-permute-start.33 = (f32[3,96,512]{2,1,0:T(8,128)S(1)}, f32[3,96,512]{2,1,0:T(8,128)S(1)}, u32[]{:S(2)}, u32[]{:S(2)}) collective-permute-start(f32[3,96,512]{2,1,0:T(8,128)S(1)} %slice_select_fusion.2), channel_id=1, source_target_pairs={{0,4},{4,0},{8,12},{12,8},{16,20},{20,16},{24,28},{28,24},{1,5},{5... | collective-permute-start | bytes 1769480 | tf_op jit(solution)/shard_map/ppermute | solution.py:675
  444.9 26.7 %collective-permute-start.32 = (f32[1,48,3072]{2,1,0:T(8,128)S(1)}, f32[1,48,3072]{2,1,0:T(8,128)}, u32[]{:S(2)}, u32[]{:S(2)}) collective-permute-start(f32[1,48,3072]{2,1,0:T(8,128)S(1)} %select_add_fusion), channel_id=1, source_target_pairs={{0,2},{1,3},{2,0},{3,1},{4,6},{5,7},{6,4},{7,5},{8,10},{9,11},{10,... | collective-permute-start | bytes 1769480 | tf_op jit(solution)/shard_map/ppermute | solution.py:764
  472.7 21.7 %collective-permute-start.36 = (f32[1,48,3072]{2,1,0:T(8,128)S(1)}, f32[1,48,3072]{2,1,0:T(8,128)S(1)}, u32[]{:S(2)}, u32[]{:S(2)}) collective-permute-start(f32[1,48,3072]{2,1,0:T(8,128)S(1)} %add.213), channel_id=1, source_target_pairs={{0,1},{1,0},{2,3},{3,2},{4,5},{5,4},{6,7},{7,6},{8,9},{9,8},{10,11... | collective-permute-start | bytes 1769480 | tf_op jit(solution)/shard_map/ppermute | solution.py:764
  472.8 15.7 %collective-permute-start.34 = (f32[8,768]{1,0:T(8,128)S(1)}, f32[8,768]{1,0:T(8,128)S(1)}, u32[]{:S(2)}, u32[]{:S(2)}) collective-permute-start(f32[8,768]{1,0:T(8,128)S(1)} %copy-done.33), channel_id=1, source_target_pairs={{0,1},{1,0},{2,3},{3,2},{4,5},{5,4},{6,7},{7,6},{8,9},{9,8},{10,11... | collective-permute-start | bytes 73736 | tf_op jit(solution)/shard_map/ppermute | solution.py:764
  488.6 4.7 collective-permute-start.35
  (44 other events, 298.9 us)
Sparse Core Ops, SparseCore 0:
  9.9 77.6 all-gather.4
  89.4 32.1 all-gather.6
  124.1 43.9 all-gather.8
  174.1 43.0 reduce-scatter.12
  220.0 43.9 reduce-scatter.14
  266.9 43.9 reduce-scatter.16
  338.8 57.1 reduce-scatter.18

commit v7 on v5

--- a/solution.py
+++ b/solution.py
@@ -161,7 +161,7 @@
             jax.ShapeDtypeStruct((total, model), BF16),
             jax.ShapeDtypeStruct((total, model), BF16),
         ],
-        cost_estimate=cost(20),
+        cost_estimate=cost(0.5),
         compiler_params=params(),
     )(far, near, own, gain, bias, w_full, cosine, sine)
 
@@ -246,7 +246,7 @@
         out_specs=pl.BlockSpec((rows, 128), lambda p: (0, p)),
         out_shape=jax.ShapeDtypeStruct((rows, model), F32),
         scratch_shapes=[pltpu.VMEM((rows, total - rows + BLK), F32)],
-        cost_estimate=cost(24),
+        cost_estimate=cost(0.5),
         compiler_params=params(),
     )(q_rot, kv, kv, seg_q, seg_k)
 
@@ -355,8 +355,7 @@
 
 def mlp_kernel(count, begun, chip_ref, resid_ref, other_ref, cot_ref, cot_other_ref, gain_ref, bias_ref,
                scale_ref, *refs):
-    up_refs, down_refs = refs[:count], refs[count:2 * count]
-    refs = refs[2 * count:]
+    weight_refs, refs = refs[:max(1, 2 * count)], refs[max(1, 2 * count):]
     so_far, refs = refs[:2 * begun], refs[2 * begun:]
     out_ref, gnorm_ref, grad_ref = refs[:3]
     (x_hi, x_lo, xt_hi, xt_lo, g_hi, g_lo, up_hi, up_lo, down_hi, down_lo) = refs[3:]
@@ -378,21 +377,29 @@
             out_ref[...] = jnp.zeros_like(out_ref)
             gnorm_ref[...] = jnp.zeros_like(gnorm_ref)
 
-    for at in range(count):
-        spot = (chip_ref[0] ^ at) if count > 1 else 0
-        up_rows = up_refs[at].shape[0]
-        high, low = split(up_refs[at][...])
-        here = pl.ds(pl.multiple_of(spot * up_rows, up_rows), up_rows)
-        up_hi[here], up_lo[here] = high, low
-        block = down_refs[at][...]
-        block = block.reshape(-1, block.shape[-1])
-        high, low = split(block)
-        here = pl.ds(pl.multiple_of(spot * block.shape[0], block.shape[0]), block.shape[0])
-        down_hi[here], down_lo[here] = high, low
-
     chips, _, tall, width = grad_ref.shape
     up_tall = up_hi.shape[0] // chips
     deep = down_hi.shape[0] // chips
+    half = deep // 2
+
+    def place(spot, values, targets, folded):
+        for part, target in zip(split(values), targets):
+            if folded:
+                here = pl.ds(pl.multiple_of(spot * deep, deep), deep)
+                target[here, :width] = part[:deep]
+                target[here, width:] = jnp.concatenate(
+                    [part[deep:, :width // 2], part[deep:, width // 2:]], axis=0
+                )
+            else:
+                target[pl.ds(pl.multiple_of(spot * up_tall, up_tall), up_tall)] = part
+
+    for at in range(count):
+        place(chip_ref[0] ^ at, weight_refs[at][...], (up_hi, up_lo), False)
+        place(chip_ref[0] ^ at, weight_refs[count + at][...], (down_hi, down_lo), True)
+    if count == 0:
+        for at in range(chips):
+            place(at, weight_refs[0][at, :up_tall], (up_hi, up_lo), False)
+            place(at, weight_refs[0][at, up_tall:], (down_hi, down_lo), True)
     up = (up_hi[...], up_lo[...])
     down = (down_hi[...], down_lo[...])
     normed = (x_hi[...], x_lo[...])
@@ -412,7 +419,6 @@
     gnorm_ref[...] += three(dot_nt, grad_pre, up)
     gup = three(dot_nn, normed_t, grad_pre)
     gdown = three(dot_tn, act2, grad_block)
-    half = deep // 2
     for chip in range(chips):
         grad_ref[chip, 0, :up_tall] = gup[chip * up_tall:(chip + 1) * up_tall]
         part = gdown[chip * deep:(chip + 1) * deep]
@@ -422,25 +428,27 @@
         )
 
 
-def mlp(first, steps, so_far, chip, chips, resid, other, cot, cot_other, gain, bias, scale, ups, downs):
+def mlp(so_far, weights, chip, chips, resid, other, cot, cot_other, gain, bias, scale):
     rows, model = resid.shape
     width = 512
     up_tall = model // chips
     deep = width // chips
     fixed = lambda shape: pl.BlockSpec(shape, lambda j, c: (0, 0))
-    if len(ups) > 1:
-        down_spec = pl.BlockSpec((deep, model), lambda j, c: (first + j, 0))
+    if len(weights) > 1:
+        specs = [
+            pl.BlockSpec((up_tall, width), lambda j, c, at=at: (at, 0)) for _, at in weights
+        ]
+        weights = [value for value, _ in weights]
     else:
-        downs = [downs[0].reshape(chips, -1, model)]
-        down_spec = pl.BlockSpec((chips, deep, model), lambda j, c: (0, first + j, 0))
+        specs = [pl.BlockSpec(weights[0].shape, lambda j, c: (0, 0, 0))]
+    count = len(weights) // 2
     tall = up_tall + deep + deep // 2
     grid_spec = pltpu.PrefetchScalarGridSpec(
         num_scalar_prefetch=1,
-        grid=(steps,),
+        grid=(1,),
         in_specs=[fixed((rows, model))] * 4 + [fixed((1, model))] * 2
         + [pl.BlockSpec(memory_space=pltpu.SMEM)]
-        + [pl.BlockSpec((up.shape[0], width), lambda j, c: (0, first + j)) for up in ups]
-        + [down_spec] * len(downs)
+        + specs
         + [fixed((2 * rows, model))] * len(so_far),
         out_specs=[
             fixed((2 * rows, model)), fixed((2 * rows, model)),
@@ -455,16 +463,28 @@
         ],
     )
     return pl.pallas_call(
-        functools.partial(mlp_kernel, len(ups), len(so_far) // 2),
+        functools.partial(mlp_kernel, count, len(so_far) // 2),
         grid_spec=grid_spec,
         out_shape=[
             jax.ShapeDtypeStruct((2 * rows, model), F32),
             jax.ShapeDtypeStruct((2 * rows, model), F32),
-            jax.ShapeDtypeStruct((chips, steps, tall, width), F32),
-        ],
-        cost_estimate=cost(18 * steps),
+            jax.ShapeDtypeStruct((chips, 1, tall, width), F32),
+        ],
+        cost_estimate=cost(18),
         compiler_params=params(),
-    )(chip, resid, other, cot, cot_other, gain, bias, scale, *ups, *downs, *so_far)
+    )(chip, resid, other, cot, cot_other, gain, bias, scale, *weights, *so_far)
+
+
+def fold_rows(values, width):
+    rows = values.shape[0]
+    right = values[:, width:]
+    return jnp.concatenate(
+        [
+            values[:, :width],
+            jnp.concatenate([right[:rows // 2], right[rows // 2:]], axis=1),
+        ],
+        axis=0,
+    )
 
 
 def unpack_grads(up, down, sibling_swap, core, chips):
@@ -655,23 +675,44 @@
     up_chip = jnp.concatenate(
         [jnp.where(core == 0, mine, given), jnp.where(core == 0, given, mine)], axis=0
     )
-    if chips == 4:
-        up_x, down_x = exchange(up_chip, 2), exchange(w_down, 2)
-        up_y, down_y = exchange(up_chip, 4), exchange(w_down, 4)
-        ups = [up_chip, up_x, up_y, exchange(up_y, 2)]
-        downs = [w_down, down_x, down_y, exchange(down_x, 4)]
-    else:
-        ups, downs = (
-            [lax.all_gather(v, "dp", axis=0, tiled=True, axis_index_groups=same_core)]
-            for v in (up_chip, w_down)
-        )
-
-    seg_own = segments + 1
-    near = lax.ppermute(block_input, "seq", ahead)
-    seg_near = lax.ppermute(seg_own, "seq", ahead)
+    width = up_chip.shape[1] // 3
+    together = lax.optimization_barrier
+    thirds = [
+        (up_chip[:, i * width:(i + 1) * width], fold_rows(w_down[i * third:(i + 1) * third], width))
+        for i in range(3)
+    ]
+    first_own = jnp.concatenate(thirds[0], axis=0)
+    rest_own = jnp.concatenate([thirds[1][0], thirds[2][0], thirds[1][1], thirds[2][1]], axis=0)
+
+    def sides_of(own):
+        return [exchange(own, 2), exchange(own, 4)] if chips == 4 else []
+
+    def diagonal_of(sides):
+        if chips != 4:
+            return []
+        middle = sides[0].shape[0] // 2
+        return [exchange(sides[1][:middle], 2), exchange(sides[0][middle:], 4)]
+
+    def pieces(own, sides, diagonal, at):
+        if chips != 4:
+            own = own.reshape(2, -1, up_chip.shape[0], width)[:, at].reshape(-1, width)
+            return [
+                lax.all_gather(own, "dp", axis=0, axis_index_groups=same_core)
+            ]
+        below = own.shape[0] // up_chip.shape[0] // 2
+        ups = [(own, at), (sides[0], at), (sides[1], at), (diagonal[0], at)]
+        downs = [(value, below + at) for value in (own, *sides)] + [(diagonal[1], at)]
+        return ups + downs
+
+    first_sides = sides_of(first_own)
+    first_diagonal = diagonal_of(first_sides)
+
+    numbers = jnp.pad((segments + 1).astype(F32), ((0, 7), (0, model - rows)))
+    near = lax.ppermute(jnp.concatenate([block_input, numbers], axis=0), "seq", ahead)
     far = lax.ppermute(near, "seq", ahead)
-    seg_far = lax.ppermute(seg_near, "seq", ahead)
-    seg_all = jnp.concatenate([seg_far, seg_near, seg_own], axis=1)
+    seg_all = jnp.concatenate(
+        [far[rows:rows + 1, :rows], near[rows:rows + 1, :rows], numbers[:1, :rows]], axis=1
+    ).astype(jnp.int32)
     seg_k_row = jnp.broadcast_to(seg_all, (8, halo + rows))
     seg_k_col = jnp.broadcast_to(seg_all.reshape(-1, 1), (halo + rows, 128))
     seg_q_row = seg_k_row[:, halo:]
@@ -684,21 +725,27 @@
     earlier = (embedding, earlier_outs[0], earlier_outs[1], earlier_outs[2])
     base = sum(dwa_weights[i] * value for i, value in enumerate(earlier))
     dots = jnp.stack([jnp.sum(cotangent * value) for value in earlier])
-    far, base, dots = lax.optimization_barrier((far, base, dots))
+    qkv_full, rest_own, far, base, dots, first_sides, first_diagonal = together(
+        (qkv_full, rest_own, far, base, dots, first_sides, first_diagonal)
+    )
+    rest_sides = sides_of(rest_own)
 
     q_rot, kv, normed_hi, normed_lo = project(
         far, near, block_input, gain1, bias1, qkv_full, cosine, sine
     )
     attended = attend(q_rot, kv, seg_q_col, seg_k_row)
+    attended, rest_sides = together((attended, rest_sides))
+    rest_diagonal = diagonal_of(rest_sides)
 
     out_full = gather(w_out)
     resid = block_input + matmul(attended, out_full)
     resid_other = swap(resid)
+    resid_other, rest_diagonal = together((resid_other, rest_diagonal))
     cot_other = swap(cotangent)
     scale = dwa_weights[4].reshape(1, 1)
     call = functools.partial(
         mlp, chip=chip, chips=chips, resid=resid, other=resid_other, cot=cotangent,
-        cot_other=cot_other, gain=gain2, bias=bias2, scale=scale, ups=ups, downs=downs,
+        cot_other=cot_other, gain=gain2, bias=bias2, scale=scale,
     )
     scatter = lambda v: lax.psum_scatter(v, "dp", scatter_dimension=0, tiled=True)
     scatter_chips = lambda v: lax.psum_scatter(
@@ -706,7 +753,11 @@
     )
     so_far, shards = (), []
     for third_at in range(3):
-        out_part, gnorm_part, grads = call(third_at, 1, so_far)
+        if third_at == 0:
+            weights = pieces(first_own, first_sides, first_diagonal, 0)
+        else:
+            weights = pieces(rest_own, rest_sides, rest_diagonal, third_at - 1)
+        out_part, gnorm_part, grads = call(so_far, weights)
         so_far = (out_part, gnorm_part)
         shards.append(scatter_chips(grads)[0])
     given = swap(gnorm_part[rows:])
@@ -731,7 +782,6 @@
         other = shift(kept, 1)
         return jnp.where(even, kept, other), jnp.where(even, other, kept)
 
-    together = lax.optimization_barrier
     shards[0], given = together((shards[0], given))
     line_a = line_start(shards[0])
     grad_resid, grad_attended, sums_two = resid_back(
@@ -770,25 +820,25 @@
     grads_c, out_part = together((grads_c, out_part))
     shard_c = scatter_chips(grads_c)[0]
     out_sib = swap(out_part[rows:])
-    ends_b, dk, dv = together((ends_b, dk, dv))
-    dkv = jnp.concatenate([dk, dv], axis=1)
 
     block_out = resid + out_part[:rows] + out_sib
     output = base + dwa_weights[4] * block_out
     dwa_local = jnp.concatenate([dots, jnp.sum(cotangent * block_out)[None]])
 
-    wq, wkv = qkv_full[:, :model], qkv_full[:, model:]
-    partial = outer_cols(dkv, wkv)
-    line_c, partial = together((line_c, partial))
+    wq, wk, wv = (qkv_full[:, i * model:(i + 1) * model] for i in range(3))
+    part_far = outer_cols(dk[:rows], wk) + outer_cols(dv[:rows], wv)
+    dk_rest, dv_rest, far, near, part_far = together((dk[rows:], dv[rows:], far, near, part_far))
+    given_near = lax.ppermute(part_far, "seq", behind)
+    part_rest = outer_cols(dk_rest, wk) + outer_cols(dv_rest, wv)
+    own_part = part_rest[rows:] + outer_cols(dq, wq)
+    line_c, ends_b, part_rest, own_part = together((line_c, ends_b, part_rest, own_part))
     ends_c = line_end(line_c)
-    own_part = partial[halo:] + outer_cols(dq, wq)
-    (sent,) = together((partial,))
-    back_near = sent[rows:halo] + lax.ppermute(sent[:rows], "seq", behind)
+    back_near = part_rest[:rows] + given_near
 
     xhat1, rate1 = norm_stats(block_input)
     terms = (
-        (norm_stats(far)[0], partial[:rows]),
-        (norm_stats(near)[0], partial[rows:halo]),
+        (norm_stats(far[:rows])[0], part_far),
+        (norm_stats(near[:rows])[0], part_rest[:rows]),
         (xhat1, own_part),
     )
     grad_gain_one = sum(jnp.sum(xhat * part, axis=0) for xhat, part in terms)

time: 501 us -> 531 us (1.060)
  waiting for transfers between devices: 140 us -> 156 us
  local copies, waits for them, and re-layouts: 36 us -> 51.1 us
  Pallas kernels: 188 us -> 196 us
    ppermute x4 -> x2, waiting for transfers between devices: 48 us -> 20.2 us  [the longest x1 20.2 us: body(): lax.ppermute(jnp.concatenate([block_input, numbers], axis=0), 'seq', ahead)]
    ppermute x17 -> x19, waiting for transfers between devices: 14.2 us -> 36.7 us  [body(): lax.ppermute(v, 'dp', [(i, i ^ bit) for i in range(devices)])]
    ppermute x14, waiting for transfers between devices: 74.3 us -> 85.9 us  [body(): lax.ppermute(v, 'seq', [(i, i ^ bit) for i in range(groups)])]
    pallas_call x3, Pallas kernels: 62 us -> 71.5 us  [mlp(): pl.pallas_call(functools.partial(mlp_kernel, count, len(so_far) // 2), gr...]
    ppermute x4 -> x2, starting transfers between devices: 15.3 us -> 6.12 us  [the longest x1 4.58 us: body(): lax.ppermute(jnp.concatenate([block_input, numbers], axis=0), 'seq', ahead)]
    slice x1 -> x10, local copies, waits for them, and re-layouts: 1.09 us -> 9.05 us  [the longest x4 3.3 us: diagonal_of(): return [exchange(sides[1][:middle], 2), exchange(sides[0][middle:], 4)]]
    dot_general x2 -> x5, matrix products: 17.6 us -> 15.1 us  [outer_cols(): lax.dot_general(left, right, (((1,), (1,)), ((), ())), precision=HIGH)]
    ppermute x17 -> x19, starting transfers between devices: 11.9 us -> 13.9 us  [body(): lax.ppermute(v, 'dp', [(i, i ^ bit) for i in range(devices)])]
  transfers between devices with their start and end apart: 43 -> 43, of which waited for: 18 -> 21; matrix products, arithmetic and copies ran while one was open for 18% -> 19% of each run, Pallas kernels for 34% -> 32%
where the time goes in v7:
time: 531 us; the launch traced here: 526 us
  Pallas kernels  196 us (37%)
  waiting for transfers between devices  156 us (29%)
  local copies, waits for them, and re-layouts  51.1 us (10%)
  starting transfers between devices  44.5 us (8%)
  other arithmetic  43.9 us (8%)
  matrix products  18.9 us (4%)
  between operations  15.8 us (3%)
    ppermute x14, waiting for transfers between devices, body(): lax.ppermute(v, 'seq', [(i, i ^ bit) for i in range(groups)])  85.9 us
    pallas_call x3, Pallas kernels, mlp(): pl.pallas_call(functools.partial(mlp_kernel, count, len(so_far) // 2), gr...  71.5 us
    pallas_call x2, Pallas kernels, attend_back(): pl.pallas_call(attend_back_kernel, grid=(count,), in_specs=[pl.BlockSpec(...  46.7 us
    ppermute x19, waiting for transfers between devices, body(): lax.ppermute(v, 'dp', [(i, i ^ bit) for i in range(devices)])  36.7 us
    pallas_call x2, Pallas kernels, weight_call(): pl.pallas_call(kernel, grid_spec=pltpu.PrefetchScalarGridSpec(num_scalar_...  26.1 us
    pallas_call x1, Pallas kernels, attend(): pl.pallas_call(attend_kernel, grid=(pairs,), in_specs=[pl.BlockSpec((rows...  23.2 us
    pallas_call x1, Pallas kernels, project(): pl.pallas_call(qkv_kernel, grid=(3 * third,), in_specs=[whole((rows, mode...  21.6 us
    ppermute x1, waiting for transfers between devices, body(): lax.ppermute(jnp.concatenate([block_input, numbers], axis=0), 'seq', ahead)  20.2 us
  transfers between devices with their start and end apart: 43, of which 21 were waited for; matrix products, arithmetic and copies ran while one was open for 19% of the time, Pallas kernels for 32%

profile of v7, /device:TPU:0, one launch (start us, length us, event | category | flops | bytes accessed | tf_op | source)
XLA Modules:
  0.0 526.3 jit_solution(1695245647393079831)
XLA Ops:
  13.1 4.6 collective-permute-start.1
  24.1 20.2 %collective-permute-done.1.near_ref = f32[392,768]{1,0:T(8,128)S(1)} collective-permute-done((f32[392,768]{1,0:T(8,128)}, f32[392,768]{1,0:T(8,128)S(1)}, u32[]{:S(2)}, u32[]{:S(2)}) %collective-permute-start.1) | collective-permute-done | bytes 1204256 | tf_op jit(solution)/shard_map/ppermute | solution.py:711
  44.3 4.6 collective-permute-start.2
  52.8 4.8 fusion.22
  57.6 3.3 pad_maximum_fusion.6
  60.9 9.1 %collective-permute-done.5.refs_3_ = f32[192,512]{1,0:T(8,128)S(1)} collective-permute-done((f32[192,512]{1,0:T(8,128)S(1)}, f32[192,512]{1,0:T(8,128)S(1)}, u32[]{:S(2)}, u32[]{:S(2)}) %collective-permute-start.5) | collective-permute-done | bytes 393248 | tf_op jit(solution)/shard_map/ppermute | solution.py:663
  71.5 2.7 collective-permute-done.2.far_ref
  74.2 5.2 all-gather.3.cloned.1.call-done.w_ref
  82.6 2.3 constant_dynamic-slice_fusion
  85.6 21.6 %shard_map.239 = (f32[384,768]{1,0:T(8,128)}, f32[1152,1536]{1,0:T(8,128)}, bf16[1152,768]{1,0:T(8,128)(2,1)}, bf16[1152,768]{1,0:T(8,128)(2,1)}) custom-call(f32[392,768]{1,0:T(8,128)} %copy-done.3, f32[392,768]{1,0:T(8,128)} %copy-done.5, f32[384,768]{1,0:T(8,128)} %own_ref.1, f32[1,768]{1,0:T(1,128)} %broadcast_in_dim.48.gain_ref, ...), custom_call_target="tpu_custom_call" | custom-call | flops 550000000 | bytes 1048576 | tf_op jit(solution)/shard_map/pallas_call | solution.py:144
  108.6 23.2 %shard_map.240.att_ref = f32[384,768]{1,0:T(8,128)} custom-call(f32[384,768]{1,0:T(8,128)} %get-tuple-element.145.q_ref, f32[1152,1536]{1,0:T(8,128)} %get-tuple-element.146.k_ref.v_ref, f32[1152,1536]{1,0:T(8,128)} %get-tuple-element.146.k_ref.v_ref, s32[384,128]{1,0:T(8,128)} %broadcast_in_dim.50.segq_ref, s32[8,1152]{1,0:T(8,128)} %broadcast_in_dim.51.segk_ref), custom_call_target="tpu_custom_call" | custom-call | flops 550000000 | bytes 1048576 | tf_op jit(solution)/shard_map/pallas_call | solution.py:236
  131.9 3.8 convolution_add_fusion.resid_ref
  142.7 14.5 %collective-permute-done.10.refs_3_ = f32[384,512]{1,0:T(8,128)} collective-permute-done((f32[384,512]{1,0:T(8,128)S(1)}, f32[384,512]{1,0:T(8,128)}, u32[]{:S(2)}, u32[]{:S(2)}) %collective-permute-start.10) | collective-permute-done | bytes 786464 | tf_op jit(solution)/shard_map/ppermute | solution.py:663
  157.2 3.1 collective-permute-done.11.refs_7_
  160.3 29.4 %shard_map.241 = (f32[768,768]{1,0:T(8,128)}, f32[768,768]{1,0:T(8,128)}, f32[4,1,384,512]{3,2,1,0:T(8,128)}) custom-call(s32[1]{0:T(128)} %bitcast.17.chip_ref, f32[384,768]{1,0:T(8,128)} %copy-done.13, f32[384,768]{1,0:T(8,128)} %collective-permute-done.9.other_ref, f32[384,768]{1,0:T(8,128)} %cot_ref.7, f32[384,768]{1,0:T(8,128)} %collective-permute-done.12.cot_other_ref, ...), custom_call_target="tpu_custom_call" | custom-call | flops 19800000512 | bytes 1048576 | tf_op jit(solution)/shard_map/pallas_call | solution.py:465
  189.8 21.0 %shard_map.242 = (f32[768,768]{1,0:T(8,128)}, f32[768,768]{1,0:T(8,128)}, f32[4,1,384,512]{3,2,1,0:T(8,128)}) custom-call(s32[1]{0:T(128)} %bitcast.17.chip_ref, f32[384,768]{1,0:T(8,128)} %copy-done.13, f32[384,768]{1,0:T(8,128)} %collective-permute-done.9.other_ref, f32[384,768]{1,0:T(8,128)} %cot_ref.7, f32[384,768]{1,0:T(8,128)} %collective-permute-done.12.cot_other_ref, ...), custom_call_target="tpu_custom_call" | custom-call | flops 19800000512 | bytes 1048576 | tf_op jit(solution)/shard_map/pallas_call | solution.py:465
  211.1 21.1 %shard_map.243 = (f32[768,768]{1,0:T(8,128)}, f32[768,768]{1,0:T(8,128)}, f32[4,1,384,512]{3,2,1,0:T(8,128)}) custom-call(s32[1]{0:T(128)} %bitcast.17.chip_ref, f32[384,768]{1,0:T(8,128)} %copy-done.13, f32[384,768]{1,0:T(8,128)} %collective-permute-done.9.other_ref, f32[384,768]{1,0:T(8,128)} %cot_ref.7, f32[384,768]{1,0:T(8,128)} %collective-permute-done.12.cot_other_ref, ...), custom_call_target="tpu_custom_call" | custom-call | flops 19800000512 | bytes 1048576 | tf_op jit(solution)/shard_map/pallas_call | solution.py:465
  234.2 2.3 collective-permute-done.13.given_ref
  239.6 7.2 %shard_map.244 = (f32[384,768]{1,0:T(8,128)}, f32[384,768]{1,0:T(8,128)}, f32[8,768]{1,0:T(8,128)}) custom-call(f32[768,768]{1,0:T(8,128)} %get-tuple-element.127.part_ref, f32[384,768]{1,0:T(8,128)} %copy-done.47, f32[384,768]{1,0:T(8,128)} %copy-done.13, f32[384,768]{1,0:T(8,128)} %cot_ref.7, f32[1,768]{1,0:T(1,128)} %broadcast_in_dim.52.gain_ref, ...), custom_call_target="tpu_custom_call" | custom-call | flops 6600000000 | bytes 1048576 | tf_op jit(solution)/shard_map/pallas_call | solution.py:525
  246.8 2.5 collective-permute-done.14
  251.0 2.4 collective-permute-start.15
  253.4 23.3 %shard_map.245 = (f32[384,768]{1,0:T(8,128)}, f32[1152,768]{1,0:T(8,128)}, f32[1152,768]{1,0:T(8,128)}) custom-call(f32[384,768]{1,0:T(8,128)} %get-tuple-element.145.q_ref, f32[1152,1536]{1,0:T(8,128)} %get-tuple-element.146.k_ref.v_ref, f32[1152,1536]{1,0:T(8,128)} %get-tuple-element.146.k_ref.v_ref, f32[384,768]{1,0:T(8,128)} %get-tuple-element.147.g_ref, ...), custom_call_target="tpu_custom_call" | custom-call | flops 23100000256 | bytes 1048576 | tf_op jit(solution)/shard_map/pallas_call | solution.py:328
  276.8 4.2 reduce-scatter.15.cloned.1.call-done
  284.2 23.4 %shard_map.246 = (f32[384,768]{1,0:T(8,128)}, f32[1152,768]{1,0:T(8,128)}, f32[1152,768]{1,0:T(8,128)}) custom-call(f32[384,768]{1,0:T(8,128)} %get-tuple-element.145.q_ref, f32[1152,1536]{1,0:T(8,128)} %get-tuple-element.146.k_ref.v_ref, f32[1152,1536]{1,0:T(8,128)} %get-tuple-element.146.k_ref.v_ref, ...), custom_call_target="tpu_custom_call", output_to_operand_aliasing={{0}: (8, {}), {1}: (9, {}), {2}: (10, {})} | custom-call | flops 23100000256 | bytes 1048576 | tf_op jit(solution)/shard_map/pallas_call | solution.py:328
  308.8 2.4 collective-permute-start.19
  311.1 12.6 %shard_map.247 = f32[2,4,96,1536]{3,2,1,0:T(8,128)} custom-call(s32[1]{0:T(128)} %bitcast.16.core_ref, bf16[1152,768]{1,0:T(8,128)(2,1)} %get-tuple-element.111.hi_ref, bf16[1152,768]{1,0:T(8,128)(2,1)} %get-tuple-element.112.lo_ref, f32[384,768]{1,0:T(8,128)} %get-tuple-element.158.dq_ref, f32[1152,768]{1,0:T(8,128)} %get-tuple-element.159.dk_ref), custom_call_target="tpu_custom_call" | custom-call | flops 9900000256 | bytes 1048576 | tf_op jit(solution)/shard_map/pallas_call | solution.py:604
  323.8 3.3 slice_bitcast_fusion
  329.2 2.1 slice_select_fusion.5
  331.8 13.5 %shard_map.248 = f32[2,4,96,1536]{3,2,1,0:T(8,128)} custom-call(s32[1]{0:T(128)} %bitcast.16.core_ref, bf16[1152,768]{1,0:T(8,128)(2,1)} %get-tuple-element.111.hi_ref, bf16[1152,768]{1,0:T(8,128)(2,1)} %get-tuple-element.112.lo_ref, f32[1152,768]{1,0:T(8,128)} %get-tuple-element.165.dv_ref, f32[384,768]{1,0:T(8,128)} %shard_map.240.att_ref, ...), custom_call_target="tpu_custom_call" | custom-call | flops 9900000256 | bytes 1048576 | tf_op jit(solution)/shard_map/pallas_call | solution.py:604
  348.5 4.1 collective-permute-done.21
  353.0 2.5 pad_maximum_fusion
  360.6 2.2 slice.291
  364.1 3.7 fusion.5
  367.8 3.3 fusion.14
  373.3 3.1 fusion.3
  376.4 3.2 fusion.11
  382.5 3.2 collective-permute-start.23
  387.2 31.6 %collective-permute-done.23 = f32[1,192,512]{2,1,0:T(8,128)S(1)} collective-permute-done((f32[1,192,512]{2,1,0:T(8,128)S(1)}, f32[1,192,512]{2,1,0:T(8,128)S(1)}, u32[]{:S(2)}, u32[]{:S(2)}) %collective-permute-start.23) | collective-permute-done | bytes 393248 | tf_op jit(solution)/shard_map/ppermute | solution.py:765
  422.5 2.5 multiply_reduce_fusion.1
  435.4 2.1 broadcast_select_fusion.6
  440.0 2.1 collective-permute-start.30
  444.1 12.2 %collective-permute-done.30 = f32[1,48,3072]{2,1,0:T(8,128)S(1)} collective-permute-done((f32[1,48,3072]{2,1,0:T(8,128)S(1)}, f32[1,48,3072]{2,1,0:T(8,128)S(1)}, u32[]{:S(2)}, u32[]{:S(2)}) %collective-permute-start.30) | collective-permute-done | bytes 589856 | tf_op jit(solution)/shard_map/ppermute | solution.py:765
  459.6 2.1 stack.30
  463.1 2.1 stack.29
  468.3 2.6 reshape.239
  470.9 27.0 %collective-permute-done.31 = f32[1,48,3072]{2,1,0:T(8,128)} collective-permute-done((f32[1,48,3072]{2,1,0:T(8,128)}, f32[1,48,3072]{2,1,0:T(8,128)}, u32[]{:S(2)}, u32[]{:S(2)}) %collective-permute-start.31) | collective-permute-done | bytes 589856 | tf_op jit(solution)/shard_map/ppermute | solution.py:765
  503.2 2.1 collective-permute-done.34
  506.8 9.0 %collective-permute-done.35 = f32[8,768]{1,0:T(8,128)S(1)} collective-permute-done((f32[8,768]{1,0:T(8,128)S(1)}, f32[8,768]{1,0:T(8,128)S(1)}, u32[]{:S(2)}, u32[]{:S(2)}) %collective-permute-start.35) | collective-permute-done | bytes 24608 | tf_op jit(solution)/shard_map/ppermute | solution.py:765
  (290 shorter events, 96.3 us)
Async XLA Ops:
  7.2 72.2 %all-gather.3.cloned.1.call-start = ((), (), s32[]{:S(2)}) async-start(), calls=%async_computation.4 | async-start | bytes 7962624 | tf_op jit(solution)/shard_map/all_gather | solution.py:666
  7.9 124.0 %all-gather.5.cloned.1.call-start = ((), (), s32[]{:S(2)}) async-start(), calls=%async_computation.5 | async-start | bytes 2654208 | tf_op jit(solution)/shard_map/all_gather | solution.py:666
  11.5 7.8 %collective-permute-start = (f32[96,1536]{1,0:T(8,128)}, f32[96,1536]{1,0:T(8,128)S(1)}, u32[]{:S(2)}, u32[]{:S(2)}) collective-permute-start(f32[96,1536]{1,0:T(8,128)} %select_n.145), channel_id=1, source_target_pairs={{0,4},{4,0},{8,12},{12,8},{16,20},{20,16},{24,28},{28,24},{1,5},{5... | collective-permute-start | bytes 1769480 | tf_op jit(solution)/shard_map/ppermute | solution.py:663
  13.1 31.2 %collective-permute-start.1 = (f32[392,768]{1,0:T(8,128)}, f32[392,768]{1,0:T(8,128)S(1)}, u32[]{:S(2)}, u32[]{:S(2)}) collective-permute-start(f32[392,768]{1,0:T(8,128)} %select_maximum_fusion), channel_id=1, source_target_pairs={{0,1},{1,2},{2,3},{4,5},{5,6},{6,7},{8,9},{9,10},{10,11},{12,13},{... | collective-permute-start | bytes 3612680 | tf_op jit(solution)/shard_map/ppermute | solution.py:711
  17.7 218.7 %reduce-scatter.13.cloned.1.call-start = ((), (), s32[]{:S(2)}) async-start(), calls=%async_computation.6 | async-start | bytes 3932160
  19.4 33.3 %copy-start.28 = (f32[384,768]{1,0:T(8,128)S(1)}, f32[384,768]{1,0:T(8,128)}, u32[]{:S(2)}) copy-start(f32[384,768]{1,0:T(8,128)} %param.17) | copy-start | bytes 3538948
  20.9 31.8 %copy-start.15 = (f32[3,384,768]{2,1,0:T(8,128)S(1)}, f32[3,384,768]{2,1,0:T(8,128)}, u32[]{:S(2)}) copy-start(f32[3,384,768]{2,1,0:T(8,128)} %param.18) | copy-start | bytes 10616836
  21.1 31.7 %copy-start.9 = (f32[384,768]{1,0:T(8,128)S(1)}, f32[384,768]{1,0:T(8,128)}, u32[]{:S(2)}) copy-start(f32[384,768]{1,0:T(8,128)} %cot_ref.7) | copy-start | bytes 3538948
  21.1 28.7 %collective-permute-start.4 = (f32[384,512]{1,0:T(8,128)S(1)}, f32[384,512]{1,0:T(8,128)S(1)}, u32[]{:S(2)}, u32[]{:S(2)}) collective-permute-start(f32[384,512]{1,0:T(8,128)S(1)} %fusion.26.refs_0_.refs_4_), channel_id=1, source_target_pairs={{0,16},{4,20},{8,24},{12,28},{16,0},{20,4},{24,8},{28,12},{1,17},{... | collective-permute-start | bytes 2359304 | tf_op jit(solution)/shard_map/ppermute | solution.py:663
  22.6 28.8 %collective-permute-start.3 = (f32[384,512]{1,0:T(8,128)S(1)}, f32[384,512]{1,0:T(8,128)S(1)}, u32[]{:S(2)}, u32[]{:S(2)}) collective-permute-start(f32[384,512]{1,0:T(8,128)S(1)} %fusion.26.refs_0_.refs_4_), channel_id=1, source_target_pairs={{0,8},{4,12},{8,0},{12,4},{16,24},{20,28},{24,16},{28,20},{1,9},{5... | collective-permute-start | bytes 2359304 | tf_op jit(solution)/shard_map/ppermute | solution.py:663
  44.3 40.6 %copy-start.5 = (f32[392,768]{1,0:T(8,128)}, f32[392,768]{1,0:T(8,128)S(1)}, u32[]{:S(2)}) copy-start(f32[392,768]{1,0:T(8,128)S(1)} %collective-permute-done.1.near_ref) | copy-start | bytes 3612676
  44.3 29.9 %collective-permute-start.2 = (f32[392,768]{1,0:T(8,128)S(1)}, f32[392,768]{1,0:T(8,128)S(1)}, u32[]{:S(2)}, u32[]{:S(2)}) collective-permute-start(f32[392,768]{1,0:T(8,128)S(1)} %collective-permute-done.1.near_ref), channel_id=1, source_target_pairs={{0,1},{1,2},{2,3},{4,5},{5,6},{6,7},{8,9},{9,10},{10,11},{12,13},{... | collective-permute-start | bytes 3612680 | tf_op jit(solution)/shard_map/ppermute | solution.py:712
  49.8 20.1 %collective-permute-start.5 = (f32[192,512]{1,0:T(8,128)S(1)}, f32[192,512]{1,0:T(8,128)S(1)}, u32[]{:S(2)}, u32[]{:S(2)}) collective-permute-start(f32[192,512]{1,0:T(8,128)S(1)} %slice.322), channel_id=1, source_target_pairs={{0,8},{4,12},{8,0},{12,4},{16,24},{20,28},{24,16},{28,20},{1,9},{5... | collective-permute-start | bytes 1179656 | tf_op jit(solution)/shard_map/ppermute | solution.py:663
  51.4 20.0 %collective-permute-start.6 = (f32[192,512]{1,0:T(8,128)S(1)}, f32[192,512]{1,0:T(8,128)S(1)}, u32[]{:S(2)}, u32[]{:S(2)}) collective-permute-start(f32[192,512]{1,0:T(8,128)S(1)} %slice.323), channel_id=1, source_target_pairs={{0,16},{4,20},{8,24},{12,28},{16,0},{20,4},{24,8},{28,12},{1,17},{... | collective-permute-start | bytes 1179656 | tf_op jit(solution)/shard_map/ppermute | solution.py:663
  79.4 52.5 %collective-permute-start.7 = (f32[768,512]{1,0:T(8,128)}, f32[768,512]{1,0:T(8,128)}, u32[]{:S(2)}, u32[]{:S(2)}) collective-permute-start(f32[768,512]{1,0:T(8,128)} %copy-done.34), channel_id=1, source_target_pairs={{0,8},{4,12},{8,0},{12,4},{16,24},{20,28},{24,16},{28,20},{1,9},{5... | collective-permute-start | bytes 4718600 | tf_op jit(solution)/shard_map/ppermute | solution.py:663
  80.8 51.0 %collective-permute-start.8 = (f32[768,512]{1,0:T(8,128)}, f32[768,512]{1,0:T(8,128)}, u32[]{:S(2)}, u32[]{:S(2)}) collective-permute-start(f32[768,512]{1,0:T(8,128)} %copy-done.34), channel_id=1, source_target_pairs={{0,16},{4,20},{8,24},{12,28},{16,0},{20,4},{24,8},{28,12},{1,17},{... | collective-permute-start | bytes 4718600 | tf_op jit(solution)/shard_map/ppermute | solution.py:663
  135.7 24.6 %collective-permute-start.9 = (f32[384,768]{1,0:T(8,128)S(1)}, f32[384,768]{1,0:T(8,128)}, u32[]{:S(2)}, u32[]{:S(2)}) collective-permute-start(f32[384,768]{1,0:T(8,128)S(1)} %convolution_add_fusion.resid_ref), channel_id=1, source_target_pairs={{0,4},{4,0},{8,12},{12,8},{16,20},{20,16},{24,28},{28,24},{1,5},{5... | collective-permute-start | bytes 3538952 | tf_op jit(solution)/shard_map/ppermute | solution.py:663
  135.8 24.5 %collective-permute-start.12 = (f32[384,768]{1,0:T(8,128)S(1)}, f32[384,768]{1,0:T(8,128)}, u32[]{:S(2)}, u32[]{:S(2)}) collective-permute-start(f32[384,768]{1,0:T(8,128)S(1)} %copy-done.10), channel_id=1, source_target_pairs={{0,4},{4,0},{8,12},{12,8},{16,20},{20,16},{24,28},{28,24},{1,5},{5... | collective-permute-start | bytes 3538952 | tf_op jit(solution)/shard_map/ppermute | solution.py:663
  137.5 19.7 %collective-permute-start.10 = (f32[384,512]{1,0:T(8,128)S(1)}, f32[384,512]{1,0:T(8,128)}, u32[]{:S(2)}, u32[]{:S(2)}) collective-permute-start(f32[384,512]{1,0:T(8,128)S(1)} %slice.273), channel_id=1, source_target_pairs={{0,8},{4,12},{8,0},{12,4},{16,24},{20,28},{24,16},{28,20},{1,9},{5... | collective-permute-start | bytes 2359304 | tf_op jit(solution)/shard_map/ppermute | solution.py:663
  140.7 19.6 %collective-permute-start.11 = (f32[384,512]{1,0:T(8,128)}, f32[384,512]{1,0:T(8,128)}, u32[]{:S(2)}, u32[]{:S(2)}) collective-permute-start(f32[384,512]{1,0:T(8,128)} %slice.274), channel_id=1, source_target_pairs={{0,16},{4,20},{8,24},{12,28},{16,0},{20,4},{24,8},{28,12},{1,17},{... | collective-permute-start | bytes 2359304 | tf_op jit(solution)/shard_map/ppermute | solution.py:663
  189.7 91.2 %reduce-scatter.15.cloned.1.call-start = ((), (), s32[]{:S(2)}) async-start(), calls=%async_computation.7 | async-start | bytes 3932160
  210.8 118.4 %reduce-scatter.17.cloned.1.call-start = ((), (), s32[]{:S(2)}) async-start(), calls=%async_computation.8 | async-start | bytes 3932160
  233.6 2.9 collective-permute-start.13
  234.1 204.4 %reduce-scatter.19.cloned.1.call-start = ((), (), s32[]{:S(2)}) async-start(), calls=%async_computation.9 | async-start | bytes 5898240
  238.1 11.2 %collective-permute-start.14 = (f32[1,192,512]{2,1,0:T(8,128)S(1)}, f32[1,192,512]{2,1,0:T(8,128)S(1)}, u32[]{:S(2)}, u32[]{:S(2)}) collective-permute-start(f32[1,192,512]{2,1,0:T(8,128)S(1)} %slice_select_fusion.7), channel_id=1, source_target_pairs={{0,1},{1,0},{2,3},{3,2},{4,5},{5,4},{6,7},{7,6},{8,9},{9,8},{10,11... | collective-permute-start | bytes 1179656 | tf_op jit(solution)/shard_map/ppermute | solution.py:765
  251.0 25.7 %collective-permute-start.15 = (f32[1,192,512]{2,1,0:T(8,128)S(1)}, f32[1,192,512]{2,1,0:T(8,128)S(1)}, u32[]{:S(2)}, u32[]{:S(2)}) collective-permute-start(f32[1,192,512]{2,1,0:T(8,128)S(1)} %select_add_fusion.3), channel_id=1, source_target_pairs={{0,2},{1,3},{2,0},{3,1},{4,6},{5,7},{6,4},{7,5},{8,10},{9,11},{10,... | collective-permute-start | bytes 1179656 | tf_op jit(solution)/shard_map/ppermute | solution.py:765
  282.1 25.5 %collective-permute-start.16 = (f32[1,192,512]{2,1,0:T(8,128)S(1)}, f32[1,192,512]{2,1,0:T(8,128)S(1)}, u32[]{:S(2)}, u32[]{:S(2)}) collective-permute-start(f32[1,192,512]{2,1,0:T(8,128)S(1)} %slice_select_fusion.6), channel_id=1, source_target_pairs={{0,1},{1,0},{2,3},{3,2},{4,5},{5,4},{6,7},{7,6},{8,9},{9,8},{10,11... | collective-permute-start | bytes 1179656 | tf_op jit(solution)/shard_map/ppermute | solution.py:765
  283.7 24.1 %collective-permute-start.17 = (f32[1,192,512]{2,1,0:T(8,128)S(1)}, f32[1,192,512]{2,1,0:T(8,128)S(1)}, u32[]{:S(2)}, u32[]{:S(2)}) collective-permute-start(f32[1,192,512]{2,1,0:T(8,128)S(1)} %add.196), channel_id=1, source_target_pairs={{0,1},{1,0},{2,3},{3,2},{4,5},{5,4},{6,7},{7,6},{8,9},{9,8},{10,11... | collective-permute-start | bytes 1179656 | tf_op jit(solution)/shard_map/ppermute | solution.py:765
  308.8 19.6 %collective-permute-start.19 = (f32[1,192,512]{2,1,0:T(8,128)S(1)}, f32[1,192,512]{2,1,0:T(8,128)S(1)}, u32[]{:S(2)}, u32[]{:S(2)}) collective-permute-start(f32[1,192,512]{2,1,0:T(8,128)S(1)} %select_add_fusion.2), channel_id=1, source_target_pairs={{0,2},{1,3},{2,0},{3,1},{4,6},{5,7},{6,4},{7,5},{8,10},{9,11},{10,... | collective-permute-start | bytes 1179656 | tf_op jit(solution)/shard_map/ppermute | solution.py:765
  327.0 21.0 %collective-permute-start.18 = (f32[4,96,1536]{2,1,0:T(8,128)}, f32[4,96,1536]{2,1,0:T(8,128)S(1)}, u32[]{:S(2)}, u32[]{:S(2)}) collective-permute-start(f32[4,96,1536]{2,1,0:T(8,128)} %slice_bitcast_fusion), channel_id=1, source_target_pairs={{0,4},{4,0},{8,12},{12,8},{16,20},{20,16},{24,28},{28,24},{1,5},{5... | collective-permute-start | bytes 7077896 | tf_op jit(solution)/shard_map/ppermute | solution.py:663
  331.3 14.0 %collective-permute-start.20 = (f32[1,192,512]{2,1,0:T(8,128)}, f32[1,192,512]{2,1,0:T(8,128)S(1)}, u32[]{:S(2)}, u32[]{:S(2)}) collective-permute-start(f32[1,192,512]{2,1,0:T(8,128)} %slice_select_fusion.5), channel_id=1, source_target_pairs={{0,1},{1,0},{2,3},{3,2},{4,5},{5,4},{6,7},{7,6},{8,9},{9,8},{10,11... | collective-permute-start | bytes 1179656 | tf_op jit(solution)/shard_map/ppermute | solution.py:765
  348.0 4.6 collective-permute-start.21
  357.1 62.5 %copy-start.36 = (f32[384]{0:T(512)}, f32[384]{0:T(512)S(1)}, u32[]{:S(2)}) copy-start(f32[384]{0:T(512)S(1)} %add_rsqrt_fusion.2) | copy-start | bytes 4612
  362.7 23.5 %collective-permute-start.24 = (f32[1,192,512]{2,1,0:T(8,128)S(1)}, f32[1,192,512]{2,1,0:T(8,128)S(1)}, u32[]{:S(2)}, u32[]{:S(2)}) collective-permute-start(f32[1,192,512]{2,1,0:T(8,128)S(1)} %copy-done.25), channel_id=1, source_target_pairs={{0,1},{1,0},{2,3},{3,2},{4,5},{5,4},{6,7},{7,6},{8,9},{9,8},{10,11... | collective-permute-start | bytes 1179656 | tf_op jit(solution)/shard_map/ppermute | solution.py:765
  371.1 48.8 %collective-permute-start.26 = (f32[384,768]{1,0:T(8,128)S(1)}, f32[384,768]{1,0:T(8,128)S(1)}, u32[]{:S(2)}, u32[]{:S(2)}) collective-permute-start(f32[384,768]{1,0:T(8,128)S(1)} %fusion.14), channel_id=1, source_target_pairs={{1,0},{2,1},{3,2},{5,4},{6,5},{7,6},{9,8},{10,9},{11,10},{13,12},{... | collective-permute-start | bytes 3538952 | tf_op jit(solution)/shard_map/ppermute | solution.py:831
  382.5 36.3 %collective-permute-start.23 = (f32[1,192,512]{2,1,0:T(8,128)S(1)}, f32[1,192,512]{2,1,0:T(8,128)S(1)}, u32[]{:S(2)}, u32[]{:S(2)}) collective-permute-start(f32[1,192,512]{2,1,0:T(8,128)S(1)} %copy-done.26), channel_id=1, source_target_pairs={{0,2},{1,3},{2,0},{3,1},{4,6},{5,7},{6,4},{7,5},{8,10},{9,11},{10,... | collective-permute-start | bytes 1179656 | tf_op jit(solution)/shard_map/ppermute | solution.py:765
  386.1 36.3 %collective-permute-start.22 = (f32[384,768]{1,0:T(8,128)S(1)}, f32[384,768]{1,0:T(8,128)S(1)}, u32[]{:S(2)}, u32[]{:S(2)}) collective-permute-start(f32[384,768]{1,0:T(8,128)S(1)} %slice.289), channel_id=1, source_target_pairs={{0,4},{4,0},{8,12},{12,8},{16,20},{20,16},{24,28},{28,24},{1,5},{5... | collective-permute-start | bytes 3538952 | tf_op jit(solution)/shard_map/ppermute | solution.py:663
  419.6 15.8 %collective-permute-start.25 = (f32[1,192,512]{2,1,0:T(8,128)}, f32[1,192,512]{2,1,0:T(8,128)}, u32[]{:S(2)}, u32[]{:S(2)}) collective-permute-start(f32[1,192,512]{2,1,0:T(8,128)} %add.206), channel_id=1, source_target_pairs={{0,1},{1,0},{2,3},{3,2},{4,5},{5,4},{6,7},{7,6},{8,9},{9,8},{10,11... | collective-permute-start | bytes 1179656 | tf_op jit(solution)/shard_map/ppermute | solution.py:765
  427.7 1.8 collective-permute-start.27
  430.2 3.8 collective-permute-start.28
  434.1 3.8 collective-permute-start.29
  440.0 16.3 %collective-permute-start.30 = (f32[1,48,3072]{2,1,0:T(8,128)S(1)}, f32[1,48,3072]{2,1,0:T(8,128)S(1)}, u32[]{:S(2)}, u32[]{:S(2)}) collective-permute-start(f32[1,48,3072]{2,1,0:T(8,128)S(1)} %slice_select_fusion.4), channel_id=1, source_target_pairs={{0,1},{1,0},{2,3},{3,2},{4,5},{5,4},{6,7},{7,6},{8,9},{9,8},{10,11... | collective-permute-start | bytes 1769480 | tf_op jit(solution)/shard_map/ppermute | solution.py:765
  442.3 16.1 %collective-permute-start.32 = (f32[3,96,512]{2,1,0:T(8,128)S(1)}, f32[3,96,512]{2,1,0:T(8,128)S(1)}, u32[]{:S(2)}, u32[]{:S(2)}) collective-permute-start(f32[3,96,512]{2,1,0:T(8,128)S(1)} %slice_select_fusion.2), channel_id=1, source_target_pairs={{0,4},{4,0},{8,12},{12,8},{16,20},{20,16},{24,28},{28,24},{1,5},{5... | collective-permute-start | bytes 1769480 | tf_op jit(solution)/shard_map/ppermute | solution.py:663
  442.4 56.9 %collective-permute-start.33 = (f32[384,768]{1,0:T(8,128)}, f32[384,768]{1,0:T(8,128)}, u32[]{:S(2)}, u32[]{:S(2)}) collective-permute-start(f32[384,768]{1,0:T(8,128)} %get-tuple-element.191), channel_id=1, source_target_pairs={{1,0},{2,1},{3,2},{5,4},{6,5},{7,6},{9,8},{10,9},{11,10},{13,12},{... | collective-permute-start | bytes 3538952 | tf_op jit(solution)/shard_map/ppermute | solution.py:860
  457.2 40.7 %collective-permute-start.31 = (f32[1,48,3072]{2,1,0:T(8,128)}, f32[1,48,3072]{2,1,0:T(8,128)}, u32[]{:S(2)}, u32[]{:S(2)}) collective-permute-start(f32[1,48,3072]{2,1,0:T(8,128)} %select_add_fusion), channel_id=1, source_target_pairs={{0,2},{1,3},{2,0},{3,1},{4,6},{5,7},{6,4},{7,5},{8,10},{9,11},{10,... | collective-permute-start | bytes 1769480 | tf_op jit(solution)/shard_map/ppermute | solution.py:765
  501.1 4.2 collective-permute-start.34
  501.2 15.8 %collective-permute-start.36 = (f32[1,48,3072]{2,1,0:T(8,128)S(1)}, f32[1,48,3072]{2,1,0:T(8,128)S(1)}, u32[]{:S(2)}, u32[]{:S(2)}) collective-permute-start(f32[1,48,3072]{2,1,0:T(8,128)S(1)} %add.223), channel_id=1, source_target_pairs={{0,1},{1,0},{2,3},{3,2},{4,5},{5,4},{6,7},{7,6},{8,9},{9,8},{10,11... | collective-permute-start | bytes 1769480 | tf_op jit(solution)/shard_map/ppermute | solution.py:765
  505.4 10.4 %collective-permute-start.35 = (f32[8,768]{1,0:T(8,128)S(1)}, f32[8,768]{1,0:T(8,128)S(1)}, u32[]{:S(2)}, u32[]{:S(2)}) collective-permute-start(f32[8,768]{1,0:T(8,128)S(1)} %add.226), channel_id=1, source_target_pairs={{0,2},{1,3},{2,0},{3,1},{4,6},{5,7},{6,4},{7,5},{8,10},{9,11},{10,... | collective-permute-start | bytes 73736 | tf_op jit(solution)/shard_map/ppermute | solution.py:765
  (49 other events, 447.6 us)
Sparse Core Ops, SparseCore 0:
  9.9 69.4 all-gather.2
  81.3 38.7 all-gather.4
  189.8 44.2 reduce-scatter.12
  237.0 43.9 reduce-scatter.14
  283.8 43.9 reduce-scatter.16
  355.6 57.1 reduce-scatter.18

commit v8 on v5

--- a/solution.py
+++ b/solution.py
@@ -161,7 +161,7 @@
             jax.ShapeDtypeStruct((total, model), BF16),
             jax.ShapeDtypeStruct((total, model), BF16),
         ],
-        cost_estimate=cost(20),
+        cost_estimate=cost(0.3),
         compiler_params=params(),
     )(far, near, own, gain, bias, w_full, cosine, sine)
 
@@ -246,7 +246,7 @@
         out_specs=pl.BlockSpec((rows, 128), lambda p: (0, p)),
         out_shape=jax.ShapeDtypeStruct((rows, model), F32),
         scratch_shapes=[pltpu.VMEM((rows, total - rows + BLK), F32)],
-        cost_estimate=cost(24),
+        cost_estimate=cost(0.3),
         compiler_params=params(),
     )(q_rot, kv, kv, seg_q, seg_k)
 
@@ -348,7 +348,7 @@
         ],
         scratch_shapes=[pltpu.VMEM((total - rows + BLK, rows), F32)],
         input_output_aliases={8 + i: i for i in range(len(before))},
-        cost_estimate=cost(7 * count),
+        cost_estimate=cost(0.3),
         compiler_params=params(),
     )(q_rot, kv, kv, grad, seg_q, seg_k, cosine, sine, *before)
 
@@ -357,9 +357,9 @@
                scale_ref, *refs):
     up_refs, down_refs = refs[:count], refs[count:2 * count]
     refs = refs[2 * count:]
-    so_far, refs = refs[:2 * begun], refs[2 * begun:]
-    out_ref, gnorm_ref, grad_ref = refs[:3]
-    (x_hi, x_lo, xt_hi, xt_lo, g_hi, g_lo, up_hi, up_lo, down_hi, down_lo) = refs[3:]
+    so_far, refs = refs[:4 * begun], refs[4 * begun:]
+    sums, grad_refs = refs[:4], refs[4:-10]
+    (x_hi, x_lo, xt_hi, xt_lo, g_hi, g_lo, up_hi, up_lo, down_hi, down_lo) = refs[-10:]
     step = pl.program_id(0)
     rows = resid_ref.shape[0]
 
@@ -371,12 +371,8 @@
             x_hi[at:at + rows], x_lo[at:at + rows] = split(normed)
             xt_hi[:, at:at + rows], xt_lo[:, at:at + rows] = split(normed.T)
             g_hi[at:at + rows], g_lo[at:at + rows] = split(cot[...] * scale_ref[0, 0])
-        if begun:
-            out_ref[...] = so_far[0][...]
-            gnorm_ref[...] = so_far[1][...]
-        else:
-            out_ref[...] = jnp.zeros_like(out_ref)
-            gnorm_ref[...] = jnp.zeros_like(gnorm_ref)
+        for at, ref in enumerate(sums):
+            ref[...] = so_far[at][...] if begun else jnp.zeros_like(ref)
 
     for at in range(count):
         spot = (chip_ref[0] ^ at) if count > 1 else 0
@@ -390,7 +386,7 @@
         here = pl.ds(pl.multiple_of(spot * block.shape[0], block.shape[0]), block.shape[0])
         down_hi[here], down_lo[here] = high, low
 
-    chips, _, tall, width = grad_ref.shape
+    chips, tall, width = grad_refs[0].shape
     up_tall = up_hi.shape[0] // chips
     deep = down_hi.shape[0] // chips
     up = (up_hi[...], up_lo[...])
@@ -408,18 +404,24 @@
     )
     act2 = split(act)
     grad_pre = split(grad_act * slope)
-    out_ref[...] += three(dot_nn, act2, down)
-    gnorm_ref[...] += three(dot_nt, grad_pre, up)
+    for at, total in enumerate((three(dot_nn, act2, down), three(dot_nt, grad_pre, up))):
+        sums[2 * at][...] += total[:rows]
+        sums[2 * at + 1][...] += total[rows:]
     gup = three(dot_nn, normed_t, grad_pre)
     gdown = three(dot_tn, act2, grad_block)
     half = deep // 2
-    for chip in range(chips):
-        grad_ref[chip, 0, :up_tall] = gup[chip * up_tall:(chip + 1) * up_tall]
-        part = gdown[chip * deep:(chip + 1) * deep]
-        grad_ref[chip, 0, up_tall:up_tall + deep] = part[:, :width]
-        grad_ref[chip, 0, up_tall + deep:] = jnp.concatenate(
-            [part[:half, width:], part[half:, width:]], axis=1
-        )
+
+    def store(grad_ref):
+        for chip in range(chips):
+            grad_ref[chip, :up_tall] = gup[chip * up_tall:(chip + 1) * up_tall]
+            part = gdown[chip * deep:(chip + 1) * deep]
+            grad_ref[chip, up_tall:up_tall + deep] = part[:, :width]
+            grad_ref[chip, up_tall + deep:] = jnp.concatenate(
+                [part[:half, width:], part[half:, width:]], axis=1
+            )
+
+    for at, ref in enumerate(grad_refs):
+        pl.when(step == at)(functools.partial(store, ref))
 
 
 def mlp(first, steps, so_far, chip, chips, resid, other, cot, cot_other, gain, bias, scale, ups, downs):
@@ -441,11 +443,9 @@
         + [pl.BlockSpec(memory_space=pltpu.SMEM)]
         + [pl.BlockSpec((up.shape[0], width), lambda j, c: (0, first + j)) for up in ups]
         + [down_spec] * len(downs)
-        + [fixed((2 * rows, model))] * len(so_far),
-        out_specs=[
-            fixed((2 * rows, model)), fixed((2 * rows, model)),
-            pl.BlockSpec((chips, 1, tall, width), lambda j, c: (0, j, 0, 0)),
-        ],
+        + [fixed((rows, model))] * len(so_far),
+        out_specs=[fixed((rows, model))] * 4
+        + [pl.BlockSpec((chips, tall, width), lambda j, c: (0, 0, 0))] * steps,
         scratch_shapes=[
             pltpu.VMEM((2 * rows, model), BF16), pltpu.VMEM((2 * rows, model), BF16),
             pltpu.VMEM((model, 2 * rows), BF16), pltpu.VMEM((model, 2 * rows), BF16),
@@ -455,14 +455,13 @@
         ],
     )
     return pl.pallas_call(
-        functools.partial(mlp_kernel, len(ups), len(so_far) // 2),
+        functools.partial(mlp_kernel, len(ups), len(so_far) // 4),
         grid_spec=grid_spec,
         out_shape=[
-            jax.ShapeDtypeStruct((2 * rows, model), F32),
-            jax.ShapeDtypeStruct((2 * rows, model), F32),
-            jax.ShapeDtypeStruct((chips, steps, tall, width), F32),
-        ],
-        cost_estimate=cost(18 * steps),
+            *[jax.ShapeDtypeStruct((rows, model), F32)] * 4,
+            *[jax.ShapeDtypeStruct((chips, tall, width), F32)] * steps,
+        ],
+        cost_estimate=cost(0.3),
         compiler_params=params(),
     )(chip, resid, other, cot, cot_other, gain, bias, scale, *ups, *downs, *so_far)
 
@@ -513,19 +512,25 @@
             jax.ShapeDtypeStruct((rows, model), F32),
             jax.ShapeDtypeStruct((8, model), F32),
         ],
-        cost_estimate=cost(6),
+        cost_estimate=cost(0.3),
         compiler_params=params(),
     )(part, given, resid, cot, gain, scale, w_full)
 
 
-def place_rows(core_ref, out_ref, got):
-    chips = out_ref.shape[1]
-    tall = out_ref.shape[2]
-    for block in range(2 * chips):
-        out_ref[(block & 1) ^ core_ref[0], block // 2] = got[block * tall:(block + 1) * tall]
-
-
-def weights_qk_kernel(core_ref, hi_ref, lo_ref, dq_ref, dk_ref, out_ref, nt_hi, nt_lo):
+def place_rows(core_ref, out_refs, got):
+    chips, tall = out_refs[0].shape[:2]
+
+    def store(core):
+        for block in range(2 * chips):
+            ref = out_refs[(block & 1) ^ core]
+            ref[block // 2] = got[block * tall:(block + 1) * tall]
+
+    for core in range(2):
+        pl.when(core_ref[0] == core)(functools.partial(store, core))
+
+
+def weights_qk_kernel(core_ref, hi_ref, lo_ref, dq_ref, dk_ref, own_ref, sib_ref, nt_hi, nt_lo):
+    out_ref = (own_ref, sib_ref)
     step = pl.program_id(0)
     part = pl.num_programs(0) // 2
     halo = hi_ref.shape[0] - dq_ref.shape[0]
@@ -546,8 +551,9 @@
         place_rows(core_ref, out_ref, three(dot_nn, left, split(dk_ref[...])))
 
 
-def weights_vo_kernel(core_ref, hi_ref, lo_ref, dv_ref, att_ref, res_ref, out_ref,
+def weights_vo_kernel(core_ref, hi_ref, lo_ref, dv_ref, att_ref, res_ref, own_ref, sib_ref,
                       nt_hi, nt_lo, at_hi, at_lo):
+    out_ref = (own_ref, sib_ref)
     step = pl.program_id(0)
     part = pl.num_programs(0) // 2
 
@@ -587,11 +593,11 @@
             num_scalar_prefetch=1,
             grid=(2 * part,),
             in_specs=[fixed(v) for v in fixed_args] + specs,
-            out_specs=pl.BlockSpec((2, chips, tall, wide), lambda j, c: (0, 0, 0, j)),
+            out_specs=[pl.BlockSpec((chips, tall, wide), lambda j, c: (0, 0, j))] * 2,
             scratch_shapes=[pltpu.VMEM((model, n), BF16) for n in scratch],
         ),
-        out_shape=jax.ShapeDtypeStruct((2, chips, tall, 2 * model), F32),
-        cost_estimate=cost(micros),
+        out_shape=[jax.ShapeDtypeStruct((chips, tall, 2 * model), F32)] * 2,
+        cost_estimate=cost(0.3),
         compiler_params=params(),
     )(core, *fixed_args, *args)
 
@@ -666,12 +672,12 @@
             for v in (up_chip, w_down)
         )
 
-    seg_own = segments + 1
-    near = lax.ppermute(block_input, "seq", ahead)
-    seg_near = lax.ppermute(seg_own, "seq", ahead)
+    numbers = jnp.pad((segments + 1).astype(F32), ((0, 7), (0, model - rows)))
+    near = lax.ppermute(jnp.concatenate([block_input, numbers], axis=0), "seq", ahead)
     far = lax.ppermute(near, "seq", ahead)
-    seg_far = lax.ppermute(seg_near, "seq", ahead)
-    seg_all = jnp.concatenate([seg_far, seg_near, seg_own], axis=1)
+    seg_all = jnp.concatenate(
+        [far[rows:rows + 1, :rows], near[rows:rows + 1, :rows], numbers[:1, :rows]], axis=1
+    ).astype(jnp.int32)
     seg_k_row = jnp.broadcast_to(seg_all, (8, halo + rows))
     seg_k_col = jnp.broadcast_to(seg_all.reshape(-1, 1), (halo + rows, 128))
     seg_q_row = seg_k_row[:, halo:]
@@ -704,12 +710,11 @@
     scatter_chips = lambda v: lax.psum_scatter(
         v, "dp", scatter_dimension=0, tiled=True, axis_index_groups=same_core
     )
-    so_far, shards = (), []
-    for third_at in range(3):
-        out_part, gnorm_part, grads = call(third_at, 1, so_far)
-        so_far = (out_part, gnorm_part)
-        shards.append(scatter_chips(grads)[0])
-    given = swap(gnorm_part[rows:])
+    *so_far, grads = call(0, 1, ())
+    *so_far, grads_next, grads_last = call(1, 2, tuple(so_far))
+    out_own, out_part, gnorm_own, gnorm_part = so_far
+    shards = [scatter_chips(value) for value in (grads, grads_next, grads_last)]
+    given = swap(gnorm_part)
 
     shift = lambda v, bit: lax.ppermute(v, "seq", [(i, i ^ bit) for i in range(groups)])
     even = place % 2 == 0
@@ -735,7 +740,7 @@
     shards[0], given = together((shards[0], given))
     line_a = line_start(shards[0])
     grad_resid, grad_attended, sums_two = resid_back(
-        gnorm_part, given, resid, cotangent, gain2, scale, out_full
+        gnorm_own, given, resid, cotangent, gain2, scale, out_full
     )
 
     back_args = (q_rot, kv, grad_attended, seg_q_row, seg_k_col, cosine, sine)
@@ -764,31 +769,32 @@
         weights_vo_kernel, 9, core_at, chips, normed_parts,
         [(dv, 0), (attended, None), (grad_resid, 1)], [halo + rows] * 2 + [rows] * 2,
     )
-    line_c, grads_vo = together((line_c, grads_vo))
+    line_c, ends_b, grads_vo = together((line_c, ends_b, grads_vo))
     line_c = line_middle(line_c)
     grads_c = jnp.concatenate([grads_qk[0] + given_qk, grads_vo[0] + swap(grads_vo[1])], axis=2)
     grads_c, out_part = together((grads_c, out_part))
     shard_c = scatter_chips(grads_c)[0]
-    out_sib = swap(out_part[rows:])
-    ends_b, dk, dv = together((ends_b, dk, dv))
-    dkv = jnp.concatenate([dk, dv], axis=1)
-
-    block_out = resid + out_part[:rows] + out_sib
+    out_sib = swap(out_part)
+
+    block_out = resid + out_own + out_sib
     output = base + dwa_weights[4] * block_out
     dwa_local = jnp.concatenate([dots, jnp.sum(cotangent * block_out)[None]])
 
-    wq, wkv = qkv_full[:, :model], qkv_full[:, model:]
-    partial = outer_cols(dkv, wkv)
-    line_c, partial = together((line_c, partial))
+    wq, wk, wv = (qkv_full[:, i * model:(i + 1) * model] for i in range(3))
+    part_far = outer_cols(dk[:rows], wk) + outer_cols(dv[:rows], wv)
+    dk_rest, dv_rest, far, near, part_far, line_c = together(
+        (dk[rows:], dv[rows:], far, near, part_far, line_c)
+    )
     ends_c = line_end(line_c)
-    own_part = partial[halo:] + outer_cols(dq, wq)
-    (sent,) = together((partial,))
-    back_near = sent[rows:halo] + lax.ppermute(sent[:rows], "seq", behind)
+    given_near = lax.ppermute(part_far, "seq", behind)
+    part_rest = outer_cols(dk_rest, wk) + outer_cols(dv_rest, wv)
+    own_part = part_rest[rows:] + outer_cols(dq, wq)
+    back_near = part_rest[:rows] + given_near
 
     xhat1, rate1 = norm_stats(block_input)
     terms = (
-        (norm_stats(far)[0], partial[:rows]),
-        (norm_stats(near)[0], partial[rows:halo]),
+        (norm_stats(far[:rows])[0], part_far),
+        (norm_stats(near[:rows])[0], part_rest[:rows]),
         (xhat1, own_part),
     )
     grad_gain_one = sum(jnp.sum(xhat * part, axis=0) for xhat, part in terms)

time: 501 us -> 544 us (1.086); the launches traced: 497 us -> 534 us
  waiting for transfers between devices: 140 us -> 180 us
  starting transfers between devices: 48.6 us -> 35.3 us
  Pallas kernels: 188 us -> 195 us
  local copies, waits for them, and re-layouts: 36 us -> 42.1 us
    ppermute x17, waiting for transfers between devices: 14.2 us -> 52.8 us  [body(): lax.ppermute(v, 'dp', [(i, i ^ bit) for i in range(devices)])]
    ppermute x14, waiting for transfers between devices: 74.3 us -> 83.6 us  [body(): lax.ppermute(v, 'seq', [(i, i ^ bit) for i in range(groups)])]
    ppermute x4 -> x2, starting transfers between devices: 15.3 us -> 7.45 us  [the longest x1 5.96 us: body(): lax.ppermute(jnp.concatenate([block_input, numbers], axis=0), 'seq', ahead)]
    pallas_call x3 -> x2, Pallas kernels: 62 us -> 69.2 us  [mlp(): pl.pallas_call(functools.partial(mlp_kernel, len(ups), len(so_far) // 4),...]
    ppermute x4 -> x2, waiting for transfers between devices: 48 us -> 41.5 us  [the longest x1 24.7 us: body(): given_near = lax.ppermute(part_far, 'seq', behind)]
    dot_general x2 -> x5, matrix products: 17.6 us -> 16.5 us  [outer_cols(): lax.dot_general(left, right, (((1,), (1,)), ((), ())), precision=HIGH)]
  transfers between devices with their start and end apart: 43 -> 41, of which waited for: 18 -> 17; matrix products, arithmetic and copies ran while one was open for 18% -> 18% of each run, Pallas kernels for 34% -> 33%
where the time goes in v8:
time: 544 us; the launch traced here: 534 us
  Pallas kernels  195 us (36%)
  waiting for transfers between devices  180 us (33%)
  other arithmetic  46.4 us (9%)
  local copies, waits for them, and re-layouts  42.1 us (8%)
  starting transfers between devices  35.3 us (6%)
  matrix products  20.2 us (4%)
  between operations  15.5 us (3%)
    ppermute x14, waiting for transfers between devices, body(): lax.ppermute(v, 'seq', [(i, i ^ bit) for i in range(groups)])  83.6 us
    pallas_call x2, Pallas kernels, mlp(): pl.pallas_call(functools.partial(mlp_kernel, len(ups), len(so_far) // 4),...  69.2 us
    ppermute x17, waiting for transfers between devices, body(): lax.ppermute(v, 'dp', [(i, i ^ bit) for i in range(devices)])  52.8 us
    pallas_call x2, Pallas kernels, attend_back(): pl.pallas_call(attend_back_kernel, grid=(count,), in_specs=[pl.BlockSpec(...  47 us
    pallas_call x2, Pallas kernels, weight_call(): pl.pallas_call(kernel, grid_spec=pltpu.PrefetchScalarGridSpec(num_scalar_...  26.4 us
    ppermute x1, waiting for transfers between devices, body(): given_near = lax.ppermute(part_far, 'seq', behind)  24.7 us
    pallas_call x1, Pallas kernels, attend(): pl.pallas_call(attend_kernel, grid=(pairs,), in_specs=[pl.BlockSpec((rows...  23.1 us
    pallas_call x1, Pallas kernels, project(): pl.pallas_call(qkv_kernel, grid=(3 * third,), in_specs=[whole((rows, mode...  21.6 us
  transfers between devices with their start and end apart: 41, of which 17 were waited for; matrix products, arithmetic and copies ran while one was open for 18% of the time, Pallas kernels for 33%

profile of v8, /device:TPU:0, one launch (start us, length us, event | category | flops | bytes accessed | tf_op | source)
XLA Modules:
  0.0 534.1 jit_solution(11777968474985966585)
XLA Ops:
  10.0 6.0 %collective-permute-start = (f32[392,768]{1,0:T(8,128)}, f32[392,768]{1,0:T(8,128)}, u32[]{:S(2)}, u32[]{:S(2)}) collective-permute-start(f32[392,768]{1,0:T(8,128)} %select_maximum_fusion), channel_id=1, source_target_pairs={{0,1},{1,2},{2,3},{4,5},{5,6},{6,7},{8,9},{9,10},{10,11},{12,13},{... | collective-permute-start | bytes 3612680 | tf_op jit(solution)/shard_map/ppermute | solution.py:676
  15.9 1.9 reshape.237
  24.1 16.8 %collective-permute-done.near_ref = f32[392,768]{1,0:T(8,128)} collective-permute-done((f32[392,768]{1,0:T(8,128)}, f32[392,768]{1,0:T(8,128)}, u32[]{:S(2)}, u32[]{:S(2)}) %collective-permute-start) | collective-permute-done | bytes 1204256 | tf_op jit(solution)/shard_map/ppermute | solution.py:676
  40.9 4.4 collective-permute-start.1
  50.4 4.9 fusion.21
  55.3 3.2 pad_maximum_fusion.6
  59.8 5.2 collective-permute-done.8.refs_5_
  65.7 36.9 %collective-permute-done.6.refs_2_ = f32[192,1536]{1,0:T(8,128)} collective-permute-done((f32[192,1536]{1,0:T(8,128)}, f32[192,1536]{1,0:T(8,128)}, u32[]{:S(2)}, u32[]{:S(2)}) %collective-permute-start.6) | collective-permute-done | bytes 1179680 | tf_op jit(solution)/shard_map/ppermute | solution.py:649
  105.3 21.6 %shard_map.239 = (f32[384,768]{1,0:T(8,128)}, f32[1152,1536]{1,0:T(8,128)}, bf16[1152,768]{1,0:T(8,128)(2,1)}, bf16[1152,768]{1,0:T(8,128)(2,1)}) custom-call(f32[392,768]{1,0:T(8,128)} %copy-done.7, f32[392,768]{1,0:T(8,128)} %collective-permute-done.near_ref, f32[384,768]{1,0:T(8,128)} %own_ref.1, f32[1,768]{1,0:T(1,128)} %broadcast_in_dim.48.gain_ref, ...), custom_call_target="tpu_custom_call" | custom-call | flops 330000000 | bytes 1048576 | tf_op jit(solution)/shard_map/pallas_call | solution.py:144
  128.3 23.1 %shard_map.240.att_ref = f32[384,768]{1,0:T(8,128)} custom-call(f32[384,768]{1,0:T(8,128)} %get-tuple-element.128.q_ref, f32[1152,1536]{1,0:T(8,128)} %get-tuple-element.129.k_ref.v_ref, f32[1152,1536]{1,0:T(8,128)} %get-tuple-element.129.k_ref.v_ref, s32[384,128]{1,0:T(8,128)} %broadcast_in_dim.50.segq_ref, s32[8,1152]{1,0:T(8,128)} %broadcast_in_dim.51.segk_ref), custom_call_target="tpu_custom_call" | custom-call | flops 330000000 | bytes 1048576 | tf_op jit(solution)/shard_map/pallas_call | solution.py:236
  151.5 3.7 convolution_add_fusion.resid_ref
  159.1 19.5 %shard_map.241 = (f32[384,768]{1,0:T(8,128)}, f32[384,768]{1,0:T(8,128)}, f32[384,768]{1,0:T(8,128)}, f32[384,768]{1,0:T(8,128)}, f32[4,384,512]{2,1,0:T(8,128)}) custom-call(s32[1]{0:T(128)} %bitcast.15.chip_ref, f32[384,768]{1,0:T(8,128)} %copy-done.5, f32[384,768]{1,0:T(8,128)} %copy-done.13, f32[384,768]{1,0:T(8,128)} %cot_ref.5, ...), custom_call_target="tpu_custom_call" | custom-call | flops 330000000 | bytes 1048576 | tf_op jit(solution)/shard_map/pallas_call | solution.py:457
  178.7 49.7 %shard_map.242 = (f32[384,768]{1,0:T(8,128)}, f32[384,768]{1,0:T(8,128)}, f32[384,768]{1,0:T(8,128)}, f32[384,768]{1,0:T(8,128)}, f32[4,384,512]{2,1,0:T(8,128)}, /*index=5*/f32[4,384,512]{2,1,0:T(8,128)}) custom-call(s32[1]{0:T(128)} %bitcast.15.chip_ref, f32[384,768]{1,0:T(8,128)} %copy-done.5, f32[384,768]{1,0:T(8,128)} %copy-done.13, ...), custom_call_target="tpu_custom_call" | custom-call | flops 330000000 | bytes 1048576 | tf_op jit(solution)/shard_map/pallas_call | solution.py:457
  229.3 2.9 collective-permute-done.11.given_ref
  234.9 7.3 %shard_map.243 = (f32[384,768]{1,0:T(8,128)}, f32[384,768]{1,0:T(8,128)}, f32[8,768]{1,0:T(8,128)}) custom-call(f32[384,768]{1,0:T(8,128)} %get-tuple-element.111.part_ref, f32[384,768]{1,0:T(8,128)} %copy-done.27, f32[384,768]{1,0:T(8,128)} %copy-done.5, f32[384,768]{1,0:T(8,128)} %cot_ref.5, f32[1,768]{1,0:T(1,128)} %broadcast_in_dim.52.gain_ref, ...), custom_call_target="tpu_custom_call" | custom-call | flops 330000000 | bytes 1048576 | tf_op jit(solution)/shard_map/pallas_call | solution.py:504
  242.3 2.8 collective-permute-done.12
  246.8 2.0 collective-permute-start.13
  248.8 23.3 %shard_map.244 = (f32[384,768]{1,0:T(8,128)}, f32[1152,768]{1,0:T(8,128)}, f32[1152,768]{1,0:T(8,128)}) custom-call(f32[384,768]{1,0:T(8,128)} %get-tuple-element.128.q_ref, f32[1152,1536]{1,0:T(8,128)} %get-tuple-element.129.k_ref.v_ref, f32[1152,1536]{1,0:T(8,128)} %get-tuple-element.129.k_ref.v_ref, f32[384,768]{1,0:T(8,128)} %get-tuple-element.130.g_ref, ...), custom_call_target="tpu_custom_call" | custom-call | flops 330000000 | bytes 1048576 | tf_op jit(solution)/shard_map/pallas_call | solution.py:328
  275.5 23.7 %shard_map.245 = (f32[384,768]{1,0:T(8,128)}, f32[1152,768]{1,0:T(8,128)}, f32[1152,768]{1,0:T(8,128)}) custom-call(f32[384,768]{1,0:T(8,128)} %get-tuple-element.128.q_ref, f32[1152,1536]{1,0:T(8,128)} %get-tuple-element.129.k_ref.v_ref, f32[1152,1536]{1,0:T(8,128)} %get-tuple-element.129.k_ref.v_ref, ...), custom_call_target="tpu_custom_call", output_to_operand_aliasing={{0}: (8, {}), {1}: (9, {}), {2}: (10, {})} | custom-call | flops 330000000 | bytes 1048576 | tf_op jit(solution)/shard_map/pallas_call | solution.py:328
  301.5 17.7 %collective-permute-done.17 = f32[1,192,512]{2,1,0:T(8,128)S(1)} collective-permute-done((f32[1,192,512]{2,1,0:T(8,128)S(1)}, f32[1,192,512]{2,1,0:T(8,128)S(1)}, u32[]{:S(2)}, u32[]{:S(2)}) %collective-permute-start.17) | collective-permute-done | bytes 393248 | tf_op jit(solution)/shard_map/ppermute | solution.py:719
  320.7 1.8 collective-permute-start.19
  322.5 12.7 %shard_map.246 = (f32[4,96,1536]{2,1,0:T(8,128)}, f32[4,96,1536]{2,1,0:T(8,128)}) custom-call(s32[1]{0:T(128)} %bitcast.18.core_ref, bf16[1152,768]{1,0:T(8,128)(2,1)} %get-tuple-element.106.hi_ref, bf16[1152,768]{1,0:T(8,128)(2,1)} %get-tuple-element.107.lo_ref, f32[384,768]{1,0:T(8,128)} %get-tuple-element.141.dq_ref, f32[1152,768]{1,0:T(8,128)} %get-tuple-element.142.dk_ref), custom_call_target="tpu_custom_call" | custom-call | flops 330000000 | bytes 1048576 | tf_op jit(solution)/shard_map/pallas_call | solution.py:590
  335.3 13.6 %shard_map.247 = (f32[4,96,1536]{2,1,0:T(8,128)}, f32[4,96,1536]{2,1,0:T(8,128)}) custom-call(s32[1]{0:T(128)} %bitcast.18.core_ref, bf16[1152,768]{1,0:T(8,128)(2,1)} %get-tuple-element.106.hi_ref, bf16[1152,768]{1,0:T(8,128)(2,1)} %get-tuple-element.107.lo_ref, f32[1152,768]{1,0:T(8,128)} %get-tuple-element.151.dv_ref, f32[384,768]{1,0:T(8,128)} %shard_map.240.att_ref, ...), custom_call_target="tpu_custom_call" | custom-call | flops 330000000 | bytes 1048576 | tf_op jit(solution)/shard_map/pallas_call | solution.py:590
  351.2 3.7 collective-permute-done.20
  355.3 2.4 pad_maximum_fusion
  359.5 1.9 slice.180
  362.2 4.1 fusion
  367.5 3.4 fusion.4
  371.1 2.9 fusion.13
  374.1 12.9 %collective-permute-done.22 = f32[1,192,512]{2,1,0:T(8,128)S(1)} collective-permute-done((f32[1,192,512]{2,1,0:T(8,128)S(1)}, f32[1,192,512]{2,1,0:T(8,128)S(1)}, u32[]{:S(2)}, u32[]{:S(2)}) %collective-permute-start.22) | collective-permute-done | bytes 393248 | tf_op jit(solution)/shard_map/ppermute | solution.py:719
  391.5 3.0 fusion.2
  394.5 3.0 fusion.10
  397.7 1.9 multiply_reduce_fusion.4
  399.6 24.7 %collective-permute-done.24 = f32[384,768]{1,0:T(8,128)S(1)} collective-permute-done((f32[384,768]{1,0:T(8,128)S(1)}, f32[384,768]{1,0:T(8,128)S(1)}, u32[]{:S(2)}, u32[]{:S(2)}) %collective-permute-start.24) | collective-permute-done | bytes 1179680 | tf_op jit(solution)/shard_map/ppermute | solution.py:789
  424.3 2.8 fusion.30
  428.4 2.6 multiply_reduce_fusion.1
  438.2 1.8 collective-permute-done.26
  440.2 2.1 broadcast_select_fusion.6
  450.1 12.1 %collective-permute-done.28 = f32[1,48,3072]{2,1,0:T(8,128)S(1)} collective-permute-done((f32[1,48,3072]{2,1,0:T(8,128)S(1)}, f32[1,48,3072]{2,1,0:T(8,128)S(1)}, u32[]{:S(2)}, u32[]{:S(2)}) %collective-permute-start.28) | collective-permute-done | bytes 589856 | tf_op jit(solution)/shard_map/ppermute | solution.py:719
  466.5 2.1 stack.30
  468.6 2.3 copy.39
  470.9 2.1 stack.29
  476.2 2.6 reshape.239
  478.8 26.9 %collective-permute-done.29 = f32[1,48,3072]{2,1,0:T(8,128)} collective-permute-done((f32[1,48,3072]{2,1,0:T(8,128)}, f32[1,48,3072]{2,1,0:T(8,128)}, u32[]{:S(2)}, u32[]{:S(2)}) %collective-permute-start.29) | collective-permute-done | bytes 589856 | tf_op jit(solution)/shard_map/ppermute | solution.py:719
  507.0 1.9 fusion.31
  509.1 2.0 collective-permute-start.34
  511.1 2.1 collective-permute-done.32
  514.6 9.0 %collective-permute-done.33 = f32[8,768]{1,0:T(8,128)S(1)} collective-permute-done((f32[8,768]{1,0:T(8,128)S(1)}, f32[8,768]{1,0:T(8,128)S(1)}, u32[]{:S(2)}, u32[]{:S(2)}) %collective-permute-start.33) | collective-permute-done | bytes 24608 | tf_op jit(solution)/shard_map/ppermute | solution.py:719
  (252 shorter events, 77.2 us)
Async XLA Ops:
  7.2 98.1 %all-gather.3.cloned.1.call-start = ((), (), s32[]{:S(2)}) async-start(), calls=%async_computation.4 | async-start | bytes 7962624 | tf_op jit(solution)/shard_map/all_gather | solution.py:652
  7.9 143.5 %all-gather.5.cloned.1.call-start = ((), (), s32[]{:S(2)}) async-start(), calls=%async_computation.5 | async-start | bytes 2654208 | tf_op jit(solution)/shard_map/all_gather | solution.py:652
  8.7 223.6 %reduce-scatter.13.cloned.1.call-start = ((), (), s32[]{:S(2)}) async-start(), calls=%async_computation.6 | async-start | bytes 3932160
  10.0 31.0 %collective-permute-start = (f32[392,768]{1,0:T(8,128)}, f32[392,768]{1,0:T(8,128)}, u32[]{:S(2)}, u32[]{:S(2)}) collective-permute-start(f32[392,768]{1,0:T(8,128)} %select_maximum_fusion), channel_id=1, source_target_pairs={{0,1},{1,2},{2,3},{4,5},{5,6},{6,7},{8,9},{9,10},{10,11},{12,13},{... | collective-permute-start | bytes 3612680 | tf_op jit(solution)/shard_map/ppermute | solution.py:676
  19.4 4.6 collective-permute-start.4
  19.4 45.6 %collective-permute-start.8 = (f32[384,768]{1,0:T(8,128)}, f32[384,768]{1,0:T(8,128)}, u32[]{:S(2)}, u32[]{:S(2)}) collective-permute-start(f32[384,768]{1,0:T(8,128)} %refs_4_.3), channel_id=1, source_target_pairs={{0,8},{4,12},{8,0},{12,4},{16,24},{20,28},{24,16},{28,20},{1,9},{5... | collective-permute-start | bytes 3538952 | tf_op jit(solution)/shard_map/ppermute | solution.py:649
  20.9 136.4 %collective-permute-start.9 = (f32[384,768]{1,0:T(8,128)}, f32[384,768]{1,0:T(8,128)}, u32[]{:S(2)}, u32[]{:S(2)}) collective-permute-start(f32[384,768]{1,0:T(8,128)} %refs_4_.3), channel_id=1, source_target_pairs={{0,16},{4,20},{8,24},{12,28},{16,0},{20,4},{24,8},{28,12},{1,17},{... | collective-permute-start | bytes 3538952 | tf_op jit(solution)/shard_map/ppermute | solution.py:649
  22.4 132.8 %collective-permute-start.3 = (f32[384,768]{1,0:T(8,128)S(1)}, f32[384,768]{1,0:T(8,128)}, u32[]{:S(2)}, u32[]{:S(2)}) collective-permute-start(f32[384,768]{1,0:T(8,128)S(1)} %copy-done.3), channel_id=1, source_target_pairs={{0,4},{4,0},{8,12},{12,8},{16,20},{20,16},{24,28},{28,24},{1,5},{5... | collective-permute-start | bytes 3538952 | tf_op jit(solution)/shard_map/ppermute | solution.py:649
  40.9 62.0 %collective-permute-start.1 = (f32[392,768]{1,0:T(8,128)}, f32[392,768]{1,0:T(8,128)S(1)}, u32[]{:S(2)}, u32[]{:S(2)}) collective-permute-start(f32[392,768]{1,0:T(8,128)} %collective-permute-done.near_ref), channel_id=1, source_target_pairs={{0,1},{1,2},{2,3},{4,5},{5,6},{6,7},{8,9},{9,10},{10,11},{12,13},{... | collective-permute-start | bytes 3612680 | tf_op jit(solution)/shard_map/ppermute | solution.py:677
  46.5 56.1 %collective-permute-start.6 = (f32[192,1536]{1,0:T(8,128)}, f32[192,1536]{1,0:T(8,128)}, u32[]{:S(2)}, u32[]{:S(2)}) collective-permute-start(f32[192,1536]{1,0:T(8,128)} %pad_maximum_fusion.1.refs_0_), channel_id=1, source_target_pairs={{0,16},{4,20},{8,24},{12,28},{16,0},{20,4},{24,8},{28,12},{1,17},{... | collective-permute-start | bytes 3538952 | tf_op jit(solution)/shard_map/ppermute | solution.py:649
  65.0 92.3 %collective-permute-start.5 = (f32[192,1536]{1,0:T(8,128)}, f32[192,1536]{1,0:T(8,128)}, u32[]{:S(2)}, u32[]{:S(2)}) collective-permute-start(f32[192,1536]{1,0:T(8,128)} %pad_maximum_fusion.1.refs_0_), channel_id=1, source_target_pairs={{0,8},{4,12},{8,0},{12,4},{16,24},{20,28},{24,16},{28,20},{1,9},{5... | collective-permute-start | bytes 3538952 | tf_op jit(solution)/shard_map/ppermute | solution.py:649
  102.7 54.6 %collective-permute-start.10 = (f32[384,768]{1,0:T(8,128)}, f32[384,768]{1,0:T(8,128)}, u32[]{:S(2)}, u32[]{:S(2)}) collective-permute-start(f32[384,768]{1,0:T(8,128)} %collective-permute-done.8.refs_5_), channel_id=1, source_target_pairs={{0,16},{4,20},{8,24},{12,28},{16,0},{20,4},{24,8},{28,12},{1,17},{... | collective-permute-start | bytes 3538952 | tf_op jit(solution)/shard_map/ppermute | solution.py:649
  103.0 54.3 %collective-permute-start.7 = (f32[192,1536]{1,0:T(8,128)}, f32[192,1536]{1,0:T(8,128)}, u32[]{:S(2)}, u32[]{:S(2)}) collective-permute-start(f32[192,1536]{1,0:T(8,128)} %collective-permute-done.6.refs_2_), channel_id=1, source_target_pairs={{0,8},{4,12},{8,0},{12,4},{16,24},{20,28},{24,16},{28,20},{1,9},{5... | collective-permute-start | bytes 3538952 | tf_op jit(solution)/shard_map/ppermute | solution.py:649
  155.2 2.9 collective-permute-start.2
  178.7 93.6 %reduce-scatter.15.cloned.1.call-start = ((), (), s32[]{:S(2)}) async-start(), calls=%async_computation.7 | async-start | bytes 3932160
  228.4 90.8 %reduce-scatter.17.cloned.1.call-start = ((), (), s32[]{:S(2)}) async-start(), calls=%async_computation.8 | async-start | bytes 3932160
  229.1 215.4 %reduce-scatter.19.cloned.1.call-start = ((), (), s32[]{:S(2)}) async-start(), calls=%async_computation.9 | async-start | bytes 5898240
  229.1 3.1 collective-permute-start.11
  233.9 11.2 %collective-permute-start.12 = (f32[1,192,512]{2,1,0:T(8,128)S(1)}, f32[1,192,512]{2,1,0:T(8,128)S(1)}, u32[]{:S(2)}, u32[]{:S(2)}) collective-permute-start(f32[1,192,512]{2,1,0:T(8,128)S(1)} %slice_select_fusion.7), channel_id=1, source_target_pairs={{0,1},{1,0},{2,3},{3,2},{4,5},{5,4},{6,7},{7,6},{8,9},{9,8},{10,11... | collective-permute-start | bytes 1179656 | tf_op jit(solution)/shard_map/ppermute | solution.py:719
  246.8 25.4 %collective-permute-start.13 = (f32[1,192,512]{2,1,0:T(8,128)S(1)}, f32[1,192,512]{2,1,0:T(8,128)S(1)}, u32[]{:S(2)}, u32[]{:S(2)}) collective-permute-start(f32[1,192,512]{2,1,0:T(8,128)S(1)} %select_add_fusion.3), channel_id=1, source_target_pairs={{0,2},{1,3},{2,0},{3,1},{4,6},{5,7},{6,4},{7,5},{8,10},{9,11},{10,... | collective-permute-start | bytes 1179656 | tf_op jit(solution)/shard_map/ppermute | solution.py:719
  273.5 25.8 %collective-permute-start.14 = (f32[1,192,512]{2,1,0:T(8,128)S(1)}, f32[1,192,512]{2,1,0:T(8,128)S(1)}, u32[]{:S(2)}, u32[]{:S(2)}) collective-permute-start(f32[1,192,512]{2,1,0:T(8,128)S(1)} %slice_select_fusion.6), channel_id=1, source_target_pairs={{0,1},{1,0},{2,3},{3,2},{4,5},{5,4},{6,7},{7,6},{8,9},{9,8},{10,11... | collective-permute-start | bytes 1179656 | tf_op jit(solution)/shard_map/ppermute | solution.py:719
  273.9 25.4 %collective-permute-start.15 = (f32[1,192,512]{2,1,0:T(8,128)S(1)}, f32[1,192,512]{2,1,0:T(8,128)S(1)}, u32[]{:S(2)}, u32[]{:S(2)}) collective-permute-start(f32[1,192,512]{2,1,0:T(8,128)S(1)} %add.197), channel_id=1, source_target_pairs={{0,1},{1,0},{2,3},{3,2},{4,5},{5,4},{6,7},{7,6},{8,9},{9,8},{10,11... | collective-permute-start | bytes 1179656 | tf_op jit(solution)/shard_map/ppermute | solution.py:719
  300.2 19.0 %collective-permute-start.17 = (f32[1,192,512]{2,1,0:T(8,128)S(1)}, f32[1,192,512]{2,1,0:T(8,128)S(1)}, u32[]{:S(2)}, u32[]{:S(2)}) collective-permute-start(f32[1,192,512]{2,1,0:T(8,128)S(1)} %select_add_fusion.2), channel_id=1, source_target_pairs={{0,2},{1,3},{2,0},{3,1},{4,6},{5,7},{6,4},{7,5},{8,10},{9,11},{10,... | collective-permute-start | bytes 1179656 | tf_op jit(solution)/shard_map/ppermute | solution.py:719
  320.4 28.5 %collective-permute-start.18 = (f32[1,192,512]{2,1,0:T(8,128)S(1)}, f32[1,192,512]{2,1,0:T(8,128)S(1)}, u32[]{:S(2)}, u32[]{:S(2)}) collective-permute-start(f32[1,192,512]{2,1,0:T(8,128)S(1)} %slice_select_fusion.5), channel_id=1, source_target_pairs={{0,1},{1,0},{2,3},{3,2},{4,5},{5,4},{6,7},{7,6},{8,9},{9,8},{10,11... | collective-permute-start | bytes 1179656 | tf_op jit(solution)/shard_map/ppermute | solution.py:719
  320.7 28.3 %collective-permute-start.19 = (f32[1,192,512]{2,1,0:T(8,128)S(1)}, f32[1,192,512]{2,1,0:T(8,128)S(1)}, u32[]{:S(2)}, u32[]{:S(2)}) collective-permute-start(f32[1,192,512]{2,1,0:T(8,128)S(1)} %add.200), channel_id=1, source_target_pairs={{0,1},{1,0},{2,3},{3,2},{4,5},{5,4},{6,7},{7,6},{8,9},{9,8},{10,11... | collective-permute-start | bytes 1179656 | tf_op jit(solution)/shard_map/ppermute | solution.py:719
  335.2 15.3 %collective-permute-start.16 = (f32[4,96,1536]{2,1,0:T(8,128)}, f32[4,96,1536]{2,1,0:T(8,128)S(1)}, u32[]{:S(2)}, u32[]{:S(2)}) collective-permute-start(f32[4,96,1536]{2,1,0:T(8,128)} %get-tuple-element.144), channel_id=1, source_target_pairs={{0,4},{4,0},{8,12},{12,8},{16,20},{20,16},{24,28},{28,24},{1,5},{5... | collective-permute-start | bytes 7077896 | tf_op jit(solution)/shard_map/ppermute | solution.py:649
  350.0 4.9 collective-permute-start.20
  358.2 66.2 %copy-start.32 = (f32[384]{0:T(512)}, f32[384]{0:T(512)S(1)}, u32[]{:S(2)}) copy-start(f32[384]{0:T(512)S(1)} %add_rsqrt_fusion.2) | copy-start | bytes 4612
  366.3 58.0 %copy-start.9 = (f32[384,768]{1,0:T(8,128)}, f32[384,768]{1,0:T(8,128)S(1)}, u32[]{:S(2)}) copy-start(f32[384,768]{1,0:T(8,128)S(1)} %fusion) | copy-start | bytes 3538948
  366.3 20.6 %collective-permute-start.22 = (f32[1,192,512]{2,1,0:T(8,128)S(1)}, f32[1,192,512]{2,1,0:T(8,128)S(1)}, u32[]{:S(2)}, u32[]{:S(2)}) collective-permute-start(f32[1,192,512]{2,1,0:T(8,128)S(1)} %select_add_fusion.1), channel_id=1, source_target_pairs={{0,2},{1,3},{2,0},{3,1},{4,6},{5,7},{6,4},{7,5},{8,10},{9,11},{10,... | collective-permute-start | bytes 1179656 | tf_op jit(solution)/shard_map/ppermute | solution.py:719
  387.8 52.5 %collective-permute-start.23 = (f32[1,192,512]{2,1,0:T(8,128)}, f32[1,192,512]{2,1,0:T(8,128)}, u32[]{:S(2)}, u32[]{:S(2)}) collective-permute-start(f32[1,192,512]{2,1,0:T(8,128)} %add.207), channel_id=1, source_target_pairs={{0,1},{1,0},{2,3},{3,2},{4,5},{5,4},{6,7},{7,6},{8,9},{9,8},{10,11... | collective-permute-start | bytes 1179656 | tf_op jit(solution)/shard_map/ppermute | solution.py:719
  387.8 36.6 %collective-permute-start.24 = (f32[384,768]{1,0:T(8,128)S(1)}, f32[384,768]{1,0:T(8,128)S(1)}, u32[]{:S(2)}, u32[]{:S(2)}) collective-permute-start(f32[384,768]{1,0:T(8,128)S(1)} %fusion.13), channel_id=1, source_target_pairs={{1,0},{2,1},{3,2},{5,4},{6,5},{7,6},{9,8},{10,9},{11,10},{13,12},{... | collective-permute-start | bytes 3538952 | tf_op jit(solution)/shard_map/ppermute | solution.py:789
  397.6 30.7 %collective-permute-start.21 = (f32[384,768]{1,0:T(8,128)S(1)}, f32[384,768]{1,0:T(8,128)S(1)}, u32[]{:S(2)}, u32[]{:S(2)}) collective-permute-start(f32[384,768]{1,0:T(8,128)S(1)} %copy-done.43), channel_id=1, source_target_pairs={{0,4},{4,0},{8,12},{12,8},{16,20},{20,16},{24,28},{28,24},{1,5},{5... | collective-permute-start | bytes 3538952 | tf_op jit(solution)/shard_map/ppermute | solution.py:649
  399.6 28.8 %copy-start.4 = (f32[384,768]{1,0:T(8,128)S(1)}, f32[384,768]{1,0:T(8,128)}, u32[]{:S(2)}) copy-start(f32[384,768]{1,0:T(8,128)} %cot_ref.5) | copy-start | bytes 3538948
  399.6 28.7 %copy-start.6 = (f32[384,768]{1,0:T(8,128)S(1)}, f32[384,768]{1,0:T(8,128)}, u32[]{:S(2)}) copy-start(f32[384,768]{1,0:T(8,128)} %copy-done.5) | copy-start | bytes 3538948
  399.6 28.7 %copy-start.16 = (f32[384,768]{1,0:T(8,128)S(1)}, f32[384,768]{1,0:T(8,128)}, u32[]{:S(2)}) copy-start(f32[384,768]{1,0:T(8,128)} %get-tuple-element.97) | copy-start | bytes 3538948
  399.6 28.7 %copy-start.28 = (f32[384,768]{1,0:T(8,128)S(1)}, f32[384,768]{1,0:T(8,128)}, u32[]{:S(2)}) copy-start(f32[384,768]{1,0:T(8,128)} %get-tuple-element.105) | copy-start | bytes 3538948
  433.7 1.8 collective-permute-start.25
  436.2 3.8 collective-permute-start.26
  440.0 3.8 collective-permute-start.27
  445.9 16.3 %collective-permute-start.28 = (f32[1,48,3072]{2,1,0:T(8,128)S(1)}, f32[1,48,3072]{2,1,0:T(8,128)S(1)}, u32[]{:S(2)}, u32[]{:S(2)}) collective-permute-start(f32[1,48,3072]{2,1,0:T(8,128)S(1)} %slice_select_fusion.4), channel_id=1, source_target_pairs={{0,1},{1,0},{2,3},{3,2},{4,5},{5,4},{6,7},{7,6},{8,9},{9,8},{10,11... | collective-permute-start | bytes 1769480 | tf_op jit(solution)/shard_map/ppermute | solution.py:719
  448.3 17.0 %collective-permute-start.30 = (f32[3,96,512]{2,1,0:T(8,128)S(1)}, f32[3,96,512]{2,1,0:T(8,128)S(1)}, u32[]{:S(2)}, u32[]{:S(2)}) collective-permute-start(f32[3,96,512]{2,1,0:T(8,128)S(1)} %slice_select_fusion.2), channel_id=1, source_target_pairs={{0,4},{4,0},{8,12},{12,8},{16,20},{20,16},{24,28},{28,24},{1,5},{5... | collective-permute-start | bytes 1769480 | tf_op jit(solution)/shard_map/ppermute | solution.py:649
  448.4 58.6 %collective-permute-start.31 = (f32[384,768]{1,0:T(8,128)}, f32[384,768]{1,0:T(8,128)}, u32[]{:S(2)}, u32[]{:S(2)}) collective-permute-start(f32[384,768]{1,0:T(8,128)} %get-tuple-element.177), channel_id=1, source_target_pairs={{1,0},{2,1},{3,2},{5,4},{6,5},{7,6},{9,8},{10,9},{11,10},{13,12},{... | collective-permute-start | bytes 3538952 | tf_op jit(solution)/shard_map/ppermute | solution.py:816
  463.2 42.5 %collective-permute-start.29 = (f32[1,48,3072]{2,1,0:T(8,128)}, f32[1,48,3072]{2,1,0:T(8,128)}, u32[]{:S(2)}, u32[]{:S(2)}) collective-permute-start(f32[1,48,3072]{2,1,0:T(8,128)} %select_add_fusion), channel_id=1, source_target_pairs={{0,2},{1,3},{2,0},{3,1},{4,6},{5,7},{6,4},{7,5},{8,10},{9,11},{10,... | collective-permute-start | bytes 1769480 | tf_op jit(solution)/shard_map/ppermute | solution.py:719
  478.8 28.2 %copy-start.35 = (f32[768]{0:T(1024)S(1)}, f32[768]{0:T(1024)}, u32[]{:S(2)}) copy-start(f32[768]{0:T(1024)} %param.20) | copy-start | bytes 9220
  509.0 4.2 collective-permute-start.32
  509.1 15.8 %collective-permute-start.34 = (f32[1,48,3072]{2,1,0:T(8,128)S(1)}, f32[1,48,3072]{2,1,0:T(8,128)S(1)}, u32[]{:S(2)}, u32[]{:S(2)}) collective-permute-start(f32[1,48,3072]{2,1,0:T(8,128)S(1)} %add.223), channel_id=1, source_target_pairs={{0,1},{1,0},{2,3},{3,2},{4,5},{5,4},{6,7},{7,6},{8,9},{9,8},{10,11... | collective-permute-start | bytes 1769480 | tf_op jit(solution)/shard_map/ppermute | solution.py:719
  513.2 10.4 %collective-permute-start.33 = (f32[8,768]{1,0:T(8,128)S(1)}, f32[8,768]{1,0:T(8,128)S(1)}, u32[]{:S(2)}, u32[]{:S(2)}) collective-permute-start(f32[8,768]{1,0:T(8,128)S(1)} %add.226), channel_id=1, source_target_pairs={{0,2},{1,3},{2,0},{3,1},{4,6},{5,7},{6,4},{7,5},{8,10},{9,11},{10,... | collective-permute-start | bytes 73736 | tf_op jit(solution)/shard_map/ppermute | solution.py:719
  (39 other events, 330.9 us)
Sparse Core Ops, SparseCore 0:
  9.9 80.2 all-gather.2
  92.1 38.6 all-gather.4
  178.8 42.5 reduce-scatter.12
  228.6 42.5 reduce-scatter.14
  274.0 43.9 reduce-scatter.16
  357.8 56.6 reduce-scatter.18

commit v9 on v8

--- a/solution.py
+++ b/solution.py
@@ -161,7 +161,7 @@
             jax.ShapeDtypeStruct((total, model), BF16),
             jax.ShapeDtypeStruct((total, model), BF16),
         ],
-        cost_estimate=cost(0.3),
+        cost_estimate=cost(20),
         compiler_params=params(),
     )(far, near, own, gain, bias, w_full, cosine, sine)
 
@@ -246,7 +246,7 @@
         out_specs=pl.BlockSpec((rows, 128), lambda p: (0, p)),
         out_shape=jax.ShapeDtypeStruct((rows, model), F32),
         scratch_shapes=[pltpu.VMEM((rows, total - rows + BLK), F32)],
-        cost_estimate=cost(0.3),
+        cost_estimate=cost(24),
         compiler_params=params(),
     )(q_rot, kv, kv, seg_q, seg_k)
 
@@ -348,7 +348,7 @@
         ],
         scratch_shapes=[pltpu.VMEM((total - rows + BLK, rows), F32)],
         input_output_aliases={8 + i: i for i in range(len(before))},
-        cost_estimate=cost(0.3),
+        cost_estimate=cost(7 * count),
         compiler_params=params(),
     )(q_rot, kv, kv, grad, seg_q, seg_k, cosine, sine, *before)
 
@@ -358,8 +358,8 @@
     up_refs, down_refs = refs[:count], refs[count:2 * count]
     refs = refs[2 * count:]
     so_far, refs = refs[:4 * begun], refs[4 * begun:]
-    sums, grad_refs = refs[:4], refs[4:-10]
-    (x_hi, x_lo, xt_hi, xt_lo, g_hi, g_lo, up_hi, up_lo, down_hi, down_lo) = refs[-10:]
+    sums, grad_ref = refs[:4], refs[4]
+    (x_hi, x_lo, xt_hi, xt_lo, g_hi, g_lo, up_hi, up_lo, down_hi, down_lo) = refs[5:]
     step = pl.program_id(0)
     rows = resid_ref.shape[0]
 
@@ -386,7 +386,7 @@
         here = pl.ds(pl.multiple_of(spot * block.shape[0], block.shape[0]), block.shape[0])
         down_hi[here], down_lo[here] = high, low
 
-    chips, tall, width = grad_refs[0].shape
+    chips, _, tall, width = grad_ref.shape
     up_tall = up_hi.shape[0] // chips
     deep = down_hi.shape[0] // chips
     up = (up_hi[...], up_lo[...])
@@ -410,18 +410,13 @@
     gup = three(dot_nn, normed_t, grad_pre)
     gdown = three(dot_tn, act2, grad_block)
     half = deep // 2
-
-    def store(grad_ref):
-        for chip in range(chips):
-            grad_ref[chip, :up_tall] = gup[chip * up_tall:(chip + 1) * up_tall]
-            part = gdown[chip * deep:(chip + 1) * deep]
-            grad_ref[chip, up_tall:up_tall + deep] = part[:, :width]
-            grad_ref[chip, up_tall + deep:] = jnp.concatenate(
-                [part[:half, width:], part[half:, width:]], axis=1
-            )
-
-    for at, ref in enumerate(grad_refs):
-        pl.when(step == at)(functools.partial(store, ref))
+    for chip in range(chips):
+        grad_ref[chip, 0, :up_tall] = gup[chip * up_tall:(chip + 1) * up_tall]
+        part = gdown[chip * deep:(chip + 1) * deep]
+        grad_ref[chip, 0, up_tall:up_tall + deep] = part[:, :width]
+        grad_ref[chip, 0, up_tall + deep:] = jnp.concatenate(
+            [part[:half, width:], part[half:, width:]], axis=1
+        )
 
 
 def mlp(first, steps, so_far, chip, chips, resid, other, cot, cot_other, gain, bias, scale, ups, downs):
@@ -444,8 +439,10 @@
         + [pl.BlockSpec((up.shape[0], width), lambda j, c: (0, first + j)) for up in ups]
         + [down_spec] * len(downs)
         + [fixed((rows, model))] * len(so_far),
-        out_specs=[fixed((rows, model))] * 4
-        + [pl.BlockSpec((chips, tall, width), lambda j, c: (0, 0, 0))] * steps,
+        out_specs=[
+            *[fixed((rows, model))] * 4,
+            pl.BlockSpec((chips, 1, tall, width), lambda j, c: (0, j, 0, 0)),
+        ],
         scratch_shapes=[
             pltpu.VMEM((2 * rows, model), BF16), pltpu.VMEM((2 * rows, model), BF16),
             pltpu.VMEM((model, 2 * rows), BF16), pltpu.VMEM((model, 2 * rows), BF16),
@@ -459,9 +456,9 @@
         grid_spec=grid_spec,
         out_shape=[
             *[jax.ShapeDtypeStruct((rows, model), F32)] * 4,
-            *[jax.ShapeDtypeStruct((chips, tall, width), F32)] * steps,
-        ],
-        cost_estimate=cost(0.3),
+            jax.ShapeDtypeStruct((chips, steps, tall, width), F32),
+        ],
+        cost_estimate=cost(18 * steps),
         compiler_params=params(),
     )(chip, resid, other, cot, cot_other, gain, bias, scale, *ups, *downs, *so_far)
 
@@ -512,7 +509,7 @@
             jax.ShapeDtypeStruct((rows, model), F32),
             jax.ShapeDtypeStruct((8, model), F32),
         ],
-        cost_estimate=cost(0.3),
+        cost_estimate=cost(6),
         compiler_params=params(),
     )(part, given, resid, cot, gain, scale, w_full)
 
@@ -597,7 +594,7 @@
             scratch_shapes=[pltpu.VMEM((model, n), BF16) for n in scratch],
         ),
         out_shape=[jax.ShapeDtypeStruct((chips, tall, 2 * model), F32)] * 2,
-        cost_estimate=cost(0.3),
+        cost_estimate=cost(micros),
         compiler_params=params(),
     )(core, *fixed_args, *args)
 
@@ -672,12 +669,12 @@
             for v in (up_chip, w_down)
         )
 
-    numbers = jnp.pad((segments + 1).astype(F32), ((0, 7), (0, model - rows)))
-    near = lax.ppermute(jnp.concatenate([block_input, numbers], axis=0), "seq", ahead)
+    seg_own = segments + 1
+    near = lax.ppermute(block_input, "seq", ahead)
+    seg_near = lax.ppermute(seg_own, "seq", ahead)
     far = lax.ppermute(near, "seq", ahead)
-    seg_all = jnp.concatenate(
-        [far[rows:rows + 1, :rows], near[rows:rows + 1, :rows], numbers[:1, :rows]], axis=1
-    ).astype(jnp.int32)
+    seg_far = lax.ppermute(seg_near, "seq", ahead)
+    seg_all = jnp.concatenate([seg_far, seg_near, seg_own], axis=1)
     seg_k_row = jnp.broadcast_to(seg_all, (8, halo + rows))
     seg_k_col = jnp.broadcast_to(seg_all.reshape(-1, 1), (halo + rows, 128))
     seg_q_row = seg_k_row[:, halo:]
@@ -710,10 +707,11 @@
     scatter_chips = lambda v: lax.psum_scatter(
         v, "dp", scatter_dimension=0, tiled=True, axis_index_groups=same_core
     )
-    *so_far, grads = call(0, 1, ())
-    *so_far, grads_next, grads_last = call(1, 2, tuple(so_far))
+    so_far, shards = (), []
+    for third_at in range(3):
+        *so_far, grads = call(third_at, 1, tuple(so_far))
+        shards.append(scatter_chips(grads)[0])
     out_own, out_part, gnorm_own, gnorm_part = so_far
-    shards = [scatter_chips(value) for value in (grads, grads_next, grads_last)]
     given = swap(gnorm_part)
 
     shift = lambda v, bit: lax.ppermute(v, "seq", [(i, i ^ bit) for i in range(groups)])
@@ -782,19 +780,19 @@
 
     wq, wk, wv = (qkv_full[:, i * model:(i + 1) * model] for i in range(3))
     part_far = outer_cols(dk[:rows], wk) + outer_cols(dv[:rows], wv)
-    dk_rest, dv_rest, far, near, part_far, line_c = together(
-        (dk[rows:], dv[rows:], far, near, part_far, line_c)
-    )
-    ends_c = line_end(line_c)
+    dk_rest, dv_rest, far, near, part_far = together((dk[rows:], dv[rows:], far, near, part_far))
     given_near = lax.ppermute(part_far, "seq", behind)
     part_rest = outer_cols(dk_rest, wk) + outer_cols(dv_rest, wv)
     own_part = part_rest[rows:] + outer_cols(dq, wq)
-    back_near = part_rest[:rows] + given_near
+    line_c, part_rest = together((line_c, part_rest))
+    ends_c = line_end(line_c)
+    (near_rows,) = together((part_rest[:rows],))
+    back_near = near_rows + given_near
 
     xhat1, rate1 = norm_stats(block_input)
     terms = (
-        (norm_stats(far[:rows])[0], part_far),
-        (norm_stats(near[:rows])[0], part_rest[:rows]),
+        (norm_stats(far)[0], part_far),
+        (norm_stats(near)[0], part_rest[:rows]),
         (xhat1, own_part),
     )
     grad_gain_one = sum(jnp.sum(xhat * part, axis=0) for xhat, part in terms)
@@ -811,7 +809,7 @@
     while bit < devices:
         small = small + exchange(small, bit)
         bit *= 2
-    shard_c, ends_c, back_near, small = together((shard_c, ends_c, back_near, small))
+    shard_c, back_near, small = together((shard_c, back_near, small))
     last = line_middle(line_start(shard_c[None]))
     given_back = lax.ppermute(back_near, "seq", behind)
     grad_up, grad_down = unpack_grads(

time: 544 us -> 523 us (0.961)
  waiting for transfers between devices: 180 us -> 140 us
  starting transfers between devices: 35.3 us -> 51.1 us
  matrix products: 20.2 us -> 26.4 us
    ppermute x17, waiting for transfers between devices: 52.8 us -> 16.8 us  [body(): lax.ppermute(v, 'dp', [(i, i ^ bit) for i in range(devices)])]
    ppermute x1, waiting for transfers between devices: 24.7 us -> 0.01 us  [body(): given_near = lax.ppermute(part_far, 'seq', behind)]
    ppermute x1 -> x3, waiting for transfers between devices: 16.8 us -> 29.9 us  [the longest x1 18 us: body(): near = lax.ppermute(block_input, 'seq', ahead)]
    ppermute x1 -> x3, starting transfers between devices: 5.96 us -> 13.2 us  [the longest x1 4.69 us: body(): seg_far = lax.ppermute(seg_near, 'seq', ahead)]
    dot_general x5, matrix products: 16.5 us -> 22.7 us  [outer_cols(): lax.dot_general(left, right, (((1,), (1,)), ((), ())), precision=HIGH)]
    ppermute x14, starting transfers between devices: 12.8 us -> 18.4 us  [body(): lax.ppermute(v, 'seq', [(i, i ^ bit) for i in range(groups)])]
    pallas_call x2 -> x3, Pallas kernels: 69.2 us -> 71.2 us  [mlp(): pl.pallas_call(functools.partial(mlp_kernel, len(ups), len(so_far) // 4),...]
  transfers between devices with their start and end apart: 41 -> 43, of which waited for: 17 -> 18; matrix products, arithmetic and copies ran while one was open for 18% -> 20% of each run, Pallas kernels for 33% -> 32%
where the time goes in v9:
time: 523 us; the launch traced here: 518 us
  Pallas kernels  197 us (38%)
  waiting for transfers between devices  140 us (27%)
  starting transfers between devices  51.1 us (10%)
  other arithmetic  47.3 us (9%)
  local copies, waits for them, and re-layouts  42 us (8%)
  matrix products  26.4 us (5%)
  between operations  15.5 us (3%)
    ppermute x14, waiting for transfers between devices, body(): lax.ppermute(v, 'seq', [(i, i ^ bit) for i in range(groups)])  87.8 us
    pallas_call x3, Pallas kernels, mlp(): pl.pallas_call(functools.partial(mlp_kernel, len(ups), len(so_far) // 4),...  71.2 us
    pallas_call x2, Pallas kernels, attend_back(): pl.pallas_call(attend_back_kernel, grid=(count,), in_specs=[pl.BlockSpec(...  46.8 us
    pallas_call x2, Pallas kernels, weight_call(): pl.pallas_call(kernel, grid_spec=pltpu.PrefetchScalarGridSpec(num_scalar_...  26.4 us
    pallas_call x1, Pallas kernels, attend(): pl.pallas_call(attend_kernel, grid=(pairs,), in_specs=[pl.BlockSpec((rows...  23.2 us
    dot_general x5, matrix products, outer_cols(): lax.dot_general(left, right, (((1,), (1,)), ((), ())), precision=HIGH)  22.7 us
    pallas_call x1, Pallas kernels, project(): pl.pallas_call(qkv_kernel, grid=(3 * third,), in_specs=[whole((rows, mode...  21.7 us
    ppermute x14, starting transfers between devices, body(): lax.ppermute(v, 'seq', [(i, i ^ bit) for i in range(groups)])  18.4 us
  transfers between devices with their start and end apart: 43, of which 18 were waited for; matrix products, arithmetic and copies ran while one was open for 20% of the time, Pallas kernels for 32%

profile of v9, /device:TPU:0, one launch (start us, length us, event | category | flops | bytes accessed | tf_op | source)
XLA Modules:
  0.0 518.4 jit_solution(9605608208877583581)
XLA Ops:
  11.9 4.6 collective-permute-start
  24.2 18.0 %collective-permute-done.near_ref = f32[384,768]{1,0:T(8,128)S(1)} collective-permute-done((f32[384,768]{1,0:T(8,128)S(1)}, f32[384,768]{1,0:T(8,128)S(1)}, u32[]{:S(2)}, u32[]{:S(2)}) %collective-permute-start) | collective-permute-done | bytes 1179680 | tf_op jit(solution)/shard_map/ppermute | solution.py:673
  42.3 4.4 collective-permute-start.1
  46.7 4.0 collective-permute-start.2
  51.4 7.4 %fusion.23 = (f32[]{:T(128)}, f32[]{:T(128)}, f32[]{:T(128)}, f32[]{:T(128)}, f32[384,768]{1,0:T(8,128)}) fusion(f32[384,768]{1,0:T(8,128)S(1)} %copy-done.14, f32[3,384,768]{2,1,0:T(8,128)} %param.18, f32[384,768]{1,0:T(8,128)} %param.17, f32[]{:T(128)} %bitcast.5, f32[]{:T(128)} %bitcast.3, f32[]{:T(128)} %bitcast.1, f32[]{:T(128)} %bitcast), kind=kLoop, calls=%fused_computation.39 | loop fusion | flops 4423676 | bytes 7077920 | tf_op jit(solution)/shard_map/reduce_sum | solution.py:689
  59.9 11.9 %collective-permute-done.2 = s32[1,384]{1,0:T(1,128)} collective-permute-done((s32[1,384]{1,0:T(1,128)S(1)}, s32[1,384]{1,0:T(1,128)}, u32[]{:S(2)}, u32[]{:S(2)}) %collective-permute-start.2) | collective-permute-done | bytes 1568 | tf_op jit(solution)/shard_map/ppermute | solution.py:674
  71.8 4.7 collective-permute-start.3
  76.5 3.1 pad_maximum_fusion.6
  86.1 21.7 %shard_map.239 = (f32[384,768]{1,0:T(8,128)}, f32[1152,1536]{1,0:T(8,128)}, bf16[1152,768]{1,0:T(8,128)(2,1)}, bf16[1152,768]{1,0:T(8,128)(2,1)}) custom-call(f32[384,768]{1,0:T(8,128)} %copy-done.3, f32[384,768]{1,0:T(8,128)} %copy-done.6, f32[384,768]{1,0:T(8,128)} %own_ref.1, f32[1,768]{1,0:T(1,128)} %broadcast_in_dim.50.gain_ref, ...), custom_call_target="tpu_custom_call" | custom-call | flops 22000001024 | bytes 1048576 | tf_op jit(solution)/shard_map/pallas_call | solution.py:144
  109.2 23.2 %shard_map.240.att_ref = f32[384,768]{1,0:T(8,128)} custom-call(f32[384,768]{1,0:T(8,128)} %get-tuple-element.135.q_ref, f32[1152,1536]{1,0:T(8,128)} %get-tuple-element.136.k_ref.v_ref, f32[1152,1536]{1,0:T(8,128)} %get-tuple-element.136.k_ref.v_ref, s32[384,128]{1,0:T(8,128)} %broadcast_in_dim.52.segq_ref, s32[8,1152]{1,0:T(8,128)} %broadcast_in_dim.54.segk_ref), custom_call_target="tpu_custom_call" | custom-call | flops 26400000000 | bytes 1048576 | tf_op jit(solution)/shard_map/pallas_call | solution.py:236
  132.5 3.7 convolution_add_fusion.resid_ref
  138.3 4.1 collective-permute-done.12.refs_7_
  145.4 29.1 %shard_map.241 = (f32[384,768]{1,0:T(8,128)}, f32[384,768]{1,0:T(8,128)}, f32[384,768]{1,0:T(8,128)}, f32[384,768]{1,0:T(8,128)}, f32[4,1,384,512]{3,2,1,0:T(8,128)}) custom-call(s32[1]{0:T(128)} %bitcast.12.chip_ref, f32[384,768]{1,0:T(8,128)} %copy-done.17, f32[384,768]{1,0:T(8,128)} %copy-done.48, f32[384,768]{1,0:T(8,128)} %cot_ref.7, ...), custom_call_target="tpu_custom_call" | custom-call | flops 19800000512 | bytes 1048576 | tf_op jit(solution)/shard_map/pallas_call | solution.py:454
  174.6 21.0 %shard_map.242 = (f32[384,768]{1,0:T(8,128)}, f32[384,768]{1,0:T(8,128)}, f32[384,768]{1,0:T(8,128)}, f32[384,768]{1,0:T(8,128)}, f32[4,1,384,512]{3,2,1,0:T(8,128)}) custom-call(s32[1]{0:T(128)} %bitcast.12.chip_ref, f32[384,768]{1,0:T(8,128)} %copy-done.17, f32[384,768]{1,0:T(8,128)} %copy-done.48, f32[384,768]{1,0:T(8,128)} %cot_ref.7, ...), custom_call_target="tpu_custom_call" | custom-call | flops 19800000512 | bytes 1048576 | tf_op jit(solution)/shard_map/pallas_call | solution.py:454
  195.8 21.1 %shard_map.243 = (f32[384,768]{1,0:T(8,128)}, f32[384,768]{1,0:T(8,128)}, f32[384,768]{1,0:T(8,128)}, f32[384,768]{1,0:T(8,128)}, f32[4,1,384,512]{3,2,1,0:T(8,128)}) custom-call(s32[1]{0:T(128)} %bitcast.12.chip_ref, f32[384,768]{1,0:T(8,128)} %copy-done.17, f32[384,768]{1,0:T(8,128)} %copy-done.48, f32[384,768]{1,0:T(8,128)} %cot_ref.7, ...), custom_call_target="tpu_custom_call" | custom-call | flops 19800000512 | bytes 1048576 | tf_op jit(solution)/shard_map/pallas_call | solution.py:454
  217.4 2.6 collective-permute-done.13.given_ref
  223.3 7.3 %shard_map.244 = (f32[384,768]{1,0:T(8,128)}, f32[384,768]{1,0:T(8,128)}, f32[8,768]{1,0:T(8,128)}) custom-call(f32[384,768]{1,0:T(8,128)} %get-tuple-element.118.part_ref, f32[384,768]{1,0:T(8,128)} %copy-done.49, f32[384,768]{1,0:T(8,128)} %copy-done.17, f32[384,768]{1,0:T(8,128)} %cot_ref.7, f32[1,768]{1,0:T(1,128)} %broadcast_in_dim.55.gain_ref, ...), custom_call_target="tpu_custom_call" | custom-call | flops 6600000000 | bytes 1048576 | tf_op jit(solution)/shard_map/pallas_call | solution.py:501
  230.6 2.2 collective-permute-done.14
  234.6 2.6 collective-permute-start.15
  237.2 23.3 %shard_map.245 = (f32[384,768]{1,0:T(8,128)}, f32[1152,768]{1,0:T(8,128)}, f32[1152,768]{1,0:T(8,128)}) custom-call(f32[384,768]{1,0:T(8,128)} %get-tuple-element.135.q_ref, f32[1152,1536]{1,0:T(8,128)} %get-tuple-element.136.k_ref.v_ref, f32[1152,1536]{1,0:T(8,128)} %get-tuple-element.136.k_ref.v_ref, f32[384,768]{1,0:T(8,128)} %get-tuple-element.137.g_ref, ...), custom_call_target="tpu_custom_call" | custom-call | flops 23100000256 | bytes 1048576 | tf_op jit(solution)/shard_map/pallas_call | solution.py:328
  260.6 4.2 reduce-scatter.15.cloned.1.call-done
  268.0 23.5 %shard_map.246 = (f32[384,768]{1,0:T(8,128)}, f32[1152,768]{1,0:T(8,128)}, f32[1152,768]{1,0:T(8,128)}) custom-call(f32[384,768]{1,0:T(8,128)} %get-tuple-element.135.q_ref, f32[1152,1536]{1,0:T(8,128)} %get-tuple-element.136.k_ref.v_ref, f32[1152,1536]{1,0:T(8,128)} %get-tuple-element.136.k_ref.v_ref, ...), custom_call_target="tpu_custom_call", output_to_operand_aliasing={{0}: (8, {}), {1}: (9, {}), {2}: (10, {})} | custom-call | flops 23100000256 | bytes 1048576 | tf_op jit(solution)/shard_map/pallas_call | solution.py:328
  292.6 2.4 collective-permute-start.19
  295.0 12.8 %shard_map.247 = (f32[4,96,1536]{2,1,0:T(8,128)}, f32[4,96,1536]{2,1,0:T(8,128)}) custom-call(s32[1]{0:T(128)} %bitcast.15.core_ref, bf16[1152,768]{1,0:T(8,128)(2,1)} %get-tuple-element.113.hi_ref, bf16[1152,768]{1,0:T(8,128)(2,1)} %get-tuple-element.114.lo_ref, f32[384,768]{1,0:T(8,128)} %get-tuple-element.148.dq_ref, f32[1152,768]{1,0:T(8,128)} %get-tuple-element.149.dk_ref), custom_call_target="tpu_custom_call" | custom-call | flops 9900000256 | bytes 1048576 | tf_op jit(solution)/shard_map/pallas_call | solution.py:587
  307.8 4.4 collective-permute-done.19
  315.5 13.6 %shard_map.248 = (f32[4,96,1536]{2,1,0:T(8,128)}, f32[4,96,1536]{2,1,0:T(8,128)}) custom-call(s32[1]{0:T(128)} %bitcast.15.core_ref, bf16[1152,768]{1,0:T(8,128)(2,1)} %get-tuple-element.113.hi_ref, bf16[1152,768]{1,0:T(8,128)(2,1)} %get-tuple-element.114.lo_ref, f32[1152,768]{1,0:T(8,128)} %get-tuple-element.158.dv_ref, f32[384,768]{1,0:T(8,128)} %shard_map.240.att_ref, ...), custom_call_target="tpu_custom_call" | custom-call | flops 9900000256 | bytes 1048576 | tf_op jit(solution)/shard_map/pallas_call | solution.py:587
  333.4 4.3 collective-permute-done.22
  338.1 2.5 pad_maximum_fusion
  343.7 3.3 slice.156
  348.6 3.4 fusion.4
  352.0 4.8 fusion.13
  360.5 5.2 %fusion.2 = f32[768,768]{1,0:T(8,128)S(1)} fusion(f32[768,768]{1,0:T(8,128)S(1)} %copy-done.9, f32[768,2304]{1,0:T(8,128)} %all-gather.3.cloned.1.call-done.w_ref), kind=kOutput, calls=%fused_computation.3 | convolution fusion | flops 2717908992 | bytes 7077888 | tf_op jit(solution)/shard_map/dot_general | solution.py:611
  365.7 4.9 fusion.10
  371.6 3.4 collective-permute-start.24
  375.1 4.5 fusion.27
  379.5 25.8 %collective-permute-done.24 = f32[1,192,512]{2,1,0:T(8,128)S(1)} collective-permute-done((f32[1,192,512]{2,1,0:T(8,128)S(1)}, f32[1,192,512]{2,1,0:T(8,128)S(1)}, u32[]{:S(2)}, u32[]{:S(2)}) %collective-permute-start.24) | collective-permute-done | bytes 393248 | tf_op jit(solution)/shard_map/ppermute | solution.py:717
  408.6 2.6 multiply_reduce_fusion.1
  417.4 2.4 collective-permute-done.27
  421.3 2.8 add.208
  428.1 5.5 %collective-permute-done.31 = f32[1,192,512]{2,1,0:T(8,128)} collective-permute-done((f32[1,192,512]{2,1,0:T(8,128)}, f32[1,192,512]{2,1,0:T(8,128)}, u32[]{:S(2)}, u32[]{:S(2)}) %collective-permute-start.31) | collective-permute-done | bytes 393248 | tf_op jit(solution)/shard_map/ppermute | solution.py:717
  437.8 8.4 %collective-permute-done.29 = f32[1,48,3072]{2,1,0:T(8,128)S(1)} collective-permute-done((f32[1,48,3072]{2,1,0:T(8,128)S(1)}, f32[1,48,3072]{2,1,0:T(8,128)S(1)}, u32[]{:S(2)}, u32[]{:S(2)}) %collective-permute-start.29) | collective-permute-done | bytes 589856 | tf_op jit(solution)/shard_map/ppermute | solution.py:717
  449.4 2.1 stack.30
  451.5 2.3 copy.39
  453.8 2.1 stack.29
  459.0 2.6 reshape.143
  461.6 29.0 %collective-permute-done.30 = f32[1,48,3072]{2,1,0:T(8,128)} collective-permute-done((f32[1,48,3072]{2,1,0:T(8,128)}, f32[1,48,3072]{2,1,0:T(8,128)}, u32[]{:S(2)}, u32[]{:S(2)}) %collective-permute-start.30) | collective-permute-done | bytes 589856 | tf_op jit(solution)/shard_map/ppermute | solution.py:717
  496.0 2.1 collective-permute-done.34
  499.6 8.4 %collective-permute-done.35 = f32[8,768]{1,0:T(8,128)S(1)} collective-permute-done((f32[8,768]{1,0:T(8,128)S(1)}, f32[8,768]{1,0:T(8,128)S(1)}, u32[]{:S(2)}, u32[]{:S(2)}) %collective-permute-start.35) | collective-permute-done | bytes 24608 | tf_op jit(solution)/shard_map/ppermute | solution.py:717
  (254 shorter events, 89.7 us)
Async XLA Ops:
  7.2 78.5 %all-gather.3.cloned.1.call-start = ((), (), s32[]{:S(2)}) async-start(), calls=%async_computation.4 | async-start | bytes 7962624 | tf_op jit(solution)/shard_map/all_gather | solution.py:649
  7.9 124.5 %all-gather.5.cloned.1.call-start = ((), (), s32[]{:S(2)}) async-start(), calls=%async_computation.5 | async-start | bytes 2654208 | tf_op jit(solution)/shard_map/all_gather | solution.py:649
  11.4 8.9 %collective-permute-start.6 = (f32[96,1536]{1,0:T(8,128)}, f32[96,1536]{1,0:T(8,128)}, u32[]{:S(2)}, u32[]{:S(2)}) collective-permute-start(f32[96,1536]{1,0:T(8,128)} %select_n.147), channel_id=1, source_target_pairs={{0,4},{4,0},{8,12},{12,8},{16,20},{20,16},{24,28},{28,24},{1,5},{5... | collective-permute-start | bytes 1769480 | tf_op jit(solution)/shard_map/ppermute | solution.py:646
  11.9 30.4 %collective-permute-start = (f32[384,768]{1,0:T(8,128)S(1)}, f32[384,768]{1,0:T(8,128)S(1)}, u32[]{:S(2)}, u32[]{:S(2)}) collective-permute-start(f32[384,768]{1,0:T(8,128)S(1)} %copy-done), channel_id=1, source_target_pairs={{0,1},{1,2},{2,3},{4,5},{5,6},{6,7},{8,9},{9,10},{10,11},{12,13},{... | collective-permute-start | bytes 3538952 | tf_op jit(solution)/shard_map/ppermute | solution.py:673
  16.5 66.6 %collective-permute-start.10 = (f32[384,768]{1,0:T(8,128)}, f32[384,768]{1,0:T(8,128)}, u32[]{:S(2)}, u32[]{:S(2)}) collective-permute-start(f32[384,768]{1,0:T(8,128)} %refs_4_.5), channel_id=1, source_target_pairs={{0,8},{4,12},{8,0},{12,4},{16,24},{20,28},{24,16},{28,20},{1,9},{5... | collective-permute-start | bytes 3538952 | tf_op jit(solution)/shard_map/ppermute | solution.py:646
  22.7 61.9 %collective-permute-start.8 = (f32[192,1536]{1,0:T(8,128)}, f32[192,1536]{1,0:T(8,128)}, u32[]{:S(2)}, u32[]{:S(2)}) collective-permute-start(f32[192,1536]{1,0:T(8,128)} %pad_maximum_fusion.3.refs_0_), channel_id=1, source_target_pairs={{0,16},{4,20},{8,24},{12,28},{16,0},{20,4},{24,8},{28,12},{1,17},{... | collective-permute-start | bytes 3538952 | tf_op jit(solution)/shard_map/ppermute | solution.py:646
  42.3 42.8 %collective-permute-start.1 = (f32[384,768]{1,0:T(8,128)S(1)}, f32[384,768]{1,0:T(8,128)S(1)}, u32[]{:S(2)}, u32[]{:S(2)}) collective-permute-start(f32[384,768]{1,0:T(8,128)S(1)} %collective-permute-done.near_ref), channel_id=1, source_target_pairs={{0,1},{1,2},{2,3},{4,5},{5,6},{6,7},{8,9},{9,10},{10,11},{12,13},{... | collective-permute-start | bytes 3538952 | tf_op jit(solution)/shard_map/ppermute | solution.py:675
  46.7 25.1 %collective-permute-start.2 = (s32[1,384]{1,0:T(1,128)S(1)}, s32[1,384]{1,0:T(1,128)}, u32[]{:S(2)}, u32[]{:S(2)}) collective-permute-start(s32[1,384]{1,0:T(1,128)S(1)} %get-tuple-element.224), channel_id=1, source_target_pairs={{0,1},{1,2},{2,3},{4,5},{5,6},{6,7},{8,9},{9,10},{10,11},{12,13},{... | collective-permute-start | bytes 4616 | tf_op jit(solution)/shard_map/ppermute | solution.py:674
  50.7 85.5 %collective-permute-start.5 = (f32[384,768]{1,0:T(8,128)S(1)}, f32[384,768]{1,0:T(8,128)}, u32[]{:S(2)}, u32[]{:S(2)}) collective-permute-start(f32[384,768]{1,0:T(8,128)S(1)} %copy-done.14), channel_id=1, source_target_pairs={{0,4},{4,0},{8,12},{12,8},{16,20},{20,16},{24,28},{28,24},{1,5},{5... | collective-permute-start | bytes 3538952 | tf_op jit(solution)/shard_map/ppermute | solution.py:646
  50.7 169.3 %reduce-scatter.13.cloned.1.call-start = ((), (), s32[]{:S(2)}) async-start(), calls=%async_computation.6 | async-start | bytes 3932160
  71.8 9.0 %collective-permute-start.3 = (s32[1,384]{1,0:T(1,128)}, s32[1,384]{1,0:T(1,128)S(1)}, u32[]{:S(2)}, u32[]{:S(2)}) collective-permute-start(s32[1,384]{1,0:T(1,128)} %collective-permute-done.2), channel_id=1, source_target_pairs={{0,1},{1,2},{2,3},{4,5},{5,6},{6,7},{8,9},{9,10},{10,11},{12,13},{... | collective-permute-start | bytes 4616 | tf_op jit(solution)/shard_map/ppermute | solution.py:676
  80.8 57.4 %collective-permute-start.11 = (f32[384,768]{1,0:T(8,128)}, f32[384,768]{1,0:T(8,128)}, u32[]{:S(2)}, u32[]{:S(2)}) collective-permute-start(f32[384,768]{1,0:T(8,128)} %refs_4_.5), channel_id=1, source_target_pairs={{0,16},{4,20},{8,24},{12,28},{16,0},{20,4},{24,8},{28,12},{1,17},{... | collective-permute-start | bytes 3538952 | tf_op jit(solution)/shard_map/ppermute | solution.py:646
  83.1 55.2 %collective-permute-start.7 = (f32[192,1536]{1,0:T(8,128)}, f32[192,1536]{1,0:T(8,128)}, u32[]{:S(2)}, u32[]{:S(2)}) collective-permute-start(f32[192,1536]{1,0:T(8,128)} %pad_maximum_fusion.3.refs_0_), channel_id=1, source_target_pairs={{0,8},{4,12},{8,0},{12,4},{16,24},{20,28},{24,16},{28,20},{1,9},{5... | collective-permute-start | bytes 3538952 | tf_op jit(solution)/shard_map/ppermute | solution.py:646
  84.6 57.8 %collective-permute-start.12 = (f32[384,768]{1,0:T(8,128)}, f32[384,768]{1,0:T(8,128)}, u32[]{:S(2)}, u32[]{:S(2)}) collective-permute-start(f32[384,768]{1,0:T(8,128)} %collective-permute-done.10.refs_5_), channel_id=1, source_target_pairs={{0,16},{4,20},{8,24},{12,28},{16,0},{20,4},{24,8},{28,12},{1,17},{... | collective-permute-start | bytes 3538952 | tf_op jit(solution)/shard_map/ppermute | solution.py:646
  85.1 59.3 %collective-permute-start.9 = (f32[192,1536]{1,0:T(8,128)}, f32[192,1536]{1,0:T(8,128)}, u32[]{:S(2)}, u32[]{:S(2)}) collective-permute-start(f32[192,1536]{1,0:T(8,128)} %collective-permute-done.8.refs_2_), channel_id=1, source_target_pairs={{0,8},{4,12},{8,0},{12,4},{16,24},{20,28},{24,16},{28,20},{1,9},{5... | collective-permute-start | bytes 3538952 | tf_op jit(solution)/shard_map/ppermute | solution.py:646
  136.2 8.2 %collective-permute-start.4 = (f32[384,768]{1,0:T(8,128)S(1)}, f32[384,768]{1,0:T(8,128)S(1)}, u32[]{:S(2)}, u32[]{:S(2)}) collective-permute-start(f32[384,768]{1,0:T(8,128)S(1)} %convolution_add_fusion.resid_ref), channel_id=1, source_target_pairs={{0,4},{4,0},{8,12},{12,8},{16,20},{20,16},{24,28},{28,24},{1,5},{5... | collective-permute-start | bytes 3538952 | tf_op jit(solution)/shard_map/ppermute | solution.py:646
  174.5 90.2 %reduce-scatter.15.cloned.1.call-start = ((), (), s32[]{:S(2)}) async-start(), calls=%async_computation.7 | async-start | bytes 3932160
  195.6 116.7 %reduce-scatter.17.cloned.1.call-start = ((), (), s32[]{:S(2)}) async-start(), calls=%async_computation.8 | async-start | bytes 3932160
  216.9 3.1 collective-permute-start.13
  217.0 207.7 %reduce-scatter.19.cloned.1.call-start = ((), (), s32[]{:S(2)}) async-start(), calls=%async_computation.9 | async-start | bytes 5898240
  221.6 11.2 %collective-permute-start.14 = (f32[1,192,512]{2,1,0:T(8,128)S(1)}, f32[1,192,512]{2,1,0:T(8,128)S(1)}, u32[]{:S(2)}, u32[]{:S(2)}) collective-permute-start(f32[1,192,512]{2,1,0:T(8,128)S(1)} %slice_select_fusion.7), channel_id=1, source_target_pairs={{0,1},{1,0},{2,3},{3,2},{4,5},{5,4},{6,7},{7,6},{8,9},{9,8},{10,11... | collective-permute-start | bytes 1179656 | tf_op jit(solution)/shard_map/ppermute | solution.py:717
  234.6 25.9 %collective-permute-start.15 = (f32[1,192,512]{2,1,0:T(8,128)S(1)}, f32[1,192,512]{2,1,0:T(8,128)S(1)}, u32[]{:S(2)}, u32[]{:S(2)}) collective-permute-start(f32[1,192,512]{2,1,0:T(8,128)S(1)} %select_add_fusion.3), channel_id=1, source_target_pairs={{0,2},{1,3},{2,0},{3,1},{4,6},{5,7},{6,4},{7,5},{8,10},{9,11},{10,... | collective-permute-start | bytes 1179656 | tf_op jit(solution)/shard_map/ppermute | solution.py:717
  265.9 25.5 %collective-permute-start.16 = (f32[1,192,512]{2,1,0:T(8,128)S(1)}, f32[1,192,512]{2,1,0:T(8,128)S(1)}, u32[]{:S(2)}, u32[]{:S(2)}) collective-permute-start(f32[1,192,512]{2,1,0:T(8,128)S(1)} %slice_select_fusion.6), channel_id=1, source_target_pairs={{0,1},{1,0},{2,3},{3,2},{4,5},{5,4},{6,7},{7,6},{8,9},{9,8},{10,11... | collective-permute-start | bytes 1179656 | tf_op jit(solution)/shard_map/ppermute | solution.py:717
  267.5 24.1 %collective-permute-start.17 = (f32[1,192,512]{2,1,0:T(8,128)S(1)}, f32[1,192,512]{2,1,0:T(8,128)S(1)}, u32[]{:S(2)}, u32[]{:S(2)}) collective-permute-start(f32[1,192,512]{2,1,0:T(8,128)S(1)} %add.195), channel_id=1, source_target_pairs={{0,1},{1,0},{2,3},{3,2},{4,5},{5,4},{6,7},{7,6},{8,9},{9,8},{10,11... | collective-permute-start | bytes 1179656 | tf_op jit(solution)/shard_map/ppermute | solution.py:717
  292.6 19.6 %collective-permute-start.19 = (f32[1,192,512]{2,1,0:T(8,128)S(1)}, f32[1,192,512]{2,1,0:T(8,128)S(1)}, u32[]{:S(2)}, u32[]{:S(2)}) collective-permute-start(f32[1,192,512]{2,1,0:T(8,128)S(1)} %select_add_fusion.2), channel_id=1, source_target_pairs={{0,2},{1,3},{2,0},{3,1},{4,6},{5,7},{6,4},{7,5},{8,10},{9,11},{10,... | collective-permute-start | bytes 1179656 | tf_op jit(solution)/shard_map/ppermute | solution.py:717
  307.8 25.2 %collective-permute-start.18 = (f32[4,96,1536]{2,1,0:T(8,128)}, f32[4,96,1536]{2,1,0:T(8,128)S(1)}, u32[]{:S(2)}, u32[]{:S(2)}) collective-permute-start(f32[4,96,1536]{2,1,0:T(8,128)} %get-tuple-element.151), channel_id=1, source_target_pairs={{0,4},{4,0},{8,12},{12,8},{16,20},{20,16},{24,28},{28,24},{1,5},{5... | collective-permute-start | bytes 7077896 | tf_op jit(solution)/shard_map/ppermute | solution.py:646
  313.5 15.7 %collective-permute-start.20 = (f32[1,192,512]{2,1,0:T(8,128)S(1)}, f32[1,192,512]{2,1,0:T(8,128)S(1)}, u32[]{:S(2)}, u32[]{:S(2)}) collective-permute-start(f32[1,192,512]{2,1,0:T(8,128)S(1)} %slice_select_fusion.5), channel_id=1, source_target_pairs={{0,1},{1,0},{2,3},{3,2},{4,5},{5,4},{6,7},{7,6},{8,9},{9,8},{10,11... | collective-permute-start | bytes 1179656 | tf_op jit(solution)/shard_map/ppermute | solution.py:717
  314.3 17.8 %collective-permute-start.21 = (f32[1,192,512]{2,1,0:T(8,128)S(1)}, f32[1,192,512]{2,1,0:T(8,128)S(1)}, u32[]{:S(2)}, u32[]{:S(2)}) collective-permute-start(f32[1,192,512]{2,1,0:T(8,128)S(1)} %add.198), channel_id=1, source_target_pairs={{0,1},{1,0},{2,3},{3,2},{4,5},{5,4},{6,7},{7,6},{8,9},{9,8},{10,11... | collective-permute-start | bytes 1179656 | tf_op jit(solution)/shard_map/ppermute | solution.py:717
  333.0 4.7 collective-permute-start.22
  342.3 32.8 %copy-start.38 = (f32[384]{0:T(512)}, f32[384]{0:T(512)S(1)}, u32[]{:S(2)}) copy-start(f32[384]{0:T(512)S(1)} %add_rsqrt_fusion.2) | copy-start | bytes 4612
  356.9 64.3 %collective-permute-start.25 = (f32[384,768]{1,0:T(8,128)}, f32[384,768]{1,0:T(8,128)}, u32[]{:S(2)}, u32[]{:S(2)}) collective-permute-start(f32[384,768]{1,0:T(8,128)} %fusion.13), channel_id=1, source_target_pairs={{1,0},{2,1},{3,2},{5,4},{6,5},{7,6},{9,8},{10,9},{11,10},{13,12},{... | collective-permute-start | bytes 3538952 | tf_op jit(solution)/shard_map/ppermute | solution.py:784
  370.6 37.9 %collective-permute-start.23 = (f32[384,768]{1,0:T(8,128)S(1)}, f32[384,768]{1,0:T(8,128)S(1)}, u32[]{:S(2)}, u32[]{:S(2)}) collective-permute-start(f32[384,768]{1,0:T(8,128)S(1)} %copy-done.47), channel_id=1, source_target_pairs={{0,4},{4,0},{8,12},{12,8},{16,20},{20,16},{24,28},{28,24},{1,5},{5... | collective-permute-start | bytes 3538952 | tf_op jit(solution)/shard_map/ppermute | solution.py:646
  371.6 33.7 %collective-permute-start.24 = (f32[1,192,512]{2,1,0:T(8,128)S(1)}, f32[1,192,512]{2,1,0:T(8,128)S(1)}, u32[]{:S(2)}, u32[]{:S(2)}) collective-permute-start(f32[1,192,512]{2,1,0:T(8,128)S(1)} %copy-done.31), channel_id=1, source_target_pairs={{0,2},{1,3},{2,0},{3,1},{4,6},{5,7},{6,4},{7,5},{8,10},{9,11},{10,... | collective-permute-start | bytes 1179656 | tf_op jit(solution)/shard_map/ppermute | solution.py:717
  375.1 33.5 %copy-start.33 = (f32[384,768]{1,0:T(8,128)S(1)}, f32[384,768]{1,0:T(8,128)}, u32[]{:S(2)}) copy-start(f32[384,768]{1,0:T(8,128)} %get-tuple-element.112) | copy-start | bytes 3538948
  413.8 1.4 collective-permute-start.26
  416.0 3.8 collective-permute-start.27
  419.8 4.2 collective-permute-start.28
  421.2 12.4 %collective-permute-start.31 = (f32[1,192,512]{2,1,0:T(8,128)}, f32[1,192,512]{2,1,0:T(8,128)}, u32[]{:S(2)}, u32[]{:S(2)}) collective-permute-start(f32[1,192,512]{2,1,0:T(8,128)} %add.207), channel_id=1, source_target_pairs={{0,1},{1,0},{2,3},{3,2},{4,5},{5,4},{6,7},{7,6},{8,9},{9,8},{10,11... | collective-permute-start | bytes 1179656 | tf_op jit(solution)/shard_map/ppermute | solution.py:717
  426.0 20.1 %collective-permute-start.29 = (f32[1,48,3072]{2,1,0:T(8,128)S(1)}, f32[1,48,3072]{2,1,0:T(8,128)S(1)}, u32[]{:S(2)}, u32[]{:S(2)}) collective-permute-start(f32[1,48,3072]{2,1,0:T(8,128)S(1)} %slice_select_fusion.4), channel_id=1, source_target_pairs={{0,1},{1,0},{2,3},{3,2},{4,5},{5,4},{6,7},{7,6},{8,9},{9,8},{10,11... | collective-permute-start | bytes 1769480 | tf_op jit(solution)/shard_map/ppermute | solution.py:717
  434.9 13.2 %collective-permute-start.32 = (f32[3,96,512]{2,1,0:T(8,128)S(1)}, f32[3,96,512]{2,1,0:T(8,128)S(1)}, u32[]{:S(2)}, u32[]{:S(2)}) collective-permute-start(f32[3,96,512]{2,1,0:T(8,128)S(1)} %slice_select_fusion.2), channel_id=1, source_target_pairs={{0,4},{4,0},{8,12},{12,8},{16,20},{20,16},{24,28},{28,24},{1,5},{5... | collective-permute-start | bytes 1769480 | tf_op jit(solution)/shard_map/ppermute | solution.py:646
  436.1 55.8 %collective-permute-start.33 = (f32[384,768]{1,0:T(8,128)}, f32[384,768]{1,0:T(8,128)}, u32[]{:S(2)}, u32[]{:S(2)}) collective-permute-start(f32[384,768]{1,0:T(8,128)} %add.208), channel_id=1, source_target_pairs={{1,0},{2,1},{3,2},{5,4},{6,5},{7,6},{9,8},{10,9},{11,10},{13,12},{... | collective-permute-start | bytes 3538952 | tf_op jit(solution)/shard_map/ppermute | solution.py:814
  447.1 43.5 %collective-permute-start.30 = (f32[1,48,3072]{2,1,0:T(8,128)}, f32[1,48,3072]{2,1,0:T(8,128)}, u32[]{:S(2)}, u32[]{:S(2)}) collective-permute-start(f32[1,48,3072]{2,1,0:T(8,128)} %select_add_fusion), channel_id=1, source_target_pairs={{0,2},{1,3},{2,0},{3,1},{4,6},{5,7},{6,4},{7,5},{8,10},{9,11},{10,... | collective-permute-start | bytes 1769480 | tf_op jit(solution)/shard_map/ppermute | solution.py:717
  461.6 30.3 %copy-start.13 = (f32[384,768]{1,0:T(8,128)S(1)}, f32[384,768]{1,0:T(8,128)}, u32[]{:S(2)}) copy-start(f32[384,768]{1,0:T(8,128)} %get-tuple-element.231) | copy-start | bytes 3538948
  461.6 30.3 %copy-start.39 = (f32[384]{0:T(512)S(1)}, f32[384]{0:T(512)}, u32[]{:S(2)}) copy-start(f32[384]{0:T(512)} %copy-done.38) | copy-start | bytes 4612
  461.6 30.3 %copy-start.41 = (f32[768]{0:T(1024)S(1)}, f32[768]{0:T(1024)}, u32[]{:S(2)}) copy-start(f32[768]{0:T(1024)} %param.20) | copy-start | bytes 9220
  493.9 4.2 collective-permute-start.34
  494.0 15.1 %collective-permute-start.36 = (f32[1,48,3072]{2,1,0:T(8,128)S(1)}, f32[1,48,3072]{2,1,0:T(8,128)S(1)}, u32[]{:S(2)}, u32[]{:S(2)}) collective-permute-start(f32[1,48,3072]{2,1,0:T(8,128)S(1)} %add.221), channel_id=1, source_target_pairs={{0,1},{1,0},{2,3},{3,2},{4,5},{5,4},{6,7},{7,6},{8,9},{9,8},{10,11... | collective-permute-start | bytes 1769480 | tf_op jit(solution)/shard_map/ppermute | solution.py:717
  498.1 9.8 %collective-permute-start.35 = (f32[8,768]{1,0:T(8,128)S(1)}, f32[8,768]{1,0:T(8,128)S(1)}, u32[]{:S(2)}, u32[]{:S(2)}) collective-permute-start(f32[8,768]{1,0:T(8,128)S(1)} %add.224), channel_id=1, source_target_pairs={{0,2},{1,3},{2,0},{3,1},{4,6},{5,7},{6,4},{7,5},{8,10},{9,11},{10,... | collective-permute-start | bytes 73736 | tf_op jit(solution)/shard_map/ppermute | solution.py:717
  (45 other events, 382.2 us)
Sparse Core Ops, SparseCore 0:
  9.9 69.1 all-gather.2
  81.0 38.7 all-gather.4
  174.7 43.2 reduce-scatter.12
  220.8 43.9 reduce-scatter.14
  267.6 43.9 reduce-scatter.16
  340.7 57.9 reduce-scatter.18

commit v10 on v9

--- a/solution.py
+++ b/solution.py
@@ -357,9 +357,9 @@
                scale_ref, *refs):
     up_refs, down_refs = refs[:count], refs[count:2 * count]
     refs = refs[2 * count:]
-    so_far, refs = refs[:4 * begun], refs[4 * begun:]
-    sums, grad_ref = refs[:4], refs[4]
-    (x_hi, x_lo, xt_hi, xt_lo, g_hi, g_lo, up_hi, up_lo, down_hi, down_lo) = refs[5:]
+    so_far, refs = refs[:2 * begun], refs[2 * begun:]
+    out_ref, gnorm_ref, grad_ref = refs[:3]
+    (x_hi, x_lo, xt_hi, xt_lo, g_hi, g_lo, up_hi, up_lo, down_hi, down_lo) = refs[3:]
     step = pl.program_id(0)
     rows = resid_ref.shape[0]
 
@@ -371,8 +371,12 @@
             x_hi[at:at + rows], x_lo[at:at + rows] = split(normed)
             xt_hi[:, at:at + rows], xt_lo[:, at:at + rows] = split(normed.T)
             g_hi[at:at + rows], g_lo[at:at + rows] = split(cot[...] * scale_ref[0, 0])
-        for at, ref in enumerate(sums):
-            ref[...] = so_far[at][...] if begun else jnp.zeros_like(ref)
+        if begun:
+            out_ref[...] = so_far[0][...]
+            gnorm_ref[...] = so_far[1][...]
+        else:
+            out_ref[...] = jnp.zeros_like(out_ref)
+            gnorm_ref[...] = jnp.zeros_like(gnorm_ref)
 
     for at in range(count):
         spot = (chip_ref[0] ^ at) if count > 1 else 0
@@ -404,9 +408,8 @@
     )
     act2 = split(act)
     grad_pre = split(grad_act * slope)
-    for at, total in enumerate((three(dot_nn, act2, down), three(dot_nt, grad_pre, up))):
-        sums[2 * at][...] += total[:rows]
-        sums[2 * at + 1][...] += total[rows:]
+    out_ref[...] += three(dot_nn, act2, down)
+    gnorm_ref[...] += three(dot_nt, grad_pre, up)
     gup = three(dot_nn, normed_t, grad_pre)
     gdown = three(dot_tn, act2, grad_block)
     half = deep // 2
@@ -438,9 +441,9 @@
         + [pl.BlockSpec(memory_space=pltpu.SMEM)]
         + [pl.BlockSpec((up.shape[0], width), lambda j, c: (0, first + j)) for up in ups]
         + [down_spec] * len(downs)
-        + [fixed((rows, model))] * len(so_far),
+        + [fixed((2 * rows, model))] * len(so_far),
         out_specs=[
-            *[fixed((rows, model))] * 4,
+            fixed((2 * rows, model)), fixed((2 * rows, model)),
             pl.BlockSpec((chips, 1, tall, width), lambda j, c: (0, j, 0, 0)),
         ],
         scratch_shapes=[
@@ -452,10 +455,11 @@
         ],
     )
     return pl.pallas_call(
-        functools.partial(mlp_kernel, len(ups), len(so_far) // 4),
+        functools.partial(mlp_kernel, len(ups), len(so_far) // 2),
         grid_spec=grid_spec,
         out_shape=[
-            *[jax.ShapeDtypeStruct((rows, model), F32)] * 4,
+            jax.ShapeDtypeStruct((2 * rows, model), F32),
+            jax.ShapeDtypeStruct((2 * rows, model), F32),
             jax.ShapeDtypeStruct((chips, steps, tall, width), F32),
         ],
         cost_estimate=cost(18 * steps),
@@ -709,10 +713,10 @@
     )
     so_far, shards = (), []
     for third_at in range(3):
-        *so_far, grads = call(third_at, 1, tuple(so_far))
+        out_part, gnorm_part, grads = call(third_at, 1, so_far)
+        so_far = (out_part, gnorm_part)
         shards.append(scatter_chips(grads)[0])
-    out_own, out_part, gnorm_own, gnorm_part = so_far
-    given = swap(gnorm_part)
+    given = swap(gnorm_part[rows:])
 
     shift = lambda v, bit: lax.ppermute(v, "seq", [(i, i ^ bit) for i in range(groups)])
     even = place % 2 == 0
@@ -738,7 +742,7 @@
     shards[0], given = together((shards[0], given))
     line_a = line_start(shards[0])
     grad_resid, grad_attended, sums_two = resid_back(
-        gnorm_own, given, resid, cotangent, gain2, scale, out_full
+        gnorm_part, given, resid, cotangent, gain2, scale, out_full
     )
 
     back_args = (q_rot, kv, grad_attended, seg_q_row, seg_k_col, cosine, sine)
@@ -772,20 +776,20 @@
     grads_c = jnp.concatenate([grads_qk[0] + given_qk, grads_vo[0] + swap(grads_vo[1])], axis=2)
     grads_c, out_part = together((grads_c, out_part))
     shard_c = scatter_chips(grads_c)[0]
-    out_sib = swap(out_part)
-
-    block_out = resid + out_own + out_sib
+    out_sib = swap(out_part[rows:])
+
+    block_out = resid + out_part[:rows] + out_sib
     output = base + dwa_weights[4] * block_out
     dwa_local = jnp.concatenate([dots, jnp.sum(cotangent * block_out)[None]])
 
     wq, wk, wv = (qkv_full[:, i * model:(i + 1) * model] for i in range(3))
+    line_c, dk = together((line_c, dk))
+    ends_c = line_end(line_c)
     part_far = outer_cols(dk[:rows], wk) + outer_cols(dv[:rows], wv)
     dk_rest, dv_rest, far, near, part_far = together((dk[rows:], dv[rows:], far, near, part_far))
     given_near = lax.ppermute(part_far, "seq", behind)
     part_rest = outer_cols(dk_rest, wk) + outer_cols(dv_rest, wv)
     own_part = part_rest[rows:] + outer_cols(dq, wq)
-    line_c, part_rest = together((line_c, part_rest))
-    ends_c = line_end(line_c)
     (near_rows,) = together((part_rest[:rows],))
     back_near = near_rows + given_near
 

time: 523 us -> 508 us (0.971)
  waiting for transfers between devices: 140 us -> 120 us
    ppermute x14, waiting for transfers between devices: 87.8 us -> 70.2 us  [body(): lax.ppermute(v, 'seq', [(i, i ^ bit) for i in range(groups)])]
  transfers between devices with their start and end apart: 43 -> 43, of which waited for: 18 -> 18; matrix products, arithmetic and copies ran while one was open for 20% -> 20% of each run, Pallas kernels for 32% -> 33%
where the time goes in v10:
time: 508 us; the launch traced here: 503 us
  Pallas kernels  197 us (39%)
  waiting for transfers between devices  120 us (24%)
  starting transfers between devices  54 us (11%)
  other arithmetic  47.1 us (9%)
  local copies, waits for them, and re-layouts  43.2 us (9%)
  matrix products  26 us (5%)
  between operations  15.5 us (3%)
    pallas_call x3, Pallas kernels, mlp(): pl.pallas_call(functools.partial(mlp_kernel, len(ups), len(so_far) // 2),...  71.2 us
    ppermute x14, waiting for transfers between devices, body(): lax.ppermute(v, 'seq', [(i, i ^ bit) for i in range(groups)])  70.2 us
    pallas_call x2, Pallas kernels, attend_back(): pl.pallas_call(attend_back_kernel, grid=(count,), in_specs=[pl.BlockSpec(...  47 us
    pallas_call x2, Pallas kernels, weight_call(): pl.pallas_call(kernel, grid_spec=pltpu.PrefetchScalarGridSpec(num_scalar_...  26.4 us
    pallas_call x1, Pallas kernels, attend(): pl.pallas_call(attend_kernel, grid=(pairs,), in_specs=[pl.BlockSpec((rows...  23.2 us
    dot_general x5, matrix products, outer_cols(): lax.dot_general(left, right, (((1,), (1,)), ((), ())), precision=HIGH)  22.3 us
    pallas_call x1, Pallas kernels, project(): pl.pallas_call(qkv_kernel, grid=(3 * third,), in_specs=[whole((rows, mode...  21.7 us
    ppermute x14, starting transfers between devices, body(): lax.ppermute(v, 'seq', [(i, i ^ bit) for i in range(groups)])  21.3 us
  transfers between devices with their start and end apart: 43, of which 18 were waited for; matrix products, arithmetic and copies ran while one was open for 20% of the time, Pallas kernels for 33%

profile of v10, /device:TPU:0, one launch (start us, length us, event | category | flops | bytes accessed | tf_op | source)
XLA Modules:
  0.0 503.2 jit_solution(707693147300531095)
XLA Ops:
  11.9 4.6 collective-permute-start
  24.2 18.0 %collective-permute-done.near_ref = f32[384,768]{1,0:T(8,128)S(1)} collective-permute-done((f32[384,768]{1,0:T(8,128)S(1)}, f32[384,768]{1,0:T(8,128)S(1)}, u32[]{:S(2)}, u32[]{:S(2)}) %collective-permute-start) | collective-permute-done | bytes 1179680 | tf_op jit(solution)/shard_map/ppermute | solution.py:677
  42.3 4.4 collective-permute-start.1
  46.7 3.9 collective-permute-start.2
  51.4 7.4 %fusion.23 = (f32[]{:T(128)}, f32[]{:T(128)}, f32[]{:T(128)}, f32[]{:T(128)}, f32[384,768]{1,0:T(8,128)}) fusion(f32[384,768]{1,0:T(8,128)S(1)} %copy-done.15, f32[3,384,768]{2,1,0:T(8,128)} %param.18, f32[384,768]{1,0:T(8,128)} %param.17, f32[]{:T(128)} %bitcast.5, f32[]{:T(128)} %bitcast.3, f32[]{:T(128)} %bitcast.1, f32[]{:T(128)} %bitcast), kind=kLoop, calls=%fused_computation.39 | loop fusion | flops 4423676 | bytes 7077920 | tf_op jit(solution)/shard_map/reduce_sum | solution.py:693
  59.9 11.9 %collective-permute-done.2 = s32[1,384]{1,0:T(1,128)} collective-permute-done((s32[1,384]{1,0:T(1,128)S(1)}, s32[1,384]{1,0:T(1,128)}, u32[]{:S(2)}, u32[]{:S(2)}) %collective-permute-start.2) | collective-permute-done | bytes 1568 | tf_op jit(solution)/shard_map/ppermute | solution.py:678
  71.8 4.7 collective-permute-start.3
  76.5 3.2 pad_maximum_fusion.6
  86.1 21.7 %shard_map.239 = (f32[384,768]{1,0:T(8,128)}, f32[1152,1536]{1,0:T(8,128)}, bf16[1152,768]{1,0:T(8,128)(2,1)}, bf16[1152,768]{1,0:T(8,128)(2,1)}) custom-call(f32[384,768]{1,0:T(8,128)} %copy-done.3, f32[384,768]{1,0:T(8,128)} %copy-done.6, f32[384,768]{1,0:T(8,128)} %own_ref.1, f32[1,768]{1,0:T(1,128)} %broadcast_in_dim.50.gain_ref, ...), custom_call_target="tpu_custom_call" | custom-call | flops 22000001024 | bytes 1048576 | tf_op jit(solution)/shard_map/pallas_call | solution.py:144
  109.3 23.2 %shard_map.240.att_ref = f32[384,768]{1,0:T(8,128)} custom-call(f32[384,768]{1,0:T(8,128)} %get-tuple-element.123.q_ref, f32[1152,1536]{1,0:T(8,128)} %get-tuple-element.124.k_ref.v_ref, f32[1152,1536]{1,0:T(8,128)} %get-tuple-element.124.k_ref.v_ref, s32[384,128]{1,0:T(8,128)} %broadcast_in_dim.52.segq_ref, s32[8,1152]{1,0:T(8,128)} %broadcast_in_dim.54.segk_ref), custom_call_target="tpu_custom_call" | custom-call | flops 26400000000 | bytes 1048576 | tf_op jit(solution)/shard_map/pallas_call | solution.py:236
  132.5 3.7 convolution_add_fusion.resid_ref
  138.3 4.1 collective-permute-done.12.refs_7_
  145.5 29.1 %shard_map.241 = (f32[768,768]{1,0:T(8,128)}, f32[768,768]{1,0:T(8,128)}, f32[4,1,384,512]{3,2,1,0:T(8,128)}) custom-call(s32[1]{0:T(128)} %bitcast.13.chip_ref, f32[384,768]{1,0:T(8,128)} %copy-done.18, f32[384,768]{1,0:T(8,128)} %copy-done.48, f32[384,768]{1,0:T(8,128)} %cot_ref.7, f32[384,768]{1,0:T(8,128)} %collective-permute-done.5.cot_other_ref, ...), custom_call_target="tpu_custom_call" | custom-call | flops 19800000512 | bytes 1048576 | tf_op jit(solution)/shard_map/pallas_call | solution.py:457
  174.6 21.0 %shard_map.242 = (f32[768,768]{1,0:T(8,128)}, f32[768,768]{1,0:T(8,128)}, f32[4,1,384,512]{3,2,1,0:T(8,128)}) custom-call(s32[1]{0:T(128)} %bitcast.13.chip_ref, f32[384,768]{1,0:T(8,128)} %copy-done.18, f32[384,768]{1,0:T(8,128)} %copy-done.48, f32[384,768]{1,0:T(8,128)} %cot_ref.7, f32[384,768]{1,0:T(8,128)} %collective-permute-done.5.cot_other_ref, ...), custom_call_target="tpu_custom_call" | custom-call | flops 19800000512 | bytes 1048576 | tf_op jit(solution)/shard_map/pallas_call | solution.py:457
  195.9 21.1 %shard_map.243 = (f32[768,768]{1,0:T(8,128)}, f32[768,768]{1,0:T(8,128)}, f32[4,1,384,512]{3,2,1,0:T(8,128)}) custom-call(s32[1]{0:T(128)} %bitcast.13.chip_ref, f32[384,768]{1,0:T(8,128)} %copy-done.18, f32[384,768]{1,0:T(8,128)} %copy-done.48, f32[384,768]{1,0:T(8,128)} %cot_ref.7, f32[384,768]{1,0:T(8,128)} %collective-permute-done.5.cot_other_ref, ...), custom_call_target="tpu_custom_call" | custom-call | flops 19800000512 | bytes 1048576 | tf_op jit(solution)/shard_map/pallas_call | solution.py:457
  219.0 2.3 collective-permute-done.13.given_ref
  224.6 7.7 %shard_map.244 = (f32[384,768]{1,0:T(8,128)}, f32[384,768]{1,0:T(8,128)}, f32[8,768]{1,0:T(8,128)}) custom-call(f32[768,768]{1,0:T(8,128)} %get-tuple-element.105.part_ref, f32[384,768]{1,0:T(8,128)} %copy-done.49, f32[384,768]{1,0:T(8,128)} %copy-done.18, f32[384,768]{1,0:T(8,128)} %cot_ref.7, f32[1,768]{1,0:T(1,128)} %broadcast_in_dim.55.gain_ref, ...), custom_call_target="tpu_custom_call" | custom-call | flops 6600000000 | bytes 1048576 | tf_op jit(solution)/shard_map/pallas_call | solution.py:505
  235.9 2.6 collective-permute-start.15
  238.5 23.5 %shard_map.245 = (f32[384,768]{1,0:T(8,128)}, f32[1152,768]{1,0:T(8,128)}, f32[1152,768]{1,0:T(8,128)}) custom-call(f32[384,768]{1,0:T(8,128)} %get-tuple-element.123.q_ref, f32[1152,1536]{1,0:T(8,128)} %get-tuple-element.124.k_ref.v_ref, f32[1152,1536]{1,0:T(8,128)} %get-tuple-element.124.k_ref.v_ref, f32[384,768]{1,0:T(8,128)} %get-tuple-element.125.g_ref, ...), custom_call_target="tpu_custom_call" | custom-call | flops 23100000256 | bytes 1048576 | tf_op jit(solution)/shard_map/pallas_call | solution.py:328
  262.1 2.7 reduce-scatter.15.cloned.1.call-done
  268.0 23.4 %shard_map.246 = (f32[384,768]{1,0:T(8,128)}, f32[1152,768]{1,0:T(8,128)}, f32[1152,768]{1,0:T(8,128)}) custom-call(f32[384,768]{1,0:T(8,128)} %get-tuple-element.123.q_ref, f32[1152,1536]{1,0:T(8,128)} %get-tuple-element.124.k_ref.v_ref, f32[1152,1536]{1,0:T(8,128)} %get-tuple-element.124.k_ref.v_ref, ...), custom_call_target="tpu_custom_call", output_to_operand_aliasing={{0}: (8, {}), {1}: (9, {}), {2}: (10, {})} | custom-call | flops 23100000256 | bytes 1048576 | tf_op jit(solution)/shard_map/pallas_call | solution.py:328
  292.6 2.4 collective-permute-start.19
  295.0 12.8 %shard_map.247 = (f32[4,96,1536]{2,1,0:T(8,128)}, f32[4,96,1536]{2,1,0:T(8,128)}) custom-call(s32[1]{0:T(128)} %bitcast.12.core_ref, bf16[1152,768]{1,0:T(8,128)(2,1)} %get-tuple-element.98.hi_ref, bf16[1152,768]{1,0:T(8,128)(2,1)} %get-tuple-element.99.lo_ref, f32[384,768]{1,0:T(8,128)} %get-tuple-element.136.dq_ref, f32[1152,768]{1,0:T(8,128)} %get-tuple-element.155.dk_ref), custom_call_target="tpu_custom_call" | custom-call | flops 9900000256 | bytes 1048576 | tf_op jit(solution)/shard_map/pallas_call | solution.py:591
  307.8 4.4 collective-permute-done.19
  315.6 13.6 %shard_map.248 = (f32[4,96,1536]{2,1,0:T(8,128)}, f32[4,96,1536]{2,1,0:T(8,128)}) custom-call(s32[1]{0:T(128)} %bitcast.12.core_ref, bf16[1152,768]{1,0:T(8,128)(2,1)} %get-tuple-element.98.hi_ref, bf16[1152,768]{1,0:T(8,128)(2,1)} %get-tuple-element.99.lo_ref, f32[1152,768]{1,0:T(8,128)} %get-tuple-element.146.dv_ref, f32[384,768]{1,0:T(8,128)} %shard_map.240.att_ref, ...), custom_call_target="tpu_custom_call" | custom-call | flops 9900000256 | bytes 1048576 | tf_op jit(solution)/shard_map/pallas_call | solution.py:591
  329.3 2.8 collective-permute-done.21
  333.5 4.3 collective-permute-done.22
  338.2 2.6 pad_maximum_fusion
  343.8 3.0 collective-permute-start.24
  346.9 4.5 fusion
  352.9 3.5 fusion.4
  356.4 8.3 %collective-permute-done.24 = f32[1,192,512]{2,1,0:T(8,128)S(1)} collective-permute-done((f32[1,192,512]{2,1,0:T(8,128)S(1)}, f32[1,192,512]{2,1,0:T(8,128)S(1)}, u32[]{:S(2)}, u32[]{:S(2)}) %collective-permute-start.24) | collective-permute-done | bytes 393248 | tf_op jit(solution)/shard_map/ppermute | solution.py:721
  367.1 4.5 fusion.13
  375.4 4.9 fusion.2
  380.3 4.9 fusion.10
  390.7 2.6 multiply_reduce_fusion.1
  399.5 2.4 collective-permute-done.27
  403.3 2.8 collective-permute-start.31
  406.1 2.8 add.208
  411.0 5.5 %collective-permute-done.31 = f32[1,192,512]{2,1,0:T(8,128)} collective-permute-done((f32[1,192,512]{2,1,0:T(8,128)}, f32[1,192,512]{2,1,0:T(8,128)}, u32[]{:S(2)}, u32[]{:S(2)}) %collective-permute-start.31) | collective-permute-done | bytes 393248 | tf_op jit(solution)/shard_map/ppermute | solution.py:721
  420.6 8.4 %collective-permute-done.29 = f32[1,48,3072]{2,1,0:T(8,128)S(1)} collective-permute-done((f32[1,48,3072]{2,1,0:T(8,128)S(1)}, f32[1,48,3072]{2,1,0:T(8,128)S(1)}, u32[]{:S(2)}, u32[]{:S(2)}) %collective-permute-start.29) | collective-permute-done | bytes 589856 | tf_op jit(solution)/shard_map/ppermute | solution.py:721
  430.0 2.5 collective-permute-start.30
  434.7 2.1 stack.30
  436.8 2.3 copy.39
  444.4 2.6 reshape.143
  447.0 28.5 %collective-permute-done.30 = f32[1,48,3072]{2,1,0:T(8,128)} collective-permute-done((f32[1,48,3072]{2,1,0:T(8,128)}, f32[1,48,3072]{2,1,0:T(8,128)}, u32[]{:S(2)}, u32[]{:S(2)}) %collective-permute-start.30) | collective-permute-done | bytes 589856 | tf_op jit(solution)/shard_map/ppermute | solution.py:721
  480.9 2.1 collective-permute-done.34
  484.4 8.4 %collective-permute-done.35 = f32[8,768]{1,0:T(8,128)S(1)} collective-permute-done((f32[8,768]{1,0:T(8,128)S(1)}, f32[8,768]{1,0:T(8,128)S(1)}, u32[]{:S(2)}, u32[]{:S(2)}) %collective-permute-start.35) | collective-permute-done | bytes 24608 | tf_op jit(solution)/shard_map/ppermute | solution.py:721
  (256 shorter events, 93.7 us)
Async XLA Ops:
  7.2 78.5 %all-gather.3.cloned.1.call-start = ((), (), s32[]{:S(2)}) async-start(), calls=%async_computation.4 | async-start | bytes 7962624 | tf_op jit(solution)/shard_map/all_gather | solution.py:653
  7.9 124.6 %all-gather.5.cloned.1.call-start = ((), (), s32[]{:S(2)}) async-start(), calls=%async_computation.5 | async-start | bytes 2654208 | tf_op jit(solution)/shard_map/all_gather | solution.py:653
  11.4 8.9 %collective-permute-start.6 = (f32[96,1536]{1,0:T(8,128)}, f32[96,1536]{1,0:T(8,128)}, u32[]{:S(2)}, u32[]{:S(2)}) collective-permute-start(f32[96,1536]{1,0:T(8,128)} %select_n.149), channel_id=1, source_target_pairs={{0,4},{4,0},{8,12},{12,8},{16,20},{20,16},{24,28},{28,24},{1,5},{5... | collective-permute-start | bytes 1769480 | tf_op jit(solution)/shard_map/ppermute | solution.py:650
  11.9 30.4 %collective-permute-start = (f32[384,768]{1,0:T(8,128)S(1)}, f32[384,768]{1,0:T(8,128)S(1)}, u32[]{:S(2)}, u32[]{:S(2)}) collective-permute-start(f32[384,768]{1,0:T(8,128)S(1)} %copy-done), channel_id=1, source_target_pairs={{0,1},{1,2},{2,3},{4,5},{5,6},{6,7},{8,9},{9,10},{10,11},{12,13},{... | collective-permute-start | bytes 3538952 | tf_op jit(solution)/shard_map/ppermute | solution.py:677
  16.5 66.6 %collective-permute-start.10 = (f32[384,768]{1,0:T(8,128)}, f32[384,768]{1,0:T(8,128)}, u32[]{:S(2)}, u32[]{:S(2)}) collective-permute-start(f32[384,768]{1,0:T(8,128)} %refs_4_.5), channel_id=1, source_target_pairs={{0,8},{4,12},{8,0},{12,4},{16,24},{20,28},{24,16},{28,20},{1,9},{5... | collective-permute-start | bytes 3538952 | tf_op jit(solution)/shard_map/ppermute | solution.py:650
  21.6 29.2 %copy-start.43 = (f32[5]{0:T(128)S(1)}, f32[5]{0:T(128)}, u32[]{:S(2)}) copy-start(f32[5]{0:T(128)} %param.19) | copy-start | bytes 64
  22.7 61.9 %collective-permute-start.8 = (f32[192,1536]{1,0:T(8,128)}, f32[192,1536]{1,0:T(8,128)}, u32[]{:S(2)}, u32[]{:S(2)}) collective-permute-start(f32[192,1536]{1,0:T(8,128)} %pad_maximum_fusion.3.refs_0_), channel_id=1, source_target_pairs={{0,16},{4,20},{8,24},{12,28},{16,0},{20,4},{24,8},{28,12},{1,17},{... | collective-permute-start | bytes 3538952 | tf_op jit(solution)/shard_map/ppermute | solution.py:650
  42.3 42.9 %collective-permute-start.1 = (f32[384,768]{1,0:T(8,128)S(1)}, f32[384,768]{1,0:T(8,128)S(1)}, u32[]{:S(2)}, u32[]{:S(2)}) collective-permute-start(f32[384,768]{1,0:T(8,128)S(1)} %collective-permute-done.near_ref), channel_id=1, source_target_pairs={{0,1},{1,2},{2,3},{4,5},{5,6},{6,7},{8,9},{9,10},{10,11},{12,13},{... | collective-permute-start | bytes 3538952 | tf_op jit(solution)/shard_map/ppermute | solution.py:679
  46.7 25.1 %collective-permute-start.2 = (s32[1,384]{1,0:T(1,128)S(1)}, s32[1,384]{1,0:T(1,128)}, u32[]{:S(2)}, u32[]{:S(2)}) collective-permute-start(s32[1,384]{1,0:T(1,128)S(1)} %get-tuple-element.212), channel_id=1, source_target_pairs={{0,1},{1,2},{2,3},{4,5},{5,6},{6,7},{8,9},{9,10},{10,11},{12,13},{... | collective-permute-start | bytes 4616 | tf_op jit(solution)/shard_map/ppermute | solution.py:678
  50.7 85.5 %collective-permute-start.5 = (f32[384,768]{1,0:T(8,128)S(1)}, f32[384,768]{1,0:T(8,128)}, u32[]{:S(2)}, u32[]{:S(2)}) collective-permute-start(f32[384,768]{1,0:T(8,128)S(1)} %copy-done.15), channel_id=1, source_target_pairs={{0,4},{4,0},{8,12},{12,8},{16,20},{20,16},{24,28},{28,24},{1,5},{5... | collective-permute-start | bytes 3538952 | tf_op jit(solution)/shard_map/ppermute | solution.py:650
  50.7 170.6 %reduce-scatter.13.cloned.1.call-start = ((), (), s32[]{:S(2)}) async-start(), calls=%async_computation.6 | async-start | bytes 3932160
  71.8 9.1 %collective-permute-start.3 = (s32[1,384]{1,0:T(1,128)}, s32[1,384]{1,0:T(1,128)S(1)}, u32[]{:S(2)}, u32[]{:S(2)}) collective-permute-start(s32[1,384]{1,0:T(1,128)} %collective-permute-done.2), channel_id=1, source_target_pairs={{0,1},{1,2},{2,3},{4,5},{5,6},{6,7},{8,9},{9,10},{10,11},{12,13},{... | collective-permute-start | bytes 4616 | tf_op jit(solution)/shard_map/ppermute | solution.py:680
  80.9 57.4 %collective-permute-start.11 = (f32[384,768]{1,0:T(8,128)}, f32[384,768]{1,0:T(8,128)}, u32[]{:S(2)}, u32[]{:S(2)}) collective-permute-start(f32[384,768]{1,0:T(8,128)} %refs_4_.5), channel_id=1, source_target_pairs={{0,16},{4,20},{8,24},{12,28},{16,0},{20,4},{24,8},{28,12},{1,17},{... | collective-permute-start | bytes 3538952 | tf_op jit(solution)/shard_map/ppermute | solution.py:650
  83.1 55.2 %collective-permute-start.7 = (f32[192,1536]{1,0:T(8,128)}, f32[192,1536]{1,0:T(8,128)}, u32[]{:S(2)}, u32[]{:S(2)}) collective-permute-start(f32[192,1536]{1,0:T(8,128)} %pad_maximum_fusion.3.refs_0_), channel_id=1, source_target_pairs={{0,8},{4,12},{8,0},{12,4},{16,24},{20,28},{24,16},{28,20},{1,9},{5... | collective-permute-start | bytes 3538952 | tf_op jit(solution)/shard_map/ppermute | solution.py:650
  84.6 57.8 %collective-permute-start.12 = (f32[384,768]{1,0:T(8,128)}, f32[384,768]{1,0:T(8,128)}, u32[]{:S(2)}, u32[]{:S(2)}) collective-permute-start(f32[384,768]{1,0:T(8,128)} %collective-permute-done.10.refs_5_), channel_id=1, source_target_pairs={{0,16},{4,20},{8,24},{12,28},{16,0},{20,4},{24,8},{28,12},{1,17},{... | collective-permute-start | bytes 3538952 | tf_op jit(solution)/shard_map/ppermute | solution.py:650
  85.1 59.3 %collective-permute-start.9 = (f32[192,1536]{1,0:T(8,128)}, f32[192,1536]{1,0:T(8,128)}, u32[]{:S(2)}, u32[]{:S(2)}) collective-permute-start(f32[192,1536]{1,0:T(8,128)} %collective-permute-done.8.refs_2_), channel_id=1, source_target_pairs={{0,8},{4,12},{8,0},{12,4},{16,24},{20,28},{24,16},{28,20},{1,9},{5... | collective-permute-start | bytes 3538952 | tf_op jit(solution)/shard_map/ppermute | solution.py:650
  136.2 8.2 %collective-permute-start.4 = (f32[384,768]{1,0:T(8,128)S(1)}, f32[384,768]{1,0:T(8,128)S(1)}, u32[]{:S(2)}, u32[]{:S(2)}) collective-permute-start(f32[384,768]{1,0:T(8,128)S(1)} %convolution_add_fusion.resid_ref), channel_id=1, source_target_pairs={{0,4},{4,0},{8,12},{12,8},{16,20},{20,16},{24,28},{28,24},{1,5},{5... | collective-permute-start | bytes 3538952 | tf_op jit(solution)/shard_map/ppermute | solution.py:650
  174.6 90.2 %reduce-scatter.15.cloned.1.call-start = ((), (), s32[]{:S(2)}) async-start(), calls=%async_computation.7 | async-start | bytes 3932160
  195.6 116.7 %reduce-scatter.17.cloned.1.call-start = ((), (), s32[]{:S(2)}) async-start(), calls=%async_computation.8 | async-start | bytes 3932160
  218.4 2.9 collective-permute-start.13
  218.5 191.1 %reduce-scatter.19.cloned.1.call-start = ((), (), s32[]{:S(2)}) async-start(), calls=%async_computation.9 | async-start | bytes 5898240
  222.9 11.2 %collective-permute-start.14 = (f32[1,192,512]{2,1,0:T(8,128)S(1)}, f32[1,192,512]{2,1,0:T(8,128)S(1)}, u32[]{:S(2)}, u32[]{:S(2)}) collective-permute-start(f32[1,192,512]{2,1,0:T(8,128)S(1)} %slice_select_fusion.7), channel_id=1, source_target_pairs={{0,1},{1,0},{2,3},{3,2},{4,5},{5,4},{6,7},{7,6},{8,9},{9,8},{10,11... | collective-permute-start | bytes 1179656 | tf_op jit(solution)/shard_map/ppermute | solution.py:721
  235.9 26.2 %collective-permute-start.15 = (f32[1,192,512]{2,1,0:T(8,128)S(1)}, f32[1,192,512]{2,1,0:T(8,128)S(1)}, u32[]{:S(2)}, u32[]{:S(2)}) collective-permute-start(f32[1,192,512]{2,1,0:T(8,128)S(1)} %select_add_fusion.3), channel_id=1, source_target_pairs={{0,2},{1,3},{2,0},{3,1},{4,6},{5,7},{6,4},{7,5},{8,10},{9,11},{10,... | collective-permute-start | bytes 1179656 | tf_op jit(solution)/shard_map/ppermute | solution.py:721
  266.0 25.5 %collective-permute-start.16 = (f32[1,192,512]{2,1,0:T(8,128)S(1)}, f32[1,192,512]{2,1,0:T(8,128)S(1)}, u32[]{:S(2)}, u32[]{:S(2)}) collective-permute-start(f32[1,192,512]{2,1,0:T(8,128)S(1)} %slice_select_fusion.6), channel_id=1, source_target_pairs={{0,1},{1,0},{2,3},{3,2},{4,5},{5,4},{6,7},{7,6},{8,9},{9,8},{10,11... | collective-permute-start | bytes 1179656 | tf_op jit(solution)/shard_map/ppermute | solution.py:721
  267.5 24.1 %collective-permute-start.17 = (f32[1,192,512]{2,1,0:T(8,128)S(1)}, f32[1,192,512]{2,1,0:T(8,128)S(1)}, u32[]{:S(2)}, u32[]{:S(2)}) collective-permute-start(f32[1,192,512]{2,1,0:T(8,128)S(1)} %add.194), channel_id=1, source_target_pairs={{0,1},{1,0},{2,3},{3,2},{4,5},{5,4},{6,7},{7,6},{8,9},{9,8},{10,11... | collective-permute-start | bytes 1179656 | tf_op jit(solution)/shard_map/ppermute | solution.py:721
  292.6 19.6 %collective-permute-start.19 = (f32[1,192,512]{2,1,0:T(8,128)S(1)}, f32[1,192,512]{2,1,0:T(8,128)S(1)}, u32[]{:S(2)}, u32[]{:S(2)}) collective-permute-start(f32[1,192,512]{2,1,0:T(8,128)S(1)} %select_add_fusion.2), channel_id=1, source_target_pairs={{0,2},{1,3},{2,0},{3,1},{4,6},{5,7},{6,4},{7,5},{8,10},{9,11},{10,... | collective-permute-start | bytes 1179656 | tf_op jit(solution)/shard_map/ppermute | solution.py:721
  307.8 25.3 %collective-permute-start.18 = (f32[4,96,1536]{2,1,0:T(8,128)}, f32[4,96,1536]{2,1,0:T(8,128)S(1)}, u32[]{:S(2)}, u32[]{:S(2)}) collective-permute-start(f32[4,96,1536]{2,1,0:T(8,128)} %get-tuple-element.139), channel_id=1, source_target_pairs={{0,4},{4,0},{8,12},{12,8},{16,20},{20,16},{24,28},{28,24},{1,5},{5... | collective-permute-start | bytes 7077896 | tf_op jit(solution)/shard_map/ppermute | solution.py:650
  313.5 15.7 %collective-permute-start.20 = (f32[1,192,512]{2,1,0:T(8,128)S(1)}, f32[1,192,512]{2,1,0:T(8,128)S(1)}, u32[]{:S(2)}, u32[]{:S(2)}) collective-permute-start(f32[1,192,512]{2,1,0:T(8,128)S(1)} %slice_select_fusion.5), channel_id=1, source_target_pairs={{0,1},{1,0},{2,3},{3,2},{4,5},{5,4},{6,7},{7,6},{8,9},{9,8},{10,11... | collective-permute-start | bytes 1179656 | tf_op jit(solution)/shard_map/ppermute | solution.py:721
  314.3 17.8 %collective-permute-start.21 = (f32[1,192,512]{2,1,0:T(8,128)S(1)}, f32[1,192,512]{2,1,0:T(8,128)S(1)}, u32[]{:S(2)}, u32[]{:S(2)}) collective-permute-start(f32[1,192,512]{2,1,0:T(8,128)S(1)} %add.197), channel_id=1, source_target_pairs={{0,1},{1,0},{2,3},{3,2},{4,5},{5,4},{6,7},{7,6},{8,9},{9,8},{10,11... | collective-permute-start | bytes 1179656 | tf_op jit(solution)/shard_map/ppermute | solution.py:721
  333.1 4.7 collective-permute-start.22
  342.5 43.0 %copy-start.39 = (f32[384]{0:T(512)}, f32[384]{0:T(512)S(1)}, u32[]{:S(2)}) copy-start(f32[384]{0:T(512)S(1)} %add_rsqrt_fusion.2) | copy-start | bytes 4612
  343.8 20.9 %collective-permute-start.24 = (f32[1,192,512]{2,1,0:T(8,128)S(1)}, f32[1,192,512]{2,1,0:T(8,128)S(1)}, u32[]{:S(2)}, u32[]{:S(2)}) collective-permute-start(f32[1,192,512]{2,1,0:T(8,128)S(1)} %select_add_fusion.1), channel_id=1, source_target_pairs={{0,2},{1,3},{2,0},{3,1},{4,6},{5,7},{6,4},{7,5},{8,10},{9,11},{10,... | collective-permute-start | bytes 1179656 | tf_op jit(solution)/shard_map/ppermute | solution.py:721
  371.8 34.4 %collective-permute-start.25 = (f32[384,768]{1,0:T(8,128)}, f32[384,768]{1,0:T(8,128)}, u32[]{:S(2)}, u32[]{:S(2)}) collective-permute-start(f32[384,768]{1,0:T(8,128)} %fusion.13), channel_id=1, source_target_pairs={{1,0},{2,1},{3,2},{5,4},{6,5},{7,6},{9,8},{10,9},{11,10},{13,12},{... | collective-permute-start | bytes 3538952 | tf_op jit(solution)/shard_map/ppermute | solution.py:790
  385.4 5.0 collective-permute-start.23
  396.0 1.4 collective-permute-start.26
  398.1 3.8 collective-permute-start.27
  402.0 7.0 %collective-permute-start.28 = (f32[8,768]{1,0:T(8,128)S(1)}, f32[8,768]{1,0:T(8,128)S(1)}, u32[]{:S(2)}, u32[]{:S(2)}) collective-permute-start(f32[8,768]{1,0:T(8,128)S(1)} %add.218), channel_id=1, source_target_pairs={{0,16},{4,20},{8,24},{12,28},{16,0},{20,4},{24,8},{28,12},{1,17},{... | collective-permute-start | bytes 73736 | tf_op jit(solution)/shard_map/ppermute | solution.py:650
  403.3 13.1 %collective-permute-start.31 = (f32[1,192,512]{2,1,0:T(8,128)}, f32[1,192,512]{2,1,0:T(8,128)}, u32[]{:S(2)}, u32[]{:S(2)}) collective-permute-start(f32[1,192,512]{2,1,0:T(8,128)} %add.204), channel_id=1, source_target_pairs={{0,1},{1,0},{2,3},{3,2},{4,5},{5,4},{6,7},{7,6},{8,9},{9,8},{10,11... | collective-permute-start | bytes 1179656 | tf_op jit(solution)/shard_map/ppermute | solution.py:721
  410.9 18.1 %collective-permute-start.29 = (f32[1,48,3072]{2,1,0:T(8,128)S(1)}, f32[1,48,3072]{2,1,0:T(8,128)S(1)}, u32[]{:S(2)}, u32[]{:S(2)}) collective-permute-start(f32[1,48,3072]{2,1,0:T(8,128)S(1)} %slice_select_fusion.4), channel_id=1, source_target_pairs={{0,1},{1,0},{2,3},{3,2},{4,5},{5,4},{6,7},{7,6},{8,9},{9,8},{10,11... | collective-permute-start | bytes 1769480 | tf_op jit(solution)/shard_map/ppermute | solution.py:721
  417.8 15.8 %collective-permute-start.32 = (f32[3,96,512]{2,1,0:T(8,128)S(1)}, f32[3,96,512]{2,1,0:T(8,128)S(1)}, u32[]{:S(2)}, u32[]{:S(2)}) collective-permute-start(f32[3,96,512]{2,1,0:T(8,128)S(1)} %slice_select_fusion.2), channel_id=1, source_target_pairs={{0,4},{4,0},{8,12},{12,8},{16,20},{20,16},{24,28},{28,24},{1,5},{5... | collective-permute-start | bytes 1769480 | tf_op jit(solution)/shard_map/ppermute | solution.py:650
  418.9 57.9 %collective-permute-start.33 = (f32[384,768]{1,0:T(8,128)}, f32[384,768]{1,0:T(8,128)}, u32[]{:S(2)}, u32[]{:S(2)}) collective-permute-start(f32[384,768]{1,0:T(8,128)} %add.208), channel_id=1, source_target_pairs={{1,0},{2,1},{3,2},{5,4},{6,5},{7,6},{9,8},{10,9},{11,10},{13,12},{... | collective-permute-start | bytes 3538952 | tf_op jit(solution)/shard_map/ppermute | solution.py:818
  430.0 45.5 %collective-permute-start.30 = (f32[1,48,3072]{2,1,0:T(8,128)}, f32[1,48,3072]{2,1,0:T(8,128)}, u32[]{:S(2)}, u32[]{:S(2)}) collective-permute-start(f32[1,48,3072]{2,1,0:T(8,128)} %select_add_fusion), channel_id=1, source_target_pairs={{0,2},{1,3},{2,0},{3,1},{4,6},{5,7},{6,4},{7,5},{8,10},{9,11},{10,... | collective-permute-start | bytes 1769480 | tf_op jit(solution)/shard_map/ppermute | solution.py:721
  447.0 29.8 %copy-start.10 = (f32[384,768]{1,0:T(8,128)S(1)}, f32[384,768]{1,0:T(8,128)}, u32[]{:S(2)}) copy-start(f32[384,768]{1,0:T(8,128)} %fusion) | copy-start | bytes 3538948
  447.0 29.8 %copy-start.40 = (f32[384]{0:T(512)S(1)}, f32[384]{0:T(512)}, u32[]{:S(2)}) copy-start(f32[384]{0:T(512)} %copy-done.39) | copy-start | bytes 4612
  447.0 29.8 %copy-start.42 = (f32[768]{0:T(1024)S(1)}, f32[768]{0:T(1024)}, u32[]{:S(2)}) copy-start(f32[768]{0:T(1024)} %param.20) | copy-start | bytes 9220
  478.8 4.2 collective-permute-start.34
  478.9 15.1 %collective-permute-start.36 = (f32[1,48,3072]{2,1,0:T(8,128)S(1)}, f32[1,48,3072]{2,1,0:T(8,128)S(1)}, u32[]{:S(2)}, u32[]{:S(2)}) collective-permute-start(f32[1,48,3072]{2,1,0:T(8,128)S(1)} %add.221), channel_id=1, source_target_pairs={{0,1},{1,0},{2,3},{3,2},{4,5},{5,4},{6,7},{7,6},{8,9},{9,8},{10,11... | collective-permute-start | bytes 1769480 | tf_op jit(solution)/shard_map/ppermute | solution.py:721
  483.0 9.8 %collective-permute-start.35 = (f32[8,768]{1,0:T(8,128)S(1)}, f32[8,768]{1,0:T(8,128)S(1)}, u32[]{:S(2)}, u32[]{:S(2)}) collective-permute-start(f32[8,768]{1,0:T(8,128)S(1)} %add.224), channel_id=1, source_target_pairs={{0,2},{1,3},{2,0},{3,1},{4,6},{5,7},{6,4},{7,5},{8,10},{9,11},{10,... | collective-permute-start | bytes 73736 | tf_op jit(solution)/shard_map/ppermute | solution.py:721
  (45 other events, 333.7 us)
Sparse Core Ops, SparseCore 0:
  9.9 69.1 all-gather.2
  81.0 38.7 all-gather.4
  174.7 43.2 reduce-scatter.12
  220.8 43.9 reduce-scatter.14
  267.6 43.9 reduce-scatter.16
  340.9 57.9 reduce-scatter.18

commit v11 on v10

--- a/solution.py
+++ b/solution.py
@@ -603,6 +603,44 @@
     )(core, *fixed_args, *args)
 
 
+def partial_kernel(count, *refs):
+    grads, w_ref, out_ref = refs[:count], refs[count], refs[count + 1]
+    held = refs[count + 2:]
+    model = grads[0].shape[1]
+    first = 3 - count
+
+    @pl.when(pl.program_id(0) == 0)
+    def _():
+        for at, ref in enumerate(grads):
+            held[2 * at][...], held[2 * at + 1][...] = split(ref[...])
+
+    total = None
+    for at in range(count):
+        weights = split(w_ref[:, (first + at) * model:(first + at + 1) * model])
+        term = three(dot_nt, (held[2 * at][...], held[2 * at + 1][...]), weights)
+        total = term if total is None else total + term
+    out_ref[...] = total
+
+
+def partial_rows(block, grads, w_full):
+    model = w_full.shape[0]
+    rows = grads[0].shape[0] if len(grads) == 3 else grads[0].shape[0] // 3
+    wide = 256
+    specs = [pl.BlockSpec((rows, model), lambda j: (block, 0))] * 2
+    if len(grads) == 3:
+        specs = [pl.BlockSpec((rows, model), lambda j: (0, 0))] + specs
+    return pl.pallas_call(
+        functools.partial(partial_kernel, len(grads)),
+        grid=(model // wide,),
+        in_specs=specs + [pl.BlockSpec((wide, 3 * model), lambda j: (j, 0))],
+        out_specs=pl.BlockSpec((rows, wide), lambda j: (0, j)),
+        out_shape=jax.ShapeDtypeStruct((rows, model), F32),
+        scratch_shapes=[pltpu.VMEM((rows, model), BF16)] * (2 * len(grads)),
+        cost_estimate=cost(6),
+        compiler_params=params(),
+    )(*grads, w_full)
+
+
 def matmul(left, right):
     return jnp.dot(left, right, precision=HIGH)
 
@@ -782,21 +820,20 @@
     output = base + dwa_weights[4] * block_out
     dwa_local = jnp.concatenate([dots, jnp.sum(cotangent * block_out)[None]])
 
-    wq, wk, wv = (qkv_full[:, i * model:(i + 1) * model] for i in range(3))
-    line_c, dk = together((line_c, dk))
+    part_far = partial_rows(0, (dk, dv), qkv_full)
+    given_near = lax.ppermute(part_far, "seq", behind)
+    dk, far, near, line_c, part_far = together((dk, far, near, line_c, part_far))
     ends_c = line_end(line_c)
-    part_far = outer_cols(dk[:rows], wk) + outer_cols(dv[:rows], wv)
-    dk_rest, dv_rest, far, near, part_far = together((dk[rows:], dv[rows:], far, near, part_far))
-    given_near = lax.ppermute(part_far, "seq", behind)
-    part_rest = outer_cols(dk_rest, wk) + outer_cols(dv_rest, wv)
-    own_part = part_rest[rows:] + outer_cols(dq, wq)
-    (near_rows,) = together((part_rest[:rows],))
-    back_near = near_rows + given_near
+    part_near = partial_rows(1, (dk, dv), qkv_full)
+    own_part = partial_rows(2, (dq, dk, dv), qkv_full)
+    own_part, ends_c = together((own_part, ends_c))
+    (sent,) = together((part_near,))
+    back_near = sent + given_near
 
     xhat1, rate1 = norm_stats(block_input)
     terms = (
         (norm_stats(far)[0], part_far),
-        (norm_stats(near)[0], part_rest[:rows]),
+        (norm_stats(near)[0], part_near),
         (xhat1, own_part),
     )
     grad_gain_one = sum(jnp.sum(xhat * part, axis=0) for xhat, part in terms)

time: 508 us -> 499 us (0.982)
  matrix products: 26 us -> 3.7 us
  Pallas kernels: 197 us -> 213 us
  waiting for transfers between devices: 120 us -> 134 us
  local copies, waits for them, and re-layouts: 43.2 us -> 31.5 us
  starting transfers between devices: 54 us -> 48.6 us
    pallas_call x0 -> x3, Pallas kernels: none -> 24.9 us  [partial_rows(): pl.pallas_call(functools.partial(partial_kernel, len(grads)), grid=(model...]
    dot_general x5 -> x0, matrix products: 22.3 us -> none  [outer_cols(): lax.dot_general(left, right, (((1,), (1,)), ((), ())), precision=HIGH)]
    ppermute x14, waiting for transfers between devices: 70.2 us -> 84.8 us  [body(): lax.ppermute(v, 'seq', [(i, i ^ bit) for i in range(groups)])]
    pallas_call x3, Pallas kernels: 71.2 us -> 62 us  [mlp(): pl.pallas_call(functools.partial(mlp_kernel, len(ups), len(so_far) // 2),...]
  transfers between devices with their start and end apart: 43 -> 43, of which waited for: 18 -> 18; matrix products, arithmetic and copies ran while one was open for 20% -> 14% of each run, Pallas kernels for 33% -> 39%
where the time goes in v11:
time: 499 us; the launch traced here: 494 us
  Pallas kernels  213 us (43%)
  waiting for transfers between devices  134 us (27%)
  starting transfers between devices  48.6 us (10%)
  other arithmetic  48.1 us (10%)
  local copies, waits for them, and re-layouts  31.5 us (6%)
  between operations  15.2 us (3%)
    ppermute x14, waiting for transfers between devices, body(): lax.ppermute(v, 'seq', [(i, i ^ bit) for i in range(groups)])  84.8 us
    pallas_call x3, Pallas kernels, mlp(): pl.pallas_call(functools.partial(mlp_kernel, len(ups), len(so_far) // 2),...  62 us
    pallas_call x2, Pallas kernels, attend_back(): pl.pallas_call(attend_back_kernel, grid=(count,), in_specs=[pl.BlockSpec(...  47.3 us
    pallas_call x2, Pallas kernels, weight_call(): pl.pallas_call(kernel, grid_spec=pltpu.PrefetchScalarGridSpec(num_scalar_...  26.4 us
    pallas_call x3, Pallas kernels, partial_rows(): pl.pallas_call(functools.partial(partial_kernel, len(grads)), grid=(model...  24.9 us
    pallas_call x1, Pallas kernels, attend(): pl.pallas_call(attend_kernel, grid=(pairs,), in_specs=[pl.BlockSpec((rows...  23 us
    pallas_call x1, Pallas kernels, project(): pl.pallas_call(qkv_kernel, grid=(3 * third,), in_specs=[whole((rows, mode...  21.7 us
    ppermute x1, waiting for transfers between devices, body(): near = lax.ppermute(block_input, 'seq', ahead)  18 us
  transfers between devices with their start and end apart: 43, of which 18 were waited for; matrix products, arithmetic and copies ran while one was open for 14% of the time, Pallas kernels for 39%

profile of v11, /device:TPU:0, one launch (start us, length us, event | category | flops | bytes accessed | tf_op | source)
XLA Modules:
  0.0 493.9 jit_solution(18384899618017105373)
XLA Ops:
  8.0 1.9 reshape.142
  11.9 4.6 collective-permute-start
  24.2 18.0 %collective-permute-done.near_ref = f32[384,768]{1,0:T(8,128)S(1)} collective-permute-done((f32[384,768]{1,0:T(8,128)S(1)}, f32[384,768]{1,0:T(8,128)S(1)}, u32[]{:S(2)}, u32[]{:S(2)}) %collective-permute-start) | collective-permute-done | bytes 1179680 | tf_op jit(solution)/shard_map/ppermute | solution.py:715
  42.3 4.4 collective-permute-start.1
  46.7 4.0 collective-permute-start.2
  51.4 7.4 %fusion.5 = (f32[]{:T(128)}, f32[]{:T(128)}, f32[]{:T(128)}, f32[]{:T(128)}, f32[384,768]{1,0:T(8,128)}) fusion(f32[384,768]{1,0:T(8,128)S(1)} %copy-done.12, f32[3,384,768]{2,1,0:T(8,128)} %param.18, f32[384,768]{1,0:T(8,128)} %param.17, f32[]{:T(128)} %bitcast.5, f32[]{:T(128)} %bitcast.3, f32[]{:T(128)} %bitcast.1, f32[]{:T(128)} %bitcast), kind=kLoop, calls=%fused_computation.17 | loop fusion | flops 4423676 | bytes 7077920 | tf_op jit(solution)/shard_map/reduce_sum | solution.py:731
  60.0 11.8 %collective-permute-done.2 = s32[1,384]{1,0:T(1,128)} collective-permute-done((s32[1,384]{1,0:T(1,128)S(1)}, s32[1,384]{1,0:T(1,128)}, u32[]{:S(2)}, u32[]{:S(2)}) %collective-permute-start.2) | collective-permute-done | bytes 1568 | tf_op jit(solution)/shard_map/ppermute | solution.py:716
  71.8 5.0 %collective-permute-start.3 = (s32[1,384]{1,0:T(1,128)}, s32[1,384]{1,0:T(1,128)S(1)}, u32[]{:S(2)}, u32[]{:S(2)}) collective-permute-start(s32[1,384]{1,0:T(1,128)} %collective-permute-done.2), channel_id=1, source_target_pairs={{0,1},{1,2},{2,3},{4,5},{5,6},{6,7},{8,9},{9,10},{10,11},{12,13},{... | collective-permute-start | bytes 4616 | tf_op jit(solution)/shard_map/ppermute | solution.py:718
  76.8 3.2 pad_maximum_fusion.2
  86.5 21.7 %shard_map.239 = (f32[384,768]{1,0:T(8,128)}, f32[1152,1536]{1,0:T(8,128)}, bf16[1152,768]{1,0:T(8,128)(2,1)}, bf16[1152,768]{1,0:T(8,128)(2,1)}) custom-call(f32[384,768]{1,0:T(8,128)} %copy-done.5, f32[384,768]{1,0:T(8,128)} %copy-done.3, f32[384,768]{1,0:T(8,128)} %own_ref.1, f32[1,768]{1,0:T(1,128)} %broadcast_in_dim.50.gain_ref, ...), custom_call_target="tpu_custom_call" | custom-call | flops 22000001024 | bytes 1048576 | tf_op jit(solution)/shard_map/pallas_call | solution.py:144
  109.6 23.0 %shard_map.240.att_ref = f32[384,768]{1,0:T(8,128)} custom-call(f32[384,768]{1,0:T(8,128)} %get-tuple-element.124.q_ref, f32[1152,1536]{1,0:T(8,128)} %get-tuple-element.125.k_ref.v_ref, f32[1152,1536]{1,0:T(8,128)} %get-tuple-element.125.k_ref.v_ref, s32[384,128]{1,0:T(8,128)} %broadcast_in_dim.52.segq_ref, s32[8,1152]{1,0:T(8,128)} %broadcast_in_dim.54.segk_ref), custom_call_target="tpu_custom_call" | custom-call | flops 26400000000 | bytes 1048576 | tf_op jit(solution)/shard_map/pallas_call | solution.py:236
  132.7 3.7 convolution_add_fusion.resid_ref
  138.5 4.2 collective-permute-done.12.refs_7_
  142.8 2.0 collective-permute-done.9.refs_3_
  145.8 19.9 %shard_map.241 = (f32[768,768]{1,0:T(8,128)}, f32[768,768]{1,0:T(8,128)}, f32[4,1,384,512]{3,2,1,0:T(8,128)}) custom-call(s32[1]{0:T(128)} %bitcast.13.chip_ref, f32[384,768]{1,0:T(8,128)} %copy-done.15, f32[384,768]{1,0:T(8,128)} %copy-done.41, f32[384,768]{1,0:T(8,128)} %cot_ref.7, f32[384,768]{1,0:T(8,128)} %collective-permute-done.5.cot_other_ref, ...), custom_call_target="tpu_custom_call" | custom-call | flops 19800000512 | bytes 1048576 | tf_op jit(solution)/shard_map/pallas_call | solution.py:457
  165.8 20.9 %shard_map.242 = (f32[768,768]{1,0:T(8,128)}, f32[768,768]{1,0:T(8,128)}, f32[4,1,384,512]{3,2,1,0:T(8,128)}) custom-call(s32[1]{0:T(128)} %bitcast.13.chip_ref, f32[384,768]{1,0:T(8,128)} %copy-done.15, f32[384,768]{1,0:T(8,128)} %copy-done.41, f32[384,768]{1,0:T(8,128)} %cot_ref.7, f32[384,768]{1,0:T(8,128)} %collective-permute-done.5.cot_other_ref, ...), custom_call_target="tpu_custom_call" | custom-call | flops 19800000512 | bytes 1048576 | tf_op jit(solution)/shard_map/pallas_call | solution.py:457
  187.0 21.2 %shard_map.243 = (f32[768,768]{1,0:T(8,128)}, f32[768,768]{1,0:T(8,128)}, f32[4,1,384,512]{3,2,1,0:T(8,128)}) custom-call(s32[1]{0:T(128)} %bitcast.13.chip_ref, f32[384,768]{1,0:T(8,128)} %copy-done.15, f32[384,768]{1,0:T(8,128)} %copy-done.41, f32[384,768]{1,0:T(8,128)} %cot_ref.7, f32[384,768]{1,0:T(8,128)} %collective-permute-done.5.cot_other_ref, ...), custom_call_target="tpu_custom_call" | custom-call | flops 19800000512 | bytes 1048576 | tf_op jit(solution)/shard_map/pallas_call | solution.py:457
  209.9 2.5 collective-permute-done.13.given_ref
  214.0 1.7 collective-permute-start.14
  215.7 7.7 %shard_map.244 = (f32[384,768]{1,0:T(8,128)}, f32[384,768]{1,0:T(8,128)}, f32[8,768]{1,0:T(8,128)}) custom-call(f32[768,768]{1,0:T(8,128)} %get-tuple-element.106.part_ref, f32[384,768]{1,0:T(8,128)} %copy-done.42, f32[384,768]{1,0:T(8,128)} %copy-done.15, f32[384,768]{1,0:T(8,128)} %cot_ref.7, f32[1,768]{1,0:T(1,128)} %broadcast_in_dim.55.gain_ref, ...), custom_call_target="tpu_custom_call" | custom-call | flops 6600000000 | bytes 1048576 | tf_op jit(solution)/shard_map/pallas_call | solution.py:505
  223.4 1.8 collective-permute-done.14
  227.0 2.6 collective-permute-start.15
  229.6 23.6 %shard_map.245 = (f32[384,768]{1,0:T(8,128)}, f32[1152,768]{1,0:T(8,128)}, f32[1152,768]{1,0:T(8,128)}) custom-call(f32[384,768]{1,0:T(8,128)} %get-tuple-element.124.q_ref, f32[1152,1536]{1,0:T(8,128)} %get-tuple-element.125.k_ref.v_ref, f32[1152,1536]{1,0:T(8,128)} %get-tuple-element.125.k_ref.v_ref, f32[384,768]{1,0:T(8,128)} %get-tuple-element.126.g_ref, ...), custom_call_target="tpu_custom_call" | custom-call | flops 23100000256 | bytes 1048576 | tf_op jit(solution)/shard_map/pallas_call | solution.py:328
  253.2 2.7 reduce-scatter.15.cloned.1.call-done
  259.2 23.7 %shard_map.246 = (f32[384,768]{1,0:T(8,128)}, f32[1152,768]{1,0:T(8,128)}, f32[1152,768]{1,0:T(8,128)}) custom-call(f32[384,768]{1,0:T(8,128)} %get-tuple-element.124.q_ref, f32[1152,1536]{1,0:T(8,128)} %get-tuple-element.125.k_ref.v_ref, f32[1152,1536]{1,0:T(8,128)} %get-tuple-element.125.k_ref.v_ref, ...), custom_call_target="tpu_custom_call", output_to_operand_aliasing={{0}: (8, {}), {1}: (9, {}), {2}: (10, {})} | custom-call | flops 23100000256 | bytes 1048576 | tf_op jit(solution)/shard_map/pallas_call | solution.py:328
  283.9 2.4 collective-permute-start.19
  286.4 12.7 %shard_map.247 = (f32[4,96,1536]{2,1,0:T(8,128)}, f32[4,96,1536]{2,1,0:T(8,128)}) custom-call(s32[1]{0:T(128)} %bitcast.12.core_ref, bf16[1152,768]{1,0:T(8,128)(2,1)} %get-tuple-element.99.hi_ref, bf16[1152,768]{1,0:T(8,128)(2,1)} %get-tuple-element.100.lo_ref, f32[384,768]{1,0:T(8,128)} %get-tuple-element.137.dq_ref.refs_0_, ...), custom_call_target="tpu_custom_call" | custom-call | flops 9900000256 | bytes 1048576 | tf_op jit(solution)/shard_map/pallas_call | solution.py:591
  299.1 4.5 collective-permute-done.19
  307.0 13.6 %shard_map.248 = (f32[4,96,1536]{2,1,0:T(8,128)}, f32[4,96,1536]{2,1,0:T(8,128)}) custom-call(s32[1]{0:T(128)} %bitcast.12.core_ref, bf16[1152,768]{1,0:T(8,128)(2,1)} %get-tuple-element.99.hi_ref, bf16[1152,768]{1,0:T(8,128)(2,1)} %get-tuple-element.100.lo_ref, f32[1152,768]{1,0:T(8,128)} %get-tuple-element.147.dv_ref.refs_1_.refs_2_, ...), custom_call_target="tpu_custom_call" | custom-call | flops 9900000256 | bytes 1048576 | tf_op jit(solution)/shard_map/pallas_call | solution.py:591
  321.4 2.0 collective-permute-done.21
  324.8 4.3 collective-permute-done.22
  329.5 2.4 pad_maximum_fusion
  334.4 3.1 collective-permute-start.24
  337.5 8.0 %shard_map.249 = f32[384,768]{1,0:T(8,128)} custom-call(f32[1152,768]{1,0:T(8,128)} %get-tuple-element.156.dk_ref.refs_0_.refs_1_, f32[1152,768]{1,0:T(8,128)} %get-tuple-element.147.dv_ref.refs_1_.refs_2_, f32[768,2304]{1,0:T(8,128)} %all-gather.3.cloned.1.call-done.w_ref.refs_2_.refs_3_), custom_call_target="tpu_custom_call" | custom-call | flops 6600000000 | bytes 1048576 | tf_op jit(solution)/shard_map/pallas_call | solution.py:632
  346.9 9.1 %collective-permute-done.24 = f32[1,192,512]{2,1,0:T(8,128)S(1)} collective-permute-done((f32[1,192,512]{2,1,0:T(8,128)}, f32[1,192,512]{2,1,0:T(8,128)S(1)}, u32[]{:S(2)}, u32[]{:S(2)}) %collective-permute-start.24) | collective-permute-done | bytes 393248 | tf_op jit(solution)/shard_map/ppermute | solution.py:759
  356.0 1.8 add.195
  360.9 9.2 %shard_map.250 = f32[384,768]{1,0:T(8,128)} custom-call(f32[384,768]{1,0:T(8,128)} %get-tuple-element.137.dq_ref.refs_0_, f32[1152,768]{1,0:T(8,128)} %get-tuple-element.156.dk_ref.refs_0_.refs_1_, f32[1152,768]{1,0:T(8,128)} %get-tuple-element.147.dv_ref.refs_1_.refs_2_, f32[768,2304]{1,0:T(8,128)} %all-gather.3.cloned.1.call-done.w_ref.refs_2_.refs_3_), custom_call_target="tpu_custom_call" | custom-call | flops 6600000000 | bytes 1048576 | tf_op jit(solution)/shard_map/pallas_call | solution.py:632
  370.1 7.7 %shard_map.251 = f32[384,768]{1,0:T(8,128)} custom-call(f32[1152,768]{1,0:T(8,128)} %get-tuple-element.156.dk_ref.refs_0_.refs_1_, f32[1152,768]{1,0:T(8,128)} %get-tuple-element.147.dv_ref.refs_1_.refs_2_, f32[768,2304]{1,0:T(8,128)} %all-gather.3.cloned.1.call-done.w_ref.refs_2_.refs_3_), custom_call_target="tpu_custom_call" | custom-call | flops 6600000000 | bytes 1048576 | tf_op jit(solution)/shard_map/pallas_call | solution.py:632
  379.7 9.6 %collective-permute-done.25 = f32[1,192,512]{2,1,0:T(8,128)} collective-permute-done((f32[1,192,512]{2,1,0:T(8,128)}, f32[1,192,512]{2,1,0:T(8,128)}, u32[]{:S(2)}, u32[]{:S(2)}) %collective-permute-start.25) | collective-permute-done | bytes 393248 | tf_op jit(solution)/shard_map/ppermute | solution.py:759
  389.3 2.1 broadcast_select_fusion.6
  393.1 2.7 multiply_reduce_fusion.1
  404.1 2.5 add.196
  411.0 13.9 %collective-permute-done.30 = f32[1,48,3072]{2,1,0:T(8,128)S(1)} collective-permute-done((f32[1,48,3072]{2,1,0:T(8,128)S(1)}, f32[1,48,3072]{2,1,0:T(8,128)S(1)}, u32[]{:S(2)}, u32[]{:S(2)}) %collective-permute-start.30) | collective-permute-done | bytes 589856 | tf_op jit(solution)/shard_map/ppermute | solution.py:759
  433.1 33.2 %collective-permute-done.31 = f32[1,48,3072]{2,1,0:T(8,128)} collective-permute-done((f32[1,48,3072]{2,1,0:T(8,128)}, f32[1,48,3072]{2,1,0:T(8,128)}, u32[]{:S(2)}, u32[]{:S(2)}) %collective-permute-start.31) | collective-permute-done | bytes 589856 | tf_op jit(solution)/shard_map/ppermute | solution.py:759
  467.6 1.9 fusion.7
  469.7 2.0 collective-permute-start.36
  471.7 2.1 collective-permute-done.34
  475.2 8.6 %collective-permute-done.35 = f32[8,768]{1,0:T(8,128)S(1)} collective-permute-done((f32[8,768]{1,0:T(8,128)S(1)}, f32[8,768]{1,0:T(8,128)S(1)}, u32[]{:S(2)}, u32[]{:S(2)}) %collective-permute-start.35) | collective-permute-done | bytes 24608 | tf_op jit(solution)/shard_map/ppermute | solution.py:759
  (244 shorter events, 75.8 us)
Async XLA Ops:
  7.2 78.8 %all-gather.3.cloned.1.call-start = ((), (), s32[]{:S(2)}) async-start(), calls=%async_computation.4 | async-start | bytes 7962624 | tf_op jit(solution)/shard_map/all_gather | solution.py:691
  7.9 124.8 %all-gather.5.cloned.1.call-start = ((), (), s32[]{:S(2)}) async-start(), calls=%async_computation.5 | async-start | bytes 2654208 | tf_op jit(solution)/shard_map/all_gather | solution.py:691
  11.4 8.9 %collective-permute-start.6 = (f32[96,1536]{1,0:T(8,128)}, f32[96,1536]{1,0:T(8,128)}, u32[]{:S(2)}, u32[]{:S(2)}) collective-permute-start(f32[96,1536]{1,0:T(8,128)} %select_n.149), channel_id=1, source_target_pairs={{0,4},{4,0},{8,12},{12,8},{16,20},{20,16},{24,28},{28,24},{1,5},{5... | collective-permute-start | bytes 1769480 | tf_op jit(solution)/shard_map/ppermute | solution.py:688
  11.9 30.4 %collective-permute-start = (f32[384,768]{1,0:T(8,128)S(1)}, f32[384,768]{1,0:T(8,128)S(1)}, u32[]{:S(2)}, u32[]{:S(2)}) collective-permute-start(f32[384,768]{1,0:T(8,128)S(1)} %copy-done), channel_id=1, source_target_pairs={{0,1},{1,2},{2,3},{4,5},{5,6},{6,7},{8,9},{9,10},{10,11},{12,13},{... | collective-permute-start | bytes 3538952 | tf_op jit(solution)/shard_map/ppermute | solution.py:715
  16.5 66.9 %collective-permute-start.10 = (f32[384,768]{1,0:T(8,128)}, f32[384,768]{1,0:T(8,128)}, u32[]{:S(2)}, u32[]{:S(2)}) collective-permute-start(f32[384,768]{1,0:T(8,128)} %refs_4_.5), channel_id=1, source_target_pairs={{0,8},{4,12},{8,0},{12,4},{16,24},{20,28},{24,16},{28,20},{1,9},{5... | collective-permute-start | bytes 3538952 | tf_op jit(solution)/shard_map/ppermute | solution.py:688
  21.6 29.1 %copy-start.12 = (f32[384,768]{1,0:T(8,128)S(1)}, f32[384,768]{1,0:T(8,128)}, u32[]{:S(2)}) copy-start(f32[384,768]{1,0:T(8,128)} %cot_ref.7) | copy-start | bytes 3538948
  21.6 29.2 %copy-start.35 = (f32[5]{0:T(128)S(1)}, f32[5]{0:T(128)}, u32[]{:S(2)}) copy-start(f32[5]{0:T(128)} %param.19) | copy-start | bytes 64
  22.7 62.3 %collective-permute-start.8 = (f32[192,1536]{1,0:T(8,128)}, f32[192,1536]{1,0:T(8,128)}, u32[]{:S(2)}, u32[]{:S(2)}) collective-permute-start(f32[192,1536]{1,0:T(8,128)} %pad_maximum_fusion.1.refs_0_), channel_id=1, source_target_pairs={{0,16},{4,20},{8,24},{12,28},{16,0},{20,4},{24,8},{28,12},{1,17},{... | collective-permute-start | bytes 3538952 | tf_op jit(solution)/shard_map/ppermute | solution.py:688
  42.3 43.2 %collective-permute-start.1 = (f32[384,768]{1,0:T(8,128)S(1)}, f32[384,768]{1,0:T(8,128)S(1)}, u32[]{:S(2)}, u32[]{:S(2)}) collective-permute-start(f32[384,768]{1,0:T(8,128)S(1)} %collective-permute-done.near_ref), channel_id=1, source_target_pairs={{0,1},{1,2},{2,3},{4,5},{5,6},{6,7},{8,9},{9,10},{10,11},{12,13},{... | collective-permute-start | bytes 3538952 | tf_op jit(solution)/shard_map/ppermute | solution.py:717
  46.7 25.1 %collective-permute-start.2 = (s32[1,384]{1,0:T(1,128)S(1)}, s32[1,384]{1,0:T(1,128)}, u32[]{:S(2)}, u32[]{:S(2)}) collective-permute-start(s32[1,384]{1,0:T(1,128)S(1)} %get-tuple-element.215), channel_id=1, source_target_pairs={{0,1},{1,2},{2,3},{4,5},{5,6},{6,7},{8,9},{9,10},{10,11},{12,13},{... | collective-permute-start | bytes 4616 | tf_op jit(solution)/shard_map/ppermute | solution.py:716
  50.7 85.7 %collective-permute-start.5 = (f32[384,768]{1,0:T(8,128)S(1)}, f32[384,768]{1,0:T(8,128)}, u32[]{:S(2)}, u32[]{:S(2)}) collective-permute-start(f32[384,768]{1,0:T(8,128)S(1)} %copy-done.12), channel_id=1, source_target_pairs={{0,4},{4,0},{8,12},{12,8},{16,20},{20,16},{24,28},{28,24},{1,5},{5... | collective-permute-start | bytes 3538952 | tf_op jit(solution)/shard_map/ppermute | solution.py:688
  50.8 161.6 %reduce-scatter.13.cloned.1.call-start = ((), (), s32[]{:S(2)}) async-start(), calls=%async_computation.6 | async-start | bytes 3932160
  71.8 9.4 %collective-permute-start.3 = (s32[1,384]{1,0:T(1,128)}, s32[1,384]{1,0:T(1,128)S(1)}, u32[]{:S(2)}, u32[]{:S(2)}) collective-permute-start(s32[1,384]{1,0:T(1,128)} %collective-permute-done.2), channel_id=1, source_target_pairs={{0,1},{1,2},{2,3},{4,5},{5,6},{6,7},{8,9},{9,10},{10,11},{12,13},{... | collective-permute-start | bytes 4616 | tf_op jit(solution)/shard_map/ppermute | solution.py:718
  81.2 57.3 %collective-permute-start.11 = (f32[384,768]{1,0:T(8,128)}, f32[384,768]{1,0:T(8,128)}, u32[]{:S(2)}, u32[]{:S(2)}) collective-permute-start(f32[384,768]{1,0:T(8,128)} %refs_4_.5), channel_id=1, source_target_pairs={{0,16},{4,20},{8,24},{12,28},{16,0},{20,4},{24,8},{28,12},{1,17},{... | collective-permute-start | bytes 3538952 | tf_op jit(solution)/shard_map/ppermute | solution.py:688
  83.4 55.1 %collective-permute-start.7 = (f32[192,1536]{1,0:T(8,128)}, f32[192,1536]{1,0:T(8,128)}, u32[]{:S(2)}, u32[]{:S(2)}) collective-permute-start(f32[192,1536]{1,0:T(8,128)} %pad_maximum_fusion.1.refs_0_), channel_id=1, source_target_pairs={{0,8},{4,12},{8,0},{12,4},{16,24},{20,28},{24,16},{28,20},{1,9},{5... | collective-permute-start | bytes 3538952 | tf_op jit(solution)/shard_map/ppermute | solution.py:688
  85.0 57.8 %collective-permute-start.12 = (f32[384,768]{1,0:T(8,128)}, f32[384,768]{1,0:T(8,128)}, u32[]{:S(2)}, u32[]{:S(2)}) collective-permute-start(f32[384,768]{1,0:T(8,128)} %collective-permute-done.10.refs_5_), channel_id=1, source_target_pairs={{0,16},{4,20},{8,24},{12,28},{16,0},{20,4},{24,8},{28,12},{1,17},{... | collective-permute-start | bytes 3538952 | tf_op jit(solution)/shard_map/ppermute | solution.py:688
  85.5 59.3 %collective-permute-start.9 = (f32[192,1536]{1,0:T(8,128)}, f32[192,1536]{1,0:T(8,128)}, u32[]{:S(2)}, u32[]{:S(2)}) collective-permute-start(f32[192,1536]{1,0:T(8,128)} %collective-permute-done.8.refs_2_), channel_id=1, source_target_pairs={{0,8},{4,12},{8,0},{12,4},{16,24},{20,28},{24,16},{28,20},{1,9},{5... | collective-permute-start | bytes 3538952 | tf_op jit(solution)/shard_map/ppermute | solution.py:688
  136.5 8.3 %collective-permute-start.4 = (f32[384,768]{1,0:T(8,128)S(1)}, f32[384,768]{1,0:T(8,128)S(1)}, u32[]{:S(2)}, u32[]{:S(2)}) collective-permute-start(f32[384,768]{1,0:T(8,128)S(1)} %convolution_add_fusion.resid_ref), channel_id=1, source_target_pairs={{0,4},{4,0},{8,12},{12,8},{16,20},{20,16},{24,28},{28,24},{1,5},{5... | collective-permute-start | bytes 3538952 | tf_op jit(solution)/shard_map/ppermute | solution.py:688
  165.7 90.2 %reduce-scatter.15.cloned.1.call-start = ((), (), s32[]{:S(2)}) async-start(), calls=%async_computation.7 | async-start | bytes 3932160
  186.7 116.9 %reduce-scatter.17.cloned.1.call-start = ((), (), s32[]{:S(2)}) async-start(), calls=%async_computation.8 | async-start | bytes 3932160
  209.5 2.9 collective-permute-start.13
  209.6 197.6 %reduce-scatter.19.cloned.1.call-start = ((), (), s32[]{:S(2)}) async-start(), calls=%async_computation.9 | async-start | bytes 5898240
  214.0 11.2 %collective-permute-start.14 = (f32[1,192,512]{2,1,0:T(8,128)S(1)}, f32[1,192,512]{2,1,0:T(8,128)S(1)}, u32[]{:S(2)}, u32[]{:S(2)}) collective-permute-start(f32[1,192,512]{2,1,0:T(8,128)S(1)} %slice_select_fusion.7), channel_id=1, source_target_pairs={{0,1},{1,0},{2,3},{3,2},{4,5},{5,4},{6,7},{7,6},{8,9},{9,8},{10,11... | collective-permute-start | bytes 1179656 | tf_op jit(solution)/shard_map/ppermute | solution.py:759
  227.0 26.2 %collective-permute-start.15 = (f32[1,192,512]{2,1,0:T(8,128)S(1)}, f32[1,192,512]{2,1,0:T(8,128)S(1)}, u32[]{:S(2)}, u32[]{:S(2)}) collective-permute-start(f32[1,192,512]{2,1,0:T(8,128)S(1)} %select_add_fusion.3), channel_id=1, source_target_pairs={{0,2},{1,3},{2,0},{3,1},{4,6},{5,7},{6,4},{7,5},{8,10},{9,11},{10,... | collective-permute-start | bytes 1179656 | tf_op jit(solution)/shard_map/ppermute | solution.py:759
  257.1 25.8 %copy-start.17 = (f32[1,1,384,512]{3,2,1,0:T(8,128)S(1)}, f32[1,1,384,512]{3,2,1,0:T(8,128)}, u32[]{:S(2)}) copy-start(f32[1,1,384,512]{3,2,1,0:T(8,128)} %reduce-scatter.15.cloned.1.call-done) | copy-start | bytes 2359300
  257.1 25.8 %collective-permute-start.16 = (f32[1,192,512]{2,1,0:T(8,128)S(1)}, f32[1,192,512]{2,1,0:T(8,128)S(1)}, u32[]{:S(2)}, u32[]{:S(2)}) collective-permute-start(f32[1,192,512]{2,1,0:T(8,128)S(1)} %slice_select_fusion.6), channel_id=1, source_target_pairs={{0,1},{1,0},{2,3},{3,2},{4,5},{5,4},{6,7},{7,6},{8,9},{9,8},{10,11... | collective-permute-start | bytes 1179656 | tf_op jit(solution)/shard_map/ppermute | solution.py:759
  258.6 24.3 %collective-permute-start.17 = (f32[1,192,512]{2,1,0:T(8,128)S(1)}, f32[1,192,512]{2,1,0:T(8,128)S(1)}, u32[]{:S(2)}, u32[]{:S(2)}) collective-permute-start(f32[1,192,512]{2,1,0:T(8,128)S(1)} %add.185), channel_id=1, source_target_pairs={{0,1},{1,0},{2,3},{3,2},{4,5},{5,4},{6,7},{7,6},{8,9},{9,8},{10,11... | collective-permute-start | bytes 1179656 | tf_op jit(solution)/shard_map/ppermute | solution.py:759
  283.9 19.6 %collective-permute-start.19 = (f32[1,192,512]{2,1,0:T(8,128)S(1)}, f32[1,192,512]{2,1,0:T(8,128)S(1)}, u32[]{:S(2)}, u32[]{:S(2)}) collective-permute-start(f32[1,192,512]{2,1,0:T(8,128)S(1)} %select_add_fusion.2), channel_id=1, source_target_pairs={{0,2},{1,3},{2,0},{3,1},{4,6},{5,7},{6,4},{7,5},{8,10},{9,11},{10,... | collective-permute-start | bytes 1179656 | tf_op jit(solution)/shard_map/ppermute | solution.py:759
  299.1 25.3 %collective-permute-start.18 = (f32[4,96,1536]{2,1,0:T(8,128)}, f32[4,96,1536]{2,1,0:T(8,128)S(1)}, u32[]{:S(2)}, u32[]{:S(2)}) collective-permute-start(f32[4,96,1536]{2,1,0:T(8,128)} %get-tuple-element.140), channel_id=1, source_target_pairs={{0,4},{4,0},{8,12},{12,8},{16,20},{20,16},{24,28},{28,24},{1,5},{5... | collective-permute-start | bytes 7077896 | tf_op jit(solution)/shard_map/ppermute | solution.py:688
  304.9 15.7 %collective-permute-start.20 = (f32[1,192,512]{2,1,0:T(8,128)S(1)}, f32[1,192,512]{2,1,0:T(8,128)S(1)}, u32[]{:S(2)}, u32[]{:S(2)}) collective-permute-start(f32[1,192,512]{2,1,0:T(8,128)S(1)} %slice_select_fusion.5), channel_id=1, source_target_pairs={{0,1},{1,0},{2,3},{3,2},{4,5},{5,4},{6,7},{7,6},{8,9},{9,8},{10,11... | collective-permute-start | bytes 1179656 | tf_op jit(solution)/shard_map/ppermute | solution.py:759
  305.4 18.0 %collective-permute-start.21 = (f32[1,192,512]{2,1,0:T(8,128)S(1)}, f32[1,192,512]{2,1,0:T(8,128)S(1)}, u32[]{:S(2)}, u32[]{:S(2)}) collective-permute-start(f32[1,192,512]{2,1,0:T(8,128)S(1)} %add.188), channel_id=1, source_target_pairs={{0,1},{1,0},{2,3},{3,2},{4,5},{5,4},{6,7},{7,6},{8,9},{9,8},{10,11... | collective-permute-start | bytes 1179656 | tf_op jit(solution)/shard_map/ppermute | solution.py:759
  324.4 4.7 collective-permute-start.22
  334.4 21.7 %collective-permute-start.24 = (f32[1,192,512]{2,1,0:T(8,128)}, f32[1,192,512]{2,1,0:T(8,128)S(1)}, u32[]{:S(2)}, u32[]{:S(2)}) collective-permute-start(f32[1,192,512]{2,1,0:T(8,128)} %select_add_fusion.1), channel_id=1, source_target_pairs={{0,2},{1,3},{2,0},{3,1},{4,6},{5,7},{6,4},{7,5},{8,10},{9,11},{10,... | collective-permute-start | bytes 1179656 | tf_op jit(solution)/shard_map/ppermute | solution.py:759
  345.5 58.6 %collective-permute-start.26 = (f32[384,768]{1,0:T(8,128)}, f32[384,768]{1,0:T(8,128)}, u32[]{:S(2)}, u32[]{:S(2)}) collective-permute-start(f32[384,768]{1,0:T(8,128)} %shard_map.249), channel_id=1, source_target_pairs={{1,0},{2,1},{3,2},{5,4},{6,5},{7,6},{9,8},{10,9},{11,10},{13,12},{... | collective-permute-start | bytes 3538952 | tf_op jit(solution)/shard_map/ppermute | solution.py:824
  357.8 31.5 %collective-permute-start.25 = (f32[1,192,512]{2,1,0:T(8,128)}, f32[1,192,512]{2,1,0:T(8,128)}, u32[]{:S(2)}, u32[]{:S(2)}) collective-permute-start(f32[1,192,512]{2,1,0:T(8,128)} %add.195), channel_id=1, source_target_pairs={{0,1},{1,0},{2,3},{3,2},{4,5},{5,4},{6,7},{7,6},{8,9},{9,8},{10,11... | collective-permute-start | bytes 1179656 | tf_op jit(solution)/shard_map/ppermute | solution.py:759
  377.8 14.0 %collective-permute-start.23 = (f32[384,768]{1,0:T(8,128)S(1)}, f32[384,768]{1,0:T(8,128)S(1)}, u32[]{:S(2)}, u32[]{:S(2)}) collective-permute-start(f32[384,768]{1,0:T(8,128)S(1)} %slice.139), channel_id=1, source_target_pairs={{0,4},{4,0},{8,12},{12,8},{16,20},{20,16},{24,28},{28,24},{1,5},{5... | collective-permute-start | bytes 3538952 | tf_op jit(solution)/shard_map/ppermute | solution.py:688
  396.5 1.3 collective-permute-start.27
  397.8 3.8 collective-permute-start.28
  401.6 4.9 collective-permute-start.29
  408.6 16.3 %collective-permute-start.30 = (f32[1,48,3072]{2,1,0:T(8,128)S(1)}, f32[1,48,3072]{2,1,0:T(8,128)S(1)}, u32[]{:S(2)}, u32[]{:S(2)}) collective-permute-start(f32[1,48,3072]{2,1,0:T(8,128)S(1)} %slice_select_fusion.4), channel_id=1, source_target_pairs={{0,1},{1,0},{2,3},{3,2},{4,5},{5,4},{6,7},{7,6},{8,9},{9,8},{10,11... | collective-permute-start | bytes 1769480 | tf_op jit(solution)/shard_map/ppermute | solution.py:759
  408.9 18.1 %collective-permute-start.32 = (f32[3,96,512]{2,1,0:T(8,128)S(1)}, f32[3,96,512]{2,1,0:T(8,128)S(1)}, u32[]{:S(2)}, u32[]{:S(2)}) collective-permute-start(f32[3,96,512]{2,1,0:T(8,128)S(1)} %slice_select_fusion.2), channel_id=1, source_target_pairs={{0,4},{4,0},{8,12},{12,8},{16,20},{20,16},{24,28},{28,24},{1,5},{5... | collective-permute-start | bytes 1769480 | tf_op jit(solution)/shard_map/ppermute | solution.py:688
  409.7 57.9 %collective-permute-start.33 = (f32[384,768]{1,0:T(8,128)}, f32[384,768]{1,0:T(8,128)}, u32[]{:S(2)}, u32[]{:S(2)}) collective-permute-start(f32[384,768]{1,0:T(8,128)} %add.196), channel_id=1, source_target_pairs={{1,0},{2,1},{3,2},{5,4},{6,5},{7,6},{9,8},{10,9},{11,10},{13,12},{... | collective-permute-start | bytes 3538952 | tf_op jit(solution)/shard_map/ppermute | solution.py:855
  425.8 40.5 %collective-permute-start.31 = (f32[1,48,3072]{2,1,0:T(8,128)}, f32[1,48,3072]{2,1,0:T(8,128)}, u32[]{:S(2)}, u32[]{:S(2)}) collective-permute-start(f32[1,48,3072]{2,1,0:T(8,128)} %select_add_fusion), channel_id=1, source_target_pairs={{0,2},{1,3},{2,0},{3,1},{4,6},{5,7},{6,4},{7,5},{8,10},{9,11},{10,... | collective-permute-start | bytes 1769480 | tf_op jit(solution)/shard_map/ppermute | solution.py:759
  433.1 34.5 %copy-start.11 = (f32[384,768]{1,0:T(8,128)S(1)}, f32[384,768]{1,0:T(8,128)}, u32[]{:S(2)}) copy-start(f32[384,768]{1,0:T(8,128)} %shard_map.250) | copy-start | bytes 3538948
  433.1 34.5 %copy-start.34 = (f32[768]{0:T(1024)S(1)}, f32[768]{0:T(1024)}, u32[]{:S(2)}) copy-start(f32[768]{0:T(1024)} %param.20) | copy-start | bytes 9220
  469.6 4.2 collective-permute-start.34
  469.7 15.3 %collective-permute-start.36 = (f32[1,48,3072]{2,1,0:T(8,128)S(1)}, f32[1,48,3072]{2,1,0:T(8,128)S(1)}, u32[]{:S(2)}, u32[]{:S(2)}) collective-permute-start(f32[1,48,3072]{2,1,0:T(8,128)S(1)} %add.209), channel_id=1, source_target_pairs={{0,1},{1,0},{2,3},{3,2},{4,5},{5,4},{6,7},{7,6},{8,9},{9,8},{10,11... | collective-permute-start | bytes 1769480 | tf_op jit(solution)/shard_map/ppermute | solution.py:759
  473.8 10.0 %collective-permute-start.35 = (f32[8,768]{1,0:T(8,128)S(1)}, f32[8,768]{1,0:T(8,128)S(1)}, u32[]{:S(2)}, u32[]{:S(2)}) collective-permute-start(f32[8,768]{1,0:T(8,128)S(1)} %add.212), channel_id=1, source_target_pairs={{0,2},{1,3},{2,0},{3,1},{4,6},{5,7},{6,4},{7,5},{8,10},{9,11},{10,... | collective-permute-start | bytes 73736 | tf_op jit(solution)/shard_map/ppermute | solution.py:759
  (38 other events, 295.7 us)
Sparse Core Ops, SparseCore 0:
  9.9 69.1 all-gather.2
  81.0 38.7 all-gather.4
  165.8 43.2 reduce-scatter.12
  211.9 43.9 reduce-scatter.14
  258.7 43.9 reduce-scatter.16
  332.1 58.0 reduce-scatter.18

commit v12 on v7

--- a/solution.py
+++ b/solution.py
@@ -538,14 +538,20 @@
     )(part, given, resid, cot, gain, scale, w_full)
 
 
-def place_rows(core_ref, out_ref, got):
-    chips = out_ref.shape[1]
-    tall = out_ref.shape[2]
-    for block in range(2 * chips):
-        out_ref[(block & 1) ^ core_ref[0], block // 2] = got[block * tall:(block + 1) * tall]
-
-
-def weights_qk_kernel(core_ref, hi_ref, lo_ref, dq_ref, dk_ref, out_ref, nt_hi, nt_lo):
+def place_rows(core_ref, out_refs, got):
+    chips, tall = out_refs[0].shape[:2]
+
+    def store(core):
+        for block in range(2 * chips):
+            ref = out_refs[(block & 1) ^ core]
+            ref[block // 2] = got[block * tall:(block + 1) * tall]
+
+    for core in range(2):
+        pl.when(core_ref[0] == core)(functools.partial(store, core))
+
+
+def weights_qk_kernel(core_ref, hi_ref, lo_ref, dq_ref, dk_ref, own_ref, sib_ref, nt_hi, nt_lo):
+    out_ref = (own_ref, sib_ref)
     step = pl.program_id(0)
     part = pl.num_programs(0) // 2
     halo = hi_ref.shape[0] - dq_ref.shape[0]
@@ -566,8 +572,9 @@
         place_rows(core_ref, out_ref, three(dot_nn, left, split(dk_ref[...])))
 
 
-def weights_vo_kernel(core_ref, hi_ref, lo_ref, dv_ref, att_ref, res_ref, out_ref,
+def weights_vo_kernel(core_ref, hi_ref, lo_ref, dv_ref, att_ref, res_ref, own_ref, sib_ref,
                       nt_hi, nt_lo, at_hi, at_lo):
+    out_ref = (own_ref, sib_ref)
     step = pl.program_id(0)
     part = pl.num_programs(0) // 2
 
@@ -607,13 +614,51 @@
             num_scalar_prefetch=1,
             grid=(2 * part,),
             in_specs=[fixed(v) for v in fixed_args] + specs,
-            out_specs=pl.BlockSpec((2, chips, tall, wide), lambda j, c: (0, 0, 0, j)),
+            out_specs=[pl.BlockSpec((chips, tall, wide), lambda j, c: (0, 0, j))] * 2,
             scratch_shapes=[pltpu.VMEM((model, n), BF16) for n in scratch],
         ),
-        out_shape=jax.ShapeDtypeStruct((2, chips, tall, 2 * model), F32),
+        out_shape=[jax.ShapeDtypeStruct((chips, tall, 2 * model), F32)] * 2,
         cost_estimate=cost(micros),
         compiler_params=params(),
     )(core, *fixed_args, *args)
+
+
+def partial_kernel(count, *refs):
+    grads, w_ref, out_ref = refs[:count], refs[count], refs[count + 1]
+    held = refs[count + 2:]
+    model = grads[0].shape[1]
+    first = 3 - count
+
+    @pl.when(pl.program_id(0) == 0)
+    def _():
+        for at, ref in enumerate(grads):
+            held[2 * at][...], held[2 * at + 1][...] = split(ref[...])
+
+    total = None
+    for at in range(count):
+        weights = split(w_ref[:, (first + at) * model:(first + at + 1) * model])
+        term = three(dot_nt, (held[2 * at][...], held[2 * at + 1][...]), weights)
+        total = term if total is None else total + term
+    out_ref[...] = total
+
+
+def partial_rows(block, grads, w_full):
+    model = w_full.shape[0]
+    rows = grads[0].shape[0] if len(grads) == 3 else grads[0].shape[0] // 3
+    wide = 256
+    specs = [pl.BlockSpec((rows, model), lambda j: (block, 0))] * 2
+    if len(grads) == 3:
+        specs = [pl.BlockSpec((rows, model), lambda j: (0, 0))] + specs
+    return pl.pallas_call(
+        functools.partial(partial_kernel, len(grads)),
+        grid=(model // wide,),
+        in_specs=specs + [pl.BlockSpec((wide, 3 * model), lambda j: (j, 0))],
+        out_specs=pl.BlockSpec((rows, wide), lambda j: (0, j)),
+        out_shape=jax.ShapeDtypeStruct((rows, model), F32),
+        scratch_shapes=[pltpu.VMEM((rows, model), BF16)] * (2 * len(grads)),
+        cost_estimate=cost(6),
+        compiler_params=params(),
+    )(*grads, w_full)
 
 
 def matmul(left, right):
@@ -704,9 +749,6 @@
         downs = [(value, below + at) for value in (own, *sides)] + [(diagonal[1], at)]
         return ups + downs
 
-    first_sides = sides_of(first_own)
-    first_diagonal = diagonal_of(first_sides)
-
     numbers = jnp.pad((segments + 1).astype(F32), ((0, 7), (0, model - rows)))
     near = lax.ppermute(jnp.concatenate([block_input, numbers], axis=0), "seq", ahead)
     far = lax.ppermute(near, "seq", ahead)
@@ -715,8 +757,6 @@
     ).astype(jnp.int32)
     seg_k_row = jnp.broadcast_to(seg_all, (8, halo + rows))
     seg_k_col = jnp.broadcast_to(seg_all.reshape(-1, 1), (halo + rows, 128))
-    seg_q_row = seg_k_row[:, halo:]
-    seg_q_col = seg_k_col[halo:]
 
     cos_all, sin_all = rotary_tables(length, halo)
     cosine = lax.dynamic_slice_in_dim(jnp.asarray(cos_all), place * rows, halo + rows, 0)
@@ -725,22 +765,26 @@
     earlier = (embedding, earlier_outs[0], earlier_outs[1], earlier_outs[2])
     base = sum(dwa_weights[i] * value for i, value in enumerate(earlier))
     dots = jnp.stack([jnp.sum(cotangent * value) for value in earlier])
-    qkv_full, rest_own, far, base, dots, first_sides, first_diagonal = together(
-        (qkv_full, rest_own, far, base, dots, first_sides, first_diagonal)
-    )
-    rest_sides = sides_of(rest_own)
+    tables = (cosine, sine, seg_k_row, seg_k_col)
+    far, base, dots, qkv_full, first_own, rest_own, tables = together(
+        (far, base, dots, qkv_full, first_own, rest_own, tables)
+    )
+    cosine, sine, seg_k_row, seg_k_col = tables
+    seg_q_row, seg_q_col = seg_k_row[:, halo:], seg_k_col[halo:]
+    first_sides, rest_sides = sides_of(first_own), sides_of(rest_own)
 
     q_rot, kv, normed_hi, normed_lo = project(
         far, near, block_input, gain1, bias1, qkv_full, cosine, sine
     )
     attended = attend(q_rot, kv, seg_q_col, seg_k_row)
-    attended, rest_sides = together((attended, rest_sides))
-    rest_diagonal = diagonal_of(rest_sides)
+    attended, first_sides = together((attended, first_sides))
+    first_diagonal = diagonal_of(first_sides)
 
     out_full = gather(w_out)
     resid = block_input + matmul(attended, out_full)
+    resid, rest_sides, first_diagonal = together((resid, rest_sides, first_diagonal))
+    rest_diagonal = diagonal_of(rest_sides)
     resid_other = swap(resid)
-    resid_other, rest_diagonal = together((resid_other, rest_diagonal))
     cot_other = swap(cotangent)
     scale = dwa_weights[4].reshape(1, 1)
     call = functools.partial(
@@ -758,6 +802,8 @@
         else:
             weights = pieces(rest_own, rest_sides, rest_diagonal, third_at - 1)
         out_part, gnorm_part, grads = call(so_far, weights)
+        if third_at == 0:
+            grads, rest_diagonal = together((grads, rest_diagonal))
         so_far = (out_part, gnorm_part)
         shards.append(scatter_chips(grads)[0])
     given = swap(gnorm_part[rows:])
@@ -814,7 +860,7 @@
         weights_vo_kernel, 9, core_at, chips, normed_parts,
         [(dv, 0), (attended, None), (grad_resid, 1)], [halo + rows] * 2 + [rows] * 2,
     )
-    line_c, grads_vo = together((line_c, grads_vo))
+    line_c, ends_b, grads_vo = together((line_c, ends_b, grads_vo))
     line_c = line_middle(line_c)
     grads_c = jnp.concatenate([grads_qk[0] + given_qk, grads_vo[0] + swap(grads_vo[1])], axis=2)
     grads_c, out_part = together((grads_c, out_part))
@@ -825,20 +871,20 @@
     output = base + dwa_weights[4] * block_out
     dwa_local = jnp.concatenate([dots, jnp.sum(cotangent * block_out)[None]])
 
-    wq, wk, wv = (qkv_full[:, i * model:(i + 1) * model] for i in range(3))
-    part_far = outer_cols(dk[:rows], wk) + outer_cols(dv[:rows], wv)
-    dk_rest, dv_rest, far, near, part_far = together((dk[rows:], dv[rows:], far, near, part_far))
+    part_far = partial_rows(0, (dk, dv), qkv_full)
     given_near = lax.ppermute(part_far, "seq", behind)
-    part_rest = outer_cols(dk_rest, wk) + outer_cols(dv_rest, wv)
-    own_part = part_rest[rows:] + outer_cols(dq, wq)
-    line_c, ends_b, part_rest, own_part = together((line_c, ends_b, part_rest, own_part))
+    dk, far, near, line_c, part_far = together((dk, far, near, line_c, part_far))
     ends_c = line_end(line_c)
-    back_near = part_rest[:rows] + given_near
+    part_near = partial_rows(1, (dk, dv), qkv_full)
+    own_part = partial_rows(2, (dq, dk, dv), qkv_full)
+    own_part, ends_c = together((own_part, ends_c))
+    (sent,) = together((part_near,))
+    back_near = sent + given_near
 
     xhat1, rate1 = norm_stats(block_input)
     terms = (
         (norm_stats(far[:rows])[0], part_far),
-        (norm_stats(near[:rows])[0], part_rest[:rows]),
+        (norm_stats(near[:rows])[0], part_near),
         (xhat1, own_part),
     )
     grad_gain_one = sum(jnp.sum(xhat * part, axis=0) for xhat, part in terms)
@@ -855,7 +901,7 @@
     while bit < devices:
         small = small + exchange(small, bit)
         bit *= 2
-    shard_c, ends_c, back_near, small = together((shard_c, ends_c, back_near, small))
+    shard_c, back_near, small = together((shard_c, back_near, small))
     last = line_middle(line_start(shard_c[None]))
     given_back = lax.ppermute(back_near, "seq", behind)
     grad_up, grad_down = unpack_grads(

time: 531 us -> 510 us (0.960)
  Pallas kernels: 196 us -> 213 us
  matrix products: 18.9 us -> 3.7 us
  waiting for transfers between devices: 156 us -> 144 us
  local copies, waits for them, and re-layouts: 51.1 us -> 42 us
    pallas_call x0 -> x3, Pallas kernels: none -> 24.9 us  [partial_rows(): pl.pallas_call(functools.partial(partial_kernel, len(grads)), grid=(model...]
    ppermute x1, waiting for transfers between devices: 2.75 us -> 21.9 us  [body(): far = lax.ppermute(near, 'seq', ahead)]
    dot_general x5 -> x0, matrix products: 15.1 us -> none  [outer_cols(): lax.dot_general(left, right, (((1,), (1,)), ((), ())), precision=HIGH)]
    ppermute x1, waiting for transfers between devices: 20.2 us -> 5.47 us  [body(): lax.ppermute(jnp.concatenate([block_input, numbers], axis=0), 'seq', ahead)]
    ppermute x19, waiting for transfers between devices: 36.7 us -> 22.8 us  [body(): lax.ppermute(v, 'dp', [(i, i ^ bit) for i in range(devices)])]
    pallas_call x3, Pallas kernels: 71.5 us -> 62 us  [mlp(): pl.pallas_call(functools.partial(mlp_kernel, count, len(so_far) // 2), gr...]
    unnamed x113 -> x100, local copies, waits for them, and re-layouts: 6.44 us -> 13.7 us
    another operation x4, local copies, waits for them, and re-layouts: 7.09 us -> 1.22 us  [unpack_grads(): jnp.stack([jnp.where(core == 0, mine, other), jnp.where(core == 0, other,...]
  transfers between devices with their start and end apart: 43 -> 43, of which waited for: 21 -> 20; matrix products, arithmetic and copies ran while one was open for 19% -> 15% of each run, Pallas kernels for 32% -> 42%
where the time goes in v12:
time: 510 us; the launch traced here: 505 us
  Pallas kernels  213 us (42%)
  waiting for transfers between devices  144 us (28%)
  other arithmetic  46.3 us (9%)
  local copies, waits for them, and re-layouts  42 us (8%)
  starting transfers between devices  41 us (8%)
  between operations  15.3 us (3%)
    ppermute x14, waiting for transfers between devices, body(): lax.ppermute(v, 'seq', [(i, i ^ bit) for i in range(groups)])  88.1 us
    pallas_call x3, Pallas kernels, mlp(): pl.pallas_call(functools.partial(mlp_kernel, count, len(so_far) // 2), gr...  62 us
    pallas_call x2, Pallas kernels, attend_back(): pl.pallas_call(attend_back_kernel, grid=(count,), in_specs=[pl.BlockSpec(...  47.1 us
    pallas_call x2, Pallas kernels, weight_call(): pl.pallas_call(kernel, grid_spec=pltpu.PrefetchScalarGridSpec(num_scalar_...  26.4 us
    pallas_call x3, Pallas kernels, partial_rows(): pl.pallas_call(functools.partial(partial_kernel, len(grads)), grid=(model...  24.9 us
    pallas_call x1, Pallas kernels, attend(): pl.pallas_call(attend_kernel, grid=(pairs,), in_specs=[pl.BlockSpec((rows...  23.1 us
    ppermute x19, waiting for transfers between devices, body(): lax.ppermute(v, 'dp', [(i, i ^ bit) for i in range(devices)])  22.8 us
    ppermute x1, waiting for transfers between devices, body(): far = lax.ppermute(near, 'seq', ahead)  21.9 us
  transfers between devices with their start and end apart: 43, of which 20 were waited for; matrix products, arithmetic and copies ran while one was open for 15% of the time, Pallas kernels for 42%

profile of v12, /device:TPU:0, one launch (start us, length us, event | category | flops | bytes accessed | tf_op | source)
XLA Modules:
  0.0 505.3 jit_solution(17653812156427408553)
XLA Ops:
  8.6 2.4 select_maximum_fusion
  11.0 5.0 collective-permute-start
  16.0 1.9 reshape.185
  21.1 7.3 %fusion.5 = (f32[]{:T(128)}, f32[]{:T(128)}, f32[]{:T(128)}, f32[]{:T(128)}, f32[384,768]{1,0:T(8,128)}) fusion(f32[384,768]{1,0:T(8,128)S(1)} %copy-done.10, f32[3,384,768]{2,1,0:T(8,128)} %param.18, f32[384,768]{1,0:T(8,128)} %param.17, f32[]{:T(128)} %bitcast.5, f32[]{:T(128)} %bitcast.3, f32[]{:T(128)} %bitcast.1, f32[]{:T(128)} %bitcast), kind=kLoop, calls=%fused_computation.22 | loop fusion | flops 4423676 | bytes 7077920 | tf_op jit(solution)/shard_map/reduce_sum | solution.py:767
  28.8 3.2 pad_maximum_fusion.2
  33.0 2.4 constant_dynamic-slice_fusion
  36.5 5.5 %collective-permute-done.near_ref = f32[392,768]{1,0:T(8,128)S(1)} collective-permute-done((f32[392,768]{1,0:T(8,128)}, f32[392,768]{1,0:T(8,128)S(1)}, u32[]{:S(2)}, u32[]{:S(2)}) %collective-permute-start) | collective-permute-done | bytes 1204256 | tf_op jit(solution)/shard_map/ppermute | solution.py:753
  42.0 4.9 collective-permute-start.1
  49.3 21.9 %collective-permute-done.1.far_ref = f32[392,768]{1,0:T(8,128)S(1)} collective-permute-done((f32[392,768]{1,0:T(8,128)S(1)}, f32[392,768]{1,0:T(8,128)S(1)}, u32[]{:S(2)}, u32[]{:S(2)}) %collective-permute-start.1) | collective-permute-done | bytes 1204256 | tf_op jit(solution)/shard_map/ppermute | solution.py:754
  78.2 21.7 %shard_map.239 = (f32[384,768]{1,0:T(8,128)}, f32[1152,1536]{1,0:T(8,128)}, bf16[1152,768]{1,0:T(8,128)(2,1)}, bf16[1152,768]{1,0:T(8,128)(2,1)}) custom-call(f32[392,768]{1,0:T(8,128)} %copy-done.4, f32[392,768]{1,0:T(8,128)} %copy-done.2, f32[384,768]{1,0:T(8,128)} %own_ref.1, f32[1,768]{1,0:T(1,128)} %broadcast_in_dim.22.gain_ref, ...), custom_call_target="tpu_custom_call" | custom-call | flops 550000000 | bytes 1048576 | tf_op jit(solution)/shard_map/pallas_call | solution.py:144
  100.0 23.1 %shard_map.240.att_ref = f32[384,768]{1,0:T(8,128)} custom-call(f32[384,768]{1,0:T(8,128)} %get-tuple-element.160.q_ref, f32[1152,1536]{1,0:T(8,128)} %get-tuple-element.161.k_ref.v_ref, f32[1152,1536]{1,0:T(8,128)} %get-tuple-element.161.k_ref.v_ref, s32[384,128]{1,0:T(8,128)} %slice.221.segq_ref, s32[8,1152]{1,0:T(8,128)} %broadcast_in_dim.20.segk_ref), custom_call_target="tpu_custom_call" | custom-call | flops 550000000 | bytes 1048576 | tf_op jit(solution)/shard_map/pallas_call | solution.py:236
  123.0 10.2 %collective-permute-done.4.refs_2_.refs_6_ = f32[384,512]{1,0:T(8,128)S(1)} collective-permute-done((f32[384,512]{1,0:T(8,128)}, f32[384,512]{1,0:T(8,128)S(1)}, u32[]{:S(2)}, u32[]{:S(2)}) %collective-permute-start.4) | collective-permute-done | bytes 786464 | tf_op jit(solution)/shard_map/ppermute | solution.py:708
  137.4 3.7 convolution_add_fusion.resid_ref
  141.2 4.3 collective-permute-done.8.refs_7_
  153.1 19.9 %shard_map.241 = (f32[768,768]{1,0:T(8,128)}, f32[768,768]{1,0:T(8,128)}, f32[4,1,384,512]{3,2,1,0:T(8,128)}) custom-call(s32[1]{0:T(128)} %bitcast.14.chip_ref, f32[384,768]{1,0:T(8,128)} %copy-done.14, f32[384,768]{1,0:T(8,128)} %copy-done.43, f32[384,768]{1,0:T(8,128)} %cot_ref.7, f32[384,768]{1,0:T(8,128)} %collective-permute-done.10.cot_other_ref, ...), custom_call_target="tpu_custom_call" | custom-call | flops 19800000512 | bytes 1048576 | tf_op jit(solution)/shard_map/pallas_call | solution.py:465
  174.9 21.0 %shard_map.242 = (f32[768,768]{1,0:T(8,128)}, f32[768,768]{1,0:T(8,128)}, f32[4,1,384,512]{3,2,1,0:T(8,128)}) custom-call(s32[1]{0:T(128)} %bitcast.14.chip_ref, f32[384,768]{1,0:T(8,128)} %copy-done.14, f32[384,768]{1,0:T(8,128)} %copy-done.43, f32[384,768]{1,0:T(8,128)} %cot_ref.7, f32[384,768]{1,0:T(8,128)} %collective-permute-done.10.cot_other_ref, ...), custom_call_target="tpu_custom_call" | custom-call | flops 19800000512 | bytes 1048576 | tf_op jit(solution)/shard_map/pallas_call | solution.py:465
  196.2 21.1 %shard_map.243 = (f32[768,768]{1,0:T(8,128)}, f32[768,768]{1,0:T(8,128)}, f32[4,1,384,512]{3,2,1,0:T(8,128)}) custom-call(s32[1]{0:T(128)} %bitcast.14.chip_ref, f32[384,768]{1,0:T(8,128)} %copy-done.14, f32[384,768]{1,0:T(8,128)} %copy-done.43, f32[384,768]{1,0:T(8,128)} %cot_ref.7, f32[384,768]{1,0:T(8,128)} %collective-permute-done.10.cot_other_ref, ...), custom_call_target="tpu_custom_call" | custom-call | flops 19800000512 | bytes 1048576 | tf_op jit(solution)/shard_map/pallas_call | solution.py:465
  221.5 1.6 slice_select_fusion.7
  223.1 2.1 collective-permute-start.14
  225.2 7.6 %shard_map.244 = (f32[384,768]{1,0:T(8,128)}, f32[384,768]{1,0:T(8,128)}, f32[8,768]{1,0:T(8,128)}) custom-call(f32[768,768]{1,0:T(8,128)} %get-tuple-element.142.part_ref, f32[384,768]{1,0:T(8,128)} %copy-done.44, f32[384,768]{1,0:T(8,128)} %copy-done.14, f32[384,768]{1,0:T(8,128)} %cot_ref.7, f32[1,768]{1,0:T(1,128)} %broadcast_in_dim.48.gain_ref, ...), custom_call_target="tpu_custom_call" | custom-call | flops 6600000000 | bytes 1048576 | tf_op jit(solution)/shard_map/pallas_call | solution.py:525
  232.8 1.8 collective-permute-done.14
  234.7 2.7 collective-permute-start.15
  237.4 23.5 %shard_map.245 = (f32[384,768]{1,0:T(8,128)}, f32[1152,768]{1,0:T(8,128)}, f32[1152,768]{1,0:T(8,128)}) custom-call(f32[384,768]{1,0:T(8,128)} %get-tuple-element.160.q_ref, f32[1152,1536]{1,0:T(8,128)} %get-tuple-element.161.k_ref.v_ref, f32[1152,1536]{1,0:T(8,128)} %get-tuple-element.161.k_ref.v_ref, f32[384,768]{1,0:T(8,128)} %get-tuple-element.162.g_ref, ...), custom_call_target="tpu_custom_call" | custom-call | flops 23100000256 | bytes 1048576 | tf_op jit(solution)/shard_map/pallas_call | solution.py:328
  261.0 5.0 reduce-scatter.15.cloned.1.call-done
  269.3 23.6 %shard_map.246 = (f32[384,768]{1,0:T(8,128)}, f32[1152,768]{1,0:T(8,128)}, f32[1152,768]{1,0:T(8,128)}) custom-call(f32[384,768]{1,0:T(8,128)} %get-tuple-element.160.q_ref, f32[1152,1536]{1,0:T(8,128)} %get-tuple-element.161.k_ref.v_ref, f32[1152,1536]{1,0:T(8,128)} %get-tuple-element.161.k_ref.v_ref, ...), custom_call_target="tpu_custom_call", output_to_operand_aliasing={{0}: (8, {}), {1}: (9, {}), {2}: (10, {})} | custom-call | flops 23100000256 | bytes 1048576 | tf_op jit(solution)/shard_map/pallas_call | solution.py:328
  294.0 2.4 collective-permute-start.19
  296.4 12.8 %shard_map.247 = (f32[4,96,1536]{2,1,0:T(8,128)}, f32[4,96,1536]{2,1,0:T(8,128)}) custom-call(s32[1]{0:T(128)} %bitcast.13.core_ref, bf16[1152,768]{1,0:T(8,128)(2,1)} %get-tuple-element.128.hi_ref, bf16[1152,768]{1,0:T(8,128)(2,1)} %get-tuple-element.129.lo_ref, f32[384,768]{1,0:T(8,128)} %get-tuple-element.173.dq_ref.refs_0_, ...), custom_call_target="tpu_custom_call" | custom-call | flops 9900000256 | bytes 1048576 | tf_op jit(solution)/shard_map/pallas_call | solution.py:611
  309.2 4.4 collective-permute-done.19
  317.0 13.6 %shard_map.248 = (f32[4,96,1536]{2,1,0:T(8,128)}, f32[4,96,1536]{2,1,0:T(8,128)}) custom-call(s32[1]{0:T(128)} %bitcast.13.core_ref, bf16[1152,768]{1,0:T(8,128)(2,1)} %get-tuple-element.128.hi_ref, bf16[1152,768]{1,0:T(8,128)(2,1)} %get-tuple-element.129.lo_ref, f32[1152,768]{1,0:T(8,128)} %get-tuple-element.183.dv_ref.refs_1_.refs_2_, ...), custom_call_target="tpu_custom_call" | custom-call | flops 9900000256 | bytes 1048576 | tf_op jit(solution)/shard_map/pallas_call | solution.py:611
  330.7 2.7 collective-permute-done.21
  334.8 4.3 collective-permute-done.22
  339.5 2.5 pad_maximum_fusion
  344.4 3.1 collective-permute-start.24
  347.6 7.9 %shard_map.249 = f32[384,768]{1,0:T(8,128)} custom-call(f32[1152,768]{1,0:T(8,128)} %get-tuple-element.192.dk_ref.refs_0_.refs_1_, f32[1152,768]{1,0:T(8,128)} %get-tuple-element.183.dv_ref.refs_1_.refs_2_, f32[768,2304]{1,0:T(8,128)} %all-gather.3.cloned.1.call-done.w_ref.refs_2_.refs_3_), custom_call_target="tpu_custom_call" | custom-call | flops 6600000000 | bytes 1048576 | tf_op jit(solution)/shard_map/pallas_call | solution.py:652
  356.9 9.0 %collective-permute-done.24 = f32[1,192,512]{2,1,0:T(8,128)S(1)} collective-permute-done((f32[1,192,512]{2,1,0:T(8,128)S(1)}, f32[1,192,512]{2,1,0:T(8,128)S(1)}, u32[]{:S(2)}, u32[]{:S(2)}) %collective-permute-start.24) | collective-permute-done | bytes 393248 | tf_op jit(solution)/shard_map/ppermute | solution.py:811
  367.1 9.3 %shard_map.250 = f32[384,768]{1,0:T(8,128)} custom-call(f32[384,768]{1,0:T(8,128)} %get-tuple-element.173.dq_ref.refs_0_, f32[1152,768]{1,0:T(8,128)} %get-tuple-element.192.dk_ref.refs_0_.refs_1_, f32[1152,768]{1,0:T(8,128)} %get-tuple-element.183.dv_ref.refs_1_.refs_2_, f32[768,2304]{1,0:T(8,128)} %all-gather.3.cloned.1.call-done.w_ref.refs_2_.refs_3_), custom_call_target="tpu_custom_call" | custom-call | flops 6600000000 | bytes 1048576 | tf_op jit(solution)/shard_map/pallas_call | solution.py:652
  376.4 7.7 %shard_map.251 = f32[384,768]{1,0:T(8,128)} custom-call(f32[1152,768]{1,0:T(8,128)} %get-tuple-element.192.dk_ref.refs_0_.refs_1_, f32[1152,768]{1,0:T(8,128)} %get-tuple-element.183.dv_ref.refs_1_.refs_2_, f32[768,2304]{1,0:T(8,128)} %all-gather.3.cloned.1.call-done.w_ref.refs_2_.refs_3_), custom_call_target="tpu_custom_call" | custom-call | flops 6600000000 | bytes 1048576 | tf_op jit(solution)/shard_map/pallas_call | solution.py:652
  386.1 13.0 %collective-permute-done.25 = f32[1,192,512]{2,1,0:T(8,128)S(1)} collective-permute-done((f32[1,192,512]{2,1,0:T(8,128)S(1)}, f32[1,192,512]{2,1,0:T(8,128)S(1)}, u32[]{:S(2)}, u32[]{:S(2)}) %collective-permute-start.25) | collective-permute-done | bytes 393248 | tf_op jit(solution)/shard_map/ppermute | solution.py:811
  401.7 2.6 multiply_reduce_fusion.1
  409.2 1.8 constant_dynamic-update-slice_fusion.5
  413.1 1.8 constant_dynamic-update-slice_fusion.4
  414.8 2.4 add.198
  422.4 13.1 %collective-permute-done.30 = f32[1,48,3072]{2,1,0:T(8,128)S(1)} collective-permute-done((f32[1,48,3072]{2,1,0:T(8,128)S(1)}, f32[1,48,3072]{2,1,0:T(8,128)S(1)}, u32[]{:S(2)}, u32[]{:S(2)}) %collective-permute-start.30) | collective-permute-done | bytes 589856 | tf_op jit(solution)/shard_map/ppermute | solution.py:811
  444.4 33.3 %collective-permute-done.31 = f32[1,48,3072]{2,1,0:T(8,128)} collective-permute-done((f32[1,48,3072]{2,1,0:T(8,128)}, f32[1,48,3072]{2,1,0:T(8,128)}, u32[]{:S(2)}, u32[]{:S(2)}) %collective-permute-start.31) | collective-permute-done | bytes 589856 | tf_op jit(solution)/shard_map/ppermute | solution.py:811
  479.0 1.9 fusion.11
  481.0 2.0 collective-permute-start.36
  483.1 2.1 collective-permute-done.34
  486.6 8.6 %collective-permute-done.35 = f32[8,768]{1,0:T(8,128)S(1)} collective-permute-done((f32[8,768]{1,0:T(8,128)S(1)}, f32[8,768]{1,0:T(8,128)S(1)}, u32[]{:S(2)}, u32[]{:S(2)}) %collective-permute-start.35) | collective-permute-done | bytes 24608 | tf_op jit(solution)/shard_map/ppermute | solution.py:811
  (267 shorter events, 80.2 us)
Async XLA Ops:
  7.2 64.1 %all-gather.3.cloned.1.call-start = ((), (), s32[]{:S(2)}) async-start(), calls=%async_computation.4 | async-start | bytes 7962624 | tf_op jit(solution)/shard_map/all_gather | solution.py:711
  7.9 129.5 %all-gather.5.cloned.1.call-start = ((), (), s32[]{:S(2)}) async-start(), calls=%async_computation.5 | async-start | bytes 2654208 | tf_op jit(solution)/shard_map/all_gather | solution.py:711
  11.0 31.0 %collective-permute-start = (f32[392,768]{1,0:T(8,128)}, f32[392,768]{1,0:T(8,128)S(1)}, u32[]{:S(2)}, u32[]{:S(2)}) collective-permute-start(f32[392,768]{1,0:T(8,128)} %select_maximum_fusion), channel_id=1, source_target_pairs={{0,1},{1,2},{2,3},{4,5},{5,6},{6,7},{8,9},{9,10},{10,11},{12,13},{... | collective-permute-start | bytes 3612680 | tf_op jit(solution)/shard_map/ppermute | solution.py:753
  20.4 15.0 %collective-permute-start.2 = (f32[96,1536]{1,0:T(8,128)}, f32[96,1536]{1,0:T(8,128)}, u32[]{:S(2)}, u32[]{:S(2)}) collective-permute-start(f32[96,1536]{1,0:T(8,128)} %select_n.145), channel_id=1, source_target_pairs={{0,4},{4,0},{8,12},{12,8},{16,20},{20,16},{24,28},{28,24},{1,5},{5... | collective-permute-start | bytes 1769480 | tf_op jit(solution)/shard_map/ppermute | solution.py:708
  20.4 201.1 %reduce-scatter.13.cloned.1.call-start = ((), (), s32[]{:S(2)}) async-start(), calls=%async_computation.6 | async-start | bytes 3932160
  42.0 29.2 %collective-permute-start.1 = (f32[392,768]{1,0:T(8,128)S(1)}, f32[392,768]{1,0:T(8,128)S(1)}, u32[]{:S(2)}, u32[]{:S(2)}) collective-permute-start(f32[392,768]{1,0:T(8,128)S(1)} %collective-permute-done.near_ref), channel_id=1, source_target_pairs={{0,1},{1,2},{2,3},{4,5},{5,6},{6,7},{8,9},{9,10},{10,11},{12,13},{... | collective-permute-start | bytes 3612680 | tf_op jit(solution)/shard_map/ppermute | solution.py:754
  48.3 28.0 %copy-start.39 = (f32[768]{0:T(1024)S(1)}, f32[768]{0:T(1024)}, u32[]{:S(2)}) copy-start(f32[768]{0:T(1024)} %param.21) | copy-start | bytes 9220
  48.3 28.6 %copy-start.35 = (f32[768]{0:T(1024)S(1)}, f32[768]{0:T(1024)}, u32[]{:S(2)}) copy-start(f32[768]{0:T(1024)} %param.20) | copy-start | bytes 9220
  72.2 74.6 %collective-permute-start.6 = (f32[768,512]{1,0:T(8,128)}, f32[768,512]{1,0:T(8,128)}, u32[]{:S(2)}, u32[]{:S(2)}) collective-permute-start(f32[768,512]{1,0:T(8,128)} %copy-done.33), channel_id=1, source_target_pairs={{0,16},{4,20},{8,24},{12,28},{16,0},{20,4},{24,8},{28,12},{1,17},{... | collective-permute-start | bytes 4718600 | tf_op jit(solution)/shard_map/ppermute | solution.py:708
  73.8 73.0 %collective-permute-start.5 = (f32[768,512]{1,0:T(8,128)}, f32[768,512]{1,0:T(8,128)}, u32[]{:S(2)}, u32[]{:S(2)}) collective-permute-start(f32[768,512]{1,0:T(8,128)} %copy-done.33), channel_id=1, source_target_pairs={{0,8},{4,12},{8,0},{12,4},{16,24},{20,28},{24,16},{28,20},{1,9},{5... | collective-permute-start | bytes 4718600 | tf_op jit(solution)/shard_map/ppermute | solution.py:708
  75.3 58.0 %collective-permute-start.4 = (f32[384,512]{1,0:T(8,128)}, f32[384,512]{1,0:T(8,128)S(1)}, u32[]{:S(2)}, u32[]{:S(2)}) collective-permute-start(f32[384,512]{1,0:T(8,128)} %maximum_maximum_fusion.1.refs_0_.refs_4_), channel_id=1, source_target_pairs={{0,16},{4,20},{8,24},{12,28},{16,0},{20,4},{24,8},{28,12},{1,17},{... | collective-permute-start | bytes 2359304 | tf_op jit(solution)/shard_map/ppermute | solution.py:708
  75.8 57.7 %collective-permute-start.3 = (f32[384,512]{1,0:T(8,128)}, f32[384,512]{1,0:T(8,128)S(1)}, u32[]{:S(2)}, u32[]{:S(2)}) collective-permute-start(f32[384,512]{1,0:T(8,128)} %maximum_maximum_fusion.1.refs_0_.refs_4_), channel_id=1, source_target_pairs={{0,8},{4,12},{8,0},{12,4},{16,24},{20,28},{24,16},{28,20},{1,9},{5... | collective-permute-start | bytes 2359304 | tf_op jit(solution)/shard_map/ppermute | solution.py:708
  99.9 37.5 %copy-start.11 = (f32[384,768]{1,0:T(8,128)S(1)}, f32[384,768]{1,0:T(8,128)}, u32[]{:S(2)}) copy-start(f32[384,768]{1,0:T(8,128)} %cot_ref.7) | copy-start | bytes 3538948
  135.2 10.3 %collective-permute-start.8 = (f32[192,512]{1,0:T(8,128)}, f32[192,512]{1,0:T(8,128)}, u32[]{:S(2)}, u32[]{:S(2)}) collective-permute-start(f32[192,512]{1,0:T(8,128)} %slice.223), channel_id=1, source_target_pairs={{0,16},{4,20},{8,24},{12,28},{16,0},{20,4},{24,8},{28,12},{1,17},{... | collective-permute-start | bytes 1179656 | tf_op jit(solution)/shard_map/ppermute | solution.py:708
  136.7 10.1 %collective-permute-start.7 = (f32[192,512]{1,0:T(8,128)}, f32[192,512]{1,0:T(8,128)}, u32[]{:S(2)}, u32[]{:S(2)}) collective-permute-start(f32[192,512]{1,0:T(8,128)} %slice.222), channel_id=1, source_target_pairs={{0,8},{4,12},{8,0},{12,4},{16,24},{20,28},{24,16},{28,20},{1,9},{5... | collective-permute-start | bytes 1179656 | tf_op jit(solution)/shard_map/ppermute | solution.py:708
  137.4 14.7 %collective-permute-start.10 = (f32[384,768]{1,0:T(8,128)S(1)}, f32[384,768]{1,0:T(8,128)}, u32[]{:S(2)}, u32[]{:S(2)}) collective-permute-start(f32[384,768]{1,0:T(8,128)S(1)} %copy-done.11), channel_id=1, source_target_pairs={{0,4},{4,0},{8,12},{12,8},{16,20},{20,16},{24,28},{28,24},{1,5},{5... | collective-permute-start | bytes 3538952 | tf_op jit(solution)/shard_map/ppermute | solution.py:708
  146.8 5.3 %collective-permute-start.9 = (f32[384,768]{1,0:T(8,128)S(1)}, f32[384,768]{1,0:T(8,128)S(1)}, u32[]{:S(2)}, u32[]{:S(2)}) collective-permute-start(f32[384,768]{1,0:T(8,128)S(1)} %convolution_add_fusion.resid_ref), channel_id=1, source_target_pairs={{0,4},{4,0},{8,12},{12,8},{16,20},{20,16},{24,28},{28,24},{1,5},{5... | collective-permute-start | bytes 3538952 | tf_op jit(solution)/shard_map/ppermute | solution.py:708
  150.4 22.7 %collective-permute-start.12 = (f32[384,512]{1,0:T(8,128)S(1)}, f32[384,512]{1,0:T(8,128)S(1)}, u32[]{:S(2)}, u32[]{:S(2)}) collective-permute-start(f32[384,512]{1,0:T(8,128)S(1)} %slice.225), channel_id=1, source_target_pairs={{0,16},{4,20},{8,24},{12,28},{16,0},{20,4},{24,8},{28,12},{1,17},{... | collective-permute-start | bytes 2359304 | tf_op jit(solution)/shard_map/ppermute | solution.py:708
  150.9 22.2 %collective-permute-start.11 = (f32[384,512]{1,0:T(8,128)S(1)}, f32[384,512]{1,0:T(8,128)S(1)}, u32[]{:S(2)}, u32[]{:S(2)}) collective-permute-start(f32[384,512]{1,0:T(8,128)S(1)} %slice.224), channel_id=1, source_target_pairs={{0,8},{4,12},{8,0},{12,4},{16,24},{20,28},{24,16},{28,20},{1,9},{5... | collective-permute-start | bytes 2359304 | tf_op jit(solution)/shard_map/ppermute | solution.py:708
  174.8 91.2 %reduce-scatter.15.cloned.1.call-start = ((), (), s32[]{:S(2)}) async-start(), calls=%async_computation.7 | async-start | bytes 3932160
  195.9 117.7 %reduce-scatter.17.cloned.1.call-start = ((), (), s32[]{:S(2)}) async-start(), calls=%async_computation.8 | async-start | bytes 3932160
  218.6 2.9 collective-permute-start.13
  220.2 197.7 %reduce-scatter.19.cloned.1.call-start = ((), (), s32[]{:S(2)}) async-start(), calls=%async_computation.9 | async-start | bytes 5898240
  223.1 11.5 %collective-permute-start.14 = (f32[1,192,512]{2,1,0:T(8,128)S(1)}, f32[1,192,512]{2,1,0:T(8,128)S(1)}, u32[]{:S(2)}, u32[]{:S(2)}) collective-permute-start(f32[1,192,512]{2,1,0:T(8,128)S(1)} %slice_select_fusion.7), channel_id=1, source_target_pairs={{0,1},{1,0},{2,3},{3,2},{4,5},{5,4},{6,7},{7,6},{8,9},{9,8},{10,11... | collective-permute-start | bytes 1179656 | tf_op jit(solution)/shard_map/ppermute | solution.py:811
  234.7 26.2 %collective-permute-start.15 = (f32[1,192,512]{2,1,0:T(8,128)S(1)}, f32[1,192,512]{2,1,0:T(8,128)S(1)}, u32[]{:S(2)}, u32[]{:S(2)}) collective-permute-start(f32[1,192,512]{2,1,0:T(8,128)S(1)} %select_add_fusion.3), channel_id=1, source_target_pairs={{0,2},{1,3},{2,0},{3,1},{4,6},{5,7},{6,4},{7,5},{8,10},{9,11},{10,... | collective-permute-start | bytes 1179656 | tf_op jit(solution)/shard_map/ppermute | solution.py:811
  267.2 25.7 %collective-permute-start.16 = (f32[1,192,512]{2,1,0:T(8,128)S(1)}, f32[1,192,512]{2,1,0:T(8,128)S(1)}, u32[]{:S(2)}, u32[]{:S(2)}) collective-permute-start(f32[1,192,512]{2,1,0:T(8,128)S(1)} %slice_select_fusion.6), channel_id=1, source_target_pairs={{0,1},{1,0},{2,3},{3,2},{4,5},{5,4},{6,7},{7,6},{8,9},{9,8},{10,11... | collective-permute-start | bytes 1179656 | tf_op jit(solution)/shard_map/ppermute | solution.py:811
  268.7 24.3 %collective-permute-start.17 = (f32[1,192,512]{2,1,0:T(8,128)S(1)}, f32[1,192,512]{2,1,0:T(8,128)S(1)}, u32[]{:S(2)}, u32[]{:S(2)}) collective-permute-start(f32[1,192,512]{2,1,0:T(8,128)S(1)} %add.187), channel_id=1, source_target_pairs={{0,1},{1,0},{2,3},{3,2},{4,5},{5,4},{6,7},{7,6},{8,9},{9,8},{10,11... | collective-permute-start | bytes 1179656 | tf_op jit(solution)/shard_map/ppermute | solution.py:811
  294.0 19.6 %collective-permute-start.19 = (f32[1,192,512]{2,1,0:T(8,128)S(1)}, f32[1,192,512]{2,1,0:T(8,128)S(1)}, u32[]{:S(2)}, u32[]{:S(2)}) collective-permute-start(f32[1,192,512]{2,1,0:T(8,128)S(1)} %select_add_fusion.2), channel_id=1, source_target_pairs={{0,2},{1,3},{2,0},{3,1},{4,6},{5,7},{6,4},{7,5},{8,10},{9,11},{10,... | collective-permute-start | bytes 1179656 | tf_op jit(solution)/shard_map/ppermute | solution.py:811
  309.2 25.2 %collective-permute-start.18 = (f32[4,96,1536]{2,1,0:T(8,128)}, f32[4,96,1536]{2,1,0:T(8,128)S(1)}, u32[]{:S(2)}, u32[]{:S(2)}) collective-permute-start(f32[4,96,1536]{2,1,0:T(8,128)} %get-tuple-element.176), channel_id=1, source_target_pairs={{0,4},{4,0},{8,12},{12,8},{16,20},{20,16},{24,28},{28,24},{1,5},{5... | collective-permute-start | bytes 7077896 | tf_op jit(solution)/shard_map/ppermute | solution.py:708
  314.9 15.7 %collective-permute-start.20 = (f32[1,192,512]{2,1,0:T(8,128)S(1)}, f32[1,192,512]{2,1,0:T(8,128)S(1)}, u32[]{:S(2)}, u32[]{:S(2)}) collective-permute-start(f32[1,192,512]{2,1,0:T(8,128)S(1)} %slice_select_fusion.5), channel_id=1, source_target_pairs={{0,1},{1,0},{2,3},{3,2},{4,5},{5,4},{6,7},{7,6},{8,9},{9,8},{10,11... | collective-permute-start | bytes 1179656 | tf_op jit(solution)/shard_map/ppermute | solution.py:811
  315.5 17.9 %collective-permute-start.21 = (f32[1,192,512]{2,1,0:T(8,128)S(1)}, f32[1,192,512]{2,1,0:T(8,128)S(1)}, u32[]{:S(2)}, u32[]{:S(2)}) collective-permute-start(f32[1,192,512]{2,1,0:T(8,128)S(1)} %add.190), channel_id=1, source_target_pairs={{0,1},{1,0},{2,3},{3,2},{4,5},{5,4},{6,7},{7,6},{8,9},{9,8},{10,11... | collective-permute-start | bytes 1179656 | tf_op jit(solution)/shard_map/ppermute | solution.py:811
  334.4 4.7 collective-permute-start.22
  344.4 21.5 %collective-permute-start.24 = (f32[1,192,512]{2,1,0:T(8,128)S(1)}, f32[1,192,512]{2,1,0:T(8,128)S(1)}, u32[]{:S(2)}, u32[]{:S(2)}) collective-permute-start(f32[1,192,512]{2,1,0:T(8,128)S(1)} %select_add_fusion.1), channel_id=1, source_target_pairs={{0,2},{1,3},{2,0},{3,1},{4,6},{5,7},{6,4},{7,5},{8,10},{9,11},{10,... | collective-permute-start | bytes 1179656 | tf_op jit(solution)/shard_map/ppermute | solution.py:811
  355.5 59.3 %collective-permute-start.26 = (f32[384,768]{1,0:T(8,128)}, f32[384,768]{1,0:T(8,128)}, u32[]{:S(2)}, u32[]{:S(2)}) collective-permute-start(f32[384,768]{1,0:T(8,128)} %shard_map.249), channel_id=1, source_target_pairs={{1,0},{2,1},{3,2},{5,4},{6,5},{7,6},{9,8},{10,9},{11,10},{13,12},{... | collective-permute-start | bytes 3538952 | tf_op jit(solution)/shard_map/ppermute | solution.py:875
  366.0 33.1 %collective-permute-start.25 = (f32[1,192,512]{2,1,0:T(8,128)S(1)}, f32[1,192,512]{2,1,0:T(8,128)S(1)}, u32[]{:S(2)}, u32[]{:S(2)}) collective-permute-start(f32[1,192,512]{2,1,0:T(8,128)S(1)} %add.197), channel_id=1, source_target_pairs={{0,1},{1,0},{2,3},{3,2},{4,5},{5,4},{6,7},{7,6},{8,9},{9,8},{10,11... | collective-permute-start | bytes 1179656 | tf_op jit(solution)/shard_map/ppermute | solution.py:811
  384.2 16.2 %collective-permute-start.23 = (f32[384,768]{1,0:T(8,128)S(1)}, f32[384,768]{1,0:T(8,128)S(1)}, u32[]{:S(2)}, u32[]{:S(2)}) collective-permute-start(f32[384,768]{1,0:T(8,128)S(1)} %slice.235), channel_id=1, source_target_pairs={{0,4},{4,0},{8,12},{12,8},{16,20},{20,16},{24,28},{28,24},{1,5},{5... | collective-permute-start | bytes 3538952 | tf_op jit(solution)/shard_map/ppermute | solution.py:708
  405.7 1.4 collective-permute-start.27
  407.8 3.8 collective-permute-start.28
  411.7 5.6 %collective-permute-start.29 = (f32[8,768]{1,0:T(8,128)S(1)}, f32[8,768]{1,0:T(8,128)S(1)}, u32[]{:S(2)}, u32[]{:S(2)}) collective-permute-start(f32[8,768]{1,0:T(8,128)S(1)} %add.208), channel_id=1, source_target_pairs={{0,16},{4,20},{8,24},{12,28},{16,0},{20,4},{24,8},{28,12},{1,17},{... | collective-permute-start | bytes 73736 | tf_op jit(solution)/shard_map/ppermute | solution.py:708
  419.2 16.3 %collective-permute-start.30 = (f32[1,48,3072]{2,1,0:T(8,128)S(1)}, f32[1,48,3072]{2,1,0:T(8,128)S(1)}, u32[]{:S(2)}, u32[]{:S(2)}) collective-permute-start(f32[1,48,3072]{2,1,0:T(8,128)S(1)} %slice_select_fusion.4), channel_id=1, source_target_pairs={{0,1},{1,0},{2,3},{3,2},{4,5},{5,4},{6,7},{7,6},{8,9},{9,8},{10,11... | collective-permute-start | bytes 1769480 | tf_op jit(solution)/shard_map/ppermute | solution.py:811
  419.5 20.3 %collective-permute-start.32 = (f32[3,96,512]{2,1,0:T(8,128)S(1)}, f32[3,96,512]{2,1,0:T(8,128)S(1)}, u32[]{:S(2)}, u32[]{:S(2)}) collective-permute-start(f32[3,96,512]{2,1,0:T(8,128)S(1)} %slice_select_fusion.2), channel_id=1, source_target_pairs={{0,4},{4,0},{8,12},{12,8},{16,20},{20,16},{24,28},{28,24},{1,5},{5... | collective-permute-start | bytes 1769480 | tf_op jit(solution)/shard_map/ppermute | solution.py:708
  421.1 57.8 %collective-permute-start.33 = (f32[384,768]{1,0:T(8,128)}, f32[384,768]{1,0:T(8,128)}, u32[]{:S(2)}, u32[]{:S(2)}) collective-permute-start(f32[384,768]{1,0:T(8,128)} %add.198), channel_id=1, source_target_pairs={{1,0},{2,1},{3,2},{5,4},{6,5},{7,6},{9,8},{10,9},{11,10},{13,12},{... | collective-permute-start | bytes 3538952 | tf_op jit(solution)/shard_map/ppermute | solution.py:906
  436.5 41.2 %collective-permute-start.31 = (f32[1,48,3072]{2,1,0:T(8,128)}, f32[1,48,3072]{2,1,0:T(8,128)}, u32[]{:S(2)}, u32[]{:S(2)}) collective-permute-start(f32[1,48,3072]{2,1,0:T(8,128)} %select_add_fusion), channel_id=1, source_target_pairs={{0,2},{1,3},{2,0},{3,1},{4,6},{5,7},{6,4},{7,5},{8,10},{9,11},{10,... | collective-permute-start | bytes 1769480 | tf_op jit(solution)/shard_map/ppermute | solution.py:811
  444.4 34.6 %copy-start.9 = (f32[384,768]{1,0:T(8,128)S(1)}, f32[384,768]{1,0:T(8,128)}, u32[]{:S(2)}) copy-start(f32[384,768]{1,0:T(8,128)} %shard_map.250) | copy-start | bytes 3538948
  444.4 34.6 %copy-start.36 = (f32[768]{0:T(1024)S(1)}, f32[768]{0:T(1024)}, u32[]{:S(2)}) copy-start(f32[768]{0:T(1024)} %param.20) | copy-start | bytes 9220
  481.0 4.2 collective-permute-start.34
  481.0 15.3 %collective-permute-start.36 = (f32[1,48,3072]{2,1,0:T(8,128)S(1)}, f32[1,48,3072]{2,1,0:T(8,128)S(1)}, u32[]{:S(2)}, u32[]{:S(2)}) collective-permute-start(f32[1,48,3072]{2,1,0:T(8,128)S(1)} %add.211), channel_id=1, source_target_pairs={{0,1},{1,0},{2,3},{3,2},{4,5},{5,4},{6,7},{7,6},{8,9},{9,8},{10,11... | collective-permute-start | bytes 1769480 | tf_op jit(solution)/shard_map/ppermute | solution.py:811
  485.2 10.0 %collective-permute-start.35 = (f32[8,768]{1,0:T(8,128)S(1)}, f32[8,768]{1,0:T(8,128)S(1)}, u32[]{:S(2)}, u32[]{:S(2)}) collective-permute-start(f32[8,768]{1,0:T(8,128)S(1)} %add.214), channel_id=1, source_target_pairs={{0,2},{1,3},{2,0},{3,1},{4,6},{5,7},{6,4},{7,5},{8,10},{9,11},{10,... | collective-permute-start | bytes 73736 | tf_op jit(solution)/shard_map/ppermute | solution.py:811
  (42 other events, 290.1 us)
Sparse Core Ops, SparseCore 0:
  9.9 51.5 all-gather.2
  63.4 37.3 all-gather.4
  174.9 44.1 reduce-scatter.12
  222.0 43.9 reduce-scatter.14
  268.8 43.9 reduce-scatter.16
  342.1 58.0 reduce-scatter.18

commit v13 on v11

--- a/solution.py
+++ b/solution.py
@@ -809,10 +809,11 @@
         weights_vo_kernel, 9, core_at, chips, normed_parts,
         [(dv, 0), (attended, None), (grad_resid, 1)], [halo + rows] * 2 + [rows] * 2,
     )
-    line_c, ends_b, grads_vo = together((line_c, ends_b, grads_vo))
+    line_c, ends_b, grads_vo, dk = together((line_c, ends_b, grads_vo, dk))
+    part_far = partial_rows(0, (dk, dv), qkv_full)
     line_c = line_middle(line_c)
     grads_c = jnp.concatenate([grads_qk[0] + given_qk, grads_vo[0] + swap(grads_vo[1])], axis=2)
-    grads_c, out_part = together((grads_c, out_part))
+    grads_c, out_part, line_c, part_far = together((grads_c, out_part, line_c, part_far))
     shard_c = scatter_chips(grads_c)[0]
     out_sib = swap(out_part[rows:])
 
@@ -820,11 +821,10 @@
     output = base + dwa_weights[4] * block_out
     dwa_local = jnp.concatenate([dots, jnp.sum(cotangent * block_out)[None]])
 
-    part_far = partial_rows(0, (dk, dv), qkv_full)
     given_near = lax.ppermute(part_far, "seq", behind)
-    dk, far, near, line_c, part_far = together((dk, far, near, line_c, part_far))
     ends_c = line_end(line_c)
     part_near = partial_rows(1, (dk, dv), qkv_full)
+    given_near, dq = together((given_near, dq))
     own_part = partial_rows(2, (dq, dk, dv), qkv_full)
     own_part, ends_c = together((own_part, ends_c))
     (sent,) = together((part_near,))
@@ -850,9 +850,11 @@
     while bit < devices:
         small = small + exchange(small, bit)
         bit *= 2
-    shard_c, back_near, small = together((shard_c, back_near, small))
+    given_back = lax.ppermute(back_near, "seq", behind)
+    shard_c, given_back, small = together((shard_c, given_back, small))
     last = line_middle(line_start(shard_c[None]))
-    given_back = lax.ppermute(back_near, "seq", behind)
+    grad_normed_one = own_part + given_back
+    grad_input = grad_resid + norm_back(grad_normed_one, gain1, xhat1, rate1)
     grad_up, grad_down = unpack_grads(
         *(
             jnp.concatenate(parts, axis=0)
@@ -860,8 +862,8 @@
         ),
         swap, core, chips,
     )
-    last, grad_up, grad_down, small, given_back = together(
-        (last, grad_up, grad_down, small, given_back)
+    last, grad_up, grad_down, small, grad_input = together(
+        (last, grad_up, grad_down, small, grad_input)
     )
     bit = 1
     while bit < groups:
@@ -871,8 +873,6 @@
     grad_dwa = small[4, :5]
     last = jnp.concatenate(line_end(last), axis=1)[0]
     grad_qkv, grad_wout = last[:, :3 * model], last[:, 3 * model:]
-    grad_normed_one = own_part + given_back
-    grad_input = grad_resid + norm_back(grad_normed_one, gain1, xhat1, rate1)
     return (
         output,
         grad_input,

time: 499 us -> 508 us (1.018)
  starting transfers between devices: 48.6 us -> 58.4 us
    ppermute x14, starting transfers between devices: 16.4 us -> 26.3 us  [body(): lax.ppermute(v, 'seq', [(i, i ^ bit) for i in range(groups)])]
    ppermute x17, waiting for transfers between devices: 15.7 us -> 10.5 us  [body(): lax.ppermute(v, 'dp', [(i, i ^ bit) for i in range(devices)])]
  transfers between devices with their start and end apart: 43 -> 43, of which waited for: 18 -> 19; matrix products, arithmetic and copies ran while one was open for 14% -> 15% of each run, Pallas kernels for 39% -> 38%
where the time goes in v13:
time: 508 us; the launch traced here: 503 us
  Pallas kernels  213 us (42%)
  waiting for transfers between devices  130 us (26%)
  starting transfers between devices  58.4 us (11%)
  other arithmetic  50.2 us (10%)
  local copies, waits for them, and re-layouts  33.9 us (7%)
  between operations  15.2 us (3%)
    ppermute x14, waiting for transfers between devices, body(): lax.ppermute(v, 'seq', [(i, i ^ bit) for i in range(groups)])  83.5 us
    pallas_call x3, Pallas kernels, mlp(): pl.pallas_call(functools.partial(mlp_kernel, len(ups), len(so_far) // 2),...  62 us
    pallas_call x2, Pallas kernels, attend_back(): pl.pallas_call(attend_back_kernel, grid=(count,), in_specs=[pl.BlockSpec(...  47.2 us
    pallas_call x2, Pallas kernels, weight_call(): pl.pallas_call(kernel, grid_spec=pltpu.PrefetchScalarGridSpec(num_scalar_...  26.4 us
    ppermute x14, starting transfers between devices, body(): lax.ppermute(v, 'seq', [(i, i ^ bit) for i in range(groups)])  26.3 us
    pallas_call x3, Pallas kernels, partial_rows(): pl.pallas_call(functools.partial(partial_kernel, len(grads)), grid=(model...  24.4 us
    pallas_call x1, Pallas kernels, attend(): pl.pallas_call(attend_kernel, grid=(pairs,), in_specs=[pl.BlockSpec((rows...  23 us
    pallas_call x1, Pallas kernels, project(): pl.pallas_call(qkv_kernel, grid=(3 * third,), in_specs=[whole((rows, mode...  21.7 us
  transfers between devices with their start and end apart: 43, of which 19 were waited for; matrix products, arithmetic and copies ran while one was open for 15% of the time, Pallas kernels for 38%

profile of v13, /device:TPU:0, one launch (start us, length us, event | category | flops | bytes accessed | tf_op | source)
XLA Modules:
  0.0 503.3 jit_solution(6760159906871162023)
XLA Ops:
  8.0 1.9 reshape.142
  11.9 4.6 collective-permute-start
  24.2 18.0 %collective-permute-done.near_ref = f32[384,768]{1,0:T(8,128)S(1)} collective-permute-done((f32[384,768]{1,0:T(8,128)S(1)}, f32[384,768]{1,0:T(8,128)S(1)}, u32[]{:S(2)}, u32[]{:S(2)}) %collective-permute-start) | collective-permute-done | bytes 1179680 | tf_op jit(solution)/shard_map/ppermute | solution.py:715
  42.3 4.4 collective-permute-start.1
  46.7 4.0 collective-permute-start.2
  51.4 7.4 %fusion.5 = (f32[]{:T(128)}, f32[]{:T(128)}, f32[]{:T(128)}, f32[]{:T(128)}, f32[384,768]{1,0:T(8,128)}) fusion(f32[384,768]{1,0:T(8,128)S(1)} %copy-done.11, f32[3,384,768]{2,1,0:T(8,128)} %param.18, f32[384,768]{1,0:T(8,128)} %param.17, f32[]{:T(128)} %bitcast.5, f32[]{:T(128)} %bitcast.3, f32[]{:T(128)} %bitcast.1, f32[]{:T(128)} %bitcast), kind=kLoop, calls=%fused_computation.17 | loop fusion | flops 4423676 | bytes 7077920 | tf_op jit(solution)/shard_map/reduce_sum | solution.py:731
  60.0 11.9 %collective-permute-done.2 = s32[1,384]{1,0:T(1,128)} collective-permute-done((s32[1,384]{1,0:T(1,128)S(1)}, s32[1,384]{1,0:T(1,128)}, u32[]{:S(2)}, u32[]{:S(2)}) %collective-permute-start.2) | collective-permute-done | bytes 1568 | tf_op jit(solution)/shard_map/ppermute | solution.py:716
  71.8 5.0 collective-permute-start.3
  76.8 3.2 pad_maximum_fusion.2
  86.5 21.7 %shard_map.239 = (f32[384,768]{1,0:T(8,128)}, f32[1152,1536]{1,0:T(8,128)}, bf16[1152,768]{1,0:T(8,128)(2,1)}, bf16[1152,768]{1,0:T(8,128)(2,1)}) custom-call(f32[384,768]{1,0:T(8,128)} %copy-done.5, f32[384,768]{1,0:T(8,128)} %copy-done.3, f32[384,768]{1,0:T(8,128)} %own_ref.1, f32[1,768]{1,0:T(1,128)} %broadcast_in_dim.50.gain_ref, ...), custom_call_target="tpu_custom_call" | custom-call | flops 22000001024 | bytes 1048576 | tf_op jit(solution)/shard_map/pallas_call | solution.py:144
  109.6 23.0 %shard_map.240.att_ref = f32[384,768]{1,0:T(8,128)} custom-call(f32[384,768]{1,0:T(8,128)} %get-tuple-element.124.q_ref, f32[1152,1536]{1,0:T(8,128)} %get-tuple-element.125.k_ref.v_ref, f32[1152,1536]{1,0:T(8,128)} %get-tuple-element.125.k_ref.v_ref, s32[384,128]{1,0:T(8,128)} %broadcast_in_dim.52.segq_ref, s32[8,1152]{1,0:T(8,128)} %broadcast_in_dim.54.segk_ref), custom_call_target="tpu_custom_call" | custom-call | flops 26400000000 | bytes 1048576 | tf_op jit(solution)/shard_map/pallas_call | solution.py:236
  132.7 3.7 convolution_add_fusion.resid_ref
  138.5 4.2 collective-permute-done.12.refs_7_
  142.8 2.0 collective-permute-done.9.refs_3_
  145.8 20.0 %shard_map.241 = (f32[768,768]{1,0:T(8,128)}, f32[768,768]{1,0:T(8,128)}, f32[4,1,384,512]{3,2,1,0:T(8,128)}) custom-call(s32[1]{0:T(128)} %bitcast.13.chip_ref, f32[384,768]{1,0:T(8,128)} %copy-done.14, f32[384,768]{1,0:T(8,128)} %copy-done.42, f32[384,768]{1,0:T(8,128)} %cot_ref.7, f32[384,768]{1,0:T(8,128)} %collective-permute-done.5.cot_other_ref, ...), custom_call_target="tpu_custom_call" | custom-call | flops 19800000512 | bytes 1048576 | tf_op jit(solution)/shard_map/pallas_call | solution.py:457
  165.9 20.9 %shard_map.242 = (f32[768,768]{1,0:T(8,128)}, f32[768,768]{1,0:T(8,128)}, f32[4,1,384,512]{3,2,1,0:T(8,128)}) custom-call(s32[1]{0:T(128)} %bitcast.13.chip_ref, f32[384,768]{1,0:T(8,128)} %copy-done.14, f32[384,768]{1,0:T(8,128)} %copy-done.42, f32[384,768]{1,0:T(8,128)} %cot_ref.7, f32[384,768]{1,0:T(8,128)} %collective-permute-done.5.cot_other_ref, ...), custom_call_target="tpu_custom_call" | custom-call | flops 19800000512 | bytes 1048576 | tf_op jit(solution)/shard_map/pallas_call | solution.py:457
  187.0 21.0 %shard_map.243 = (f32[768,768]{1,0:T(8,128)}, f32[768,768]{1,0:T(8,128)}, f32[4,1,384,512]{3,2,1,0:T(8,128)}) custom-call(s32[1]{0:T(128)} %bitcast.13.chip_ref, f32[384,768]{1,0:T(8,128)} %copy-done.14, f32[384,768]{1,0:T(8,128)} %copy-done.42, f32[384,768]{1,0:T(8,128)} %cot_ref.7, f32[384,768]{1,0:T(8,128)} %collective-permute-done.5.cot_other_ref, ...), custom_call_target="tpu_custom_call" | custom-call | flops 19800000512 | bytes 1048576 | tf_op jit(solution)/shard_map/pallas_call | solution.py:457
  209.8 2.5 collective-permute-done.13.given_ref
  215.6 7.8 %shard_map.244 = (f32[384,768]{1,0:T(8,128)}, f32[384,768]{1,0:T(8,128)}, f32[8,768]{1,0:T(8,128)}) custom-call(f32[768,768]{1,0:T(8,128)} %get-tuple-element.106.part_ref, f32[384,768]{1,0:T(8,128)} %copy-done.43, f32[384,768]{1,0:T(8,128)} %copy-done.14, f32[384,768]{1,0:T(8,128)} %cot_ref.7, f32[1,768]{1,0:T(1,128)} %broadcast_in_dim.55.gain_ref, ...), custom_call_target="tpu_custom_call" | custom-call | flops 6600000000 | bytes 1048576 | tf_op jit(solution)/shard_map/pallas_call | solution.py:505
  226.9 2.6 collective-permute-start.15
  229.6 23.5 %shard_map.245 = (f32[384,768]{1,0:T(8,128)}, f32[1152,768]{1,0:T(8,128)}, f32[1152,768]{1,0:T(8,128)}) custom-call(f32[384,768]{1,0:T(8,128)} %get-tuple-element.124.q_ref, f32[1152,1536]{1,0:T(8,128)} %get-tuple-element.125.k_ref.v_ref, f32[1152,1536]{1,0:T(8,128)} %get-tuple-element.125.k_ref.v_ref, f32[384,768]{1,0:T(8,128)} %get-tuple-element.126.g_ref, ...), custom_call_target="tpu_custom_call" | custom-call | flops 23100000256 | bytes 1048576 | tf_op jit(solution)/shard_map/pallas_call | solution.py:328
  253.1 2.9 reduce-scatter.15.cloned.1.call-done
  259.3 23.7 %shard_map.246 = (f32[384,768]{1,0:T(8,128)}, f32[1152,768]{1,0:T(8,128)}, f32[1152,768]{1,0:T(8,128)}) custom-call(f32[384,768]{1,0:T(8,128)} %get-tuple-element.124.q_ref, f32[1152,1536]{1,0:T(8,128)} %get-tuple-element.125.k_ref.v_ref, f32[1152,1536]{1,0:T(8,128)} %get-tuple-element.125.k_ref.v_ref, ...), custom_call_target="tpu_custom_call", output_to_operand_aliasing={{0}: (8, {}), {1}: (9, {}), {2}: (10, {})} | custom-call | flops 23100000256 | bytes 1048576 | tf_op jit(solution)/shard_map/pallas_call | solution.py:328
  284.1 2.4 collective-permute-start.19
  286.5 12.8 %shard_map.247 = (f32[4,96,1536]{2,1,0:T(8,128)}, f32[4,96,1536]{2,1,0:T(8,128)}) custom-call(s32[1]{0:T(128)} %bitcast.12.core_ref, bf16[1152,768]{1,0:T(8,128)(2,1)} %get-tuple-element.99.hi_ref, bf16[1152,768]{1,0:T(8,128)(2,1)} %get-tuple-element.100.lo_ref, f32[384,768]{1,0:T(8,128)} %get-tuple-element.160.dq_ref.refs_0_, ...), custom_call_target="tpu_custom_call" | custom-call | flops 9900000256 | bytes 1048576 | tf_op jit(solution)/shard_map/pallas_call | solution.py:591
  299.3 4.4 collective-permute-done.19
  307.0 13.6 %shard_map.248 = (f32[4,96,1536]{2,1,0:T(8,128)}, f32[4,96,1536]{2,1,0:T(8,128)}) custom-call(s32[1]{0:T(128)} %bitcast.12.core_ref, bf16[1152,768]{1,0:T(8,128)(2,1)} %get-tuple-element.99.hi_ref, bf16[1152,768]{1,0:T(8,128)(2,1)} %get-tuple-element.100.lo_ref, f32[1152,768]{1,0:T(8,128)} %get-tuple-element.147.dv_ref.refs_1_.refs_2_, ...), custom_call_target="tpu_custom_call" | custom-call | flops 9900000256 | bytes 1048576 | tf_op jit(solution)/shard_map/pallas_call | solution.py:591
  320.7 2.7 collective-permute-done.21
  324.4 3.2 collective-permute-start.23
  327.6 7.6 %shard_map.249 = f32[384,768]{1,0:T(8,128)} custom-call(f32[1152,768]{1,0:T(8,128)} %get-tuple-element.155.dk_ref.refs_0_.refs_1_, f32[1152,768]{1,0:T(8,128)} %get-tuple-element.147.dv_ref.refs_1_.refs_2_, f32[768,2304]{1,0:T(8,128)} %all-gather.3.cloned.1.call-done.w_ref.refs_2_.refs_3_), custom_call_target="tpu_custom_call" | custom-call | flops 6600000000 | bytes 1048576 | tf_op jit(solution)/shard_map/pallas_call | solution.py:632
  335.2 10.6 %collective-permute-done.23 = f32[1,192,512]{2,1,0:T(8,128)S(1)} collective-permute-done((f32[1,192,512]{2,1,0:T(8,128)S(1)}, f32[1,192,512]{2,1,0:T(8,128)S(1)}, u32[]{:S(2)}, u32[]{:S(2)}) %collective-permute-start.23) | collective-permute-done | bytes 393248 | tf_op jit(solution)/shard_map/ppermute | solution.py:759
  348.3 2.0 add.190
  350.3 2.5 pad_maximum_fusion
  360.5 7.5 %shard_map.250 = f32[384,768]{1,0:T(8,128)} custom-call(f32[1152,768]{1,0:T(8,128)} %get-tuple-element.155.dk_ref.refs_0_.refs_1_, f32[1152,768]{1,0:T(8,128)} %get-tuple-element.147.dv_ref.refs_1_.refs_2_, f32[768,2304]{1,0:T(8,128)} %all-gather.3.cloned.1.call-done.w_ref.refs_2_.refs_3_), custom_call_target="tpu_custom_call" | custom-call | flops 6600000000 | bytes 1048576 | tf_op jit(solution)/shard_map/pallas_call | solution.py:632
  369.1 3.0 collective-permute-start.27
  374.2 23.2 %collective-permute-done.27 = f32[1,192,512]{2,1,0:T(8,128)S(1)} collective-permute-done((f32[1,192,512]{2,1,0:T(8,128)S(1)}, f32[1,192,512]{2,1,0:T(8,128)S(1)}, u32[]{:S(2)}, u32[]{:S(2)}) %collective-permute-start.27) | collective-permute-done | bytes 393248 | tf_op jit(solution)/shard_map/ppermute | solution.py:759
  397.6 2.4 add.195
  401.3 9.3 %shard_map.251 = f32[384,768]{1,0:T(8,128)} custom-call(f32[384,768]{1,0:T(8,128)} %get-tuple-element.160.dq_ref.refs_0_, f32[1152,768]{1,0:T(8,128)} %get-tuple-element.155.dk_ref.refs_0_.refs_1_, f32[1152,768]{1,0:T(8,128)} %get-tuple-element.147.dv_ref.refs_1_.refs_2_, f32[768,2304]{1,0:T(8,128)} %all-gather.3.cloned.1.call-done.w_ref.refs_2_.refs_3_), custom_call_target="tpu_custom_call" | custom-call | flops 6600000000 | bytes 1048576 | tf_op jit(solution)/shard_map/pallas_call | solution.py:632
  412.6 4.2 multiply_reduce_fusion.1
  427.2 2.0 collective-permute-done.26
  429.1 2.1 slice_select_fusion.4
  432.5 2.1 broadcast_select_fusion.1
  439.6 2.2 fusion.7
  441.8 3.7 collective-permute-done.31
  446.7 2.5 collective-permute-start.32
  450.6 22.6 %collective-permute-done.32 = f32[1,48,3072]{2,1,0:T(8,128)S(1)} collective-permute-done((f32[1,48,3072]{2,1,0:T(8,128)S(1)}, f32[1,48,3072]{2,1,0:T(8,128)S(1)}, u32[]{:S(2)}, u32[]{:S(2)}) %collective-permute-start.32) | collective-permute-done | bytes 589856 | tf_op jit(solution)/shard_map/ppermute | solution.py:759
  475.4 12.6 %collective-permute-done.34 = f32[8,768]{1,0:T(8,128)S(1)} collective-permute-done((f32[8,768]{1,0:T(8,128)S(1)}, f32[8,768]{1,0:T(8,128)S(1)}, u32[]{:S(2)}, u32[]{:S(2)}) %collective-permute-start.34) | collective-permute-done | bytes 24608 | tf_op jit(solution)/shard_map/ppermute | solution.py:759
  488.0 3.4 collective-permute-start.35
  (246 shorter events, 83.4 us)
Async XLA Ops:
  7.2 78.8 %all-gather.3.cloned.1.call-start = ((), (), s32[]{:S(2)}) async-start(), calls=%async_computation.4 | async-start | bytes 7962624 | tf_op jit(solution)/shard_map/all_gather | solution.py:691
  7.9 124.8 %all-gather.5.cloned.1.call-start = ((), (), s32[]{:S(2)}) async-start(), calls=%async_computation.5 | async-start | bytes 2654208 | tf_op jit(solution)/shard_map/all_gather | solution.py:691
  11.4 8.9 %collective-permute-start.6 = (f32[96,1536]{1,0:T(8,128)}, f32[96,1536]{1,0:T(8,128)}, u32[]{:S(2)}, u32[]{:S(2)}) collective-permute-start(f32[96,1536]{1,0:T(8,128)} %select_n.149), channel_id=1, source_target_pairs={{0,4},{4,0},{8,12},{12,8},{16,20},{20,16},{24,28},{28,24},{1,5},{5... | collective-permute-start | bytes 1769480 | tf_op jit(solution)/shard_map/ppermute | solution.py:688
  11.9 30.4 %collective-permute-start = (f32[384,768]{1,0:T(8,128)S(1)}, f32[384,768]{1,0:T(8,128)S(1)}, u32[]{:S(2)}, u32[]{:S(2)}) collective-permute-start(f32[384,768]{1,0:T(8,128)S(1)} %copy-done), channel_id=1, source_target_pairs={{0,1},{1,2},{2,3},{4,5},{5,6},{6,7},{8,9},{9,10},{10,11},{12,13},{... | collective-permute-start | bytes 3538952 | tf_op jit(solution)/shard_map/ppermute | solution.py:715
  16.5 66.9 %collective-permute-start.10 = (f32[384,768]{1,0:T(8,128)}, f32[384,768]{1,0:T(8,128)}, u32[]{:S(2)}, u32[]{:S(2)}) collective-permute-start(f32[384,768]{1,0:T(8,128)} %refs_4_.5), channel_id=1, source_target_pairs={{0,8},{4,12},{8,0},{12,4},{16,24},{20,28},{24,16},{28,20},{1,9},{5... | collective-permute-start | bytes 3538952 | tf_op jit(solution)/shard_map/ppermute | solution.py:688
  21.6 25.1 %copy-start.41 = (s32[1,384]{1,0:T(1,128)S(1)}, s32[1,384]{1,0:T(1,128)}, u32[]{:S(2)}) copy-start(s32[1,384]{1,0:T(1,128)} %param.28) | copy-start | bytes 4612
  21.6 29.1 %copy-start.11 = (f32[384,768]{1,0:T(8,128)S(1)}, f32[384,768]{1,0:T(8,128)}, u32[]{:S(2)}) copy-start(f32[384,768]{1,0:T(8,128)} %cot_ref.7) | copy-start | bytes 3538948
  21.6 29.2 %copy-start.36 = (f32[5]{0:T(128)S(1)}, f32[5]{0:T(128)}, u32[]{:S(2)}) copy-start(f32[5]{0:T(128)} %param.19) | copy-start | bytes 64
  22.7 62.2 %collective-permute-start.8 = (f32[192,1536]{1,0:T(8,128)}, f32[192,1536]{1,0:T(8,128)}, u32[]{:S(2)}, u32[]{:S(2)}) collective-permute-start(f32[192,1536]{1,0:T(8,128)} %pad_maximum_fusion.1.refs_0_), channel_id=1, source_target_pairs={{0,16},{4,20},{8,24},{12,28},{16,0},{20,4},{24,8},{28,12},{1,17},{... | collective-permute-start | bytes 3538952 | tf_op jit(solution)/shard_map/ppermute | solution.py:688
  42.3 43.2 %collective-permute-start.1 = (f32[384,768]{1,0:T(8,128)S(1)}, f32[384,768]{1,0:T(8,128)S(1)}, u32[]{:S(2)}, u32[]{:S(2)}) collective-permute-start(f32[384,768]{1,0:T(8,128)S(1)} %collective-permute-done.near_ref), channel_id=1, source_target_pairs={{0,1},{1,2},{2,3},{4,5},{5,6},{6,7},{8,9},{9,10},{10,11},{12,13},{... | collective-permute-start | bytes 3538952 | tf_op jit(solution)/shard_map/ppermute | solution.py:717
  46.7 25.1 %collective-permute-start.2 = (s32[1,384]{1,0:T(1,128)S(1)}, s32[1,384]{1,0:T(1,128)}, u32[]{:S(2)}, u32[]{:S(2)}) collective-permute-start(s32[1,384]{1,0:T(1,128)S(1)} %get-tuple-element.215), channel_id=1, source_target_pairs={{0,1},{1,2},{2,3},{4,5},{5,6},{6,7},{8,9},{9,10},{10,11},{12,13},{... | collective-permute-start | bytes 4616 | tf_op jit(solution)/shard_map/ppermute | solution.py:716
  50.7 85.7 %collective-permute-start.5 = (f32[384,768]{1,0:T(8,128)S(1)}, f32[384,768]{1,0:T(8,128)}, u32[]{:S(2)}, u32[]{:S(2)}) collective-permute-start(f32[384,768]{1,0:T(8,128)S(1)} %copy-done.11), channel_id=1, source_target_pairs={{0,4},{4,0},{8,12},{12,8},{16,20},{20,16},{24,28},{28,24},{1,5},{5... | collective-permute-start | bytes 3538952 | tf_op jit(solution)/shard_map/ppermute | solution.py:688
  50.8 161.6 %reduce-scatter.13.cloned.1.call-start = ((), (), s32[]{:S(2)}) async-start(), calls=%async_computation.6 | async-start | bytes 3932160
  71.8 9.4 %collective-permute-start.3 = (s32[1,384]{1,0:T(1,128)}, s32[1,384]{1,0:T(1,128)S(1)}, u32[]{:S(2)}, u32[]{:S(2)}) collective-permute-start(s32[1,384]{1,0:T(1,128)} %collective-permute-done.2), channel_id=1, source_target_pairs={{0,1},{1,2},{2,3},{4,5},{5,6},{6,7},{8,9},{9,10},{10,11},{12,13},{... | collective-permute-start | bytes 4616 | tf_op jit(solution)/shard_map/ppermute | solution.py:718
  81.2 57.3 %collective-permute-start.11 = (f32[384,768]{1,0:T(8,128)}, f32[384,768]{1,0:T(8,128)}, u32[]{:S(2)}, u32[]{:S(2)}) collective-permute-start(f32[384,768]{1,0:T(8,128)} %refs_4_.5), channel_id=1, source_target_pairs={{0,16},{4,20},{8,24},{12,28},{16,0},{20,4},{24,8},{28,12},{1,17},{... | collective-permute-start | bytes 3538952 | tf_op jit(solution)/shard_map/ppermute | solution.py:688
  83.4 55.1 %collective-permute-start.7 = (f32[192,1536]{1,0:T(8,128)}, f32[192,1536]{1,0:T(8,128)}, u32[]{:S(2)}, u32[]{:S(2)}) collective-permute-start(f32[192,1536]{1,0:T(8,128)} %pad_maximum_fusion.1.refs_0_), channel_id=1, source_target_pairs={{0,8},{4,12},{8,0},{12,4},{16,24},{20,28},{24,16},{28,20},{1,9},{5... | collective-permute-start | bytes 3538952 | tf_op jit(solution)/shard_map/ppermute | solution.py:688
  85.0 57.8 %collective-permute-start.12 = (f32[384,768]{1,0:T(8,128)}, f32[384,768]{1,0:T(8,128)}, u32[]{:S(2)}, u32[]{:S(2)}) collective-permute-start(f32[384,768]{1,0:T(8,128)} %collective-permute-done.10.refs_5_), channel_id=1, source_target_pairs={{0,16},{4,20},{8,24},{12,28},{16,0},{20,4},{24,8},{28,12},{1,17},{... | collective-permute-start | bytes 3538952 | tf_op jit(solution)/shard_map/ppermute | solution.py:688
  85.5 59.3 %collective-permute-start.9 = (f32[192,1536]{1,0:T(8,128)}, f32[192,1536]{1,0:T(8,128)}, u32[]{:S(2)}, u32[]{:S(2)}) collective-permute-start(f32[192,1536]{1,0:T(8,128)} %collective-permute-done.8.refs_2_), channel_id=1, source_target_pairs={{0,8},{4,12},{8,0},{12,4},{16,24},{20,28},{24,16},{28,20},{1,9},{5... | collective-permute-start | bytes 3538952 | tf_op jit(solution)/shard_map/ppermute | solution.py:688
  136.5 8.3 %collective-permute-start.4 = (f32[384,768]{1,0:T(8,128)S(1)}, f32[384,768]{1,0:T(8,128)S(1)}, u32[]{:S(2)}, u32[]{:S(2)}) collective-permute-start(f32[384,768]{1,0:T(8,128)S(1)} %convolution_add_fusion.resid_ref), channel_id=1, source_target_pairs={{0,4},{4,0},{8,12},{12,8},{16,20},{20,16},{24,28},{28,24},{1,5},{5... | collective-permute-start | bytes 3538952 | tf_op jit(solution)/shard_map/ppermute | solution.py:688
  165.8 90.2 %reduce-scatter.15.cloned.1.call-start = ((), (), s32[]{:S(2)}) async-start(), calls=%async_computation.7 | async-start | bytes 3932160
  186.8 116.9 %reduce-scatter.17.cloned.1.call-start = ((), (), s32[]{:S(2)}) async-start(), calls=%async_computation.8 | async-start | bytes 3932160
  209.4 2.9 collective-permute-start.13
  209.6 219.6 %reduce-scatter.19.cloned.1.call-start = ((), (), s32[]{:S(2)}) async-start(), calls=%async_computation.9 | async-start | bytes 5898240
  214.0 11.2 %collective-permute-start.14 = (f32[1,192,512]{2,1,0:T(8,128)S(1)}, f32[1,192,512]{2,1,0:T(8,128)S(1)}, u32[]{:S(2)}, u32[]{:S(2)}) collective-permute-start(f32[1,192,512]{2,1,0:T(8,128)S(1)} %slice_select_fusion.7), channel_id=1, source_target_pairs={{0,1},{1,0},{2,3},{3,2},{4,5},{5,4},{6,7},{7,6},{8,9},{9,8},{10,11... | collective-permute-start | bytes 1179656 | tf_op jit(solution)/shard_map/ppermute | solution.py:759
  226.9 26.1 %collective-permute-start.15 = (f32[1,192,512]{2,1,0:T(8,128)S(1)}, f32[1,192,512]{2,1,0:T(8,128)S(1)}, u32[]{:S(2)}, u32[]{:S(2)}) collective-permute-start(f32[1,192,512]{2,1,0:T(8,128)S(1)} %select_add_fusion.3), channel_id=1, source_target_pairs={{0,2},{1,3},{2,0},{3,1},{4,6},{5,7},{6,4},{7,5},{8,10},{9,11},{10,... | collective-permute-start | bytes 1179656 | tf_op jit(solution)/shard_map/ppermute | solution.py:759
  257.2 25.8 %copy-start.16 = (f32[1,1,384,512]{3,2,1,0:T(8,128)S(1)}, f32[1,1,384,512]{3,2,1,0:T(8,128)}, u32[]{:S(2)}) copy-start(f32[1,1,384,512]{3,2,1,0:T(8,128)} %reduce-scatter.15.cloned.1.call-done) | copy-start | bytes 2359300
  257.2 25.8 %collective-permute-start.16 = (f32[1,192,512]{2,1,0:T(8,128)S(1)}, f32[1,192,512]{2,1,0:T(8,128)S(1)}, u32[]{:S(2)}, u32[]{:S(2)}) collective-permute-start(f32[1,192,512]{2,1,0:T(8,128)S(1)} %slice_select_fusion.6), channel_id=1, source_target_pairs={{0,1},{1,0},{2,3},{3,2},{4,5},{5,4},{6,7},{7,6},{8,9},{9,8},{10,11... | collective-permute-start | bytes 1179656 | tf_op jit(solution)/shard_map/ppermute | solution.py:759
  258.8 24.4 %collective-permute-start.17 = (f32[1,192,512]{2,1,0:T(8,128)S(1)}, f32[1,192,512]{2,1,0:T(8,128)S(1)}, u32[]{:S(2)}, u32[]{:S(2)}) collective-permute-start(f32[1,192,512]{2,1,0:T(8,128)S(1)} %add.185), channel_id=1, source_target_pairs={{0,1},{1,0},{2,3},{3,2},{4,5},{5,4},{6,7},{7,6},{8,9},{9,8},{10,11... | collective-permute-start | bytes 1179656 | tf_op jit(solution)/shard_map/ppermute | solution.py:759
  284.1 19.6 %collective-permute-start.19 = (f32[1,192,512]{2,1,0:T(8,128)S(1)}, f32[1,192,512]{2,1,0:T(8,128)S(1)}, u32[]{:S(2)}, u32[]{:S(2)}) collective-permute-start(f32[1,192,512]{2,1,0:T(8,128)S(1)} %select_add_fusion.2), channel_id=1, source_target_pairs={{0,2},{1,3},{2,0},{3,1},{4,6},{5,7},{6,4},{7,5},{8,10},{9,11},{10,... | collective-permute-start | bytes 1179656 | tf_op jit(solution)/shard_map/ppermute | solution.py:759
  299.3 47.3 %collective-permute-start.18 = (f32[4,96,1536]{2,1,0:T(8,128)}, f32[4,96,1536]{2,1,0:T(8,128)S(1)}, u32[]{:S(2)}, u32[]{:S(2)}) collective-permute-start(f32[4,96,1536]{2,1,0:T(8,128)} %get-tuple-element.140), channel_id=1, source_target_pairs={{0,4},{4,0},{8,12},{12,8},{16,20},{20,16},{24,28},{28,24},{1,5},{5... | collective-permute-start | bytes 7077896 | tf_op jit(solution)/shard_map/ppermute | solution.py:688
  305.0 15.7 %collective-permute-start.20 = (f32[1,192,512]{2,1,0:T(8,128)S(1)}, f32[1,192,512]{2,1,0:T(8,128)S(1)}, u32[]{:S(2)}, u32[]{:S(2)}) collective-permute-start(f32[1,192,512]{2,1,0:T(8,128)S(1)} %slice_select_fusion.5), channel_id=1, source_target_pairs={{0,1},{1,0},{2,3},{3,2},{4,5},{5,4},{6,7},{7,6},{8,9},{9,8},{10,11... | collective-permute-start | bytes 1179656 | tf_op jit(solution)/shard_map/ppermute | solution.py:759
  305.6 17.9 %collective-permute-start.21 = (f32[1,192,512]{2,1,0:T(8,128)S(1)}, f32[1,192,512]{2,1,0:T(8,128)S(1)}, u32[]{:S(2)}, u32[]{:S(2)}) collective-permute-start(f32[1,192,512]{2,1,0:T(8,128)S(1)} %add.188), channel_id=1, source_target_pairs={{0,1},{1,0},{2,3},{3,2},{4,5},{5,4},{6,7},{7,6},{8,9},{9,8},{10,11... | collective-permute-start | bytes 1179656 | tf_op jit(solution)/shard_map/ppermute | solution.py:759
  324.4 22.6 %collective-permute-start.22 = (f32[4,96,1536]{2,1,0:T(8,128)}, f32[4,96,1536]{2,1,0:T(8,128)}, u32[]{:S(2)}, u32[]{:S(2)}) collective-permute-start(f32[4,96,1536]{2,1,0:T(8,128)} %get-tuple-element.152), channel_id=1, source_target_pairs={{0,4},{4,0},{8,12},{12,8},{16,20},{20,16},{24,28},{28,24},{1,5},{5... | collective-permute-start | bytes 7077896 | tf_op jit(solution)/shard_map/ppermute | solution.py:688
  324.4 21.4 %collective-permute-start.23 = (f32[1,192,512]{2,1,0:T(8,128)S(1)}, f32[1,192,512]{2,1,0:T(8,128)S(1)}, u32[]{:S(2)}, u32[]{:S(2)}) collective-permute-start(f32[1,192,512]{2,1,0:T(8,128)S(1)} %select_add_fusion.1), channel_id=1, source_target_pairs={{0,2},{1,3},{2,0},{3,1},{4,6},{5,7},{6,4},{7,5},{8,10},{9,11},{10,... | collective-permute-start | bytes 1179656 | tf_op jit(solution)/shard_map/ppermute | solution.py:759
  359.0 38.5 %collective-permute-start.25 = (f32[384,768]{1,0:T(8,128)}, f32[384,768]{1,0:T(8,128)}, u32[]{:S(2)}, u32[]{:S(2)}) collective-permute-start(f32[384,768]{1,0:T(8,128)} %shard_map.249), channel_id=1, source_target_pairs={{1,0},{2,1},{3,2},{5,4},{6,5},{7,6},{9,8},{10,9},{11,10},{13,12},{... | collective-permute-start | bytes 3538952 | tf_op jit(solution)/shard_map/ppermute | solution.py:824
  369.1 28.4 %collective-permute-start.27 = (f32[1,192,512]{2,1,0:T(8,128)S(1)}, f32[1,192,512]{2,1,0:T(8,128)S(1)}, u32[]{:S(2)}, u32[]{:S(2)}) collective-permute-start(f32[1,192,512]{2,1,0:T(8,128)S(1)} %copy-done.27), channel_id=1, source_target_pairs={{0,1},{1,0},{2,3},{3,2},{4,5},{5,4},{6,7},{7,6},{8,9},{9,8},{10,11... | collective-permute-start | bytes 1179656 | tf_op jit(solution)/shard_map/ppermute | solution.py:759
  372.5 39.9 %collective-permute-start.24 = (f32[384,768]{1,0:T(8,128)S(1)}, f32[384,768]{1,0:T(8,128)}, u32[]{:S(2)}, u32[]{:S(2)}) collective-permute-start(f32[384,768]{1,0:T(8,128)S(1)} %slice.139), channel_id=1, source_target_pairs={{0,4},{4,0},{8,12},{12,8},{16,20},{20,16},{24,28},{28,24},{1,5},{5... | collective-permute-start | bytes 3538952 | tf_op jit(solution)/shard_map/ppermute | solution.py:688
  400.0 29.1 %collective-permute-start.26 = (f32[384,768]{1,0:T(8,128)}, f32[384,768]{1,0:T(8,128)}, u32[]{:S(2)}, u32[]{:S(2)}) collective-permute-start(f32[384,768]{1,0:T(8,128)} %add.195), channel_id=1, source_target_pairs={{1,0},{2,1},{3,2},{5,4},{6,5},{7,6},{9,8},{10,9},{11,10},{13,12},{... | collective-permute-start | bytes 3538952 | tf_op jit(solution)/shard_map/ppermute | solution.py:853
  417.6 1.3 collective-permute-start.28
  418.9 3.8 collective-permute-start.29
  422.5 9.9 %collective-permute-start.33 = (f32[3,96,512]{2,1,0:T(8,128)S(1)}, f32[3,96,512]{2,1,0:T(8,128)}, u32[]{:S(2)}, u32[]{:S(2)}) collective-permute-start(f32[3,96,512]{2,1,0:T(8,128)S(1)} %slice_select_fusion.2), channel_id=1, source_target_pairs={{0,4},{4,0},{8,12},{12,8},{16,20},{20,16},{24,28},{28,24},{1,5},{5... | collective-permute-start | bytes 1769480 | tf_op jit(solution)/shard_map/ppermute | solution.py:688
  422.7 3.8 collective-permute-start.30
  431.3 14.2 %collective-permute-start.31 = (f32[1,48,3072]{2,1,0:T(8,128)}, f32[1,48,3072]{2,1,0:T(8,128)}, u32[]{:S(2)}, u32[]{:S(2)}) collective-permute-start(f32[1,48,3072]{2,1,0:T(8,128)} %slice_select_fusion.4), channel_id=1, source_target_pairs={{0,1},{1,0},{2,3},{3,2},{4,5},{5,4},{6,7},{7,6},{8,9},{9,8},{10,11... | collective-permute-start | bytes 1769480 | tf_op jit(solution)/shard_map/ppermute | solution.py:759
  446.7 26.6 %collective-permute-start.32 = (f32[1,48,3072]{2,1,0:T(8,128)S(1)}, f32[1,48,3072]{2,1,0:T(8,128)S(1)}, u32[]{:S(2)}, u32[]{:S(2)}) collective-permute-start(f32[1,48,3072]{2,1,0:T(8,128)S(1)} %select_add_fusion), channel_id=1, source_target_pairs={{0,2},{1,3},{2,0},{3,1},{4,6},{5,7},{6,4},{7,5},{8,10},{9,11},{10,... | collective-permute-start | bytes 1769480 | tf_op jit(solution)/shard_map/ppermute | solution.py:759
  450.6 23.4 %copy-start.31 = (f32[8,768]{1,0:T(8,128)S(1)}, f32[8,768]{1,0:T(8,128)}, u32[]{:S(2)}) copy-start(f32[8,768]{1,0:T(8,128)} %add.207) | copy-start | bytes 73732
  473.3 21.1 %collective-permute-start.36 = (f32[1,48,3072]{2,1,0:T(8,128)S(1)}, f32[1,48,3072]{2,1,0:T(8,128)S(1)}, u32[]{:S(2)}, u32[]{:S(2)}) collective-permute-start(f32[1,48,3072]{2,1,0:T(8,128)S(1)} %add.209), channel_id=1, source_target_pairs={{0,1},{1,0},{2,3},{3,2},{4,5},{5,4},{6,7},{7,6},{8,9},{9,8},{10,11... | collective-permute-start | bytes 1769480 | tf_op jit(solution)/shard_map/ppermute | solution.py:759
  474.0 14.0 %collective-permute-start.34 = (f32[8,768]{1,0:T(8,128)S(1)}, f32[8,768]{1,0:T(8,128)S(1)}, u32[]{:S(2)}, u32[]{:S(2)}) collective-permute-start(f32[8,768]{1,0:T(8,128)S(1)} %copy-done.31), channel_id=1, source_target_pairs={{0,1},{1,0},{2,3},{3,2},{4,5},{5,4},{6,7},{7,6},{8,9},{9,8},{10,11... | collective-permute-start | bytes 73736 | tf_op jit(solution)/shard_map/ppermute | solution.py:759
  488.0 5.2 %collective-permute-start.35 = (f32[8,768]{1,0:T(8,128)S(1)}, f32[8,768]{1,0:T(8,128)S(1)}, u32[]{:S(2)}, u32[]{:S(2)}) collective-permute-start(f32[8,768]{1,0:T(8,128)S(1)} %add.212), channel_id=1, source_target_pairs={{0,2},{1,3},{2,0},{3,1},{4,6},{5,7},{6,4},{7,5},{8,10},{9,11},{10,... | collective-permute-start | bytes 73736 | tf_op jit(solution)/shard_map/ppermute | solution.py:759
  (39 other events, 266.7 us)
Sparse Core Ops, SparseCore 0:
  9.9 69.1 all-gather.2
  81.0 38.7 all-gather.4
  165.9 43.2 reduce-scatter.12
  212.1 43.9 reduce-scatter.14
  258.9 43.9 reduce-scatter.16
  353.0 57.2 reduce-scatter.18

commit v14 on v13

--- a/solution.py
+++ b/solution.py
@@ -813,7 +813,7 @@
     part_far = partial_rows(0, (dk, dv), qkv_full)
     line_c = line_middle(line_c)
     grads_c = jnp.concatenate([grads_qk[0] + given_qk, grads_vo[0] + swap(grads_vo[1])], axis=2)
-    grads_c, out_part, line_c, part_far = together((grads_c, out_part, line_c, part_far))
+    grads_c, out_part, part_far = together((grads_c, out_part, part_far))
     shard_c = scatter_chips(grads_c)[0]
     out_sib = swap(out_part[rows:])
 
@@ -822,9 +822,9 @@
     dwa_local = jnp.concatenate([dots, jnp.sum(cotangent * block_out)[None]])
 
     given_near = lax.ppermute(part_far, "seq", behind)
+    part_near = partial_rows(1, (dk, dv), qkv_full)
+    given_near, line_c, dq, far, near = together((given_near, line_c, dq, far, near))
     ends_c = line_end(line_c)
-    part_near = partial_rows(1, (dk, dv), qkv_full)
-    given_near, dq = together((given_near, dq))
     own_part = partial_rows(2, (dq, dk, dv), qkv_full)
     own_part, ends_c = together((own_part, ends_c))
     (sent,) = together((part_near,))

time: 508 us -> 522 us (1.028)
  waiting for transfers between devices: 130 us -> 151 us
  starting transfers between devices: 58.4 us -> 52.2 us
    ppermute x14, waiting for transfers between devices: 83.5 us -> 105 us  [body(): lax.ppermute(v, 'seq', [(i, i ^ bit) for i in range(groups)])]
    ppermute x14, starting transfers between devices: 26.3 us -> 19.5 us  [body(): lax.ppermute(v, 'seq', [(i, i ^ bit) for i in range(groups)])]
  transfers between devices with their start and end apart: 43 -> 43, of which waited for: 19 -> 17; matrix products, arithmetic and copies ran while one was open for 15% -> 14% of each run, Pallas kernels for 38% -> 37%
where the time goes in v14:
time: 522 us; the launch traced here: 517 us
  Pallas kernels  213 us (41%)
  waiting for transfers between devices  151 us (29%)
  starting transfers between devices  52.2 us (10%)
  other arithmetic  52.1 us (10%)
  local copies, waits for them, and re-layouts  30.3 us (6%)
  between operations  15.2 us (3%)
    ppermute x14, waiting for transfers between devices, body(): lax.ppermute(v, 'seq', [(i, i ^ bit) for i in range(groups)])  105 us
    pallas_call x3, Pallas kernels, mlp(): pl.pallas_call(functools.partial(mlp_kernel, len(ups), len(so_far) // 2),...  62 us
    pallas_call x2, Pallas kernels, attend_back(): pl.pallas_call(attend_back_kernel, grid=(count,), in_specs=[pl.BlockSpec(...  47.3 us
    pallas_call x2, Pallas kernels, weight_call(): pl.pallas_call(kernel, grid_spec=pltpu.PrefetchScalarGridSpec(num_scalar_...  26.3 us
    pallas_call x3, Pallas kernels, partial_rows(): pl.pallas_call(functools.partial(partial_kernel, len(grads)), grid=(model...  24.4 us
    pallas_call x1, Pallas kernels, attend(): pl.pallas_call(attend_kernel, grid=(pairs,), in_specs=[pl.BlockSpec((rows...  23.1 us
    pallas_call x1, Pallas kernels, project(): pl.pallas_call(qkv_kernel, grid=(3 * third,), in_specs=[whole((rows, mode...  21.7 us
    ppermute x14, starting transfers between devices, body(): lax.ppermute(v, 'seq', [(i, i ^ bit) for i in range(groups)])  19.5 us
  transfers between devices with their start and end apart: 43, of which 17 were waited for; matrix products, arithmetic and copies ran while one was open for 14% of the time, Pallas kernels for 37%

profile of v14, /device:TPU:0, one launch (start us, length us, event | category | flops | bytes accessed | tf_op | source)
XLA Modules:
  0.0 517.0 jit_solution(8882708345592252288)
XLA Ops:
  8.0 1.9 reshape.142
  12.8 4.6 collective-permute-start
  25.2 17.9 %collective-permute-done.near_ref = f32[384,768]{1,0:T(8,128)S(1)} collective-permute-done((f32[384,768]{1,0:T(8,128)S(1)}, f32[384,768]{1,0:T(8,128)S(1)}, u32[]{:S(2)}, u32[]{:S(2)}) %collective-permute-start) | collective-permute-done | bytes 1179680 | tf_op jit(solution)/shard_map/ppermute | solution.py:715
  43.1 4.4 collective-permute-start.1
  47.6 4.0 collective-permute-start.2
  52.3 7.4 %fusion.5 = (f32[]{:T(128)}, f32[]{:T(128)}, f32[]{:T(128)}, f32[]{:T(128)}, f32[384,768]{1,0:T(8,128)}) fusion(f32[384,768]{1,0:T(8,128)S(1)} %copy-done.13, f32[3,384,768]{2,1,0:T(8,128)} %param.18, f32[384,768]{1,0:T(8,128)} %param.17, f32[]{:T(128)} %bitcast.5, f32[]{:T(128)} %bitcast.3, f32[]{:T(128)} %bitcast.1, f32[]{:T(128)} %bitcast), kind=kLoop, calls=%fused_computation.17 | loop fusion | flops 4423676 | bytes 7077920 | tf_op jit(solution)/shard_map/reduce_sum | solution.py:731
  60.8 11.8 %collective-permute-done.2 = s32[1,384]{1,0:T(1,128)} collective-permute-done((s32[1,384]{1,0:T(1,128)S(1)}, s32[1,384]{1,0:T(1,128)}, u32[]{:S(2)}, u32[]{:S(2)}) %collective-permute-start.2) | collective-permute-done | bytes 1568 | tf_op jit(solution)/shard_map/ppermute | solution.py:716
  72.7 5.0 collective-permute-start.3
  77.7 3.2 pad_maximum_fusion.2
  87.4 21.7 %shard_map.239 = (f32[384,768]{1,0:T(8,128)}, f32[1152,1536]{1,0:T(8,128)}, bf16[1152,768]{1,0:T(8,128)(2,1)}, bf16[1152,768]{1,0:T(8,128)(2,1)}) custom-call(f32[384,768]{1,0:T(8,128)} %copy-done.5, f32[384,768]{1,0:T(8,128)} %copy-done.3, f32[384,768]{1,0:T(8,128)} %own_ref.1, f32[1,768]{1,0:T(1,128)} %broadcast_in_dim.50.gain_ref, ...), custom_call_target="tpu_custom_call" | custom-call | flops 22000001024 | bytes 1048576 | tf_op jit(solution)/shard_map/pallas_call | solution.py:144
  110.5 23.1 %shard_map.240.att_ref = f32[384,768]{1,0:T(8,128)} custom-call(f32[384,768]{1,0:T(8,128)} %get-tuple-element.126.q_ref, f32[1152,1536]{1,0:T(8,128)} %get-tuple-element.127.k_ref.v_ref, f32[1152,1536]{1,0:T(8,128)} %get-tuple-element.127.k_ref.v_ref, s32[384,128]{1,0:T(8,128)} %broadcast_in_dim.52.segq_ref, s32[8,1152]{1,0:T(8,128)} %broadcast_in_dim.54.segk_ref), custom_call_target="tpu_custom_call" | custom-call | flops 26400000000 | bytes 1048576 | tf_op jit(solution)/shard_map/pallas_call | solution.py:236
  133.6 3.7 convolution_add_fusion.resid_ref
  139.4 4.2 collective-permute-done.12.refs_7_
  143.6 2.0 collective-permute-done.9.refs_3_
  146.6 20.1 %shard_map.241 = (f32[768,768]{1,0:T(8,128)}, f32[768,768]{1,0:T(8,128)}, f32[4,1,384,512]{3,2,1,0:T(8,128)}) custom-call(s32[1]{0:T(128)} %bitcast.13.chip_ref, f32[384,768]{1,0:T(8,128)} %copy-done.14, f32[384,768]{1,0:T(8,128)} %copy-done.44, f32[384,768]{1,0:T(8,128)} %cot_ref.7, f32[384,768]{1,0:T(8,128)} %collective-permute-done.5.cot_other_ref, ...), custom_call_target="tpu_custom_call" | custom-call | flops 19800000512 | bytes 1048576 | tf_op jit(solution)/shard_map/pallas_call | solution.py:457
  166.8 20.9 %shard_map.242 = (f32[768,768]{1,0:T(8,128)}, f32[768,768]{1,0:T(8,128)}, f32[4,1,384,512]{3,2,1,0:T(8,128)}) custom-call(s32[1]{0:T(128)} %bitcast.13.chip_ref, f32[384,768]{1,0:T(8,128)} %copy-done.14, f32[384,768]{1,0:T(8,128)} %copy-done.44, f32[384,768]{1,0:T(8,128)} %cot_ref.7, f32[384,768]{1,0:T(8,128)} %collective-permute-done.5.cot_other_ref, ...), custom_call_target="tpu_custom_call" | custom-call | flops 19800000512 | bytes 1048576 | tf_op jit(solution)/shard_map/pallas_call | solution.py:457
  187.9 21.1 %shard_map.243 = (f32[768,768]{1,0:T(8,128)}, f32[768,768]{1,0:T(8,128)}, f32[4,1,384,512]{3,2,1,0:T(8,128)}) custom-call(s32[1]{0:T(128)} %bitcast.13.chip_ref, f32[384,768]{1,0:T(8,128)} %copy-done.14, f32[384,768]{1,0:T(8,128)} %copy-done.44, f32[384,768]{1,0:T(8,128)} %cot_ref.7, f32[384,768]{1,0:T(8,128)} %collective-permute-done.5.cot_other_ref, ...), custom_call_target="tpu_custom_call" | custom-call | flops 19800000512 | bytes 1048576 | tf_op jit(solution)/shard_map/pallas_call | solution.py:457
  210.7 2.5 collective-permute-done.13.given_ref
  216.5 7.8 %shard_map.244 = (f32[384,768]{1,0:T(8,128)}, f32[384,768]{1,0:T(8,128)}, f32[8,768]{1,0:T(8,128)}) custom-call(f32[768,768]{1,0:T(8,128)} %get-tuple-element.108.part_ref, f32[384,768]{1,0:T(8,128)} %copy-done.45, f32[384,768]{1,0:T(8,128)} %copy-done.14, f32[384,768]{1,0:T(8,128)} %cot_ref.7, f32[1,768]{1,0:T(1,128)} %broadcast_in_dim.55.gain_ref, ...), custom_call_target="tpu_custom_call" | custom-call | flops 6600000000 | bytes 1048576 | tf_op jit(solution)/shard_map/pallas_call | solution.py:505
  224.3 1.8 collective-permute-done.14
  227.8 2.6 collective-permute-start.15
  230.4 23.5 %shard_map.245 = (f32[384,768]{1,0:T(8,128)}, f32[1152,768]{1,0:T(8,128)}, f32[1152,768]{1,0:T(8,128)}) custom-call(f32[384,768]{1,0:T(8,128)} %get-tuple-element.126.q_ref, f32[1152,1536]{1,0:T(8,128)} %get-tuple-element.127.k_ref.v_ref, f32[1152,1536]{1,0:T(8,128)} %get-tuple-element.127.k_ref.v_ref, f32[384,768]{1,0:T(8,128)} %get-tuple-element.128.g_ref, ...), custom_call_target="tpu_custom_call" | custom-call | flops 23100000256 | bytes 1048576 | tf_op jit(solution)/shard_map/pallas_call | solution.py:328
  254.0 2.9 reduce-scatter.15.cloned.1.call-done
  260.2 23.7 %shard_map.246 = (f32[384,768]{1,0:T(8,128)}, f32[1152,768]{1,0:T(8,128)}, f32[1152,768]{1,0:T(8,128)}) custom-call(f32[384,768]{1,0:T(8,128)} %get-tuple-element.126.q_ref, f32[1152,1536]{1,0:T(8,128)} %get-tuple-element.127.k_ref.v_ref, f32[1152,1536]{1,0:T(8,128)} %get-tuple-element.127.k_ref.v_ref, ...), custom_call_target="tpu_custom_call", output_to_operand_aliasing={{0}: (8, {}), {1}: (9, {}), {2}: (10, {})} | custom-call | flops 23100000256 | bytes 1048576 | tf_op jit(solution)/shard_map/pallas_call | solution.py:328
  285.0 2.4 collective-permute-start.19
  287.4 12.7 %shard_map.247 = (f32[4,96,1536]{2,1,0:T(8,128)}, f32[4,96,1536]{2,1,0:T(8,128)}) custom-call(s32[1]{0:T(128)} %bitcast.12.core_ref, bf16[1152,768]{1,0:T(8,128)(2,1)} %get-tuple-element.101.hi_ref, bf16[1152,768]{1,0:T(8,128)(2,1)} %get-tuple-element.102.lo_ref, f32[384,768]{1,0:T(8,128)} %get-tuple-element.164.dq_ref.refs_0_, ...), custom_call_target="tpu_custom_call" | custom-call | flops 9900000256 | bytes 1048576 | tf_op jit(solution)/shard_map/pallas_call | solution.py:591
  300.2 4.5 collective-permute-done.19
  308.0 13.6 %shard_map.248 = (f32[4,96,1536]{2,1,0:T(8,128)}, f32[4,96,1536]{2,1,0:T(8,128)}) custom-call(s32[1]{0:T(128)} %bitcast.12.core_ref, bf16[1152,768]{1,0:T(8,128)(2,1)} %get-tuple-element.101.hi_ref, bf16[1152,768]{1,0:T(8,128)(2,1)} %get-tuple-element.102.lo_ref, f32[1152,768]{1,0:T(8,128)} %get-tuple-element.149.dv_ref.refs_1_.refs_2_, ...), custom_call_target="tpu_custom_call" | custom-call | flops 9900000256 | bytes 1048576 | tf_op jit(solution)/shard_map/pallas_call | solution.py:591
  322.4 2.0 collective-permute-done.21
  325.4 7.7 %shard_map.249 = f32[384,768]{1,0:T(8,128)} custom-call(f32[1152,768]{1,0:T(8,128)} %get-tuple-element.156.dk_ref.refs_0_.refs_1_, f32[1152,768]{1,0:T(8,128)} %get-tuple-element.149.dv_ref.refs_1_.refs_2_, f32[768,2304]{1,0:T(8,128)} %all-gather.3.cloned.1.call-done.w_ref.refs_2_.refs_3_), custom_call_target="tpu_custom_call" | custom-call | flops 6600000000 | bytes 1048576 | tf_op jit(solution)/shard_map/pallas_call | solution.py:632
  334.7 2.0 add.190
  336.8 2.6 pad_maximum_fusion
  346.0 3.8 collective-permute-start.25
  349.9 7.6 %shard_map.250 = f32[384,768]{1,0:T(8,128)} custom-call(f32[1152,768]{1,0:T(8,128)} %get-tuple-element.156.dk_ref.refs_0_.refs_1_, f32[1152,768]{1,0:T(8,128)} %get-tuple-element.149.dv_ref.refs_1_.refs_2_, f32[768,2304]{1,0:T(8,128)} %all-gather.3.cloned.1.call-done.w_ref.refs_2_.refs_3_), custom_call_target="tpu_custom_call" | custom-call | flops 6600000000 | bytes 1048576 | tf_op jit(solution)/shard_map/pallas_call | solution.py:632
  357.6 34.7 %collective-permute-done.25 = f32[1,192,512]{2,1,0:T(8,128)S(1)} collective-permute-done((f32[1,192,512]{2,1,0:T(8,128)S(1)}, f32[1,192,512]{2,1,0:T(8,128)S(1)}, u32[]{:S(2)}, u32[]{:S(2)}) %collective-permute-start.25) | collective-permute-done | bytes 393248 | tf_op jit(solution)/shard_map/ppermute | solution.py:759
  395.6 2.7 collective-permute-start.27
  399.8 5.3 %multiply_reduce_fusion.1 = (f32[]{:T(128)}, f32[384,768]{1,0:T(8,128)}) fusion(f32[384,768]{1,0:T(8,128)} %cot_ref.7, f32[384,768]{1,0:T(8,128)} %collective-permute-done.23, f32[384,768]{1,0:T(8,128)} %copy-done.14, f32[768,768]{1,0:T(8,128)} %get-tuple-element.157, f32[384,768]{1,0:T(8,128)} %get-tuple-element.97, f32[]{:T(128)} %bitcast.11), kind=kLoop, calls=%fused_computation.21 | loop fusion | flops 1769471 | bytes 7077896 | tf_op jit(solution)/shard_map/reduce_sum | solution.py:822
  407.0 9.1 %shard_map.251 = f32[384,768]{1,0:T(8,128)} custom-call(f32[384,768]{1,0:T(8,128)} %get-tuple-element.164.dq_ref.refs_0_, f32[1152,768]{1,0:T(8,128)} %get-tuple-element.156.dk_ref.refs_0_.refs_1_, f32[1152,768]{1,0:T(8,128)} %get-tuple-element.149.dv_ref.refs_1_.refs_2_, f32[768,2304]{1,0:T(8,128)} %all-gather.3.cloned.1.call-done.w_ref.refs_2_.refs_3_), custom_call_target="tpu_custom_call" | custom-call | flops 6600000000 | bytes 1048576 | tf_op jit(solution)/shard_map/pallas_call | solution.py:632
  418.1 14.4 %collective-permute-done.27 = f32[1,192,512]{2,1,0:T(8,128)} collective-permute-done((f32[1,192,512]{2,1,0:T(8,128)}, f32[1,192,512]{2,1,0:T(8,128)}, u32[]{:S(2)}, u32[]{:S(2)}) %collective-permute-start.27) | collective-permute-done | bytes 393248 | tf_op jit(solution)/shard_map/ppermute | solution.py:759
  437.5 2.2 collective-permute-done.29
  444.2 2.1 slice_select_fusion.4
  446.3 2.1 broadcast_select_fusion.1
  452.0 2.2 fusion.7
  454.2 5.3 %collective-permute-done.31 = f32[1,48,3072]{2,1,0:T(8,128)} collective-permute-done((f32[1,48,3072]{2,1,0:T(8,128)}, f32[1,48,3072]{2,1,0:T(8,128)}, u32[]{:S(2)}, u32[]{:S(2)}) %collective-permute-start.31) | collective-permute-done | bytes 589856 | tf_op jit(solution)/shard_map/ppermute | solution.py:759
  462.2 24.0 %collective-permute-done.32 = f32[1,48,3072]{2,1,0:T(8,128)S(1)} collective-permute-done((f32[1,48,3072]{2,1,0:T(8,128)S(1)}, f32[1,48,3072]{2,1,0:T(8,128)S(1)}, u32[]{:S(2)}, u32[]{:S(2)}) %collective-permute-start.32) | collective-permute-done | bytes 589856 | tf_op jit(solution)/shard_map/ppermute | solution.py:759
  486.4 2.0 collective-permute-start.34
  488.4 13.7 %collective-permute-done.34 = f32[8,768]{1,0:T(8,128)S(1)} collective-permute-done((f32[8,768]{1,0:T(8,128)S(1)}, f32[8,768]{1,0:T(8,128)S(1)}, u32[]{:S(2)}, u32[]{:S(2)}) %collective-permute-start.34) | collective-permute-done | bytes 24608 | tf_op jit(solution)/shard_map/ppermute | solution.py:759
  502.2 4.7 collective-permute-done.35
  (250 shorter events, 76.3 us)
Async XLA Ops:
  7.2 79.7 %all-gather.3.cloned.1.call-start = ((), (), s32[]{:S(2)}) async-start(), calls=%async_computation.4 | async-start | bytes 7962624 | tf_op jit(solution)/shard_map/all_gather | solution.py:691
  7.9 125.7 %all-gather.5.cloned.1.call-start = ((), (), s32[]{:S(2)}) async-start(), calls=%async_computation.5 | async-start | bytes 2654208 | tf_op jit(solution)/shard_map/all_gather | solution.py:691
  12.3 8.9 %collective-permute-start.6 = (f32[96,1536]{1,0:T(8,128)}, f32[96,1536]{1,0:T(8,128)}, u32[]{:S(2)}, u32[]{:S(2)}) collective-permute-start(f32[96,1536]{1,0:T(8,128)} %select_n.149), channel_id=1, source_target_pairs={{0,4},{4,0},{8,12},{12,8},{16,20},{20,16},{24,28},{28,24},{1,5},{5... | collective-permute-start | bytes 1769480 | tf_op jit(solution)/shard_map/ppermute | solution.py:688
  12.8 30.4 %collective-permute-start = (f32[384,768]{1,0:T(8,128)S(1)}, f32[384,768]{1,0:T(8,128)S(1)}, u32[]{:S(2)}, u32[]{:S(2)}) collective-permute-start(f32[384,768]{1,0:T(8,128)S(1)} %copy-done), channel_id=1, source_target_pairs={{0,1},{1,2},{2,3},{4,5},{5,6},{6,7},{8,9},{9,10},{10,11},{12,13},{... | collective-permute-start | bytes 3538952 | tf_op jit(solution)/shard_map/ppermute | solution.py:715
  17.4 66.9 %collective-permute-start.10 = (f32[384,768]{1,0:T(8,128)}, f32[384,768]{1,0:T(8,128)}, u32[]{:S(2)}, u32[]{:S(2)}) collective-permute-start(f32[384,768]{1,0:T(8,128)} %refs_4_.5), channel_id=1, source_target_pairs={{0,8},{4,12},{8,0},{12,4},{16,24},{20,28},{24,16},{28,20},{1,9},{5... | collective-permute-start | bytes 3538952 | tf_op jit(solution)/shard_map/ppermute | solution.py:688
  22.5 29.1 %copy-start.13 = (f32[384,768]{1,0:T(8,128)S(1)}, f32[384,768]{1,0:T(8,128)}, u32[]{:S(2)}) copy-start(f32[384,768]{1,0:T(8,128)} %cot_ref.7) | copy-start | bytes 3538948
  22.5 29.1 %copy-start.36 = (f32[5]{0:T(128)S(1)}, f32[5]{0:T(128)}, u32[]{:S(2)}) copy-start(f32[5]{0:T(128)} %param.19) | copy-start | bytes 64
  23.7 62.2 %collective-permute-start.8 = (f32[192,1536]{1,0:T(8,128)}, f32[192,1536]{1,0:T(8,128)}, u32[]{:S(2)}, u32[]{:S(2)}) collective-permute-start(f32[192,1536]{1,0:T(8,128)} %pad_maximum_fusion.1.refs_0_), channel_id=1, source_target_pairs={{0,16},{4,20},{8,24},{12,28},{16,0},{20,4},{24,8},{28,12},{1,17},{... | collective-permute-start | bytes 3538952 | tf_op jit(solution)/shard_map/ppermute | solution.py:688
  43.1 43.2 %collective-permute-start.1 = (f32[384,768]{1,0:T(8,128)S(1)}, f32[384,768]{1,0:T(8,128)S(1)}, u32[]{:S(2)}, u32[]{:S(2)}) collective-permute-start(f32[384,768]{1,0:T(8,128)S(1)} %collective-permute-done.near_ref), channel_id=1, source_target_pairs={{0,1},{1,2},{2,3},{4,5},{5,6},{6,7},{8,9},{9,10},{10,11},{12,13},{... | collective-permute-start | bytes 3538952 | tf_op jit(solution)/shard_map/ppermute | solution.py:717
  47.6 25.1 %collective-permute-start.2 = (s32[1,384]{1,0:T(1,128)S(1)}, s32[1,384]{1,0:T(1,128)}, u32[]{:S(2)}, u32[]{:S(2)}) collective-permute-start(s32[1,384]{1,0:T(1,128)S(1)} %get-tuple-element.219), channel_id=1, source_target_pairs={{0,1},{1,2},{2,3},{4,5},{5,6},{6,7},{8,9},{9,10},{10,11},{12,13},{... | collective-permute-start | bytes 4616 | tf_op jit(solution)/shard_map/ppermute | solution.py:716
  51.6 85.8 %collective-permute-start.5 = (f32[384,768]{1,0:T(8,128)S(1)}, f32[384,768]{1,0:T(8,128)}, u32[]{:S(2)}, u32[]{:S(2)}) collective-permute-start(f32[384,768]{1,0:T(8,128)S(1)} %copy-done.13), channel_id=1, source_target_pairs={{0,4},{4,0},{8,12},{12,8},{16,20},{20,16},{24,28},{28,24},{1,5},{5... | collective-permute-start | bytes 3538952 | tf_op jit(solution)/shard_map/ppermute | solution.py:688
  51.6 161.6 %reduce-scatter.13.cloned.1.call-start = ((), (), s32[]{:S(2)}) async-start(), calls=%async_computation.6 | async-start | bytes 3932160
  72.7 9.4 %collective-permute-start.3 = (s32[1,384]{1,0:T(1,128)}, s32[1,384]{1,0:T(1,128)S(1)}, u32[]{:S(2)}, u32[]{:S(2)}) collective-permute-start(s32[1,384]{1,0:T(1,128)} %collective-permute-done.2), channel_id=1, source_target_pairs={{0,1},{1,2},{2,3},{4,5},{5,6},{6,7},{8,9},{9,10},{10,11},{12,13},{... | collective-permute-start | bytes 4616 | tf_op jit(solution)/shard_map/ppermute | solution.py:718
  82.1 57.4 %collective-permute-start.11 = (f32[384,768]{1,0:T(8,128)}, f32[384,768]{1,0:T(8,128)}, u32[]{:S(2)}, u32[]{:S(2)}) collective-permute-start(f32[384,768]{1,0:T(8,128)} %refs_4_.5), channel_id=1, source_target_pairs={{0,16},{4,20},{8,24},{12,28},{16,0},{20,4},{24,8},{28,12},{1,17},{... | collective-permute-start | bytes 3538952 | tf_op jit(solution)/shard_map/ppermute | solution.py:688
  84.3 55.2 %collective-permute-start.7 = (f32[192,1536]{1,0:T(8,128)}, f32[192,1536]{1,0:T(8,128)}, u32[]{:S(2)}, u32[]{:S(2)}) collective-permute-start(f32[192,1536]{1,0:T(8,128)} %pad_maximum_fusion.1.refs_0_), channel_id=1, source_target_pairs={{0,8},{4,12},{8,0},{12,4},{16,24},{20,28},{24,16},{28,20},{1,9},{5... | collective-permute-start | bytes 3538952 | tf_op jit(solution)/shard_map/ppermute | solution.py:688
  85.8 57.8 %collective-permute-start.12 = (f32[384,768]{1,0:T(8,128)}, f32[384,768]{1,0:T(8,128)}, u32[]{:S(2)}, u32[]{:S(2)}) collective-permute-start(f32[384,768]{1,0:T(8,128)} %collective-permute-done.10.refs_5_), channel_id=1, source_target_pairs={{0,16},{4,20},{8,24},{12,28},{16,0},{20,4},{24,8},{28,12},{1,17},{... | collective-permute-start | bytes 3538952 | tf_op jit(solution)/shard_map/ppermute | solution.py:688
  86.4 59.3 %collective-permute-start.9 = (f32[192,1536]{1,0:T(8,128)}, f32[192,1536]{1,0:T(8,128)}, u32[]{:S(2)}, u32[]{:S(2)}) collective-permute-start(f32[192,1536]{1,0:T(8,128)} %collective-permute-done.8.refs_2_), channel_id=1, source_target_pairs={{0,8},{4,12},{8,0},{12,4},{16,24},{20,28},{24,16},{28,20},{1,9},{5... | collective-permute-start | bytes 3538952 | tf_op jit(solution)/shard_map/ppermute | solution.py:688
  137.4 8.3 %collective-permute-start.4 = (f32[384,768]{1,0:T(8,128)S(1)}, f32[384,768]{1,0:T(8,128)S(1)}, u32[]{:S(2)}, u32[]{:S(2)}) collective-permute-start(f32[384,768]{1,0:T(8,128)S(1)} %convolution_add_fusion.resid_ref), channel_id=1, source_target_pairs={{0,4},{4,0},{8,12},{12,8},{16,20},{20,16},{24,28},{28,24},{1,5},{5... | collective-permute-start | bytes 3538952 | tf_op jit(solution)/shard_map/ppermute | solution.py:688
  166.7 90.2 %reduce-scatter.15.cloned.1.call-start = ((), (), s32[]{:S(2)}) async-start(), calls=%async_computation.7 | async-start | bytes 3932160
  187.7 117.0 %reduce-scatter.17.cloned.1.call-start = ((), (), s32[]{:S(2)}) async-start(), calls=%async_computation.8 | async-start | bytes 3932160
  210.3 2.9 collective-permute-start.13
  210.5 233.7 %reduce-scatter.19.cloned.1.call-start = ((), (), s32[]{:S(2)}) async-start(), calls=%async_computation.9 | async-start | bytes 5898240
  214.9 11.2 %collective-permute-start.14 = (f32[1,192,512]{2,1,0:T(8,128)S(1)}, f32[1,192,512]{2,1,0:T(8,128)S(1)}, u32[]{:S(2)}, u32[]{:S(2)}) collective-permute-start(f32[1,192,512]{2,1,0:T(8,128)S(1)} %slice_select_fusion.7), channel_id=1, source_target_pairs={{0,1},{1,0},{2,3},{3,2},{4,5},{5,4},{6,7},{7,6},{8,9},{9,8},{10,11... | collective-permute-start | bytes 1179656 | tf_op jit(solution)/shard_map/ppermute | solution.py:759
  227.8 26.1 %collective-permute-start.15 = (f32[1,192,512]{2,1,0:T(8,128)S(1)}, f32[1,192,512]{2,1,0:T(8,128)S(1)}, u32[]{:S(2)}, u32[]{:S(2)}) collective-permute-start(f32[1,192,512]{2,1,0:T(8,128)S(1)} %select_add_fusion.3), channel_id=1, source_target_pairs={{0,2},{1,3},{2,0},{3,1},{4,6},{5,7},{6,4},{7,5},{8,10},{9,11},{10,... | collective-permute-start | bytes 1179656 | tf_op jit(solution)/shard_map/ppermute | solution.py:759
  258.1 25.8 %collective-permute-start.16 = (f32[1,192,512]{2,1,0:T(8,128)S(1)}, f32[1,192,512]{2,1,0:T(8,128)S(1)}, u32[]{:S(2)}, u32[]{:S(2)}) collective-permute-start(f32[1,192,512]{2,1,0:T(8,128)S(1)} %slice_select_fusion.6), channel_id=1, source_target_pairs={{0,1},{1,0},{2,3},{3,2},{4,5},{5,4},{6,7},{7,6},{8,9},{9,8},{10,11... | collective-permute-start | bytes 1179656 | tf_op jit(solution)/shard_map/ppermute | solution.py:759
  259.7 24.4 %collective-permute-start.17 = (f32[1,192,512]{2,1,0:T(8,128)S(1)}, f32[1,192,512]{2,1,0:T(8,128)S(1)}, u32[]{:S(2)}, u32[]{:S(2)}) collective-permute-start(f32[1,192,512]{2,1,0:T(8,128)S(1)} %add.185), channel_id=1, source_target_pairs={{0,1},{1,0},{2,3},{3,2},{4,5},{5,4},{6,7},{7,6},{8,9},{9,8},{10,11... | collective-permute-start | bytes 1179656 | tf_op jit(solution)/shard_map/ppermute | solution.py:759
  285.0 19.6 %collective-permute-start.19 = (f32[1,192,512]{2,1,0:T(8,128)S(1)}, f32[1,192,512]{2,1,0:T(8,128)S(1)}, u32[]{:S(2)}, u32[]{:S(2)}) collective-permute-start(f32[1,192,512]{2,1,0:T(8,128)S(1)} %select_add_fusion.2), channel_id=1, source_target_pairs={{0,2},{1,3},{2,0},{3,1},{4,6},{5,7},{6,4},{7,5},{8,10},{9,11},{10,... | collective-permute-start | bytes 1179656 | tf_op jit(solution)/shard_map/ppermute | solution.py:759
  300.2 32.9 %collective-permute-start.18 = (f32[4,96,1536]{2,1,0:T(8,128)}, f32[4,96,1536]{2,1,0:T(8,128)S(1)}, u32[]{:S(2)}, u32[]{:S(2)}) collective-permute-start(f32[4,96,1536]{2,1,0:T(8,128)} %get-tuple-element.142), channel_id=1, source_target_pairs={{0,4},{4,0},{8,12},{12,8},{16,20},{20,16},{24,28},{28,24},{1,5},{5... | collective-permute-start | bytes 7077896 | tf_op jit(solution)/shard_map/ppermute | solution.py:688
  305.9 15.6 %collective-permute-start.20 = (f32[1,192,512]{2,1,0:T(8,128)S(1)}, f32[1,192,512]{2,1,0:T(8,128)S(1)}, u32[]{:S(2)}, u32[]{:S(2)}) collective-permute-start(f32[1,192,512]{2,1,0:T(8,128)S(1)} %slice_select_fusion.5), channel_id=1, source_target_pairs={{0,1},{1,0},{2,3},{3,2},{4,5},{5,4},{6,7},{7,6},{8,9},{9,8},{10,11... | collective-permute-start | bytes 1179656 | tf_op jit(solution)/shard_map/ppermute | solution.py:759
  306.5 18.0 %collective-permute-start.21 = (f32[1,192,512]{2,1,0:T(8,128)S(1)}, f32[1,192,512]{2,1,0:T(8,128)S(1)}, u32[]{:S(2)}, u32[]{:S(2)}) collective-permute-start(f32[1,192,512]{2,1,0:T(8,128)S(1)} %add.188), channel_id=1, source_target_pairs={{0,1},{1,0},{2,3},{3,2},{4,5},{5,4},{6,7},{7,6},{8,9},{9,8},{10,11... | collective-permute-start | bytes 1179656 | tf_op jit(solution)/shard_map/ppermute | solution.py:759
  325.4 8.1 %collective-permute-start.22 = (f32[4,96,1536]{2,1,0:T(8,128)}, f32[4,96,1536]{2,1,0:T(8,128)}, u32[]{:S(2)}, u32[]{:S(2)}) collective-permute-start(f32[4,96,1536]{2,1,0:T(8,128)} %get-tuple-element.154), channel_id=1, source_target_pairs={{0,4},{4,0},{8,12},{12,8},{16,20},{20,16},{24,28},{28,24},{1,5},{5... | collective-permute-start | bytes 7077896 | tf_op jit(solution)/shard_map/ppermute | solution.py:688
  343.4 56.4 %collective-permute-start.23 = (f32[384,768]{1,0:T(8,128)}, f32[384,768]{1,0:T(8,128)}, u32[]{:S(2)}, u32[]{:S(2)}) collective-permute-start(f32[384,768]{1,0:T(8,128)} %slice.139), channel_id=1, source_target_pairs={{0,4},{4,0},{8,12},{12,8},{16,20},{20,16},{24,28},{28,24},{1,5},{5... | collective-permute-start | bytes 3538952 | tf_op jit(solution)/shard_map/ppermute | solution.py:688
  343.9 49.2 %collective-permute-start.24 = (f32[384,768]{1,0:T(8,128)}, f32[384,768]{1,0:T(8,128)S(1)}, u32[]{:S(2)}, u32[]{:S(2)}) collective-permute-start(f32[384,768]{1,0:T(8,128)} %shard_map.249), channel_id=1, source_target_pairs={{1,0},{2,1},{3,2},{5,4},{6,5},{7,6},{9,8},{10,9},{11,10},{13,12},{... | collective-permute-start | bytes 3538952 | tf_op jit(solution)/shard_map/ppermute | solution.py:824
  346.0 46.2 %collective-permute-start.25 = (f32[1,192,512]{2,1,0:T(8,128)S(1)}, f32[1,192,512]{2,1,0:T(8,128)S(1)}, u32[]{:S(2)}, u32[]{:S(2)}) collective-permute-start(f32[1,192,512]{2,1,0:T(8,128)S(1)} %copy-done.29), channel_id=1, source_target_pairs={{0,2},{1,3},{2,0},{3,1},{4,6},{5,7},{6,4},{7,5},{8,10},{9,11},{10,... | collective-permute-start | bytes 1179656 | tf_op jit(solution)/shard_map/ppermute | solution.py:759
  357.5 36.7 %copy-start.7 = (f32[3,192,512]{2,1,0:T(8,128)}, f32[3,192,512]{2,1,0:T(8,128)S(1)}, u32[]{:S(2)}) copy-start(f32[3,192,512]{2,1,0:T(8,128)S(1)} %constant_dynamic-update-slice_fusion.1) | copy-start | bytes 3538948
  357.5 35.5 %copy-start.10 = (f32[384,768]{1,0:T(8,128)S(1)}, f32[384,768]{1,0:T(8,128)}, u32[]{:S(2)}) copy-start(f32[384,768]{1,0:T(8,128)} %shard_map.250) | copy-start | bytes 3538948
  357.6 36.7 %copy-start.23 = (f32[3,192,512]{2,1,0:T(8,128)}, f32[3,192,512]{2,1,0:T(8,128)S(1)}, u32[]{:S(2)}) copy-start(f32[3,192,512]{2,1,0:T(8,128)S(1)} %constant_dynamic-update-slice_fusion.4) | copy-start | bytes 3538948
  394.2 49.9 %collective-permute-start.26 = (f32[384,768]{1,0:T(8,128)}, f32[384,768]{1,0:T(8,128)}, u32[]{:S(2)}, u32[]{:S(2)}) collective-permute-start(f32[384,768]{1,0:T(8,128)} %add.195), channel_id=1, source_target_pairs={{1,0},{2,1},{3,2},{5,4},{6,5},{7,6},{9,8},{10,9},{11,10},{13,12},{... | collective-permute-start | bytes 3538952 | tf_op jit(solution)/shard_map/ppermute | solution.py:853
  395.6 36.8 %collective-permute-start.27 = (f32[1,192,512]{2,1,0:T(8,128)}, f32[1,192,512]{2,1,0:T(8,128)}, u32[]{:S(2)}, u32[]{:S(2)}) collective-permute-start(f32[1,192,512]{2,1,0:T(8,128)} %add.194), channel_id=1, source_target_pairs={{0,1},{1,0},{2,3},{3,2},{4,5},{5,4},{6,7},{7,6},{8,9},{9,8},{10,11... | collective-permute-start | bytes 1179656 | tf_op jit(solution)/shard_map/ppermute | solution.py:759
  434.4 1.4 collective-permute-start.28
  435.8 3.9 collective-permute-start.29
  437.4 8.9 %collective-permute-start.33 = (f32[3,96,512]{2,1,0:T(8,128)S(1)}, f32[3,96,512]{2,1,0:T(8,128)}, u32[]{:S(2)}, u32[]{:S(2)}) collective-permute-start(f32[3,96,512]{2,1,0:T(8,128)S(1)} %slice_select_fusion.2), channel_id=1, source_target_pairs={{0,4},{4,0},{8,12},{12,8},{16,20},{20,16},{24,28},{28,24},{1,5},{5... | collective-permute-start | bytes 1769480 | tf_op jit(solution)/shard_map/ppermute | solution.py:688
  439.7 3.8 collective-permute-start.30
  446.3 13.2 %collective-permute-start.31 = (f32[1,48,3072]{2,1,0:T(8,128)}, f32[1,48,3072]{2,1,0:T(8,128)}, u32[]{:S(2)}, u32[]{:S(2)}) collective-permute-start(f32[1,48,3072]{2,1,0:T(8,128)} %slice_select_fusion.4), channel_id=1, source_target_pairs={{0,1},{1,0},{2,3},{3,2},{4,5},{5,4},{6,7},{7,6},{8,9},{9,8},{10,11... | collective-permute-start | bytes 1769480 | tf_op jit(solution)/shard_map/ppermute | solution.py:759
  460.7 25.6 %collective-permute-start.32 = (f32[1,48,3072]{2,1,0:T(8,128)S(1)}, f32[1,48,3072]{2,1,0:T(8,128)S(1)}, u32[]{:S(2)}, u32[]{:S(2)}) collective-permute-start(f32[1,48,3072]{2,1,0:T(8,128)S(1)} %select_add_fusion), channel_id=1, source_target_pairs={{0,2},{1,3},{2,0},{3,1},{4,6},{5,7},{6,4},{7,5},{8,10},{9,11},{10,... | collective-permute-start | bytes 1769480 | tf_op jit(solution)/shard_map/ppermute | solution.py:759
  486.3 21.7 %collective-permute-start.36 = (f32[1,48,3072]{2,1,0:T(8,128)S(1)}, f32[1,48,3072]{2,1,0:T(8,128)S(1)}, u32[]{:S(2)}, u32[]{:S(2)}) collective-permute-start(f32[1,48,3072]{2,1,0:T(8,128)S(1)} %add.209), channel_id=1, source_target_pairs={{0,1},{1,0},{2,3},{3,2},{4,5},{5,4},{6,7},{7,6},{8,9},{9,8},{10,11... | collective-permute-start | bytes 1769480 | tf_op jit(solution)/shard_map/ppermute | solution.py:759
  486.4 15.8 %collective-permute-start.34 = (f32[8,768]{1,0:T(8,128)S(1)}, f32[8,768]{1,0:T(8,128)S(1)}, u32[]{:S(2)}, u32[]{:S(2)}) collective-permute-start(f32[8,768]{1,0:T(8,128)S(1)} %copy-done.33), channel_id=1, source_target_pairs={{0,1},{1,0},{2,3},{3,2},{4,5},{5,4},{6,7},{7,6},{8,9},{9,8},{10,11... | collective-permute-start | bytes 73736 | tf_op jit(solution)/shard_map/ppermute | solution.py:759
  502.2 4.7 collective-permute-start.35
  (41 other events, 332.6 us)
Sparse Core Ops, SparseCore 0:
  9.9 69.1 all-gather.2
  81.0 38.7 all-gather.4
  166.8 43.2 reduce-scatter.12
  212.9 43.9 reduce-scatter.14
  259.8 43.9 reduce-scatter.16
  339.5 58.2 reduce-scatter.18

commit v15 on v11

--- a/solution.py
+++ b/solution.py
@@ -27,9 +27,11 @@
     )
 
 
-def params():
+def params(fused=False):
     return pltpu.CompilerParams(
-        dimension_semantics=("arbitrary",), vmem_limit_bytes=VMEM_LIMIT
+        dimension_semantics=("arbitrary",),
+        vmem_limit_bytes=VMEM_LIMIT,
+        fuse_transposed_lhs_in_matmul=fused,
     )
 
 
@@ -349,7 +351,7 @@
         scratch_shapes=[pltpu.VMEM((total - rows + BLK, rows), F32)],
         input_output_aliases={8 + i: i for i in range(len(before))},
         cost_estimate=cost(7 * count),
-        compiler_params=params(),
+        compiler_params=params(True),
     )(q_rot, kv, kv, grad, seg_q, seg_k, cosine, sine, *before)
 
 
@@ -463,7 +465,7 @@
             jax.ShapeDtypeStruct((chips, steps, tall, width), F32),
         ],
         cost_estimate=cost(18 * steps),
-        compiler_params=params(),
+        compiler_params=params(True),
     )(chip, resid, other, cot, cot_other, gain, bias, scale, *ups, *downs, *so_far)
 
 
@@ -826,7 +828,6 @@
     ends_c = line_end(line_c)
     part_near = partial_rows(1, (dk, dv), qkv_full)
     own_part = partial_rows(2, (dq, dk, dv), qkv_full)
-    own_part, ends_c = together((own_part, ends_c))
     (sent,) = together((part_near,))
     back_near = sent + given_near
 

time: 499 us -> 503 us (level)
  Pallas kernels: 213 us -> 223 us
  starting transfers between devices: 48.6 us -> 42.7 us
    pallas_call x3, Pallas kernels: 62 us -> 71.4 us  [mlp(): pl.pallas_call(functools.partial(mlp_kernel, len(ups), len(so_far) // 2),...]
  transfers between devices with their start and end apart: 43 -> 43, of which waited for: 18 -> 18; matrix products, arithmetic and copies ran while one was open for 14% -> 15% of each run, Pallas kernels for 39% -> 40%
where the time goes in v15:
time: 503 us; the launch traced here: 499 us
  Pallas kernels  223 us (44%)
  waiting for transfers between devices  132 us (26%)
  other arithmetic  49.4 us (10%)
  starting transfers between devices  42.7 us (8%)
  local copies, waits for them, and re-layouts  32.9 us (7%)
  between operations  15.2 us (3%)
    ppermute x14, waiting for transfers between devices, body(): lax.ppermute(v, 'seq', [(i, i ^ bit) for i in range(groups)])  83.6 us
    pallas_call x3, Pallas kernels, mlp(): pl.pallas_call(functools.partial(mlp_kernel, len(ups), len(so_far) // 2),...  71.4 us
    pallas_call x2, Pallas kernels, attend_back(): pl.pallas_call(attend_back_kernel, grid=(count,), in_specs=[pl.BlockSpec(...  47.3 us
    pallas_call x2, Pallas kernels, weight_call(): pl.pallas_call(kernel, grid_spec=pltpu.PrefetchScalarGridSpec(num_scalar_...  26.6 us
    pallas_call x3, Pallas kernels, partial_rows(): pl.pallas_call(functools.partial(partial_kernel, len(grads)), grid=(model...  24.8 us
    pallas_call x1, Pallas kernels, attend(): pl.pallas_call(attend_kernel, grid=(pairs,), in_specs=[pl.BlockSpec((rows...  23.4 us
    pallas_call x1, Pallas kernels, project(): pl.pallas_call(qkv_kernel, grid=(3 * third,), in_specs=[whole((rows, mode...  21.7 us
    ppermute x1, waiting for transfers between devices, body(): near = lax.ppermute(block_input, 'seq', ahead)  18.2 us
  transfers between devices with their start and end apart: 43, of which 18 were waited for; matrix products, arithmetic and copies ran while one was open for 15% of the time, Pallas kernels for 40%

profile of v15, /device:TPU:0, one launch (start us, length us, event | category | flops | bytes accessed | tf_op | source)
XLA Modules:
  0.0 498.5 jit_solution(11436769254561860715)
XLA Ops:
  8.0 1.9 reshape.142
  11.2 2.1 select_n.149
  13.8 4.5 collective-permute-start
  26.0 18.2 %collective-permute-done.near_ref = f32[384,768]{1,0:T(8,128)S(1)} collective-permute-done((f32[384,768]{1,0:T(8,128)S(1)}, f32[384,768]{1,0:T(8,128)S(1)}, u32[]{:S(2)}, u32[]{:S(2)}) %collective-permute-start) | collective-permute-done | bytes 1179680 | tf_op jit(solution)/shard_map/ppermute | solution.py:717
  44.1 4.4 collective-permute-start.1
  48.6 4.0 collective-permute-start.2
  53.3 7.4 %fusion.7 = (f32[]{:T(128)}, f32[]{:T(128)}, f32[]{:T(128)}, f32[]{:T(128)}, f32[384,768]{1,0:T(8,128)}) fusion(f32[384,768]{1,0:T(8,128)S(1)} %copy-done.10, f32[3,384,768]{2,1,0:T(8,128)} %param.18, f32[384,768]{1,0:T(8,128)} %param.17, f32[]{:T(128)} %bitcast.5, f32[]{:T(128)} %bitcast.3, f32[]{:T(128)} %bitcast.1, f32[]{:T(128)} %bitcast), kind=kLoop, calls=%fused_computation.26 | loop fusion | flops 4423676 | bytes 7077920 | tf_op jit(solution)/shard_map/reduce_sum | solution.py:733
  61.8 11.9 %collective-permute-done.2 = s32[1,384]{1,0:T(1,128)} collective-permute-done((s32[1,384]{1,0:T(1,128)S(1)}, s32[1,384]{1,0:T(1,128)}, u32[]{:S(2)}, u32[]{:S(2)}) %collective-permute-start.2) | collective-permute-done | bytes 1568 | tf_op jit(solution)/shard_map/ppermute | solution.py:718
  73.7 4.8 collective-permute-start.3
  78.5 3.2 pad_maximum_fusion.6
  88.2 21.7 %shard_map.239 = (f32[384,768]{1,0:T(8,128)}, f32[1152,1536]{1,0:T(8,128)}, bf16[1152,768]{1,0:T(8,128)(2,1)}, bf16[1152,768]{1,0:T(8,128)(2,1)}) custom-call(f32[384,768]{1,0:T(8,128)} %copy-done.5, f32[384,768]{1,0:T(8,128)} %copy-done.3, f32[384,768]{1,0:T(8,128)} %own_ref.1, f32[1,768]{1,0:T(1,128)} %broadcast_in_dim.50.gain_ref, ...), custom_call_target="tpu_custom_call" | custom-call | flops 22000001024 | bytes 1048576 | tf_op jit(solution)/shard_map/pallas_call | solution.py:146
  111.3 23.4 %shard_map.240.att_ref = f32[384,768]{1,0:T(8,128)} custom-call(f32[384,768]{1,0:T(8,128)} %get-tuple-element.121.q_ref, f32[1152,1536]{1,0:T(8,128)} %get-tuple-element.122.k_ref.v_ref, f32[1152,1536]{1,0:T(8,128)} %get-tuple-element.122.k_ref.v_ref, s32[384,128]{1,0:T(8,128)} %broadcast_in_dim.52.segq_ref, s32[8,1152]{1,0:T(8,128)} %broadcast_in_dim.54.segk_ref), custom_call_target="tpu_custom_call" | custom-call | flops 26400000000 | bytes 1048576 | tf_op jit(solution)/shard_map/pallas_call | solution.py:238
  134.8 3.7 convolution_add_fusion.resid_ref
  140.6 3.9 collective-permute-done.12.refs_7_
  144.5 2.0 collective-permute-done.9.refs_3_
  147.6 22.7 %shard_map.241 = (f32[768,768]{1,0:T(8,128)}, f32[768,768]{1,0:T(8,128)}, f32[4,1,384,512]{3,2,1,0:T(8,128)}) custom-call(s32[1]{0:T(128)} %bitcast.13.chip_ref, f32[384,768]{1,0:T(8,128)} %copy-done.13, f32[384,768]{1,0:T(8,128)} %copy-done.42, f32[384,768]{1,0:T(8,128)} %cot_ref.7, f32[384,768]{1,0:T(8,128)} %collective-permute-done.5.cot_other_ref, ...), custom_call_target="tpu_custom_call" | custom-call | flops 19800000512 | bytes 1048576 | tf_op jit(solution)/shard_map/pallas_call | solution.py:459
  170.3 24.4 %shard_map.242 = (f32[768,768]{1,0:T(8,128)}, f32[768,768]{1,0:T(8,128)}, f32[4,1,384,512]{3,2,1,0:T(8,128)}) custom-call(s32[1]{0:T(128)} %bitcast.13.chip_ref, f32[384,768]{1,0:T(8,128)} %copy-done.13, f32[384,768]{1,0:T(8,128)} %copy-done.42, f32[384,768]{1,0:T(8,128)} %cot_ref.7, f32[384,768]{1,0:T(8,128)} %collective-permute-done.5.cot_other_ref, ...), custom_call_target="tpu_custom_call" | custom-call | flops 19800000512 | bytes 1048576 | tf_op jit(solution)/shard_map/pallas_call | solution.py:459
  194.8 24.4 %shard_map.243 = (f32[768,768]{1,0:T(8,128)}, f32[768,768]{1,0:T(8,128)}, f32[4,1,384,512]{3,2,1,0:T(8,128)}) custom-call(s32[1]{0:T(128)} %bitcast.13.chip_ref, f32[384,768]{1,0:T(8,128)} %copy-done.13, f32[384,768]{1,0:T(8,128)} %copy-done.42, f32[384,768]{1,0:T(8,128)} %cot_ref.7, f32[384,768]{1,0:T(8,128)} %collective-permute-done.5.cot_other_ref, ...), custom_call_target="tpu_custom_call" | custom-call | flops 19800000512 | bytes 1048576 | tf_op jit(solution)/shard_map/pallas_call | solution.py:459
  220.7 2.7 collective-permute-done.13.given_ref
  226.7 7.4 %shard_map.244 = (f32[384,768]{1,0:T(8,128)}, f32[384,768]{1,0:T(8,128)}, f32[8,768]{1,0:T(8,128)}) custom-call(f32[768,768]{1,0:T(8,128)} %get-tuple-element.103.part_ref, f32[384,768]{1,0:T(8,128)} %copy-done.43, f32[384,768]{1,0:T(8,128)} %copy-done.13, f32[384,768]{1,0:T(8,128)} %cot_ref.7, f32[1,768]{1,0:T(1,128)} %broadcast_in_dim.55.gain_ref, ...), custom_call_target="tpu_custom_call" | custom-call | flops 6600000000 | bytes 1048576 | tf_op jit(solution)/shard_map/pallas_call | solution.py:507
  234.1 2.2 collective-permute-done.14
  238.0 2.6 collective-permute-start.15
  240.6 23.6 %shard_map.245 = (f32[384,768]{1,0:T(8,128)}, f32[1152,768]{1,0:T(8,128)}, f32[1152,768]{1,0:T(8,128)}) custom-call(f32[384,768]{1,0:T(8,128)} %get-tuple-element.121.q_ref, f32[1152,1536]{1,0:T(8,128)} %get-tuple-element.122.k_ref.v_ref, f32[1152,1536]{1,0:T(8,128)} %get-tuple-element.122.k_ref.v_ref, f32[384,768]{1,0:T(8,128)} %get-tuple-element.123.g_ref, ...), custom_call_target="tpu_custom_call" | custom-call | flops 23100000256 | bytes 1048576 | tf_op jit(solution)/shard_map/pallas_call | solution.py:330
  265.8 1.8 collective-permute-start.17
  267.6 23.7 %shard_map.246 = (f32[384,768]{1,0:T(8,128)}, f32[1152,768]{1,0:T(8,128)}, f32[1152,768]{1,0:T(8,128)}) custom-call(f32[384,768]{1,0:T(8,128)} %get-tuple-element.121.q_ref, f32[1152,1536]{1,0:T(8,128)} %get-tuple-element.122.k_ref.v_ref, f32[1152,1536]{1,0:T(8,128)} %get-tuple-element.122.k_ref.v_ref, ...), custom_call_target="tpu_custom_call", output_to_operand_aliasing={{0}: (8, {}), {1}: (9, {}), {2}: (10, {})} | custom-call | flops 23100000256 | bytes 1048576 | tf_op jit(solution)/shard_map/pallas_call | solution.py:330
  292.7 12.7 %shard_map.247 = (f32[4,96,1536]{2,1,0:T(8,128)}, f32[4,96,1536]{2,1,0:T(8,128)}) custom-call(s32[1]{0:T(128)} %bitcast.12.core_ref, bf16[1152,768]{1,0:T(8,128)(2,1)} %get-tuple-element.96.hi_ref, bf16[1152,768]{1,0:T(8,128)(2,1)} %get-tuple-element.97.lo_ref, f32[384,768]{1,0:T(8,128)} %get-tuple-element.134.dq_ref.refs_0_, ...), custom_call_target="tpu_custom_call" | custom-call | flops 9900000256 | bytes 1048576 | tf_op jit(solution)/shard_map/pallas_call | solution.py:593
  305.4 5.8 %collective-permute-done.19 = f32[1,192,512]{2,1,0:T(8,128)S(1)} collective-permute-done((f32[1,192,512]{2,1,0:T(8,128)S(1)}, f32[1,192,512]{2,1,0:T(8,128)S(1)}, u32[]{:S(2)}, u32[]{:S(2)}) %collective-permute-start.19) | collective-permute-done | bytes 393248 | tf_op jit(solution)/shard_map/ppermute | solution.py:761
  312.6 2.0 collective-permute-start.21
  314.6 13.8 %shard_map.248 = (f32[4,96,1536]{2,1,0:T(8,128)}, f32[4,96,1536]{2,1,0:T(8,128)}) custom-call(s32[1]{0:T(128)} %bitcast.12.core_ref, bf16[1152,768]{1,0:T(8,128)(2,1)} %get-tuple-element.96.hi_ref, bf16[1152,768]{1,0:T(8,128)(2,1)} %get-tuple-element.97.lo_ref, f32[1152,768]{1,0:T(8,128)} %get-tuple-element.144.dv_ref.refs_1_.refs_2_, ...), custom_call_target="tpu_custom_call" | custom-call | flops 9900000256 | bytes 1048576 | tf_op jit(solution)/shard_map/pallas_call | solution.py:593
  329.3 2.7 collective-permute-done.21
  333.5 4.3 collective-permute-done.22
  338.2 2.4 pad_maximum_fusion
  343.2 8.0 %shard_map.249 = f32[384,768]{1,0:T(8,128)} custom-call(f32[1152,768]{1,0:T(8,128)} %get-tuple-element.153.dk_ref.refs_0_.refs_1_, f32[1152,768]{1,0:T(8,128)} %get-tuple-element.144.dv_ref.refs_1_.refs_2_, f32[768,2304]{1,0:T(8,128)} %all-gather.3.cloned.1.call-done.w_ref.refs_2_.refs_3_), custom_call_target="tpu_custom_call" | custom-call | flops 6600000000 | bytes 1048576 | tf_op jit(solution)/shard_map/pallas_call | solution.py:634
  352.6 11.0 %collective-permute-done.24 = f32[1,192,512]{2,1,0:T(8,128)S(1)} collective-permute-done((f32[1,192,512]{2,1,0:T(8,128)}, f32[1,192,512]{2,1,0:T(8,128)S(1)}, u32[]{:S(2)}, u32[]{:S(2)}) %collective-permute-start.24) | collective-permute-done | bytes 393248 | tf_op jit(solution)/shard_map/ppermute | solution.py:761
  363.6 1.8 add.195
  368.1 9.2 %shard_map.250 = f32[384,768]{1,0:T(8,128)} custom-call(f32[384,768]{1,0:T(8,128)} %get-tuple-element.134.dq_ref.refs_0_, f32[1152,768]{1,0:T(8,128)} %get-tuple-element.153.dk_ref.refs_0_.refs_1_, f32[1152,768]{1,0:T(8,128)} %get-tuple-element.144.dv_ref.refs_1_.refs_2_, f32[768,2304]{1,0:T(8,128)} %all-gather.3.cloned.1.call-done.w_ref.refs_2_.refs_3_), custom_call_target="tpu_custom_call" | custom-call | flops 6600000000 | bytes 1048576 | tf_op jit(solution)/shard_map/pallas_call | solution.py:634
  379.2 2.0 copy-done.22
  381.4 7.7 %shard_map.251 = f32[384,768]{1,0:T(8,128)} custom-call(f32[1152,768]{1,0:T(8,128)} %get-tuple-element.153.dk_ref.refs_0_.refs_1_, f32[1152,768]{1,0:T(8,128)} %get-tuple-element.144.dv_ref.refs_1_.refs_2_, f32[768,2304]{1,0:T(8,128)} %all-gather.3.cloned.1.call-done.w_ref.refs_2_.refs_3_), custom_call_target="tpu_custom_call" | custom-call | flops 6600000000 | bytes 1048576 | tf_op jit(solution)/shard_map/pallas_call | solution.py:634
  393.0 4.0 multiply_reduce_fusion.1
  400.6 2.3 collective-permute-done.27
  403.1 2.4 add.196
  409.5 5.6 %collective-permute-done.31 = f32[1,192,512]{2,1,0:T(8,128)S(1)} collective-permute-done((f32[1,192,512]{2,1,0:T(8,128)S(1)}, f32[1,192,512]{2,1,0:T(8,128)S(1)}, u32[]{:S(2)}, u32[]{:S(2)}) %collective-permute-start.31) | collective-permute-done | bytes 393248 | tf_op jit(solution)/shard_map/ppermute | solution.py:761
  418.0 9.8 %collective-permute-done.29 = f32[1,48,3072]{2,1,0:T(8,128)S(1)} collective-permute-done((f32[1,48,3072]{2,1,0:T(8,128)S(1)}, f32[1,48,3072]{2,1,0:T(8,128)S(1)}, u32[]{:S(2)}, u32[]{:S(2)}) %collective-permute-start.29) | collective-permute-done | bytes 589856 | tf_op jit(solution)/shard_map/ppermute | solution.py:761
  435.2 35.9 %collective-permute-done.30 = f32[1,48,3072]{2,1,0:T(8,128)} collective-permute-done((f32[1,48,3072]{2,1,0:T(8,128)}, f32[1,48,3072]{2,1,0:T(8,128)}, u32[]{:S(2)}, u32[]{:S(2)}) %collective-permute-start.30) | collective-permute-done | bytes 589856 | tf_op jit(solution)/shard_map/ppermute | solution.py:761
  472.5 1.9 fusion.9
  474.5 2.0 collective-permute-start.36
  476.5 2.1 collective-permute-done.34
  480.1 8.4 %collective-permute-done.35 = f32[8,768]{1,0:T(8,128)S(1)} collective-permute-done((f32[8,768]{1,0:T(8,128)S(1)}, f32[8,768]{1,0:T(8,128)S(1)}, u32[]{:S(2)}, u32[]{:S(2)}) %collective-permute-start.35) | collective-permute-done | bytes 24608 | tf_op jit(solution)/shard_map/ppermute | solution.py:761
  (241 shorter events, 72.7 us)
Async XLA Ops:
  7.2 80.5 %all-gather.3.cloned.1.call-start = ((), (), s32[]{:S(2)}) async-start(), calls=%async_computation.4 | async-start | bytes 7962624 | tf_op jit(solution)/shard_map/all_gather | solution.py:693
  7.9 126.8 %all-gather.5.cloned.1.call-start = ((), (), s32[]{:S(2)}) async-start(), calls=%async_computation.5 | async-start | bytes 2654208 | tf_op jit(solution)/shard_map/all_gather | solution.py:693
  13.3 8.9 %collective-permute-start.6 = (f32[96,1536]{1,0:T(8,128)}, f32[96,1536]{1,0:T(8,128)}, u32[]{:S(2)}, u32[]{:S(2)}) collective-permute-start(f32[96,1536]{1,0:T(8,128)} %select_n.149), channel_id=1, source_target_pairs={{0,4},{4,0},{8,12},{12,8},{16,20},{20,16},{24,28},{28,24},{1,5},{5... | collective-permute-start | bytes 1769480 | tf_op jit(solution)/shard_map/ppermute | solution.py:690
  13.8 30.4 %collective-permute-start = (f32[384,768]{1,0:T(8,128)S(1)}, f32[384,768]{1,0:T(8,128)S(1)}, u32[]{:S(2)}, u32[]{:S(2)}) collective-permute-start(f32[384,768]{1,0:T(8,128)S(1)} %copy-done), channel_id=1, source_target_pairs={{0,1},{1,2},{2,3},{4,5},{5,6},{6,7},{8,9},{9,10},{10,11},{12,13},{... | collective-permute-start | bytes 3538952 | tf_op jit(solution)/shard_map/ppermute | solution.py:717
  18.3 66.8 %collective-permute-start.10 = (f32[384,768]{1,0:T(8,128)}, f32[384,768]{1,0:T(8,128)}, u32[]{:S(2)}, u32[]{:S(2)}) collective-permute-start(f32[384,768]{1,0:T(8,128)} %refs_4_.5), channel_id=1, source_target_pairs={{0,8},{4,12},{8,0},{12,4},{16,24},{20,28},{24,16},{28,20},{1,9},{5... | collective-permute-start | bytes 3538952 | tf_op jit(solution)/shard_map/ppermute | solution.py:690
  23.4 29.3 %copy-start.10 = (f32[384,768]{1,0:T(8,128)S(1)}, f32[384,768]{1,0:T(8,128)}, u32[]{:S(2)}) copy-start(f32[384,768]{1,0:T(8,128)} %cot_ref.7) | copy-start | bytes 3538948
  23.4 29.3 %copy-start.34 = (f32[5]{0:T(128)S(1)}, f32[5]{0:T(128)}, u32[]{:S(2)}) copy-start(f32[5]{0:T(128)} %param.19) | copy-start | bytes 64
  24.5 62.2 %collective-permute-start.8 = (f32[192,1536]{1,0:T(8,128)}, f32[192,1536]{1,0:T(8,128)}, u32[]{:S(2)}, u32[]{:S(2)}) collective-permute-start(f32[192,1536]{1,0:T(8,128)} %pad_maximum_fusion.3.refs_0_), channel_id=1, source_target_pairs={{0,16},{4,20},{8,24},{12,28},{16,0},{20,4},{24,8},{28,12},{1,17},{... | collective-permute-start | bytes 3538952 | tf_op jit(solution)/shard_map/ppermute | solution.py:690
  44.1 43.0 %collective-permute-start.1 = (f32[384,768]{1,0:T(8,128)S(1)}, f32[384,768]{1,0:T(8,128)S(1)}, u32[]{:S(2)}, u32[]{:S(2)}) collective-permute-start(f32[384,768]{1,0:T(8,128)S(1)} %collective-permute-done.near_ref), channel_id=1, source_target_pairs={{0,1},{1,2},{2,3},{4,5},{5,6},{6,7},{8,9},{9,10},{10,11},{12,13},{... | collective-permute-start | bytes 3538952 | tf_op jit(solution)/shard_map/ppermute | solution.py:719
  48.6 25.1 %collective-permute-start.2 = (s32[1,384]{1,0:T(1,128)S(1)}, s32[1,384]{1,0:T(1,128)}, u32[]{:S(2)}, u32[]{:S(2)}) collective-permute-start(s32[1,384]{1,0:T(1,128)S(1)} %get-tuple-element.207), channel_id=1, source_target_pairs={{0,1},{1,2},{2,3},{4,5},{5,6},{6,7},{8,9},{9,10},{10,11},{12,13},{... | collective-permute-start | bytes 4616 | tf_op jit(solution)/shard_map/ppermute | solution.py:718
  52.6 85.8 %collective-permute-start.5 = (f32[384,768]{1,0:T(8,128)S(1)}, f32[384,768]{1,0:T(8,128)}, u32[]{:S(2)}, u32[]{:S(2)}) collective-permute-start(f32[384,768]{1,0:T(8,128)S(1)} %copy-done.10), channel_id=1, source_target_pairs={{0,4},{4,0},{8,12},{12,8},{16,20},{20,16},{24,28},{28,24},{1,5},{5... | collective-permute-start | bytes 3538952 | tf_op jit(solution)/shard_map/ppermute | solution.py:690
  52.7 170.7 %reduce-scatter.13.cloned.1.call-start = ((), (), s32[]{:S(2)}) async-start(), calls=%async_computation.6 | async-start | bytes 3932160
  73.7 9.1 %collective-permute-start.3 = (s32[1,384]{1,0:T(1,128)}, s32[1,384]{1,0:T(1,128)S(1)}, u32[]{:S(2)}, u32[]{:S(2)}) collective-permute-start(s32[1,384]{1,0:T(1,128)} %collective-permute-done.2), channel_id=1, source_target_pairs={{0,1},{1,2},{2,3},{4,5},{5,6},{6,7},{8,9},{9,10},{10,11},{12,13},{... | collective-permute-start | bytes 4616 | tf_op jit(solution)/shard_map/ppermute | solution.py:720
  82.9 57.7 %collective-permute-start.11 = (f32[384,768]{1,0:T(8,128)}, f32[384,768]{1,0:T(8,128)}, u32[]{:S(2)}, u32[]{:S(2)}) collective-permute-start(f32[384,768]{1,0:T(8,128)} %refs_4_.5), channel_id=1, source_target_pairs={{0,16},{4,20},{8,24},{12,28},{16,0},{20,4},{24,8},{28,12},{1,17},{... | collective-permute-start | bytes 3538952 | tf_op jit(solution)/shard_map/ppermute | solution.py:690
  85.1 55.5 %collective-permute-start.7 = (f32[192,1536]{1,0:T(8,128)}, f32[192,1536]{1,0:T(8,128)}, u32[]{:S(2)}, u32[]{:S(2)}) collective-permute-start(f32[192,1536]{1,0:T(8,128)} %pad_maximum_fusion.3.refs_0_), channel_id=1, source_target_pairs={{0,8},{4,12},{8,0},{12,4},{16,24},{20,28},{24,16},{28,20},{1,9},{5... | collective-permute-start | bytes 3538952 | tf_op jit(solution)/shard_map/ppermute | solution.py:690
  86.7 57.8 %collective-permute-start.12 = (f32[384,768]{1,0:T(8,128)}, f32[384,768]{1,0:T(8,128)}, u32[]{:S(2)}, u32[]{:S(2)}) collective-permute-start(f32[384,768]{1,0:T(8,128)} %collective-permute-done.10.refs_5_), channel_id=1, source_target_pairs={{0,16},{4,20},{8,24},{12,28},{16,0},{20,4},{24,8},{28,12},{1,17},{... | collective-permute-start | bytes 3538952 | tf_op jit(solution)/shard_map/ppermute | solution.py:690
  87.2 59.3 %collective-permute-start.9 = (f32[192,1536]{1,0:T(8,128)}, f32[192,1536]{1,0:T(8,128)}, u32[]{:S(2)}, u32[]{:S(2)}) collective-permute-start(f32[192,1536]{1,0:T(8,128)} %collective-permute-done.8.refs_2_), channel_id=1, source_target_pairs={{0,8},{4,12},{8,0},{12,4},{16,24},{20,28},{24,16},{28,20},{1,9},{5... | collective-permute-start | bytes 3538952 | tf_op jit(solution)/shard_map/ppermute | solution.py:690
  138.5 8.0 %collective-permute-start.4 = (f32[384,768]{1,0:T(8,128)S(1)}, f32[384,768]{1,0:T(8,128)S(1)}, u32[]{:S(2)}, u32[]{:S(2)}) collective-permute-start(f32[384,768]{1,0:T(8,128)S(1)} %convolution_add_fusion.resid_ref), channel_id=1, source_target_pairs={{0,4},{4,0},{8,12},{12,8},{16,20},{20,16},{24,28},{28,24},{1,5},{5... | collective-permute-start | bytes 3538952 | tf_op jit(solution)/shard_map/ppermute | solution.py:690
  170.3 94.0 %reduce-scatter.15.cloned.1.call-start = ((), (), s32[]{:S(2)}) async-start(), calls=%async_computation.7 | async-start | bytes 3932160
  194.7 116.6 %reduce-scatter.17.cloned.1.call-start = ((), (), s32[]{:S(2)}) async-start(), calls=%async_computation.8 | async-start | bytes 3932160
  220.5 2.9 collective-permute-start.13
  220.6 186.8 %reduce-scatter.19.cloned.1.call-start = ((), (), s32[]{:S(2)}) async-start(), calls=%async_computation.9 | async-start | bytes 5898240
  225.0 11.2 %collective-permute-start.14 = (f32[1,192,512]{2,1,0:T(8,128)S(1)}, f32[1,192,512]{2,1,0:T(8,128)S(1)}, u32[]{:S(2)}, u32[]{:S(2)}) collective-permute-start(f32[1,192,512]{2,1,0:T(8,128)S(1)} %slice_select_fusion.7), channel_id=1, source_target_pairs={{0,1},{1,0},{2,3},{3,2},{4,5},{5,4},{6,7},{7,6},{8,9},{9,8},{10,11... | collective-permute-start | bytes 1179656 | tf_op jit(solution)/shard_map/ppermute | solution.py:761
  238.0 26.2 %collective-permute-start.15 = (f32[1,192,512]{2,1,0:T(8,128)S(1)}, f32[1,192,512]{2,1,0:T(8,128)S(1)}, u32[]{:S(2)}, u32[]{:S(2)}) collective-permute-start(f32[1,192,512]{2,1,0:T(8,128)S(1)} %select_add_fusion.3), channel_id=1, source_target_pairs={{0,2},{1,3},{2,0},{3,1},{4,6},{5,7},{6,4},{7,5},{8,10},{9,11},{10,... | collective-permute-start | bytes 1179656 | tf_op jit(solution)/shard_map/ppermute | solution.py:761
  265.5 25.8 %copy-start.17 = (f32[1,1,384,512]{3,2,1,0:T(8,128)S(1)}, f32[1,1,384,512]{3,2,1,0:T(8,128)}, u32[]{:S(2)}) copy-start(f32[1,1,384,512]{3,2,1,0:T(8,128)} %reduce-scatter.15.cloned.1.call-done) | copy-start | bytes 2359300
  265.5 25.8 %collective-permute-start.16 = (f32[1,192,512]{2,1,0:T(8,128)S(1)}, f32[1,192,512]{2,1,0:T(8,128)S(1)}, u32[]{:S(2)}, u32[]{:S(2)}) collective-permute-start(f32[1,192,512]{2,1,0:T(8,128)S(1)} %slice_select_fusion.6), channel_id=1, source_target_pairs={{0,1},{1,0},{2,3},{3,2},{4,5},{5,4},{6,7},{7,6},{8,9},{9,8},{10,11... | collective-permute-start | bytes 1179656 | tf_op jit(solution)/shard_map/ppermute | solution.py:761
  265.8 25.6 %collective-permute-start.17 = (f32[1,192,512]{2,1,0:T(8,128)S(1)}, f32[1,192,512]{2,1,0:T(8,128)S(1)}, u32[]{:S(2)}, u32[]{:S(2)}) collective-permute-start(f32[1,192,512]{2,1,0:T(8,128)S(1)} %add.185), channel_id=1, source_target_pairs={{0,1},{1,0},{2,3},{3,2},{4,5},{5,4},{6,7},{7,6},{8,9},{9,8},{10,11... | collective-permute-start | bytes 1179656 | tf_op jit(solution)/shard_map/ppermute | solution.py:761
  292.4 18.9 %collective-permute-start.19 = (f32[1,192,512]{2,1,0:T(8,128)S(1)}, f32[1,192,512]{2,1,0:T(8,128)S(1)}, u32[]{:S(2)}, u32[]{:S(2)}) collective-permute-start(f32[1,192,512]{2,1,0:T(8,128)S(1)} %select_add_fusion.2), channel_id=1, source_target_pairs={{0,2},{1,3},{2,0},{3,1},{4,6},{5,7},{6,4},{7,5},{8,10},{9,11},{10,... | collective-permute-start | bytes 1179656 | tf_op jit(solution)/shard_map/ppermute | solution.py:761
  305.4 27.6 %collective-permute-start.18 = (f32[4,96,1536]{2,1,0:T(8,128)}, f32[4,96,1536]{2,1,0:T(8,128)S(1)}, u32[]{:S(2)}, u32[]{:S(2)}) collective-permute-start(f32[4,96,1536]{2,1,0:T(8,128)} %get-tuple-element.137), channel_id=1, source_target_pairs={{0,4},{4,0},{8,12},{12,8},{16,20},{20,16},{24,28},{28,24},{1,5},{5... | collective-permute-start | bytes 7077896 | tf_op jit(solution)/shard_map/ppermute | solution.py:690
  312.5 15.9 %collective-permute-start.20 = (f32[1,192,512]{2,1,0:T(8,128)S(1)}, f32[1,192,512]{2,1,0:T(8,128)S(1)}, u32[]{:S(2)}, u32[]{:S(2)}) collective-permute-start(f32[1,192,512]{2,1,0:T(8,128)S(1)} %slice_select_fusion.5), channel_id=1, source_target_pairs={{0,1},{1,0},{2,3},{3,2},{4,5},{5,4},{6,7},{7,6},{8,9},{9,8},{10,11... | collective-permute-start | bytes 1179656 | tf_op jit(solution)/shard_map/ppermute | solution.py:761
  312.6 19.4 %collective-permute-start.21 = (f32[1,192,512]{2,1,0:T(8,128)S(1)}, f32[1,192,512]{2,1,0:T(8,128)S(1)}, u32[]{:S(2)}, u32[]{:S(2)}) collective-permute-start(f32[1,192,512]{2,1,0:T(8,128)S(1)} %add.188), channel_id=1, source_target_pairs={{0,1},{1,0},{2,3},{3,2},{4,5},{5,4},{6,7},{7,6},{8,9},{9,8},{10,11... | collective-permute-start | bytes 1179656 | tf_op jit(solution)/shard_map/ppermute | solution.py:761
  333.1 4.7 collective-permute-start.22
  343.1 20.5 %collective-permute-start.24 = (f32[1,192,512]{2,1,0:T(8,128)}, f32[1,192,512]{2,1,0:T(8,128)S(1)}, u32[]{:S(2)}, u32[]{:S(2)}) collective-permute-start(f32[1,192,512]{2,1,0:T(8,128)} %select_add_fusion.1), channel_id=1, source_target_pairs={{0,2},{1,3},{2,0},{3,1},{4,6},{5,7},{6,4},{7,5},{8,10},{9,11},{10,... | collective-permute-start | bytes 1179656 | tf_op jit(solution)/shard_map/ppermute | solution.py:761
  351.2 51.9 %collective-permute-start.25 = (f32[384,768]{1,0:T(8,128)}, f32[384,768]{1,0:T(8,128)}, u32[]{:S(2)}, u32[]{:S(2)}) collective-permute-start(f32[384,768]{1,0:T(8,128)} %shard_map.249), channel_id=1, source_target_pairs={{1,0},{2,1},{3,2},{5,4},{6,5},{7,6},{9,8},{10,9},{11,10},{13,12},{... | collective-permute-start | bytes 3538952 | tf_op jit(solution)/shard_map/ppermute | solution.py:826
  381.3 10.7 %collective-permute-start.23 = (f32[384,768]{1,0:T(8,128)S(1)}, f32[384,768]{1,0:T(8,128)S(1)}, u32[]{:S(2)}, u32[]{:S(2)}) collective-permute-start(f32[384,768]{1,0:T(8,128)S(1)} %slice.139), channel_id=1, source_target_pairs={{0,4},{4,0},{8,12},{12,8},{16,20},{20,16},{24,28},{28,24},{1,5},{5... | collective-permute-start | bytes 3538952 | tf_op jit(solution)/shard_map/ppermute | solution.py:690
  397.8 1.3 collective-permute-start.26
  399.1 3.8 collective-permute-start.27
  403.0 3.8 collective-permute-start.28
  403.0 12.1 %collective-permute-start.31 = (f32[1,192,512]{2,1,0:T(8,128)S(1)}, f32[1,192,512]{2,1,0:T(8,128)S(1)}, u32[]{:S(2)}, u32[]{:S(2)}) collective-permute-start(f32[1,192,512]{2,1,0:T(8,128)S(1)} %copy-done.25), channel_id=1, source_target_pairs={{0,1},{1,0},{2,3},{3,2},{4,5},{5,4},{6,7},{7,6},{8,9},{9,8},{10,11... | collective-permute-start | bytes 1179656 | tf_op jit(solution)/shard_map/ppermute | solution.py:761
  408.7 19.0 %collective-permute-start.29 = (f32[1,48,3072]{2,1,0:T(8,128)S(1)}, f32[1,48,3072]{2,1,0:T(8,128)S(1)}, u32[]{:S(2)}, u32[]{:S(2)}) collective-permute-start(f32[1,48,3072]{2,1,0:T(8,128)S(1)} %slice_select_fusion.4), channel_id=1, source_target_pairs={{0,1},{1,0},{2,3},{3,2},{4,5},{5,4},{6,7},{7,6},{8,9},{9,8},{10,11... | collective-permute-start | bytes 1769480 | tf_op jit(solution)/shard_map/ppermute | solution.py:761
  415.4 14.6 %collective-permute-start.32 = (f32[3,96,512]{2,1,0:T(8,128)S(1)}, f32[3,96,512]{2,1,0:T(8,128)S(1)}, u32[]{:S(2)}, u32[]{:S(2)}) collective-permute-start(f32[3,96,512]{2,1,0:T(8,128)S(1)} %slice_select_fusion.2), channel_id=1, source_target_pairs={{0,4},{4,0},{8,12},{12,8},{16,20},{20,16},{24,28},{28,24},{1,5},{5... | collective-permute-start | bytes 1769480 | tf_op jit(solution)/shard_map/ppermute | solution.py:690
  416.5 55.9 %collective-permute-start.33 = (f32[384,768]{1,0:T(8,128)}, f32[384,768]{1,0:T(8,128)}, u32[]{:S(2)}, u32[]{:S(2)}) collective-permute-start(f32[384,768]{1,0:T(8,128)} %add.196), channel_id=1, source_target_pairs={{1,0},{2,1},{3,2},{5,4},{6,5},{7,6},{9,8},{10,9},{11,10},{13,12},{... | collective-permute-start | bytes 3538952 | tf_op jit(solution)/shard_map/ppermute | solution.py:856
  428.6 42.5 %collective-permute-start.30 = (f32[1,48,3072]{2,1,0:T(8,128)}, f32[1,48,3072]{2,1,0:T(8,128)}, u32[]{:S(2)}, u32[]{:S(2)}) collective-permute-start(f32[1,48,3072]{2,1,0:T(8,128)} %select_add_fusion), channel_id=1, source_target_pairs={{0,2},{1,3},{2,0},{3,1},{4,6},{5,7},{6,4},{7,5},{8,10},{9,11},{10,... | collective-permute-start | bytes 1769480 | tf_op jit(solution)/shard_map/ppermute | solution.py:761
  435.2 37.3 %copy-start.9 = (f32[384,768]{1,0:T(8,128)S(1)}, f32[384,768]{1,0:T(8,128)}, u32[]{:S(2)}) copy-start(f32[384,768]{1,0:T(8,128)} %shard_map.250) | copy-start | bytes 3538948
  435.2 37.3 %copy-start.33 = (f32[768]{0:T(1024)S(1)}, f32[768]{0:T(1024)}, u32[]{:S(2)}) copy-start(f32[768]{0:T(1024)} %param.20) | copy-start | bytes 9220
  474.4 4.2 collective-permute-start.34
  474.5 15.1 %collective-permute-start.36 = (f32[1,48,3072]{2,1,0:T(8,128)S(1)}, f32[1,48,3072]{2,1,0:T(8,128)S(1)}, u32[]{:S(2)}, u32[]{:S(2)}) collective-permute-start(f32[1,48,3072]{2,1,0:T(8,128)S(1)} %add.209), channel_id=1, source_target_pairs={{0,1},{1,0},{2,3},{3,2},{4,5},{5,4},{6,7},{7,6},{8,9},{9,8},{10,11... | collective-permute-start | bytes 1769480 | tf_op jit(solution)/shard_map/ppermute | solution.py:761
  478.6 9.8 %collective-permute-start.35 = (f32[8,768]{1,0:T(8,128)S(1)}, f32[8,768]{1,0:T(8,128)S(1)}, u32[]{:S(2)}, u32[]{:S(2)}) collective-permute-start(f32[8,768]{1,0:T(8,128)S(1)} %add.212), channel_id=1, source_target_pairs={{0,2},{1,3},{2,0},{3,1},{4,6},{5,7},{6,4},{7,5},{8,10},{9,11},{10,... | collective-permute-start | bytes 73736 | tf_op jit(solution)/shard_map/ppermute | solution.py:761
  (39 other events, 311.8 us)
Sparse Core Ops, SparseCore 0:
  9.9 69.1 all-gather.2
  81.0 38.7 all-gather.4
  170.4 43.2 reduce-scatter.12
  216.5 43.9 reduce-scatter.14
  263.3 43.9 reduce-scatter.16
  340.8 55.1 reduce-scatter.18

commit v16 on v11

--- a/solution.py
+++ b/solution.py
@@ -826,7 +826,6 @@
     ends_c = line_end(line_c)
     part_near = partial_rows(1, (dk, dv), qkv_full)
     own_part = partial_rows(2, (dq, dk, dv), qkv_full)
-    own_part, ends_c = together((own_part, ends_c))
     (sent,) = together((part_near,))
     back_near = sent + given_near
 

time: 499 us -> 500 us (level)
  waiting for transfers between devices: 134 us -> 128 us
    ppermute x14, waiting for transfers between devices: 84.8 us -> 78.6 us  [body(): lax.ppermute(v, 'seq', [(i, i ^ bit) for i in range(groups)])]
  transfers between devices with their start and end apart: 43 -> 43, of which waited for: 18 -> 18; matrix products, arithmetic and copies ran while one was open for 14% -> 15% of each run, Pallas kernels for 39% -> 39%
where the time goes in v16:
time: 500 us; the launch traced here: 495 us
  Pallas kernels  213 us (43%)
  waiting for transfers between devices  128 us (26%)
  starting transfers between devices  52.9 us (11%)
  other arithmetic  49.4 us (10%)
  local copies, waits for them, and re-layouts  32.4 us (6%)
  between operations  15.2 us (3%)
    ppermute x14, waiting for transfers between devices, body(): lax.ppermute(v, 'seq', [(i, i ^ bit) for i in range(groups)])  78.6 us
    pallas_call x3, Pallas kernels, mlp(): pl.pallas_call(functools.partial(mlp_kernel, len(ups), len(so_far) // 2),...  62 us
    pallas_call x2, Pallas kernels, attend_back(): pl.pallas_call(attend_back_kernel, grid=(count,), in_specs=[pl.BlockSpec(...  47.3 us
    pallas_call x2, Pallas kernels, weight_call(): pl.pallas_call(kernel, grid_spec=pltpu.PrefetchScalarGridSpec(num_scalar_...  26.4 us
    pallas_call x3, Pallas kernels, partial_rows(): pl.pallas_call(functools.partial(partial_kernel, len(grads)), grid=(model...  25.3 us
    pallas_call x1, Pallas kernels, attend(): pl.pallas_call(attend_kernel, grid=(pairs,), in_specs=[pl.BlockSpec((rows...  23.1 us
    pallas_call x1, Pallas kernels, project(): pl.pallas_call(qkv_kernel, grid=(3 * third,), in_specs=[whole((rows, mode...  21.7 us
    ppermute x14, starting transfers between devices, body(): lax.ppermute(v, 'seq', [(i, i ^ bit) for i in range(groups)])  19.8 us
  transfers between devices with their start and end apart: 43, of which 18 were waited for; matrix products, arithmetic and copies ran while one was open for 15% of the time, Pallas kernels for 39%

profile of v16, /device:TPU:0, one launch (start us, length us, event | category | flops | bytes accessed | tf_op | source)
XLA Modules:
  0.0 495.3 jit_solution(79406281349066888)
XLA Ops:
  8.0 1.9 reshape.142
  11.2 2.1 select_n.149
  13.8 4.5 collective-permute-start
  26.0 18.2 %collective-permute-done.near_ref = f32[384,768]{1,0:T(8,128)S(1)} collective-permute-done((f32[384,768]{1,0:T(8,128)S(1)}, f32[384,768]{1,0:T(8,128)S(1)}, u32[]{:S(2)}, u32[]{:S(2)}) %collective-permute-start) | collective-permute-done | bytes 1179680 | tf_op jit(solution)/shard_map/ppermute | solution.py:715
  44.1 4.4 collective-permute-start.1
  48.6 4.0 collective-permute-start.2
  53.3 7.4 %fusion.7 = (f32[]{:T(128)}, f32[]{:T(128)}, f32[]{:T(128)}, f32[]{:T(128)}, f32[384,768]{1,0:T(8,128)}) fusion(f32[384,768]{1,0:T(8,128)S(1)} %copy-done.10, f32[3,384,768]{2,1,0:T(8,128)} %param.18, f32[384,768]{1,0:T(8,128)} %param.17, f32[]{:T(128)} %bitcast.5, f32[]{:T(128)} %bitcast.3, f32[]{:T(128)} %bitcast.1, f32[]{:T(128)} %bitcast), kind=kLoop, calls=%fused_computation.26 | loop fusion | flops 4423676 | bytes 7077920 | tf_op jit(solution)/shard_map/reduce_sum | solution.py:731
  61.8 11.9 %collective-permute-done.2 = s32[1,384]{1,0:T(1,128)} collective-permute-done((s32[1,384]{1,0:T(1,128)S(1)}, s32[1,384]{1,0:T(1,128)}, u32[]{:S(2)}, u32[]{:S(2)}) %collective-permute-start.2) | collective-permute-done | bytes 1568 | tf_op jit(solution)/shard_map/ppermute | solution.py:716
  73.7 5.0 %collective-permute-start.3 = (s32[1,384]{1,0:T(1,128)}, s32[1,384]{1,0:T(1,128)S(1)}, u32[]{:S(2)}, u32[]{:S(2)}) collective-permute-start(s32[1,384]{1,0:T(1,128)} %collective-permute-done.2), channel_id=1, source_target_pairs={{0,1},{1,2},{2,3},{4,5},{5,6},{6,7},{8,9},{9,10},{10,11},{12,13},{... | collective-permute-start | bytes 4616 | tf_op jit(solution)/shard_map/ppermute | solution.py:718
  78.8 3.2 pad_maximum_fusion.6
  88.4 21.7 %shard_map.239 = (f32[384,768]{1,0:T(8,128)}, f32[1152,1536]{1,0:T(8,128)}, bf16[1152,768]{1,0:T(8,128)(2,1)}, bf16[1152,768]{1,0:T(8,128)(2,1)}) custom-call(f32[384,768]{1,0:T(8,128)} %copy-done.5, f32[384,768]{1,0:T(8,128)} %copy-done.3, f32[384,768]{1,0:T(8,128)} %own_ref.1, f32[1,768]{1,0:T(1,128)} %broadcast_in_dim.50.gain_ref, ...), custom_call_target="tpu_custom_call" | custom-call | flops 22000001024 | bytes 1048576 | tf_op jit(solution)/shard_map/pallas_call | solution.py:144
  111.5 23.1 %shard_map.240.att_ref = f32[384,768]{1,0:T(8,128)} custom-call(f32[384,768]{1,0:T(8,128)} %get-tuple-element.121.q_ref, f32[1152,1536]{1,0:T(8,128)} %get-tuple-element.122.k_ref.v_ref, f32[1152,1536]{1,0:T(8,128)} %get-tuple-element.122.k_ref.v_ref, s32[384,128]{1,0:T(8,128)} %broadcast_in_dim.52.segq_ref, s32[8,1152]{1,0:T(8,128)} %broadcast_in_dim.54.segk_ref), custom_call_target="tpu_custom_call" | custom-call | flops 26400000000 | bytes 1048576 | tf_op jit(solution)/shard_map/pallas_call | solution.py:236
  134.7 3.7 convolution_add_fusion.resid_ref
  140.5 4.3 collective-permute-done.12.refs_7_
  144.7 2.0 collective-permute-done.9.refs_3_
  147.8 19.9 %shard_map.241 = (f32[768,768]{1,0:T(8,128)}, f32[768,768]{1,0:T(8,128)}, f32[4,1,384,512]{3,2,1,0:T(8,128)}) custom-call(s32[1]{0:T(128)} %bitcast.13.chip_ref, f32[384,768]{1,0:T(8,128)} %copy-done.13, f32[384,768]{1,0:T(8,128)} %copy-done.42, f32[384,768]{1,0:T(8,128)} %cot_ref.7, f32[384,768]{1,0:T(8,128)} %collective-permute-done.5.cot_other_ref, ...), custom_call_target="tpu_custom_call" | custom-call | flops 19800000512 | bytes 1048576 | tf_op jit(solution)/shard_map/pallas_call | solution.py:457
  167.7 20.9 %shard_map.242 = (f32[768,768]{1,0:T(8,128)}, f32[768,768]{1,0:T(8,128)}, f32[4,1,384,512]{3,2,1,0:T(8,128)}) custom-call(s32[1]{0:T(128)} %bitcast.13.chip_ref, f32[384,768]{1,0:T(8,128)} %copy-done.13, f32[384,768]{1,0:T(8,128)} %copy-done.42, f32[384,768]{1,0:T(8,128)} %cot_ref.7, f32[384,768]{1,0:T(8,128)} %collective-permute-done.5.cot_other_ref, ...), custom_call_target="tpu_custom_call" | custom-call | flops 19800000512 | bytes 1048576 | tf_op jit(solution)/shard_map/pallas_call | solution.py:457
  188.9 21.2 %shard_map.243 = (f32[768,768]{1,0:T(8,128)}, f32[768,768]{1,0:T(8,128)}, f32[4,1,384,512]{3,2,1,0:T(8,128)}) custom-call(s32[1]{0:T(128)} %bitcast.13.chip_ref, f32[384,768]{1,0:T(8,128)} %copy-done.13, f32[384,768]{1,0:T(8,128)} %copy-done.42, f32[384,768]{1,0:T(8,128)} %cot_ref.7, f32[384,768]{1,0:T(8,128)} %collective-permute-done.5.cot_other_ref, ...), custom_call_target="tpu_custom_call" | custom-call | flops 19800000512 | bytes 1048576 | tf_op jit(solution)/shard_map/pallas_call | solution.py:457
  211.9 2.5 collective-permute-done.13.given_ref
  217.7 7.7 %shard_map.244 = (f32[384,768]{1,0:T(8,128)}, f32[384,768]{1,0:T(8,128)}, f32[8,768]{1,0:T(8,128)}) custom-call(f32[768,768]{1,0:T(8,128)} %get-tuple-element.103.part_ref, f32[384,768]{1,0:T(8,128)} %copy-done.43, f32[384,768]{1,0:T(8,128)} %copy-done.13, f32[384,768]{1,0:T(8,128)} %cot_ref.7, f32[1,768]{1,0:T(1,128)} %broadcast_in_dim.55.gain_ref, ...), custom_call_target="tpu_custom_call" | custom-call | flops 6600000000 | bytes 1048576 | tf_op jit(solution)/shard_map/pallas_call | solution.py:505
  225.4 1.8 collective-permute-done.14
  229.0 2.6 collective-permute-start.15
  231.6 23.6 %shard_map.245 = (f32[384,768]{1,0:T(8,128)}, f32[1152,768]{1,0:T(8,128)}, f32[1152,768]{1,0:T(8,128)}) custom-call(f32[384,768]{1,0:T(8,128)} %get-tuple-element.121.q_ref, f32[1152,1536]{1,0:T(8,128)} %get-tuple-element.122.k_ref.v_ref, f32[1152,1536]{1,0:T(8,128)} %get-tuple-element.122.k_ref.v_ref, f32[384,768]{1,0:T(8,128)} %get-tuple-element.123.g_ref, ...), custom_call_target="tpu_custom_call" | custom-call | flops 23100000256 | bytes 1048576 | tf_op jit(solution)/shard_map/pallas_call | solution.py:328
  255.3 2.6 reduce-scatter.15.cloned.1.call-done
  261.2 23.7 %shard_map.246 = (f32[384,768]{1,0:T(8,128)}, f32[1152,768]{1,0:T(8,128)}, f32[1152,768]{1,0:T(8,128)}) custom-call(f32[384,768]{1,0:T(8,128)} %get-tuple-element.121.q_ref, f32[1152,1536]{1,0:T(8,128)} %get-tuple-element.122.k_ref.v_ref, f32[1152,1536]{1,0:T(8,128)} %get-tuple-element.122.k_ref.v_ref, ...), custom_call_target="tpu_custom_call", output_to_operand_aliasing={{0}: (8, {}), {1}: (9, {}), {2}: (10, {})} | custom-call | flops 23100000256 | bytes 1048576 | tf_op jit(solution)/shard_map/pallas_call | solution.py:328
  286.0 2.4 collective-permute-start.19
  288.4 12.8 %shard_map.247 = (f32[4,96,1536]{2,1,0:T(8,128)}, f32[4,96,1536]{2,1,0:T(8,128)}) custom-call(s32[1]{0:T(128)} %bitcast.12.core_ref, bf16[1152,768]{1,0:T(8,128)(2,1)} %get-tuple-element.96.hi_ref, bf16[1152,768]{1,0:T(8,128)(2,1)} %get-tuple-element.97.lo_ref, f32[384,768]{1,0:T(8,128)} %get-tuple-element.134.dq_ref.refs_0_, ...), custom_call_target="tpu_custom_call" | custom-call | flops 9900000256 | bytes 1048576 | tf_op jit(solution)/shard_map/pallas_call | solution.py:591
  301.1 4.5 collective-permute-done.19
  309.0 13.6 %shard_map.248 = (f32[4,96,1536]{2,1,0:T(8,128)}, f32[4,96,1536]{2,1,0:T(8,128)}) custom-call(s32[1]{0:T(128)} %bitcast.12.core_ref, bf16[1152,768]{1,0:T(8,128)(2,1)} %get-tuple-element.96.hi_ref, bf16[1152,768]{1,0:T(8,128)(2,1)} %get-tuple-element.97.lo_ref, f32[1152,768]{1,0:T(8,128)} %get-tuple-element.144.dv_ref.refs_1_.refs_2_, ...), custom_call_target="tpu_custom_call" | custom-call | flops 9900000256 | bytes 1048576 | tf_op jit(solution)/shard_map/pallas_call | solution.py:591
  323.5 2.0 collective-permute-done.21
  326.8 4.3 collective-permute-done.22
  331.5 2.4 pad_maximum_fusion
  336.4 3.1 collective-permute-start.24
  339.6 8.0 %shard_map.249 = f32[384,768]{1,0:T(8,128)} custom-call(f32[1152,768]{1,0:T(8,128)} %get-tuple-element.153.dk_ref.refs_0_.refs_1_, f32[1152,768]{1,0:T(8,128)} %get-tuple-element.144.dv_ref.refs_1_.refs_2_, f32[768,2304]{1,0:T(8,128)} %all-gather.3.cloned.1.call-done.w_ref.refs_2_.refs_3_), custom_call_target="tpu_custom_call" | custom-call | flops 6600000000 | bytes 1048576 | tf_op jit(solution)/shard_map/pallas_call | solution.py:632
  349.0 9.1 %collective-permute-done.24 = f32[1,192,512]{2,1,0:T(8,128)S(1)} collective-permute-done((f32[1,192,512]{2,1,0:T(8,128)}, f32[1,192,512]{2,1,0:T(8,128)S(1)}, u32[]{:S(2)}, u32[]{:S(2)}) %collective-permute-start.24) | collective-permute-done | bytes 393248 | tf_op jit(solution)/shard_map/ppermute | solution.py:759
  362.6 9.2 %shard_map.250 = f32[384,768]{1,0:T(8,128)} custom-call(f32[384,768]{1,0:T(8,128)} %get-tuple-element.134.dq_ref.refs_0_, f32[1152,768]{1,0:T(8,128)} %get-tuple-element.153.dk_ref.refs_0_.refs_1_, f32[1152,768]{1,0:T(8,128)} %get-tuple-element.144.dv_ref.refs_1_.refs_2_, f32[768,2304]{1,0:T(8,128)} %all-gather.3.cloned.1.call-done.w_ref.refs_2_.refs_3_), custom_call_target="tpu_custom_call" | custom-call | flops 6600000000 | bytes 1048576 | tf_op jit(solution)/shard_map/pallas_call | solution.py:632
  375.4 8.1 %shard_map.251 = f32[384,768]{1,0:T(8,128)} custom-call(f32[1152,768]{1,0:T(8,128)} %get-tuple-element.153.dk_ref.refs_0_.refs_1_, f32[1152,768]{1,0:T(8,128)} %get-tuple-element.144.dv_ref.refs_1_.refs_2_, f32[768,2304]{1,0:T(8,128)} %all-gather.3.cloned.1.call-done.w_ref.refs_2_.refs_3_), custom_call_target="tpu_custom_call" | custom-call | flops 6600000000 | bytes 1048576 | tf_op jit(solution)/shard_map/pallas_call | solution.py:632
  387.4 4.1 multiply_reduce_fusion.1
  395.2 2.1 collective-permute-done.27
  399.2 2.4 add.196
  403.5 1.9 collective-permute-start.29
  405.4 5.6 %collective-permute-done.31 = f32[1,192,512]{2,1,0:T(8,128)S(1)} collective-permute-done((f32[1,192,512]{2,1,0:T(8,128)S(1)}, f32[1,192,512]{2,1,0:T(8,128)S(1)}, u32[]{:S(2)}, u32[]{:S(2)}) %collective-permute-start.31) | collective-permute-done | bytes 393248 | tf_op jit(solution)/shard_map/ppermute | solution.py:759
  413.9 9.8 %collective-permute-done.29 = f32[1,48,3072]{2,1,0:T(8,128)S(1)} collective-permute-done((f32[1,48,3072]{2,1,0:T(8,128)S(1)}, f32[1,48,3072]{2,1,0:T(8,128)S(1)}, u32[]{:S(2)}, u32[]{:S(2)}) %collective-permute-start.29) | collective-permute-done | bytes 589856 | tf_op jit(solution)/shard_map/ppermute | solution.py:759
  432.6 35.0 %collective-permute-done.30 = f32[1,48,3072]{2,1,0:T(8,128)} collective-permute-done((f32[1,48,3072]{2,1,0:T(8,128)}, f32[1,48,3072]{2,1,0:T(8,128)}, u32[]{:S(2)}, u32[]{:S(2)}) %collective-permute-start.30) | collective-permute-done | bytes 589856 | tf_op jit(solution)/shard_map/ppermute | solution.py:759
  468.9 1.9 fusion.9
  470.9 2.0 collective-permute-start.36
  473.0 2.1 collective-permute-done.34
  476.5 8.7 %collective-permute-done.35 = f32[8,768]{1,0:T(8,128)S(1)} collective-permute-done((f32[8,768]{1,0:T(8,128)S(1)}, f32[8,768]{1,0:T(8,128)S(1)}, u32[]{:S(2)}, u32[]{:S(2)}) %collective-permute-start.35) | collective-permute-done | bytes 24608 | tf_op jit(solution)/shard_map/ppermute | solution.py:759
  (241 shorter events, 80.9 us)
Async XLA Ops:
  7.2 80.8 %all-gather.3.cloned.1.call-start = ((), (), s32[]{:S(2)}) async-start(), calls=%async_computation.4 | async-start | bytes 7962624 | tf_op jit(solution)/shard_map/all_gather | solution.py:691
  7.9 126.8 %all-gather.5.cloned.1.call-start = ((), (), s32[]{:S(2)}) async-start(), calls=%async_computation.5 | async-start | bytes 2654208 | tf_op jit(solution)/shard_map/all_gather | solution.py:691
  13.3 8.9 %collective-permute-start.6 = (f32[96,1536]{1,0:T(8,128)}, f32[96,1536]{1,0:T(8,128)}, u32[]{:S(2)}, u32[]{:S(2)}) collective-permute-start(f32[96,1536]{1,0:T(8,128)} %select_n.149), channel_id=1, source_target_pairs={{0,4},{4,0},{8,12},{12,8},{16,20},{20,16},{24,28},{28,24},{1,5},{5... | collective-permute-start | bytes 1769480 | tf_op jit(solution)/shard_map/ppermute | solution.py:688
  13.8 30.4 %collective-permute-start = (f32[384,768]{1,0:T(8,128)S(1)}, f32[384,768]{1,0:T(8,128)S(1)}, u32[]{:S(2)}, u32[]{:S(2)}) collective-permute-start(f32[384,768]{1,0:T(8,128)S(1)} %copy-done), channel_id=1, source_target_pairs={{0,1},{1,2},{2,3},{4,5},{5,6},{6,7},{8,9},{9,10},{10,11},{12,13},{... | collective-permute-start | bytes 3538952 | tf_op jit(solution)/shard_map/ppermute | solution.py:715
  18.3 67.0 %collective-permute-start.10 = (f32[384,768]{1,0:T(8,128)}, f32[384,768]{1,0:T(8,128)}, u32[]{:S(2)}, u32[]{:S(2)}) collective-permute-start(f32[384,768]{1,0:T(8,128)} %refs_4_.5), channel_id=1, source_target_pairs={{0,8},{4,12},{8,0},{12,4},{16,24},{20,28},{24,16},{28,20},{1,9},{5... | collective-permute-start | bytes 3538952 | tf_op jit(solution)/shard_map/ppermute | solution.py:688
  23.4 29.3 %copy-start.10 = (f32[384,768]{1,0:T(8,128)S(1)}, f32[384,768]{1,0:T(8,128)}, u32[]{:S(2)}) copy-start(f32[384,768]{1,0:T(8,128)} %cot_ref.7) | copy-start | bytes 3538948
  23.4 29.3 %copy-start.34 = (f32[5]{0:T(128)S(1)}, f32[5]{0:T(128)}, u32[]{:S(2)}) copy-start(f32[5]{0:T(128)} %param.19) | copy-start | bytes 64
  24.5 62.4 %collective-permute-start.8 = (f32[192,1536]{1,0:T(8,128)}, f32[192,1536]{1,0:T(8,128)}, u32[]{:S(2)}, u32[]{:S(2)}) collective-permute-start(f32[192,1536]{1,0:T(8,128)} %pad_maximum_fusion.3.refs_0_), channel_id=1, source_target_pairs={{0,16},{4,20},{8,24},{12,28},{16,0},{20,4},{24,8},{28,12},{1,17},{... | collective-permute-start | bytes 3538952 | tf_op jit(solution)/shard_map/ppermute | solution.py:688
  44.1 43.3 %collective-permute-start.1 = (f32[384,768]{1,0:T(8,128)S(1)}, f32[384,768]{1,0:T(8,128)S(1)}, u32[]{:S(2)}, u32[]{:S(2)}) collective-permute-start(f32[384,768]{1,0:T(8,128)S(1)} %collective-permute-done.near_ref), channel_id=1, source_target_pairs={{0,1},{1,2},{2,3},{4,5},{5,6},{6,7},{8,9},{9,10},{10,11},{12,13},{... | collective-permute-start | bytes 3538952 | tf_op jit(solution)/shard_map/ppermute | solution.py:717
  48.6 25.1 %collective-permute-start.2 = (s32[1,384]{1,0:T(1,128)S(1)}, s32[1,384]{1,0:T(1,128)}, u32[]{:S(2)}, u32[]{:S(2)}) collective-permute-start(s32[1,384]{1,0:T(1,128)S(1)} %get-tuple-element.207), channel_id=1, source_target_pairs={{0,1},{1,2},{2,3},{4,5},{5,6},{6,7},{8,9},{9,10},{10,11},{12,13},{... | collective-permute-start | bytes 4616 | tf_op jit(solution)/shard_map/ppermute | solution.py:716
  52.6 85.8 %collective-permute-start.5 = (f32[384,768]{1,0:T(8,128)S(1)}, f32[384,768]{1,0:T(8,128)}, u32[]{:S(2)}, u32[]{:S(2)}) collective-permute-start(f32[384,768]{1,0:T(8,128)S(1)} %copy-done.10), channel_id=1, source_target_pairs={{0,4},{4,0},{8,12},{12,8},{16,20},{20,16},{24,28},{28,24},{1,5},{5... | collective-permute-start | bytes 3538952 | tf_op jit(solution)/shard_map/ppermute | solution.py:688
  52.7 161.8 %reduce-scatter.13.cloned.1.call-start = ((), (), s32[]{:S(2)}) async-start(), calls=%async_computation.6 | async-start | bytes 3932160
  73.7 9.4 %collective-permute-start.3 = (s32[1,384]{1,0:T(1,128)}, s32[1,384]{1,0:T(1,128)S(1)}, u32[]{:S(2)}, u32[]{:S(2)}) collective-permute-start(s32[1,384]{1,0:T(1,128)} %collective-permute-done.2), channel_id=1, source_target_pairs={{0,1},{1,2},{2,3},{4,5},{5,6},{6,7},{8,9},{9,10},{10,11},{12,13},{... | collective-permute-start | bytes 4616 | tf_op jit(solution)/shard_map/ppermute | solution.py:718
  83.1 57.4 %collective-permute-start.11 = (f32[384,768]{1,0:T(8,128)}, f32[384,768]{1,0:T(8,128)}, u32[]{:S(2)}, u32[]{:S(2)}) collective-permute-start(f32[384,768]{1,0:T(8,128)} %refs_4_.5), channel_id=1, source_target_pairs={{0,16},{4,20},{8,24},{12,28},{16,0},{20,4},{24,8},{28,12},{1,17},{... | collective-permute-start | bytes 3538952 | tf_op jit(solution)/shard_map/ppermute | solution.py:688
  85.3 55.1 %collective-permute-start.7 = (f32[192,1536]{1,0:T(8,128)}, f32[192,1536]{1,0:T(8,128)}, u32[]{:S(2)}, u32[]{:S(2)}) collective-permute-start(f32[192,1536]{1,0:T(8,128)} %pad_maximum_fusion.3.refs_0_), channel_id=1, source_target_pairs={{0,8},{4,12},{8,0},{12,4},{16,24},{20,28},{24,16},{28,20},{1,9},{5... | collective-permute-start | bytes 3538952 | tf_op jit(solution)/shard_map/ppermute | solution.py:688
  86.9 57.8 %collective-permute-start.12 = (f32[384,768]{1,0:T(8,128)}, f32[384,768]{1,0:T(8,128)}, u32[]{:S(2)}, u32[]{:S(2)}) collective-permute-start(f32[384,768]{1,0:T(8,128)} %collective-permute-done.10.refs_5_), channel_id=1, source_target_pairs={{0,16},{4,20},{8,24},{12,28},{16,0},{20,4},{24,8},{28,12},{1,17},{... | collective-permute-start | bytes 3538952 | tf_op jit(solution)/shard_map/ppermute | solution.py:688
  87.4 59.3 %collective-permute-start.9 = (f32[192,1536]{1,0:T(8,128)}, f32[192,1536]{1,0:T(8,128)}, u32[]{:S(2)}, u32[]{:S(2)}) collective-permute-start(f32[192,1536]{1,0:T(8,128)} %collective-permute-done.8.refs_2_), channel_id=1, source_target_pairs={{0,8},{4,12},{8,0},{12,4},{16,24},{20,28},{24,16},{28,20},{1,9},{5... | collective-permute-start | bytes 3538952 | tf_op jit(solution)/shard_map/ppermute | solution.py:688
  138.4 8.3 %collective-permute-start.4 = (f32[384,768]{1,0:T(8,128)S(1)}, f32[384,768]{1,0:T(8,128)S(1)}, u32[]{:S(2)}, u32[]{:S(2)}) collective-permute-start(f32[384,768]{1,0:T(8,128)S(1)} %convolution_add_fusion.resid_ref), channel_id=1, source_target_pairs={{0,4},{4,0},{8,12},{12,8},{16,20},{20,16},{24,28},{28,24},{1,5},{5... | collective-permute-start | bytes 3538952 | tf_op jit(solution)/shard_map/ppermute | solution.py:688
  167.7 90.2 %reduce-scatter.15.cloned.1.call-start = ((), (), s32[]{:S(2)}) async-start(), calls=%async_computation.7 | async-start | bytes 3932160
  188.7 117.0 %reduce-scatter.17.cloned.1.call-start = ((), (), s32[]{:S(2)}) async-start(), calls=%async_computation.8 | async-start | bytes 3932160
  211.5 2.9 collective-permute-start.13
  211.6 190.6 %reduce-scatter.19.cloned.1.call-start = ((), (), s32[]{:S(2)}) async-start(), calls=%async_computation.9 | async-start | bytes 5898240
  216.0 11.2 %collective-permute-start.14 = (f32[1,192,512]{2,1,0:T(8,128)S(1)}, f32[1,192,512]{2,1,0:T(8,128)S(1)}, u32[]{:S(2)}, u32[]{:S(2)}) collective-permute-start(f32[1,192,512]{2,1,0:T(8,128)S(1)} %slice_select_fusion.7), channel_id=1, source_target_pairs={{0,1},{1,0},{2,3},{3,2},{4,5},{5,4},{6,7},{7,6},{8,9},{9,8},{10,11... | collective-permute-start | bytes 1179656 | tf_op jit(solution)/shard_map/ppermute | solution.py:759
  229.0 26.2 %collective-permute-start.15 = (f32[1,192,512]{2,1,0:T(8,128)S(1)}, f32[1,192,512]{2,1,0:T(8,128)S(1)}, u32[]{:S(2)}, u32[]{:S(2)}) collective-permute-start(f32[1,192,512]{2,1,0:T(8,128)S(1)} %select_add_fusion.3), channel_id=1, source_target_pairs={{0,2},{1,3},{2,0},{3,1},{4,6},{5,7},{6,4},{7,5},{8,10},{9,11},{10,... | collective-permute-start | bytes 1179656 | tf_op jit(solution)/shard_map/ppermute | solution.py:759
  259.1 25.8 %copy-start.17 = (f32[1,1,384,512]{3,2,1,0:T(8,128)S(1)}, f32[1,1,384,512]{3,2,1,0:T(8,128)}, u32[]{:S(2)}) copy-start(f32[1,1,384,512]{3,2,1,0:T(8,128)} %reduce-scatter.15.cloned.1.call-done) | copy-start | bytes 2359300
  259.1 25.8 %collective-permute-start.16 = (f32[1,192,512]{2,1,0:T(8,128)S(1)}, f32[1,192,512]{2,1,0:T(8,128)S(1)}, u32[]{:S(2)}, u32[]{:S(2)}) collective-permute-start(f32[1,192,512]{2,1,0:T(8,128)S(1)} %slice_select_fusion.6), channel_id=1, source_target_pairs={{0,1},{1,0},{2,3},{3,2},{4,5},{5,4},{6,7},{7,6},{8,9},{9,8},{10,11... | collective-permute-start | bytes 1179656 | tf_op jit(solution)/shard_map/ppermute | solution.py:759
  260.6 24.4 %collective-permute-start.17 = (f32[1,192,512]{2,1,0:T(8,128)S(1)}, f32[1,192,512]{2,1,0:T(8,128)S(1)}, u32[]{:S(2)}, u32[]{:S(2)}) collective-permute-start(f32[1,192,512]{2,1,0:T(8,128)S(1)} %add.185), channel_id=1, source_target_pairs={{0,1},{1,0},{2,3},{3,2},{4,5},{5,4},{6,7},{7,6},{8,9},{9,8},{10,11... | collective-permute-start | bytes 1179656 | tf_op jit(solution)/shard_map/ppermute | solution.py:759
  286.0 19.6 %collective-permute-start.19 = (f32[1,192,512]{2,1,0:T(8,128)S(1)}, f32[1,192,512]{2,1,0:T(8,128)S(1)}, u32[]{:S(2)}, u32[]{:S(2)}) collective-permute-start(f32[1,192,512]{2,1,0:T(8,128)S(1)} %select_add_fusion.2), channel_id=1, source_target_pairs={{0,2},{1,3},{2,0},{3,1},{4,6},{5,7},{6,4},{7,5},{8,10},{9,11},{10,... | collective-permute-start | bytes 1179656 | tf_op jit(solution)/shard_map/ppermute | solution.py:759
  301.1 25.3 %collective-permute-start.18 = (f32[4,96,1536]{2,1,0:T(8,128)}, f32[4,96,1536]{2,1,0:T(8,128)S(1)}, u32[]{:S(2)}, u32[]{:S(2)}) collective-permute-start(f32[4,96,1536]{2,1,0:T(8,128)} %get-tuple-element.137), channel_id=1, source_target_pairs={{0,4},{4,0},{8,12},{12,8},{16,20},{20,16},{24,28},{28,24},{1,5},{5... | collective-permute-start | bytes 7077896 | tf_op jit(solution)/shard_map/ppermute | solution.py:688
  306.9 15.7 %collective-permute-start.20 = (f32[1,192,512]{2,1,0:T(8,128)S(1)}, f32[1,192,512]{2,1,0:T(8,128)S(1)}, u32[]{:S(2)}, u32[]{:S(2)}) collective-permute-start(f32[1,192,512]{2,1,0:T(8,128)S(1)} %slice_select_fusion.5), channel_id=1, source_target_pairs={{0,1},{1,0},{2,3},{3,2},{4,5},{5,4},{6,7},{7,6},{8,9},{9,8},{10,11... | collective-permute-start | bytes 1179656 | tf_op jit(solution)/shard_map/ppermute | solution.py:759
  307.4 18.0 %collective-permute-start.21 = (f32[1,192,512]{2,1,0:T(8,128)S(1)}, f32[1,192,512]{2,1,0:T(8,128)S(1)}, u32[]{:S(2)}, u32[]{:S(2)}) collective-permute-start(f32[1,192,512]{2,1,0:T(8,128)S(1)} %add.188), channel_id=1, source_target_pairs={{0,1},{1,0},{2,3},{3,2},{4,5},{5,4},{6,7},{7,6},{8,9},{9,8},{10,11... | collective-permute-start | bytes 1179656 | tf_op jit(solution)/shard_map/ppermute | solution.py:759
  326.4 4.7 collective-permute-start.22
  336.4 21.7 %collective-permute-start.24 = (f32[1,192,512]{2,1,0:T(8,128)}, f32[1,192,512]{2,1,0:T(8,128)S(1)}, u32[]{:S(2)}, u32[]{:S(2)}) collective-permute-start(f32[1,192,512]{2,1,0:T(8,128)} %select_add_fusion.1), channel_id=1, source_target_pairs={{0,2},{1,3},{2,0},{3,1},{4,6},{5,7},{6,4},{7,5},{8,10},{9,11},{10,... | collective-permute-start | bytes 1179656 | tf_op jit(solution)/shard_map/ppermute | solution.py:759
  347.6 51.6 %collective-permute-start.25 = (f32[384,768]{1,0:T(8,128)}, f32[384,768]{1,0:T(8,128)}, u32[]{:S(2)}, u32[]{:S(2)}) collective-permute-start(f32[384,768]{1,0:T(8,128)} %shard_map.249), channel_id=1, source_target_pairs={{1,0},{2,1},{3,2},{5,4},{6,5},{7,6},{9,8},{10,9},{11,10},{13,12},{... | collective-permute-start | bytes 3538952 | tf_op jit(solution)/shard_map/ppermute | solution.py:824
  375.3 11.0 %collective-permute-start.23 = (f32[384,768]{1,0:T(8,128)S(1)}, f32[384,768]{1,0:T(8,128)S(1)}, u32[]{:S(2)}, u32[]{:S(2)}) collective-permute-start(f32[384,768]{1,0:T(8,128)S(1)} %slice.139), channel_id=1, source_target_pairs={{0,4},{4,0},{8,12},{12,8},{16,20},{20,16},{24,28},{28,24},{1,5},{5... | collective-permute-start | bytes 3538952 | tf_op jit(solution)/shard_map/ppermute | solution.py:688
  392.2 1.3 collective-permute-start.26
  393.5 3.8 collective-permute-start.27
  397.3 4.3 collective-permute-start.28
  399.0 12.1 %collective-permute-start.31 = (f32[1,192,512]{2,1,0:T(8,128)S(1)}, f32[1,192,512]{2,1,0:T(8,128)S(1)}, u32[]{:S(2)}, u32[]{:S(2)}) collective-permute-start(f32[1,192,512]{2,1,0:T(8,128)S(1)} %copy-done.25), channel_id=1, source_target_pairs={{0,1},{1,0},{2,3},{3,2},{4,5},{5,4},{6,7},{7,6},{8,9},{9,8},{10,11... | collective-permute-start | bytes 1179656 | tf_op jit(solution)/shard_map/ppermute | solution.py:759
  403.5 20.2 %collective-permute-start.29 = (f32[1,48,3072]{2,1,0:T(8,128)S(1)}, f32[1,48,3072]{2,1,0:T(8,128)S(1)}, u32[]{:S(2)}, u32[]{:S(2)}) collective-permute-start(f32[1,48,3072]{2,1,0:T(8,128)S(1)} %slice_select_fusion.4), channel_id=1, source_target_pairs={{0,1},{1,0},{2,3},{3,2},{4,5},{5,4},{6,7},{7,6},{8,9},{9,8},{10,11... | collective-permute-start | bytes 1769480 | tf_op jit(solution)/shard_map/ppermute | solution.py:759
  411.3 16.0 %collective-permute-start.32 = (f32[3,96,512]{2,1,0:T(8,128)S(1)}, f32[3,96,512]{2,1,0:T(8,128)S(1)}, u32[]{:S(2)}, u32[]{:S(2)}) collective-permute-start(f32[3,96,512]{2,1,0:T(8,128)S(1)} %slice_select_fusion.2), channel_id=1, source_target_pairs={{0,4},{4,0},{8,12},{12,8},{16,20},{20,16},{24,28},{28,24},{1,5},{5... | collective-permute-start | bytes 1769480 | tf_op jit(solution)/shard_map/ppermute | solution.py:688
  412.5 56.4 %collective-permute-start.33 = (f32[384,768]{1,0:T(8,128)}, f32[384,768]{1,0:T(8,128)}, u32[]{:S(2)}, u32[]{:S(2)}) collective-permute-start(f32[384,768]{1,0:T(8,128)} %add.196), channel_id=1, source_target_pairs={{1,0},{2,1},{3,2},{5,4},{6,5},{7,6},{9,8},{10,9},{11,10},{13,12},{... | collective-permute-start | bytes 3538952 | tf_op jit(solution)/shard_map/ppermute | solution.py:854
  424.6 43.0 %collective-permute-start.30 = (f32[1,48,3072]{2,1,0:T(8,128)}, f32[1,48,3072]{2,1,0:T(8,128)}, u32[]{:S(2)}, u32[]{:S(2)}) collective-permute-start(f32[1,48,3072]{2,1,0:T(8,128)} %select_add_fusion), channel_id=1, source_target_pairs={{0,2},{1,3},{2,0},{3,1},{4,6},{5,7},{6,4},{7,5},{8,10},{9,11},{10,... | collective-permute-start | bytes 1769480 | tf_op jit(solution)/shard_map/ppermute | solution.py:759
  432.5 36.3 %copy-start.9 = (f32[384,768]{1,0:T(8,128)S(1)}, f32[384,768]{1,0:T(8,128)}, u32[]{:S(2)}) copy-start(f32[384,768]{1,0:T(8,128)} %shard_map.250) | copy-start | bytes 3538948
  432.6 36.3 %copy-start.33 = (f32[768]{0:T(1024)S(1)}, f32[768]{0:T(1024)}, u32[]{:S(2)}) copy-start(f32[768]{0:T(1024)} %param.20) | copy-start | bytes 9220
  470.9 4.2 collective-permute-start.34
  470.9 15.4 %collective-permute-start.36 = (f32[1,48,3072]{2,1,0:T(8,128)S(1)}, f32[1,48,3072]{2,1,0:T(8,128)S(1)}, u32[]{:S(2)}, u32[]{:S(2)}) collective-permute-start(f32[1,48,3072]{2,1,0:T(8,128)S(1)} %add.209), channel_id=1, source_target_pairs={{0,1},{1,0},{2,3},{3,2},{4,5},{5,4},{6,7},{7,6},{8,9},{9,8},{10,11... | collective-permute-start | bytes 1769480 | tf_op jit(solution)/shard_map/ppermute | solution.py:759
  475.1 10.1 %collective-permute-start.35 = (f32[8,768]{1,0:T(8,128)S(1)}, f32[8,768]{1,0:T(8,128)S(1)}, u32[]{:S(2)}, u32[]{:S(2)}) collective-permute-start(f32[8,768]{1,0:T(8,128)S(1)} %add.212), channel_id=1, source_target_pairs={{0,2},{1,3},{2,0},{3,1},{4,6},{5,7},{6,4},{7,5},{8,10},{9,11},{10,... | collective-permute-start | bytes 73736 | tf_op jit(solution)/shard_map/ppermute | solution.py:759
  (39 other events, 313.1 us)
Sparse Core Ops, SparseCore 0:
  9.9 69.1 all-gather.2
  81.0 38.7 all-gather.4
  167.8 43.2 reduce-scatter.12
  213.9 43.9 reduce-scatter.14
  260.7 43.9 reduce-scatter.16
  334.1 58.0 reduce-scatter.18
